TPU v7x, 32 devices: a whole 2x2x4 slice. The times are simulated.
32 devices in a mesh: dp: 8 (over z, x), mp: 4 (over y, core).
Axes of the slice: x: 2, y: 2, z: 4, core: 2. Of those that a mesh axis runs over, the one named last changes fastest.
Arguments:
- tokens: bfloat16 [8192, 768], P(('dp', 'mp')), may hold values from -6 to 6
- norm_gain: float32 [768], replicated, may hold values from 0.5 to 1.5
- w_query: bfloat16 [768, 768], P('dp', 'mp'), may hold values from -0.21875 to 0.21875
- w_key: bfloat16 [768, 768], P('dp', 'mp'), may hold values from -0.21875 to 0.21875
- w_value: bfloat16 [768, 768], P('dp', 'mp'), may hold values from -0.21875 to 0.21875
- w_output: bfloat16 [768, 768], P('mp', 'dp'), may hold values from -1.75 to 1.75
- bias_table: float32 [32, 12], P(None, 'mp'), may hold values from -6 to 6
- ffn_gain: float32 [768], replicated, may hold values from 0.5 to 1.5
- w_router: bfloat16 [768, 8], replicated, may hold values from -0.15625 to 0.15625
- w_in: bfloat16 [8, 768, 3072], P('dp'), may hold values from -0.21875 to 0.21875
- w_out: bfloat16 [8, 3072, 768], P('dp'), may hold values from -2 to 2
- segments: int32 [8, 1024], P('dp'), may hold values from 0 to 3, never falling along the last dimension, each value on 1 to 512 neighbouring positions
- buckets: int32 [1024], replicated, may hold values from 0 to 31
- routes: int32 [8192, 2], P(('dp', 'mp')), may hold values from 0 to 7, all different within a row; in each aligned block of 256 rows (0 to 255, 256 to 511, ...) at most 128 rows name the same one
- cotangent: bfloat16 [8192, 768], P(('dp', 'mp')), may hold values from -6 to 6
Outputs:
- block_out: bfloat16 [8192, 768], P(('dp', 'mp'))
- tokens_grad: bfloat16 [8192, 768], P(('dp', 'mp'))
- norm_gain_grad: float32 [768], replicated
- w_query_grad: float32 [768, 768], P('dp', 'mp')
- w_key_grad: float32 [768, 768], P('dp', 'mp')
- w_value_grad: float32 [768, 768], P('dp', 'mp')
- w_output_grad: float32 [768, 768], P('mp', 'dp')
- bias_table_grad: float32 [32, 12], replicated
- ffn_gain_grad: float32 [768], replicated
- w_router_grad: float32 [768, 8], replicated
- w_in_grad: float32 [8, 768, 3072], P('dp', None, 'mp')
- w_out_grad: float32 [8, 3072, 768], P('dp', 'mp')
Inputs may be any that keep to these rules, and one draw needn't show every extreme that they name: `routes`: in the rows of one device each expert is named at most 128 times, a bound that some block reaches; the two experts of a row differ. `segments`: within each sequence the numbers never fall; each document has at most 512 positions and one has exactly that many.
All inputs are finite; a program needn't handle non-finite values.
Results may differ from a plain program's by a relative error of at most 0.017.
Values may be sent and summed in bfloat16 or wider, within the bound.
No kernel may reach another device: no remote copies, remote signals or barrier semaphores. Data moves between devices by JAX's collectives and lax.ppermute only.
A program may use at most 192 MiB of HBM per device.

v0:
```python
import math

import jax
import jax.numpy as jnp
from jax import lax
from jax.sharding import PartitionSpec as P

eps = 1e-06
highest = lax.Precision.HIGHEST


def normalize(values, gain):
    inverse = lax.rsqrt(jnp.mean(values * values, axis=-1, keepdims=True) + eps)
    return (values * inverse * gain, inverse)


def norm_backward(values, inverse, gain, grad):
    scaled = grad * gain
    gain_grad = jnp.sum(grad * values * inverse, axis=0)
    inner = jnp.mean(scaled * values, axis=-1, keepdims=True)
    return (inverse * scaled - values * inverse * inverse * inverse * inner, gain_grad)


def gelu(values):
    return 0.5 * values * (1.0 + lax.erf(values * math.sqrt(0.5)))


def gelu_slope(values):
    return 0.5 * (1.0 + lax.erf(values * math.sqrt(0.5))) + values * jnp.exp(
        -0.5 * values * values
    ) / math.sqrt(2.0 * math.pi)


def one_hot(values, count):
    return (values[:, None] == jnp.arange(count, dtype=jnp.int32)[None, :]).astype(jnp.float32)


def toeplitz_bias(bias_rows, offset, block):
    heads, seq_len = bias_rows.shape
    stride = seq_len + block
    place = jnp.arange(stride, dtype=jnp.int32)
    source = jnp.where(place < seq_len, offset - place, offset + stride - place)
    source = jnp.clip(source, 0, seq_len - 1)
    line = jnp.take(bias_rows, source, axis=1)
    tiled = jnp.broadcast_to(line[:, None, :], (heads, block, stride)).reshape(
        heads, block * stride
    )
    skewed = tiled[:, : block * (stride - 1)].reshape(heads, block, stride - 1)
    return skewed[:, :, :seq_len]


def block_scores(query, key_rows, value_rows, seg_ids, bias_rows, start, block, heads):
    seq_len = bias_rows.shape[1]
    head_dim = query.shape[1] // heads
    base = start // seq_len * seq_len
    part_q = lax.dynamic_slice_in_dim(query, start, block, 0).reshape(block, heads, head_dim)
    part_k = key_rows.reshape(seq_len, heads, head_dim)
    part_v = value_rows.reshape(seq_len, heads, head_dim)
    raw = jnp.einsum(
        "qhd,khd->hqk", part_q, part_k, preferred_element_type=jnp.float32
    ) * head_dim ** (-0.5)
    place = start - base + jnp.arange(block, dtype=jnp.int32)
    distance = place[:, None] - jnp.arange(seq_len, dtype=jnp.int32)[None, :]
    bias = toeplitz_bias(bias_rows, start - base, block)
    seg_q = lax.dynamic_slice_in_dim(seg_ids, start, block, 0)
    allowed = (distance >= 0) & (seg_q[:, None] == seg_ids[None, :])
    scores = jnp.where(allowed[None], raw + bias, -1e30)
    return (scores, part_q, part_k, part_v, base)


def diagonal_sums(grad, offset, seq_len):
    heads, block, _ = grad.shape
    flipped = jnp.flip(grad, axis=2)
    padded = jnp.pad(flipped, ((0, 0), (0, 0), (0, block)))
    stride = seq_len + block
    skewed = padded.reshape(heads, block * stride)[:, : block * (stride - 1)].reshape(
        heads, block, stride - 1
    )
    totals = jnp.sum(skewed, axis=1)
    totals = jnp.pad(totals, ((0, 0), (0, seq_len - block)))
    return lax.dynamic_slice_in_dim(totals, seq_len - 1 - offset, seq_len, 1)


def on_device(
    tokens,
    norm_gain,
    w_query,
    w_key,
    w_value,
    w_output,
    bias_table,
    ffn_gain,
    w_router,
    w_in,
    w_out,
    segments,
    buckets,
    routes,
    cotangent,
):
    rows, width = tokens.shape
    heads = bias_table.shape[1]
    seq_len = buckets.shape[0]
    experts = w_router.shape[1]
    owners = lax.axis_size("dp")
    capacity = 4 * rows // experts
    resid = tokens.astype(jnp.float32)
    normed, inverse_one = normalize(resid, norm_gain)
    grouped = lax.all_gather(normed.astype(jnp.bfloat16), "mp", axis=0, tiled=True)
    group_rows = grouped.shape[0]
    weight_q, weight_k, weight_v, weight_o = (
        lax.all_gather(w_query, "dp", axis=0, tiled=True),
        lax.all_gather(w_key, "dp", axis=0, tiled=True),
        lax.all_gather(w_value, "dp", axis=0, tiled=True),
        lax.all_gather(w_output, "dp", axis=1, tiled=True),
    )
    span = weight_q.shape[1]
    scale = (span // heads) ** (-0.5)
    joined = jnp.concatenate([weight_q, weight_k, weight_v], axis=1)
    projected = jnp.dot(grouped, joined, preferred_element_type=jnp.float32).astype(jnp.bfloat16)
    query = projected[:, :span]
    key_rows = projected[:, span : 2 * span]
    value_rows = projected[:, 2 * span :]
    bucket_hot = one_hot(buckets, bias_table.shape[0])
    bias_rows = jnp.dot(bucket_hot, bias_table, precision=highest).T
    seg_ids = segments.reshape(-1)
    block = min(512, seq_len)
    starts = jnp.arange(group_rows // block, dtype=jnp.int32) * block

    def forward_block(start):
        scores, part_q, part_k, part_v, base = block_scores(
            query, key_rows, value_rows, seg_ids, bias_rows, start, block, heads
        )
        peak_row = jnp.max(scores, axis=-1, keepdims=True)
        powers = jnp.exp(scores - peak_row)
        row_total = jnp.sum(powers, axis=-1, keepdims=True)
        probs = (powers / row_total).astype(jnp.bfloat16)
        mixed_part = jnp.einsum("hqk,khd->qhd", probs, part_v, preferred_element_type=jnp.float32)
        return (mixed_part.reshape(block, span), peak_row + jnp.log(row_total))

    mixed, log_total = lax.map(forward_block, starts)
    mixed = mixed.reshape(group_rows, span).astype(jnp.bfloat16)
    attended = lax.psum_scatter(
        jnp.dot(mixed, weight_o, preferred_element_type=jnp.float32),
        "mp",
        scatter_dimension=0,
        tiled=True,
    )
    hidden = resid + attended
    normed_two, inverse_two = normalize(hidden, ffn_gain)
    ffn_input = normed_two.astype(jnp.bfloat16)
    logits = jnp.dot(ffn_input, w_router, preferred_element_type=jnp.float32)
    shifted = jnp.exp(logits - jnp.max(logits, axis=-1, keepdims=True))
    router_probs = shifted / jnp.sum(shifted, axis=-1, keepdims=True)
    gates = jnp.take_along_axis(router_probs, routes, axis=1)
    route_flat = routes.reshape(-1)
    hits = (route_flat[:, None] == jnp.arange(experts, dtype=jnp.int32)[None, :]).astype(jnp.int32)
    ranks = jnp.sum((jnp.cumsum(hits, axis=0) - 1) * hits, axis=1)
    slots = route_flat * capacity + ranks
    slot_owner = (
        jnp.zeros((experts * capacity,), jnp.int32)
        .at[slots]
        .set(jnp.arange(2 * rows, dtype=jnp.int32) + 1)
    )
    slot_token = jnp.where(slot_owner > 0, (slot_owner - 1) // 2 + 1, 0)
    padded_input = jnp.concatenate([jnp.zeros((1, width), jnp.bfloat16), ffn_input], axis=0)
    send_rows = jnp.take(padded_input, slot_token, axis=0).reshape(owners, capacity, width)
    arrived = lax.all_to_all(send_rows, "dp", split_axis=0, concat_axis=0, tiled=True).reshape(
        -1, width
    )
    pre_act = jnp.dot(arrived, w_in[0], preferred_element_type=jnp.float32)
    active = gelu(pre_act).astype(jnp.bfloat16)
    result = jnp.dot(active, w_out[0], preferred_element_type=jnp.float32).astype(jnp.bfloat16)
    returned = lax.all_to_all(
        result.reshape(owners, capacity, width), "dp", split_axis=0, concat_axis=0, tiled=True
    ).reshape(-1, width)
    picked = jnp.take(returned, slots, axis=0).astype(jnp.float32).reshape(rows, 2, width)
    block_out = (hidden + jnp.sum(gates[:, :, None] * picked, axis=1)).astype(jnp.bfloat16)
    out_grad = cotangent.astype(jnp.float32)
    gate_grad = jnp.sum(out_grad[:, None, :] * picked, axis=2)
    slot_grad = (
        (gates[:, :, None] * out_grad[:, None, :]).astype(jnp.bfloat16).reshape(2 * rows, width)
    )
    padded_grad = jnp.concatenate([jnp.zeros((1, width), jnp.bfloat16), slot_grad], axis=0)
    grad_send = jnp.take(padded_grad, slot_owner, axis=0).reshape(owners, capacity, width)
    grad_arrived = lax.all_to_all(grad_send, "dp", split_axis=0, concat_axis=0, tiled=True).reshape(
        -1, width
    )
    active_grad = jnp.einsum(
        "rd,fd->rf", grad_arrived, w_out[0], preferred_element_type=jnp.float32
    )
    pre_grad = (active_grad * gelu_slope(pre_act)).astype(jnp.bfloat16)
    back_rows = jnp.einsum(
        "rf,df->rd", pre_grad, w_in[0], preferred_element_type=jnp.float32
    ).astype(jnp.bfloat16)
    rows_all, grads_all = (
        lax.all_gather(arrived, "mp", axis=0, tiled=True),
        lax.all_gather(grad_arrived, "mp", axis=0, tiled=True),
    )
    active_part, pre_grad_part = (
        lax.all_to_all(active, "mp", split_axis=1, concat_axis=0, tiled=True),
        lax.all_to_all(pre_grad, "mp", split_axis=1, concat_axis=0, tiled=True),
    )
    w_in_grad = jnp.einsum(
        "rd,rf->df", rows_all, pre_grad_part, preferred_element_type=jnp.float32
    )[None]
    w_out_grad = jnp.einsum(
        "rf,rd->fd", active_part, grads_all, preferred_element_type=jnp.float32
    )[None]
    grad_back = lax.all_to_all(
        back_rows.reshape(owners, capacity, width), "dp", split_axis=0, concat_axis=0, tiled=True
    ).reshape(-1, width)
    expert_grad = jnp.sum(
        jnp.take(grad_back, slots, axis=0).astype(jnp.float32).reshape(rows, 2, width), axis=1
    )
    expert_ids = jnp.arange(experts, dtype=jnp.int32)[None, :]
    prob_grad = (routes[:, 0:1] == expert_ids).astype(jnp.float32) * gate_grad[:, 0:1]
    prob_grad = prob_grad + (routes[:, 1:2] == expert_ids).astype(jnp.float32) * gate_grad[:, 1:2]
    logit_grad = router_probs * (
        prob_grad - jnp.sum(router_probs * prob_grad, axis=-1, keepdims=True)
    )
    router_weight = w_router.astype(jnp.float32)
    ffn_input_grad = expert_grad + jnp.dot(logit_grad, router_weight.T, precision=highest)
    router_grad = jnp.dot(ffn_input.astype(jnp.float32).T, logit_grad, precision=highest)
    hidden_part, ffn_gain_grad = norm_backward(hidden, inverse_two, ffn_gain, ffn_input_grad)
    hidden_grad = out_grad + hidden_part
    attn_grad = hidden_grad.astype(jnp.bfloat16)
    grad_group = lax.all_gather(attn_grad, "mp", axis=0, tiled=True)
    mixed_grad = jnp.einsum(
        "td,cd->tc", grad_group, weight_o, preferred_element_type=jnp.float32
    ).astype(jnp.bfloat16)
    output_grad = jnp.einsum("tc,td->cd", mixed, grad_group, preferred_element_type=jnp.float32)

    def backward_block(carry, item):
        key_grad, value_grad, bias_grad = carry
        start, log_block = item
        scores, part_q, part_k, part_v, base = block_scores(
            query, key_rows, value_rows, seg_ids, bias_rows, start, block, heads
        )
        probs = jnp.exp(scores - log_block)
        out_part = lax.dynamic_slice_in_dim(mixed_grad, start, block, 0).reshape(part_q.shape)
        dot_grad = jnp.einsum("qhd,khd->hqk", out_part, part_v, preferred_element_type=jnp.float32)
        score_grad = (
            probs * (dot_grad - jnp.sum(probs * dot_grad, axis=-1, keepdims=True))
        ).astype(jnp.bfloat16)
        query_part = (
            jnp.einsum("hqk,khd->qhd", score_grad, part_k, preferred_element_type=jnp.float32)
            * scale
        )
        key_part = (
            jnp.einsum("hqk,qhd->khd", score_grad, part_q, preferred_element_type=jnp.float32)
            * scale
        )
        value_part = jnp.einsum(
            "hqk,qhd->khd", probs.astype(jnp.bfloat16), out_part, preferred_element_type=jnp.float32
        )
        key_old = key_grad
        key_grad = key_old + key_part.reshape(seq_len, span)
        value_old = value_grad
        value_grad = value_old + value_part.reshape(seq_len, span)
        bias_grad = bias_grad + diagonal_sums(score_grad.astype(jnp.float32), start - base, seq_len)
        return ((key_grad, value_grad, bias_grad), query_part.reshape(block, span))

    empty_rows = jnp.zeros((group_rows, span), jnp.float32)
    empty_bias = jnp.zeros((heads, seq_len), jnp.float32)
    (key_grad, value_grad, bias_grad), query_grad = lax.scan(
        backward_block, (empty_rows, empty_rows, empty_bias), (starts, log_total)
    )
    query_grad = query_grad.reshape(group_rows, span)
    proj_grad = jnp.concatenate(
        [
            query_grad.astype(jnp.bfloat16),
            key_grad.astype(jnp.bfloat16),
            value_grad.astype(jnp.bfloat16),
        ],
        axis=1,
    )
    normed_grad = lax.psum_scatter(
        jnp.einsum("tc,dc->td", proj_grad, joined, preferred_element_type=jnp.float32).astype(
            jnp.bfloat16
        ),
        "mp",
        scatter_dimension=0,
        tiled=True,
    ).astype(jnp.float32)
    joined_grad = jnp.einsum("td,tc->dc", grouped, proj_grad, preferred_element_type=jnp.float32)
    w_query_grad, w_key_grad, w_value_grad, w_output_grad = (
        lax.psum_scatter(joined_grad[:, :span], "dp", scatter_dimension=0, tiled=True),
        lax.psum_scatter(joined_grad[:, span : 2 * span], "dp", scatter_dimension=0, tiled=True),
        lax.psum_scatter(joined_grad[:, 2 * span :], "dp", scatter_dimension=0, tiled=True),
        lax.psum_scatter(output_grad, "dp", scatter_dimension=1, tiled=True),
    )
    input_part, norm_gain_grad = norm_backward(resid, inverse_one, norm_gain, normed_grad)
    tokens_grad = (hidden_grad + input_part).astype(jnp.bfloat16)
    table_local = jnp.dot(bucket_hot.T, bias_grad.T, precision=highest)
    table_full = jnp.zeros((bias_table.shape[0], heads * lax.axis_size("mp")), jnp.float32)
    table_full = lax.dynamic_update_slice_in_dim(
        table_full, table_local, lax.axis_index("mp") * heads, 1
    )
    table_sum, router_sum, gain_sum, ffn_gain_sum = lax.psum(
        (table_full, router_grad, norm_gain_grad, ffn_gain_grad), ("dp", "mp")
    )
    return (
        block_out,
        tokens_grad,
        gain_sum,
        w_query_grad,
        w_key_grad,
        w_value_grad,
        w_output_grad,
        table_sum,
        ffn_gain_sum,
        router_sum,
        w_in_grad,
        w_out_grad,
    )


def solution(mesh):
    return jax.shard_map(
        on_device,
        mesh=mesh,
        in_specs=(
            P(("dp", "mp"), None),
            P(),
            P("dp", "mp"),
            P("dp", "mp"),
            P("dp", "mp"),
            P("mp", "dp"),
            P(None, "mp"),
            P(),
            P(),
            P("dp", None, None),
            P("dp", None, None),
            P("dp", None),
            P(),
            P(("dp", "mp"), None),
            P(("dp", "mp"), None),
        ),
        out_specs=(
            P(("dp", "mp"), None),
            P(("dp", "mp"), None),
            P(),
            P("dp", "mp"),
            P("dp", "mp"),
            P("dp", "mp"),
            P("mp", "dp"),
            P(),
            P(),
            P(),
            P("dp", None, "mp"),
            P("dp", "mp", None),
        ),
        check_vma=False,
    )
```

profile of v0, /device:TPU:0, one launch (start us, length us, event | category | flops | bytes accessed | tf_op | source)
XLA Modules:
  0.0 1370.3 jit_solution(11397872883130800885)
XLA Ops:
  14.1 33.2 %all_gather.25 = bf16[768,192]{1,0:T(8,128)(2,1)S(1)} all-gather(bf16[96,192]{1,0:T(8,128)(2,1)} %param.25), channel_id=1, replica_groups=mesh['dp'=8,'mp'=4] {'dp'}, dimensions={0}, use_global_device_ids=true | all-gather | bytes 331776 | tf_op jit(solution)/shard_map/all_gather | solution.py:112
  47.3 31.3 %all_gather.26 = bf16[768,192]{1,0:T(8,128)(2,1)S(1)} all-gather(bf16[96,192]{1,0:T(8,128)(2,1)} %param.26), channel_id=1, replica_groups=mesh['dp'=8,'mp'=4] {'dp'}, dimensions={0}, use_global_device_ids=true | all-gather | bytes 331776 | tf_op jit(solution)/shard_map/all_gather | solution.py:113
  78.6 31.2 %all_gather.27 = bf16[768,192]{1,0:T(8,128)(2,1)S(1)} all-gather(bf16[96,192]{1,0:T(8,128)(2,1)S(1)} %copy-done.48), channel_id=1, replica_groups=mesh['dp'=8,'mp'=4] {'dp'}, dimensions={0}, use_global_device_ids=true | all-gather | bytes 331776 | tf_op jit(solution)/shard_map/all_gather | solution.py:114
  109.8 33.0 %all_gather.28 = bf16[192,768]{0,1:T(8,128)(2,1)} all-gather(bf16[192,96]{0,1:T(8,128)(2,1)S(1)} %copy.58), channel_id=1, replica_groups=mesh['dp'=8,'mp'=4] {'dp'}, dimensions={1}, use_global_device_ids=true | all-gather | bytes 331776 | tf_op jit(solution)/shard_map/all_gather | solution.py:115
  146.4 165.7 %while.33 = (s32[]{:T(128)}, bf16[2,512,192]{1,2,0:T(8,128)(2,1)S(1)}, f32[2,3,512,1]{2,1,3,0:T(4,128)}, s32[2]{0:T(128)S(1)}, s32[1024]{0:T(1024)S(1)}, /*index...) while((s32[]{:T(128)}, ...), condition=%wide.region_4.6_spmd, body=%wide.region_1.5_spmd.sunk | while | flops 418940928 | bytes 113303440 | solution.py:141
  156.1 19.9 %copy.106 = f32[1,3,512,1536]{3,1,2,0:T(4,128)S(1)} copy(f32[1,3,512,1536]{3,2,1,0:T(8,128)S(1)} %broadcast_bitcast_fusion.4) | data formatting | bytes 18874368 | tf_op jit(solution)/shard_map/while
  175.9 5.9 slice.136
  181.8 13.2 reshape.572
  195.0 15.6 %reshape.573 = f32[3,512,1535]{2,1,0:T(8,128)} reshape(f32[2357760]{0:T(1024)} %reshape.572) | data formatting | bytes 18862080 | tf_op jit(solution)/shard_map/while/body/eval_jaxpr/reshape | solution.py:48
  232.3 19.9 %copy.106 = f32[1,3,512,1536]{3,1,2,0:T(4,128)S(1)} copy(f32[1,3,512,1536]{3,2,1,0:T(8,128)S(1)} %broadcast_bitcast_fusion.4) | data formatting | bytes 18874368 | tf_op jit(solution)/shard_map/while
  252.2 5.9 slice.136
  258.1 13.2 reshape.572
  271.2 15.6 %reshape.573 = f32[3,512,1535]{2,1,0:T(8,128)} reshape(f32[2357760]{0:T(1024)} %reshape.572) | data formatting | bytes 18862080 | tf_op jit(solution)/shard_map/while/body/eval_jaxpr/reshape | solution.py:48
  319.3 34.1 %reduce-scatter.15.cloned.1.call-done = f32[256,768]{1,0:T(8,128)} async-done(((f32[1024,768]{1,0:T(8,128)}), f32[256,768]{1,0:T(8,128)}) %reduce-scatter.15.cloned.1.call-update) | async-done | bytes 786448 | tf_op jit(solution)/shard_map/reduce_scatter | solution.py:143
  361.9 42.3 %all_to_all.58 = bf16[8,128,768]{2,1,0:T(8,128)(2,1)S(1)} all-to-all(bf16[8,128,768]{2,1,0:T(8,128)(2,1)S(1)} %broadcast_select_fusion.1), channel_id=1, replica_groups=mesh['dp'=8,'mp'=4] {'dp'}, dimensions={0} | all-to-all | bytes 3145728 | tf_op jit(solution)/shard_map/all_to_all | solution.py:168
  404.2 10.5 multiply_convert_fusion.1
  414.7 10.7 fusion.27
  434.8 31.0 %all-to-all-done.1 = bf16[8,128,768]{2,1,0:T(8,128)(2,1)S(1)} async-done(((bf16[8,128,768]{2,1,0:T(8,128)(2,1)}), bf16[8,128,768]{2,1,0:T(8,128)(2,1)S(1)}, u32[]{:S(2)}, u32[]{:S(2)}) %all-to-all-start.1) | async-done | bytes 1572896 | tf_op jit(solution)/shard_map/all_to_all | solution.py:174
  483.0 40.6 %all_to_all.59 = bf16[8,128,768]{2,1,0:T(8,128)(2,1)S(1)} all-to-all(bf16[8,128,768]{2,1,0:T(8,128)(2,1)S(1)} %broadcast_select_fusion), channel_id=1, replica_groups=mesh['dp'=8,'mp'=4] {'dp'}, dimensions={0} | all-to-all | bytes 3145728 | tf_op jit(solution)/shard_map/all_to_all | solution.py:186
  523.6 11.4 fusion.16
  535.0 9.7 fusion.24
  544.7 40.4 %all_to_all.60 = bf16[8,128,768]{2,1,0:T(8,128)(2,1)S(1)} all-to-all(bf16[8,128,768]{2,1,0:T(8,128)(2,1)S(1)} %bitcast.257), channel_id=1, replica_groups=mesh['dp'=8,'mp'=4] {'dp'}, dimensions={0} | all-to-all | bytes 3145728 | tf_op jit(solution)/shard_map/all_to_all | solution.py:210
  599.1 17.2 %all-gather.7.cloned.1.call-done = bf16[1024,768]{1,0:T(8,128)(2,1)} async-done(((bf16[256,768]{1,0:T(8,128)(2,1)}), bf16[1024,768]{1,0:T(8,128)(2,1)}) %all-gather.7.cloned.1.call-update) | async-done | bytes 1572880 | tf_op jit(solution)/shard_map/all_gather | solution.py:228
  621.8 405.0 %while.34 = (s32[]{:T(128)}, f32[1024,192]{0,1:T(8,128)}, f32[1024,192]{0,1:T(8,128)}, f32[3,1024]{1,0:T(4,128)}, bf16[2,512,192]{1,2,0:T(8,128)(2,1)}, /*index=...) while((s32[]{:T(128)}, f32[1024,192]{0,1:T(8,128)}, ...), condition=%wide.region_21.24_spmd.clone, body=%wide.region_18.23_spmd.clone.sunk | while | flops 1028032512 | bytes 299489536 | solution.py:266
  652.5 19.9 %copy.108 = f32[1,3,512,1536]{3,1,2,0:T(4,128)S(1)} copy(f32[1,3,512,1536]{3,2,1,0:T(8,128)S(1)} %broadcast_bitcast_fusion.5) | data formatting | bytes 18874368 | tf_op jit(solution)/shard_map/while
  672.3 5.9 slice.138
  678.2 13.2 reshape.576
  691.4 15.7 %reshape.577 = f32[3,512,1535]{2,1,0:T(8,128)} reshape(f32[2357760]{0:T(1024)} %reshape.576) | data formatting | bytes 18862080 | tf_op jit(solution)/shard_map/while/body/eval_jaxpr/reshape | solution.py:48
  722.2 34.8 %rev.9 = f32[3,512,1024]{2,1,0:T(8,128)} reverse(bf16[3,512,1024]{2,1,0:T(8,128)(2,1)S(1)} %multiply_convert_fusion.5), dimensions={2} | reverse | bytes 9437184 | tf_op jit(solution)/shard_map/while/body/eval_jaxpr/jit(_flip)/rev | solution.py:73
  761.1 19.9 %copy.109 = f32[1,3,512,1536]{3,1,2,0:T(4,128)S(1)} copy(f32[1,3,512,1536]{3,2,1,0:T(8,128)S(1)} %pad_bitcast_fusion.2) | data formatting | bytes 18874368 | tf_op jit(solution)/shard_map/while
  780.9 5.9 slice.139
  786.8 13.2 reshape.578
  800.0 15.6 %reshape.579 = f32[3,512,1535]{2,1,0:T(8,128)} reshape(f32[2357760]{0:T(1024)} %reshape.578) | data formatting | bytes 18862080 | tf_op jit(solution)/shard_map/while/body/eval_jaxpr/reshape | solution.py:76
  840.4 19.9 %copy.108 = f32[1,3,512,1536]{3,1,2,0:T(4,128)S(1)} copy(f32[1,3,512,1536]{3,2,1,0:T(8,128)S(1)} %broadcast_bitcast_fusion.5) | data formatting | bytes 18874368 | tf_op jit(solution)/shard_map/while
  860.3 5.9 slice.138
  866.1 13.2 reshape.576
  879.3 15.6 %reshape.577 = f32[3,512,1535]{2,1,0:T(8,128)} reshape(f32[2357760]{0:T(1024)} %reshape.576) | data formatting | bytes 18862080 | tf_op jit(solution)/shard_map/while/body/eval_jaxpr/reshape | solution.py:48
  910.0 34.8 %rev.9 = f32[3,512,1024]{2,1,0:T(8,128)} reverse(bf16[3,512,1024]{2,1,0:T(8,128)(2,1)S(1)} %multiply_convert_fusion.5), dimensions={2} | reverse | bytes 9437184 | tf_op jit(solution)/shard_map/while/body/eval_jaxpr/jit(_flip)/rev | solution.py:73
  948.9 19.9 %copy.109 = f32[1,3,512,1536]{3,1,2,0:T(4,128)S(1)} copy(f32[1,3,512,1536]{3,2,1,0:T(8,128)S(1)} %pad_bitcast_fusion.2) | data formatting | bytes 18874368 | tf_op jit(solution)/shard_map/while
  968.8 5.9 slice.139
  974.6 13.2 reshape.578
  987.8 15.6 %reshape.579 = f32[3,512,1535]{2,1,0:T(8,128)} reshape(f32[2357760]{0:T(1024)} %reshape.578) | data formatting | bytes 18862080 | tf_op jit(solution)/shard_map/while/body/eval_jaxpr/reshape | solution.py:76
  1050.9 107.0 %all-to-all-done.4 = bf16[1024,4,768]{2,0,1:T(8,128)(2,1)} async-done(((bf16[1024,4,768]{2,0,1:T(8,128)(2,1)}), bf16[1024,4,768]{2,0,1:T(8,128)(2,1)}, u32[]{:S(2)}, u32[]{:S(2)}) %all-to-all-start.4) | async-done | bytes 6291488 | tf_op jit(solution)/shard_map/all_to_all | solution.py:202
  1173.4 10.1 convolution_bitcast_fusion.1
  1189.6 79.5 %all-reduce.4 = (f32[768]{0:T(1024)}, f32[32,12]{0,1:T(8,128)}, f32[768]{0:T(1024)}, f32[768,8]{0,1:T(8,128)}) all-reduce(f32[768]{0:T(1024)S(1)} %get-tuple-element.481, f32[32,12]{0,1:T(8,128)S(1)} %dynamic_update_slice.23, f32[768]{0:T(1024)S(1)} %copy-done.63, f32[768,8]{0,1:T(8,128)S(1)} %fusion.51), channel_id=1, replica_groups=mesh['dp'=8,'mp'=4] {'dp','mp'}, use_global_device_ids=true, to_apply=%region_25.28 | all-reduce | flops 8064 | bytes 64512 | tf_op jit(solution)/shard_map/psum | solution.py:300
  1271.5 10.1 convolution_bitcast_fusion
  1281.6 16.0 %reduce-scatter.21.cloned.1.call-done = f32[96,192]{1,0:T(8,128)} async-done(((f32[768,192]{1,0:T(8,128)}), f32[96,192]{1,0:T(8,128)}) %reduce-scatter.21.cloned.1.call-update) | async-done | bytes 73744
  1297.7 65.5 %reduce-scatter.23.cloned.1.call-done = f32[96,192]{1,0:T(8,128)} async-done(((f32[768,192]{1,0:T(8,128)}), f32[96,192]{1,0:T(8,128)}) %reduce-scatter.23.cloned.1.call-update) | async-done | bytes 73744
  (365 shorter events, 231.7 us)
Async XLA Ops:
  7.2 427.3 %copy-start = (bf16[768,8]{0,1:T(8,128)(2,1)S(1)}, bf16[768,8]{0,1:T(8,128)(2,1)}, u32[]{:S(2)}) copy-start(bf16[768,8]{0,1:T(8,128)(2,1)} %param.31) | copy-start | bytes 36868
  7.2 71.4 %copy-start.48 = (bf16[96,192]{1,0:T(8,128)(2,1)S(1)}, bf16[96,192]{1,0:T(8,128)(2,1)}, u32[]{:S(2)}) copy-start(bf16[96,192]{1,0:T(8,128)(2,1)} %param.27) | copy-start | bytes 110596
  7.2 135.5 %all-gather.5.cloned.1.call-start = ((), (), s32[]{:S(2)}) async-start(), calls=%async_computation.12 | async-start | bytes 1966080 | tf_op jit(solution)/shard_map/all_gather | solution.py:109
  10.9 342.5 %reduce-scatter.15.cloned.1.call-start = ((), (), s32[]{:S(2)}) async-start(), calls=%async_computation.13 | async-start | bytes 3932160 | tf_op jit(solution)/shard_map/reduce_scatter | solution.py:143
  47.3 95.5 %copy-start.40 = (bf16[768,192]{1,0:T(8,128)(2,1)}, bf16[768,192]{1,0:T(8,128)(2,1)S(1)}, u32[]{:S(2)}) copy-start(bf16[768,192]{1,0:T(8,128)(2,1)S(1)} %all_gather.25) | copy-start | bytes 884740
  78.6 66.8 %copy-start.42 = (bf16[768,192]{1,0:T(8,128)(2,1)}, bf16[768,192]{1,0:T(8,128)(2,1)S(1)}, u32[]{:S(2)}) copy-start(bf16[768,192]{1,0:T(8,128)(2,1)S(1)} %all_gather.26) | copy-start | bytes 884740
  109.8 35.6 %copy-start.44 = (bf16[768,192]{1,0:T(8,128)(2,1)}, bf16[768,192]{1,0:T(8,128)(2,1)S(1)}, u32[]{:S(2)}) copy-start(bf16[768,192]{1,0:T(8,128)(2,1)S(1)} %all_gather.27) | copy-start | bytes 884740
  146.4 165.8 %copy-start.31 = (bf16[192,768]{0,1:T(8,128)(2,1)S(1)}, bf16[192,768]{0,1:T(8,128)(2,1)}, u32[]{:S(2)}) copy-start(bf16[192,768]{0,1:T(8,128)(2,1)} %all_gather.28) | copy-start | bytes 884740
  312.2 41.2 %copy-start.16 = (bf16[256,768]{1,0:T(8,128)(2,1)S(1)}, bf16[256,768]{1,0:T(8,128)(2,1)}, u32[]{:S(2)}) copy-start(bf16[256,768]{1,0:T(8,128)(2,1)} %param.23) | copy-start | bytes 1179652
  314.5 40.3 %copy-start.46 = (f32[768]{0:T(1024)S(1)}, f32[768]{0:T(1024)}, u32[]{:S(2)}) copy-start(f32[768]{0:T(1024)} %param.30) | copy-start | bytes 9220
  354.7 242.5 %copy-start.14 = (f32[256,768]{1,0:T(8,128)}, f32[256,768]{1,0:T(8,128)S(1)}, u32[]{:S(2)}) copy-start(f32[256,768]{1,0:T(8,128)S(1)} %get-tuple-element.542) | copy-start | bytes 2359300
  354.7 242.5 %copy-start.51 = (f32[256]{0:T(256)}, f32[256]{0:T(256)S(1)}, u32[]{:S(2)}) copy-start(f32[256]{0:T(256)S(1)} %add_rsqrt_fusion) | copy-start | bytes 3076
  354.9 79.6 %copy-start.26 = (bf16[256,768]{1,0:T(8,128)(2,1)}, bf16[256,768]{1,0:T(8,128)(2,1)S(1)}, u32[]{:S(2)}) copy-start(bf16[256,768]{1,0:T(8,128)(2,1)S(1)} %multiply_convert_fusion.3) | copy-start | bytes 1179652
  425.5 40.4 %all-to-all-start.1 = ((bf16[8,128,768]{2,1,0:T(8,128)(2,1)}), bf16[8,128,768]{2,1,0:T(8,128)(2,1)S(1)}, u32[]{:S(2)}, u32[]{:S(2)}) async-start(bf16[8,128,768]{2,1,0:T(8,128)(2,1)} %bitcast.256), calls=%async_computation.2 | async-start | bytes 3145728 | tf_op jit(solution)/shard_map/all_to_all | solution.py:174
  429.2 187.1 %all-gather.7.cloned.1.call-start = ((), (), s32[]{:S(2)}) async-start(), calls=%async_computation.14 | async-start | bytes 1966080 | tf_op jit(solution)/shard_map/all_gather | solution.py:228
  434.5 161.3 %copy-start.57 = (s32[256,1]{0,1:T(1,128)}, s32[256,1]{0,1:T(1,128)S(1)}, u32[]{:S(2)}) copy-start(s32[256,1]{0,1:T(1,128)S(1)} %get-tuple-element.563) | copy-start | bytes 3076
  434.5 161.3 %copy-start.59 = (s32[256,1]{0,1:T(1,128)}, s32[256,1]{0,1:T(1,128)S(1)}, u32[]{:S(2)}) copy-start(s32[256,1]{0,1:T(1,128)S(1)} %get-tuple-element.564) | copy-start | bytes 3076
  470.0 125.9 %copy-start.53 = (f32[256]{0:T(256)}, f32[256]{0:T(256)S(1)}, u32[]{:S(2)}) copy-start(f32[256]{0:T(256)S(1)} %get-tuple-element.483) | copy-start | bytes 3076
  470.0 125.9 %copy-start.55 = (f32[256]{0:T(256)}, f32[256]{0:T(256)S(1)}, u32[]{:S(2)}) copy-start(f32[256]{0:T(256)S(1)} %get-tuple-element.484) | copy-start | bytes 3076
  470.1 125.8 %copy-start.2 = (f32[256,8]{0,1:T(8,128)}, f32[256,8]{0,1:T(8,128)S(1)}, u32[]{:S(2)}) copy-start(f32[256,8]{0,1:T(8,128)S(1)} %get-tuple-element.538) | copy-start | bytes 24580
  470.1 125.8 %copy-start.64 = (f32[256]{0:T(256)}, f32[256]{0:T(256)S(1)}, u32[]{:S(2)}) copy-start(f32[256]{0:T(256)S(1)} %get-tuple-element.537) | copy-start | bytes 3076
  523.6 11.4 copy-start.23
  597.3 22.3 %copy-start.18 = (f32[256,768]{1,0:T(8,128)}, f32[256,768]{1,0:T(8,128)S(1)}, u32[]{:S(2)}) copy-start(f32[256,768]{1,0:T(8,128)S(1)} %get-tuple-element.571) | copy-start | bytes 2359300
  598.3 21.2 %copy-start.32 = (bf16[192,768]{0,1:T(8,128)(2,1)S(1)}, bf16[192,768]{0,1:T(8,128)(2,1)}, u32[]{:S(2)}) copy-start(bf16[192,768]{0,1:T(8,128)(2,1)} %all_gather.28) | copy-start | bytes 884740
  598.4 575.0 %all-gather.9.cloned.1.call-start = ((), (), s32[]{:S(2)}) async-start(), calls=%async_computation.16 | async-start | bytes 7864320 | tf_op jit(solution)/shard_map/all_gather | solution.py:197
  598.9 587.7 %reduce-scatter.25.cloned.1.call-start = ((), (), s32[]{:S(2)}) async-start(), calls=%async_computation.21 | async-start | bytes 884736
  599.0 22.8 %copy-start.6 = (bf16[1024,192]{0,1:T(8,128)(2,1)S(1)}, bf16[1024,192]{0,1:T(8,128)(2,1)}, u32[]{:S(2)}) copy-start(bf16[1024,192]{0,1:T(8,128)(2,1)} %copy-done.5) | copy-start | bytes 1179652
  599.0 22.8 %copy-start.38 = (s32[1,1024]{1,0:T(1,128)S(1)}, s32[1,1024]{1,0:T(1,128)}, u32[]{:S(2)}) copy-start(s32[1,1024]{1,0:T(1,128)} %param.34) | copy-start | bytes 12292
  619.5 568.7 %reduce-scatter.17.cloned.1.call-start = ((), (), s32[]{:S(2)}) async-start(), calls=%async_computation.15 | async-start | bytes 1966080 | tf_op jit(solution)/shard_map/reduce_scatter | solution.py:278
  1033.2 238.3 %all-gather.11.cloned.1.call-start = ((), (), s32[]{:S(2)}) async-start(), calls=%async_computation.17 | async-start | bytes 7864320 | tf_op jit(solution)/shard_map/all_gather | solution.py:198
  1039.8 118.1 %all-to-all-start.4 = ((bf16[1024,4,768]{2,0,1:T(8,128)(2,1)}), bf16[1024,4,768]{2,0,1:T(8,128)(2,1)}, u32[]{:S(2)}, u32[]{:S(2)}) async-start(bf16[1024,4,768]{2,0,1:T(8,128)(2,1)} %bitcast.242), calls=%async_computation.6 | async-start | bytes 12582912 | tf_op jit(solution)/shard_map/all_to_all | solution.py:202
  1157.9 113.6 %all-to-all-start.5 = ((bf16[1024,4,768]{2,0,1:T(8,128)(2,1)}), bf16[1024,4,768]{2,0,1:T(8,128)(2,1)}, u32[]{:S(2)}, u32[]{:S(2)}) async-start(bf16[1024,4,768]{2,0,1:T(8,128)(2,1)} %bitcast.241), calls=%async_computation.7 | async-start | bytes 12582912 | tf_op jit(solution)/shard_map/all_to_all | solution.py:201
  1163.3 118.3 %reduce-scatter.19.cloned.1.call-start = ((), (), s32[]{:S(2)}) async-start(), calls=%async_computation.18 | async-start | bytes 884736
  1166.9 130.8 %reduce-scatter.21.cloned.1.call-start = ((), (), s32[]{:S(2)}) async-start(), calls=%async_computation.19 | async-start | bytes 884736
  1173.3 189.9 %reduce-scatter.23.cloned.1.call-start = ((), (), s32[]{:S(2)}) async-start(), calls=%async_computation.20 | async-start | bytes 884736
  1173.4 12.7 copy-start.39
  1173.4 12.7 copy-start.69
  1173.4 14.9 %copy-start.17 = (bf16[256,768]{1,0:T(8,128)(2,1)S(1)}, bf16[256,768]{1,0:T(8,128)(2,1)}, u32[]{:S(2)}) copy-start(bf16[256,768]{1,0:T(8,128)(2,1)} %param.23) | copy-start | bytes 1179652
  1173.4 14.9 %copy-start.49 = (f32[768]{0:T(1024)S(1)}, f32[768]{0:T(1024)}, u32[]{:S(2)}) copy-start(f32[768]{0:T(1024)} %param.24) | copy-start | bytes 9220
  1173.4 14.9 %copy-start.62 = (f32[256]{0:T(256)S(1)}, f32[256]{0:T(256)}, u32[]{:S(2)}) copy-start(f32[256]{0:T(256)} %copy-done.61) | copy-start | bytes 3076
  1183.6 85.5 %copy-start.15 = (f32[256,768]{1,0:T(8,128)S(1)}, f32[256,768]{1,0:T(8,128)}, u32[]{:S(2)}) copy-start(f32[256,768]{1,0:T(8,128)} %copy-done.14) | copy-start | bytes 2359300
  1183.6 85.5 %copy-start.19 = (f32[256,768]{1,0:T(8,128)S(1)}, f32[256,768]{1,0:T(8,128)}, u32[]{:S(2)}) copy-start(f32[256,768]{1,0:T(8,128)} %copy-done.18) | copy-start | bytes 2359300
  1183.6 85.5 %copy-start.30 = (bf16[256,768]{1,0:T(8,128)(2,1)S(1)}, bf16[256,768]{1,0:T(8,128)(2,1)}, u32[]{:S(2)}) copy-start(bf16[256,768]{1,0:T(8,128)(2,1)} %param.37) | copy-start | bytes 1179652
  1183.6 85.5 %copy-start.34 = (f32[256,768]{1,0:T(8,128)S(1)}, f32[256,768]{1,0:T(8,128)}, u32[]{:S(2)}) copy-start(f32[256,768]{1,0:T(8,128)} %multiply_reduce_fusion.2) | copy-start | bytes 2359300
  1183.6 85.5 %copy-start.47 = (f32[768]{0:T(1024)S(1)}, f32[768]{0:T(1024)}, u32[]{:S(2)}) copy-start(f32[768]{0:T(1024)} %param.30) | copy-start | bytes 9220
  1183.6 85.5 %copy-start.52 = (f32[256]{0:T(256)S(1)}, f32[256]{0:T(256)}, u32[]{:S(2)}) copy-start(f32[256]{0:T(256)} %copy-done.51) | copy-start | bytes 3076
  1183.6 85.5 %copy-start.67 = (f32[256]{0:T(256)S(1)}, f32[256]{0:T(256)}, u32[]{:S(2)}) copy-start(f32[256]{0:T(256)} %copy-done.66) | copy-start | bytes 3076
  1271.5 91.7 %copy-start.1 = (bf16[768,8]{0,1:T(8,128)(2,1)S(1)}, bf16[768,8]{0,1:T(8,128)(2,1)}, u32[]{:S(2)}) copy-start(bf16[768,8]{0,1:T(8,128)(2,1)} %param.31) | copy-start | bytes 36868
  (43 other events, 145.9 us)
Sparse Core Ops, SparseCore 0:
  11.0 22.3 all-gather.4
  314.6 38.7 reduce-scatter.14
  598.5 17.6 all-gather.6
  617.7 46.3 all-gather.8
  667.6 62.4 reduce-scatter.24
  1033.4 36.6 reduce-scatter.16
  1071.7 80.1 all-gather.10
  1168.4 63.8 reduce-scatter.18
  1236.1 61.4 reduce-scatter.20
  1301.8 61.4 reduce-scatter.22
where the time goes:
time: 1380 us; the launch traced here: 1370 us
  local copies, waits for them, and re-layouts  504 us (37%)
  blocking collectives  331 us (24%)
  waiting for transfers between devices  272 us (20%)
  matrix products  120 us (9%)
  loops' own time  61.4 us (4%)
  other arithmetic  51.3 us (4%)
  between operations  15.5 us (1%)
  starting transfers between devices  14.8 us (1%)
    while x50, local copies, waits for them, and re-layouts  220 us
    all_to_all x1, waiting for transfers between devices, on_device(): lax.all_to_all(pre_grad, 'mp', split_axis=1, concat_axis=0, tiled=True)  107 us
    unnamed x14, waiting for transfers between devices  83 us
    psum x1, blocking collectives, on_device(): lax.psum((table_full, router_grad, norm_gain_grad, ffn_gain_grad), ('dp',...  79.5 us
    rev x2, local copies, waits for them, and re-layouts, diagonal_sums(): flipped = jnp.flip(grad, axis=2)  69.7 us
    reshape x4, local copies, waits for them, and re-layouts, toeplitz_bias(): skewed = tiled[:, :block * (stride - 1)].reshape(heads, block, stride - 1)  62.5 us
    all_to_all x1, blocking collectives, on_device(): lax.all_to_all(send_rows, 'dp', split_axis=0, concat_axis=0, tiled=True)  42.3 us
    all_to_all x1, blocking collectives, on_device(): lax.all_to_all(grad_send, 'dp', split_axis=0, concat_axis=0, tiled=True)  40.6 us
  transfers between devices with their start and end apart: 13, of which 6 were waited for; matrix products, arithmetic and copies ran while one was open for 32% of the time, Pallas kernels for 0%

commit v1 on v0

v1 whole, which is shorter than its diff:
```python
import functools
import math

import jax
import jax.numpy as jnp
from jax import lax
from jax.experimental import pallas as pl
from jax.experimental.pallas import tpu as pltpu
from jax.sharding import PartitionSpec as P

eps = 1e-06
highest = lax.Precision.HIGHEST
f32, bf16 = jnp.float32, jnp.bfloat16
excluded = -1e30
reach = 512
tile = 128


def normalize(values, gain):
    inverse = lax.rsqrt(jnp.mean(values * values, axis=-1, keepdims=True) + eps)
    return (values * inverse * gain, inverse)


def dot(left, right, left_dim, right_dim, precision=None):
    return lax.dot_general(
        left,
        right,
        (((left_dim,), (right_dim,)), ((), ())),
        precision=precision,
        preferred_element_type=f32,
    )


def swap(values, axis, step):
    count = lax.axis_size(axis)
    return lax.ppermute(values, axis, [(i, i ^ step) for i in range(count)])


def call(kernel, name, operands, outs, scratch=(), flops=0, limit=32, scalars=None):
    vmem = pl.BlockSpec(memory_space=pltpu.VMEM)
    in_specs = [vmem] * len(operands)
    if scalars is not None:
        operands = [scalars] + list(operands)
        in_specs = [pl.BlockSpec(memory_space=pltpu.SMEM)] + in_specs
    moved = sum(math.prod(o.shape) * o.dtype.itemsize for o in operands)
    moved += sum(math.prod(o.shape) * o.dtype.itemsize for o in outs)
    return pl.pallas_call(
        kernel,
        name=name,
        in_specs=in_specs,
        out_specs=[vmem] * len(outs),
        out_shape=outs,
        scratch_shapes=list(scratch),
        compiler_params=pltpu.CompilerParams(vmem_limit_bytes=limit * 1024 * 1024),
        cost_estimate=pl.CostEstimate(
            flops=int(flops), bytes_accessed=int(moved), transcendentals=0
        ),
    )(*operands)


def shape(dims, dtype):
    return jax.ShapeDtypeStruct(tuple(dims), dtype)


def fill_skew(line_ref, skew, heads):
    window = reach + tile
    row = lax.broadcasted_iota(jnp.int32, (tile, window), 0)
    column = lax.broadcasted_iota(jnp.int32, (tile, window), 1)
    usable = (column - row <= reach) & (column - row >= 1)
    for head in range(heads):
        line = jnp.broadcast_to(line_ref[head : head + 1, :], (tile, window))
        rolled = pltpu.roll(line, 0, 1, stride=1, stride_axis=0)
        skew[head * tile : (head + 1) * tile, :] = jnp.where(usable, rolled, excluded)


def fill_window(source_ref, padded):
    padded[:reach, :] = jnp.zeros((reach, padded.shape[1]), bf16)
    padded[reach:, :] = source_ref[...]


def spread_heads(values, heads, scale):
    span = values.shape[1]
    size = span // heads
    lane = lax.broadcasted_iota(jnp.int32, (tile, span), 1)
    wide = values.astype(f32) * scale
    parts = [
        jnp.where((lane >= head * size) & (lane < (head + 1) * size), wide, 0.0)
        for head in range(heads)
    ]
    return jnp.concatenate(parts, axis=0).astype(bf16)


def collect_heads(stacked, heads):
    span = stacked.shape[1]
    size = span // heads
    lane = lax.broadcasted_iota(jnp.int32, (tile, span), 1)
    total = stacked[:tile, :]
    for head in range(1, heads):
        total = jnp.where(lane < head * size, total, stacked[head * tile : (head + 1) * tile, :])
    return total


def window_powers(q_all, keys, skew, seg_q_ref, seg_k_ref, start, heads):
    window = reach + tile
    seg_q = jnp.concatenate([seg_q_ref[pl.ds(start, tile), :]] * heads, axis=0)
    seg_k = seg_k_ref[:, pl.ds(start, window)]
    scores = dot(q_all, keys, 1, 1) + skew[...]
    scores = jnp.where(seg_q == seg_k, scores, excluded)
    powers = jnp.exp(scores - jnp.max(scores, axis=-1, keepdims=True))
    return powers, 1.0 / jnp.sum(powers, axis=-1, keepdims=True)


def attend_kernel(heads, place, q_ref, k_ref, v_ref, seg_q_ref, seg_k_ref, line_ref, *rest):
    *out_refs, mixed, k_pad, v_pad, skew = rest
    window = reach + tile
    scale = (q_ref.shape[1] // heads) ** (-0.5)
    fill_skew(line_ref, skew, heads)
    fill_window(k_ref, k_pad)
    fill_window(v_ref, v_pad)

    def step(index, carry):
        start = pl.multiple_of(index * tile, tile)
        q_all = spread_heads(q_ref[pl.ds(start, tile), :], heads, scale)
        powers, inverse = window_powers(
            q_all, k_pad[pl.ds(start, window), :], skew, seg_q_ref, seg_k_ref, start, heads
        )
        probs = (powers * inverse).astype(bf16)
        part = dot(probs, v_pad[pl.ds(start, window), :], 1, 0)
        mixed[pl.ds(start, tile), :] = collect_heads(part, heads).astype(bf16)
        return carry

    lax.fori_loop(0, q_ref.shape[0] // tile, step, 0)
    rows = out_refs[0].shape[0]
    for r, out_ref in enumerate(out_refs):
        out_ref[...] = mixed[pl.ds(pl.multiple_of((place[1] ^ r) * rows, rows), rows), :]


def attend(place, query, key_rows, value_rows, seg_q, seg_k, line, heads, members):
    seq_len, span = query.shape
    window = reach + tile

    def kernel(place_ref, *refs):
        attend_kernel(heads, place_ref, *refs)

    return call(
        kernel,
        "attend",
        [query, key_rows, value_rows, seg_q, seg_k, line],
        [shape((seq_len // members, span), bf16)] * members,
        scratch=[
            pltpu.VMEM((seq_len, span), bf16),
            pltpu.VMEM((seq_len + reach, span), bf16),
            pltpu.VMEM((seq_len + reach, span), bf16),
            pltpu.VMEM((heads * tile, window), f32),
        ],
        flops=4 * seq_len * window * heads * 256,
        scalars=place,
    )


def attend_back_kernel(heads, members, place, *refs):
    q_ref, k_ref, v_ref, seg_q_ref, seg_k_ref, line_ref = refs[:6]
    g_refs = refs[6 : 6 + members]
    dq_ref, dk_ref, dv_ref, line_grad_ref = refs[6 + members : 10 + members]
    grad, k_pad, v_pad, skew, dk_sum, dv_sum, bias_sum = refs[10 + members :]
    window = reach + tile
    scale = (q_ref.shape[1] // heads) ** (-0.5)
    rows = g_refs[0].shape[0]
    fill_skew(line_ref, skew, heads)
    fill_window(k_ref, k_pad)
    fill_window(v_ref, v_pad)
    dk_sum[...] = jnp.zeros_like(dk_sum)
    dv_sum[...] = jnp.zeros_like(dv_sum)
    bias_sum[...] = jnp.zeros_like(bias_sum)
    for r, g_ref in enumerate(g_refs):
        grad[pl.ds(pl.multiple_of((place[1] ^ r) * rows, rows), rows), :] = g_ref[...]

    def step(index, carry):
        start = pl.multiple_of(index * tile, tile)
        keys = k_pad[pl.ds(start, window), :]
        values = v_pad[pl.ds(start, window), :]
        q_all = spread_heads(q_ref[pl.ds(start, tile), :], heads, scale)
        g_all = spread_heads(grad[pl.ds(start, tile), :], heads, 1.0)
        powers, inverse = window_powers(q_all, keys, skew, seg_q_ref, seg_k_ref, start, heads)
        probs = powers * inverse
        dot_grad = dot(g_all, values, 1, 1)
        inner = jnp.sum(probs * dot_grad, axis=-1, keepdims=True)
        score_grad = (probs * (dot_grad - inner)).astype(bf16)
        bias_sum[...] += score_grad.astype(f32)
        part = collect_heads(dot(score_grad, keys, 1, 0), heads) * scale
        dq_ref[pl.ds(start, tile), :] = part.astype(bf16)
        dk_sum[pl.ds(start, window), :] += dot(score_grad, q_all, 0, 0)
        dv_sum[pl.ds(start, window), :] += dot(probs.astype(bf16), g_all, 0, 0)
        return carry

    lax.fori_loop(0, q_ref.shape[0] // tile, step, 0)
    dk_ref[...] = dk_sum[reach:, :].astype(bf16)
    dv_ref[...] = dv_sum[reach:, :].astype(bf16)
    line_grad_ref[...] = jnp.zeros_like(line_grad_ref)
    row = lax.broadcasted_iota(jnp.int32, (tile, tile), 0)
    column = lax.broadcasted_iota(jnp.int32, (tile, tile), 1)
    mirror = (row + column == tile - 1).astype(f32)
    for head in range(heads):
        part = bias_sum[head * tile : (head + 1) * tile, :]
        turned = dot(mirror, part, 1, 0, highest)
        straight = pltpu.roll(turned, window - tile + 1, 1, stride=1, stride_axis=0)
        line_grad_ref[head : head + 1, :] = jnp.sum(straight, axis=0, keepdims=True)


def attend_back(place, query, key_rows, value_rows, seg_q, seg_k, line, grads, heads):
    seq_len, span = query.shape
    window = reach + tile

    def kernel(place_ref, *refs):
        attend_back_kernel(heads, len(grads), place_ref, *refs)

    return call(
        kernel,
        "attend_back",
        [query, key_rows, value_rows, seg_q, seg_k, line] + grads,
        [shape((seq_len, span), bf16)] * 3 + [shape((8, window), f32)],
        scratch=[
            pltpu.VMEM((seq_len, span), bf16),
            pltpu.VMEM((seq_len + reach, span), bf16),
            pltpu.VMEM((seq_len + reach, span), bf16),
            pltpu.VMEM((heads * tile, window), f32),
            pltpu.VMEM((seq_len + reach, span), f32),
            pltpu.VMEM((seq_len + reach, span), f32),
            pltpu.VMEM((heads * tile, window), f32),
        ],
        flops=10 * seq_len * window * heads * 256,
        limit=48,
        scalars=place,
    )


def project(place, token_blocks, pack_blocks, gain, cotangent, span):
    rows, width = token_blocks[0].shape
    members = len(token_blocks)
    seq_len = rows * members
    parts = sum(len(held) for _, held in pack_blocks)
    part = width // parts

    def kernel(place_ref, gain_ref, cot_ref, *refs):
        token_refs = refs[:members]
        pack_refs = refs[members : members + len(pack_blocks)]
        (normed_ref, q_ref, k_ref, v_ref, wq_ref, wk_ref, wv_ref, wo_ref, late_ref, pack) = refs[
            members + len(pack_blocks) :
        ]
        for (_, held), ref in zip(pack_blocks, pack_refs):
            for i, r in enumerate(held):
                at = pl.multiple_of((place_ref[0] ^ r) * part, part) if parts > 1 else 0
                pack[pl.ds(at, part), :] = ref[i * part : (i + 1) * part, :]
        for at, ref in enumerate((wq_ref, wk_ref, wv_ref)):
            ref[...] = pack[:, at * span : (at + 1) * span]
        wo_ref[...] = pack[:, 3 * span :].astype(f32).T.astype(bf16)
        for r, ref in enumerate(token_refs):
            normed, _ = normalize(ref[...].astype(f32), gain_ref[...])
            normed = normed.astype(bf16)
            at = pl.ds(pl.multiple_of((place_ref[1] ^ r) * rows, rows), rows)
            normed_ref[at, :] = normed
            q_ref[at, :] = dot(normed, wq_ref[...], 1, 0).astype(bf16)
            k_ref[at, :] = dot(normed, wk_ref[...], 1, 0).astype(bf16)
            v_ref[at, :] = dot(normed, wv_ref[...], 1, 0).astype(bf16)
        late_ref[...] = cot_ref[...]

    return call(
        kernel,
        "project",
        [gain, cotangent] + list(token_blocks) + [array for array, _ in pack_blocks],
        [shape((seq_len, width), bf16)]
        + [shape((seq_len, span), bf16)] * 3
        + [shape((width, span), bf16)] * 3
        + [shape((span, width), bf16), shape((rows, width), bf16)],
        scratch=[pltpu.VMEM((width, width), bf16)],
        flops=2 * seq_len * width * 4 * span,
        scalars=place,
    )


def hot(slots_ref, first, count):
    tokens = slots_ref.shape[1]
    slot = lax.broadcasted_iota(jnp.int32, (count, tokens), 0) + first
    taken = (slot == slots_ref[0:1, :]) | (slot == slots_ref[1:2, :])
    return jnp.where(taken, 1.0, 0.0).astype(bf16)


def to_slots(name, sets, blocks, size):
    width = sets[0][0].shape[1]

    def kernel(*refs):
        out_refs = refs[2 * len(sets) :]
        for at in range(len(sets)):
            rows_ref, slots_ref = refs[2 * at], refs[2 * at + 1]
            for b, out_ref in enumerate(out_refs):
                part = dot(hot(slots_ref, b * size, size), rows_ref[...], 1, 0)
                out_ref[at * size : (at + 1) * size, :] = part.astype(bf16)

    operands = [item for pair in sets for item in pair]
    return call(
        kernel,
        name,
        operands,
        [shape((size * len(sets), width), bf16)] * blocks,
        flops=2 * len(sets) * blocks * size * sets[0][0].shape[0] * width,
    )


def from_slots(name, blocks, slots, size, dtypes):
    count, sets = len(blocks), len(slots)
    width = blocks[0].shape[1]
    rows = slots[0].shape[1]

    def kernel(*refs):
        block_refs, slot_refs, out_refs = refs[:count], refs[count : count + sets], refs[count + sets :]
        for at in range(sets):
            total = None
            for b, ref in enumerate(block_refs):
                held = ref[at * size : (at + 1) * size, :]
                part = dot(hot(slot_refs[at], b * size, size), held, 0, 0)
                total = part if total is None else total + part
            out_refs[at][...] = total.astype(out_refs[at].dtype)

    return call(
        kernel,
        name,
        list(blocks) + list(slots),
        [shape((rows, width), dtype) for dtype in dtypes],
        flops=2 * sets * count * size * rows * width,
    )


def router_softmax(values, w_router, experts):
    logits = dot(values, w_router, 1, 0)
    lane = lax.broadcasted_iota(jnp.int32, logits.shape, 1)
    logits = jnp.where(lane < experts, logits, excluded)
    powers = jnp.exp(logits - jnp.max(logits, axis=-1, keepdims=True))
    return powers / jnp.sum(powers, axis=-1, keepdims=True)


def middle(tokens, mixed, weight_o, gain, w_router, slots, experts, blocks, size):
    rows, width = tokens.shape
    members = len(mixed)

    def kernel(*refs):
        token_ref, gain_ref, router_ref, slots_ref = refs[:4]
        mixed_refs, weight_refs = refs[4 : 4 + members], refs[4 + members : 4 + 2 * members]
        hidden_ref, input_ref, probs_ref, *send_refs = refs[4 + 2 * members :]
        hidden = token_ref[...].astype(f32)
        for left, right in zip(mixed_refs, weight_refs):
            hidden = hidden + dot(left[...], right[...], 1, 0)
        hidden_ref[...] = hidden
        normed, _ = normalize(hidden, gain_ref[...])
        normed = normed.astype(bf16)
        input_ref[...] = normed
        for b, ref in enumerate(send_refs):
            ref[...] = dot(hot(slots_ref, b * size, size), normed, 1, 0).astype(bf16)
        probs_ref[...] = router_softmax(normed, router_ref[...], experts)

    return call(
        kernel,
        "middle",
        [tokens, gain, w_router, slots] + mixed + weight_o,
        [shape((rows, width), f32), shape((rows, width), bf16), shape((rows, 128), f32)]
        + [shape((size, width), bf16)] * blocks,
        flops=2 * rows * width * (width + blocks * size),
    )


def experts_kernel(count, grads, experts, me_ref, w_in_ref, w_out_ref, router_ref, *refs):
    x_refs, g_refs = refs[:count], refs[count : count + grads]
    refs = refs[count + grads :]
    back_refs, result_refs = refs[:count], refs[count : count + grads]
    active_ref, pre_grad_ref, x_all, s_all = refs[count + grads : count + grads + 4]
    gates, result_sum, back_sum = refs[count + grads + 4 :]
    step = pl.program_id(0)
    total, width = x_all.shape
    size = total // count
    chunk = min(256, total)

    def grad_rows():
        return jnp.concatenate([ref[...] for ref in g_refs], axis=0)

    @pl.when(step == 0)
    def _():
        for b, ref in enumerate(x_refs):
            x_all[b * size : (b + 1) * size, :] = ref[...]
        probs = router_softmax(x_all[...], router_ref[...], experts)
        lane = lax.broadcasted_iota(jnp.int32, probs.shape, 1)
        own = jnp.sum(jnp.where(lane == me_ref[0], probs, 0.0), axis=1, keepdims=True)
        gates[...] = jnp.broadcast_to(own, gates.shape)
        s_all[...] = (own * grad_rows().astype(f32)).astype(bf16)
        result_sum[...] = jnp.zeros_like(result_sum)
        back_sum[...] = jnp.zeros_like(back_sum)

    for c in range(total // chunk):
        at = slice(c * chunk, (c + 1) * chunk)
        pre_act = dot(x_all[at, :], w_in_ref[...], 1, 0)
        active_grad = dot(s_all[at, :], w_out_ref[...], 1, 1)
        below = 0.5 + 0.5 * lax.erf(pre_act * math.sqrt(0.5))
        active = (pre_act * below).astype(bf16)
        bell = jnp.exp(-0.5 * pre_act * pre_act) * (1.0 / math.sqrt(2.0 * math.pi))
        pre_grad = (active_grad * (below + pre_act * bell)).astype(bf16)
        active_ref[at, :] = active
        pre_grad_ref[at, :] = pre_grad
        result_sum[at, :] += dot(active, w_out_ref[...], 1, 0)
        back_sum[at, :] += dot(pre_grad, w_in_ref[...], 1, 1)

    @pl.when(step == pl.num_programs(0) - 1)
    def _():
        result = result_sum[...].astype(bf16).astype(f32)
        gate_grad = jnp.sum(grad_rows().astype(f32) * result, axis=1, keepdims=True)
        upper = gate_grad.astype(bf16).astype(f32)
        lane = lax.broadcasted_iota(jnp.int32, (total, 128), 1)
        columns = jnp.where(
            lane == me_ref[0], upper, jnp.where(lane == me_ref[0] + 64, gate_grad - upper, 0.0)
        ).astype(bf16)
        back = back_sum[...].astype(bf16)
        for b, ref in enumerate(back_refs):
            ref[:, :width] = back[b * size : (b + 1) * size, :]
            ref[:, width:] = columns[b * size : (b + 1) * size, :]
        gated = (gates[:, 0:1] * result).astype(bf16)
        each = total // grads
        for b, ref in enumerate(result_refs):
            ref[...] = gated[b * each : (b + 1) * each, :]


def run_experts(place, w_in, w_out, w_router, x_blocks, g_blocks, experts):
    width, units = w_in.shape
    count, grads = len(x_blocks), len(g_blocks)
    size, each = x_blocks[0].shape[0], g_blocks[0].shape[0]
    total = size * count
    piece = 512

    def whole(dims):
        return pl.BlockSpec(tuple(dims), lambda i: (0, 0))

    columns = pl.BlockSpec((total, piece), lambda i: (0, i))
    outs = (
        [shape((size, width + 128), bf16)] * count
        + [shape((each, width), bf16)] * grads
        + [shape((total, units), bf16)] * 2
        + [shape((total, width), bf16)] * 2
    )
    flat = pl.pallas_call(
        functools.partial(experts_kernel, count, grads, experts),
        name="run_experts",
        grid=(units // piece,),
        in_specs=[
            pl.BlockSpec(memory_space=pltpu.SMEM),
            pl.BlockSpec((width, piece), lambda i: (0, i)),
            pl.BlockSpec((piece, width), lambda i: (i, 0)),
            whole(w_router.shape),
        ]
        + [whole((size, width))] * count
        + [whole((each, width))] * grads,
        out_specs=[whole((size, width + 128))] * count
        + [whole((each, width))] * grads
        + [columns] * 2
        + [whole((total, width))] * 2,
        out_shape=outs,
        scratch_shapes=[
            pltpu.VMEM((total, 128), f32),
            pltpu.VMEM((total, width), f32),
            pltpu.VMEM((total, width), f32),
        ],
        compiler_params=pltpu.CompilerParams(vmem_limit_bytes=56 * 1024 * 1024),
        cost_estimate=pl.CostEstimate(
            flops=8 * total * width * units,
            bytes_accessed=4 * width * units + 4 * total * units,
            transcendentals=2 * total * units,
        ),
    )(place, w_in, w_out, w_router, *x_blocks, *g_blocks)
    return (
        flat[:count],
        flat[count : count + grads],
        *flat[count + grads :],
    )


def home(own_back, far_sum, slots, hidden, probs, cotangent, gain, w_router, weight_o, size):
    rows, width = hidden.shape
    count, members = len(own_back), len(weight_o)
    span = weight_o[0].shape[0]
    far = [] if far_sum is None else [far_sum]

    def kernel(*refs):
        slots_ref, hidden_ref, probs_ref, cot_ref, gain_ref, router_ref = refs[:6]
        back_refs = refs[6 : 6 + count]
        far_refs = refs[6 + count : 6 + count + len(far)]
        weight_refs = refs[6 + count + len(far) : 6 + count + len(far) + members]
        outs = refs[6 + count + len(far) + members :]
        grad_refs = outs[:members]
        attn_ref, hidden_grad_ref, gain_grad_ref, logit_ref = outs[members:]
        total = None
        for b, ref in enumerate(back_refs):
            part = dot(hot(slots_ref, b * size, size), ref[...], 0, 0)
            total = part if total is None else total + part
        for ref in far_refs:
            total = total + ref[...].astype(f32)
        columns = total[:, width:]
        lane = lax.broadcasted_iota(jnp.int32, columns.shape, 1)
        prob_grad = jnp.where(lane < 64, columns + pltpu.roll(columns, 64, 1), 0.0)
        router_probs = probs_ref[...]
        logit_grad = router_probs * (
            prob_grad - jnp.sum(router_probs * prob_grad, axis=-1, keepdims=True)
        )
        logit_ref[...] = logit_grad
        grad = total[:, :width] + dot(logit_grad, router_ref[...].astype(f32), 1, 1, highest)
        hidden_now = hidden_ref[...]
        inverse = lax.rsqrt(jnp.mean(hidden_now * hidden_now, axis=-1, keepdims=True) + eps)
        scaled = grad * gain_ref[...]
        gain_grad_ref[...] = jnp.sum(grad * hidden_now * inverse, axis=0, keepdims=True)
        inner = jnp.mean(scaled * hidden_now, axis=-1, keepdims=True)
        hidden_grad = (
            cot_ref[...].astype(f32)
            + inverse * scaled
            - hidden_now * inverse * inverse * inverse * inner
        )
        hidden_grad_ref[...] = hidden_grad
        attn_grad = hidden_grad.astype(bf16)
        attn_ref[...] = attn_grad
        for ref, weight in zip(grad_refs, weight_refs):
            ref[...] = dot(attn_grad, weight[...], 1, 1).astype(bf16)

    return call(
        kernel,
        "home",
        [slots, hidden, probs, cotangent, gain, w_router] + list(own_back) + far + weight_o,
        [shape((rows, span), bf16)] * members
        + [
            shape((rows, width), bf16),
            shape((rows, width), f32),
            shape((1, width), f32),
            shape((rows, 128), f32),
        ],
        flops=2 * rows * width * (width + size * count),
    )


def input_grads(place, proj_grads, normed, weights, output_sum, gain, members, owners):
    seq_len, width = normed.shape
    span = weights[0].shape[1]
    rows = seq_len // members
    part = width // owners
    few = owners == 8

    def kernel(place_ref, *refs):
        dq_ref, dk_ref, dv_ref, normed_ref, wq_ref, wk_ref, wv_ref, out_ref, gain_ref = refs[:9]
        near_ref, base_ref, gain_grad_ref, *weight_refs, sums = refs[9:]
        for at, ref in enumerate((dq_ref, dk_ref, dv_ref)):
            sums[:, at * span : (at + 1) * span] = dot(normed_ref[...], ref[...], 0, 0)
        sums[:, 3 * span :] = out_ref[...]
        if few:
            for r, ref in enumerate(weight_refs):
                for i, far in enumerate((0, 4)):
                    at = pl.multiple_of((place_ref[0] ^ r ^ far) * part, part)
                    ref[i * part : (i + 1) * part, :] = sums[pl.ds(at, part), :].astype(ref.dtype)
        else:
            weight_refs[0][...] = sums[...]
        gain_grad = jnp.zeros((1, width), f32)
        for r, (ref, first) in enumerate(
            ((base_ref, 0), (near_ref, 0), (base_ref, rows), (near_ref, rows))
        ):
            at = pl.ds(pl.multiple_of((place_ref[1] ^ r) * rows, rows), rows)
            grad = (
                dot(dq_ref[at, :], wq_ref[...], 1, 1)
                + dot(dk_ref[at, :], wk_ref[...], 1, 1)
                + dot(dv_ref[at, :], wv_ref[...], 1, 1)
            )
            gain_grad = gain_grad + jnp.sum(
                grad * normed_ref[at, :].astype(f32), axis=0, keepdims=True
            )
            ref[first : first + rows, :] = grad.astype(ref.dtype)
        gain_grad_ref[...] = gain_grad / gain_ref[...]

    if few:
        weight_outs = [shape((2 * part, 4 * span), f32)] + [shape((2 * part, 4 * span), bf16)] * 3
    else:
        weight_outs = [shape((width, 4 * span), f32)]
    return call(
        kernel,
        "input_grads",
        list(proj_grads) + [normed] + list(weights) + [output_sum, gain],
        [shape((2 * rows, width), bf16), shape((2 * rows, width), f32), shape((1, width), f32)]
        + weight_outs,
        scratch=[pltpu.VMEM((width, 4 * span), f32)],
        flops=4 * seq_len * width * 3 * span,
        limit=48,
        scalars=place,
    )


def gather_mp(values):
    across = swap(values, "mp", 2)
    return [values, swap(values, "mp", 1), across, swap(across, "mp", 1)]


def scatter_sum_mp(blocks):
    near = swap(jnp.concatenate([blocks[1], blocks[3]], axis=0).astype(bf16), "mp", 1)
    size = blocks[0].shape[0]
    far = blocks[2].astype(f32) + near[size:].astype(f32)
    far = swap(far.astype(bf16), "mp", 2)
    return blocks[0].astype(f32) + near[:size].astype(f32) + far.astype(f32)


def sum_all(values):
    for axis in ("mp", "dp"):
        step = 1
        while step < lax.axis_size(axis):
            values = values + swap(values, axis, step)
            step = 2 * step
    return values


def all_to_all_dp(values):
    return lax.all_to_all(values, "dp", split_axis=0, concat_axis=0, tiled=True)


def slots_of(routes, place, capacity, experts, limit):
    rows = routes.shape[0]
    expert_ids = jnp.arange(experts, dtype=jnp.int32)[None, :]
    hits = (routes[:, 0:1] == expert_ids) | (routes[:, 1:2] == expert_ids)
    earlier = jnp.arange(rows)[:, None] > jnp.arange(rows)[None, :]
    ranks = jnp.dot(earlier.astype(bf16), hits.astype(bf16), preferred_element_type=f32)
    lines = []
    for k in (0, 1):
        rank = jnp.sum(jnp.where(routes[:, k : k + 1] == expert_ids, ranks, 0.0), axis=1)
        block = routes[:, k] ^ place
        lines.append(jnp.where(block < limit, block * capacity + rank.astype(jnp.int32), -1))
    return jnp.pad(jnp.stack(lines), ((0, 6), (0, 0)), constant_values=-1)


def on_device(
    tokens,
    norm_gain,
    w_query,
    w_key,
    w_value,
    w_output,
    bias_table,
    ffn_gain,
    w_router,
    w_in,
    w_out,
    segments,
    buckets,
    routes,
    cotangent,
):
    rows, width = tokens.shape
    heads = bias_table.shape[1]
    seq_len = buckets.shape[0]
    experts = w_router.shape[1]
    owners, members = lax.axis_size("dp"), lax.axis_size("mp")
    me, member = lax.axis_index("dp"), lax.axis_index("mp")
    place = jnp.stack([me, member]).astype(jnp.int32)
    capacity = 4 * rows // experts
    span = w_query.shape[1]
    window = reach + tile
    few = owners == 8

    token_blocks = gather_mp(tokens)
    pack = jnp.concatenate([w_query, w_key, w_value, w_output.T], axis=1)
    if few:
        both = jnp.concatenate([pack, swap(pack, "dp", 4)], axis=0)
        pack_blocks = [(both, (0, 4))] + [(swap(both, "dp", r), (r, r ^ 4)) for r in (1, 2, 3)]
    else:
        pack_blocks = [(lax.all_gather(pack, "dp", axis=0, tiled=True), (0,))]
    gain_one, gain_two = norm_gain.reshape(1, width), ffn_gain.reshape(1, width)
    normed, query, key_rows, value_rows, weight_q, weight_k, weight_v, w_o, late_cotangent = (
        project(place, token_blocks, pack_blocks, gain_one, cotangent, span)
    )
    weight_o = gather_mp(w_o)

    if few:
        blocks, size = 4, capacity
        slots = [slots_of(routes, me, capacity, experts, 4)]
        slots.append(slots_of(swap(routes, "dp", 4), me, capacity, experts, 4))
    else:
        blocks, size = 1, experts * capacity
        slots = [slots_of(routes, 0, capacity, experts, experts)]

    if few:
        far_cotangent = swap(late_cotangent, "dp", 4)
        held = to_slots(
            "grads_to_slots",
            [(late_cotangent, slots[0]), (far_cotangent, slots[1])],
            blocks,
            size,
        )
        g_blocks = [held[0]] + [swap(held[r], "dp", r) for r in (1, 2, 3)]
    else:
        held = to_slots("grads_to_slots", [(late_cotangent, slots[0])], blocks, size)
        g_blocks = [all_to_all_dp(held[0])]

    line_buckets = jnp.pad(jnp.flip(buckets[: reach + 1]), (0, window - reach - 1))
    bucket_hot = (
        line_buckets[:, None] == jnp.arange(bias_table.shape[0], dtype=jnp.int32)[None, :]
    ).astype(f32)
    line = jnp.dot(bias_table.T, bucket_hot.T, precision=highest)
    line = jnp.pad(line, ((0, 8 - heads), (0, 0)))
    seg_q = segments.reshape(seq_len, 1)
    seg_k = jnp.pad(segments.reshape(1, seq_len), ((0, 0), (reach, 0)), constant_values=-1)
    mixed_out = attend(place, query, key_rows, value_rows, seg_q, seg_k, line, heads, members)
    mixed_in = [mixed_out[0]] + [swap(mixed_out[r], "mp", r) for r in range(1, members)]

    router_wide = jnp.pad(w_router, ((0, 0), (0, 128 - experts)))
    hidden, ffn_input, router_probs, *send = middle(
        tokens, mixed_in, weight_o, gain_two, router_wide, slots[0], experts, blocks, size
    )
    if few:
        far_input = swap(ffn_input, "dp", 4)
        own = [send[0]] + [swap(send[r], "dp", r) for r in (1, 2, 3)]
        far = to_slots("far_to_slots", [(far_input, slots[1])], blocks, size)
        far = [far[0]] + [swap(far[r], "dp", r) for r in (1, 2, 3)]
        x_blocks = [item for pair in zip(own, far) for item in pair]
    else:
        x_blocks = [all_to_all_dp(send[0])]

    back, result, active, pre_grad, arrived, slot_grad = run_experts(
        place, w_in[0], w_out[0], router_wide, x_blocks, g_blocks, experts
    )
    if few:
        far_back = [back[1]] + [swap(back[2 * r + 1], "dp", r) for r in (1, 2, 3)]
        (far_total,) = from_slots("back_from_slots", far_back, [slots[1]], size, [bf16])
        far_sum = swap(far_total, "dp", 4)
        own_back = [back[0]] + [swap(back[2 * r], "dp", r) for r in (1, 2, 3)]
    else:
        own_back, far_sum = [all_to_all_dp(back[0])], None

    *grad_out, attn_grad, hidden_grad, ffn_gain_grad, logit_grad = home(
        own_back,
        far_sum,
        slots[0],
        hidden,
        router_probs,
        cotangent,
        gain_two,
        router_wide,
        weight_o,
        size,
    )
    grad_in = [grad_out[0]] + [swap(grad_out[r], "mp", r) for r in range(1, members)]

    *proj_grads, line_grad = attend_back(
        place, query, key_rows, value_rows, seg_q, seg_k, line, grad_in, heads
    )
    output_sum = scatter_sum_mp([dot(attn_grad, part, 0, 0) for part in mixed_in])
    near, base, gain_part, *weight_sums = input_grads(
        place,
        proj_grads,
        normed,
        (weight_q, weight_k, weight_v),
        output_sum,
        gain_one,
        members,
        owners,
    )
    if few:
        total = weight_sums[0]
        for r in (1, 2, 3):
            total = total + swap(weight_sums[r], "dp", r).astype(f32)
        part = width // owners
        far_part = swap(total[part:].astype(bf16), "dp", 4)
        joined_grad = total[:part] + far_part.astype(f32)
    else:
        joined_grad = lax.psum_scatter(weight_sums[0], "dp", scatter_dimension=0, tiled=True)
    near = base + swap(near, "mp", 1).astype(f32)
    normed_grad = near[:rows] + swap(near[rows:].astype(bf16), "mp", 2).astype(f32)
    resid = tokens.astype(f32)
    _, inverse_one = normalize(resid, norm_gain)
    scaled = normed_grad * norm_gain
    inner = jnp.mean(scaled * resid, axis=-1, keepdims=True)
    tokens_grad = (
        hidden_grad + inverse_one * scaled - resid * inverse_one * inverse_one * inverse_one * inner
    ).astype(bf16)

    if few:
        result_in = [result[0]] + [swap(result[r], "dp", r) for r in (1, 2, 3)]
        own_result, far_result = from_slots(
            "result_from_slots", result_in, slots, size, [f32, bf16]
        )
        block_out = hidden + own_result + swap(far_result, "dp", 4).astype(f32)
    else:
        (own_result,) = from_slots(
            "result_from_slots", [all_to_all_dp(result[0])], slots, size, [f32]
        )
        block_out = hidden + own_result
    block_out = block_out.astype(bf16)

    piece = w_in.shape[2] // members

    def hidden_cut(values, axis):
        return [
            lax.dynamic_slice_in_dim(values, (member ^ r) * piece, piece, axis)
            for r in range(members)
        ]

    w_in_grad = scatter_sum_mp([dot(arrived, part, 0, 0) for part in hidden_cut(pre_grad, 1)])
    w_out_grad = scatter_sum_mp([dot(part, slot_grad, 0, 0) for part in hidden_cut(active, 1)])

    router_grad = jnp.dot(ffn_input.astype(f32).T, logit_grad[:, :experts], precision=highest)
    table_local = jnp.dot(bucket_hot.T, line_grad[:heads].T, precision=highest)
    table_full = jnp.zeros((bias_table.shape[0], heads * members), f32)
    table_full = lax.dynamic_update_slice_in_dim(table_full, table_local, member * heads, 1)
    pieces = [router_grad, table_full, gain_part, ffn_gain_grad]
    sums = sum_all(jnp.concatenate([item.reshape(-1) for item in pieces]))
    ends = [0]
    for item in pieces:
        ends.append(ends[-1] + item.size)
    router_sum, table_sum, gain_sum, ffn_gain_sum = [
        sums[ends[i] : ends[i + 1]].reshape(pieces[i].shape) for i in range(4)
    ]
    return (
        block_out,
        tokens_grad,
        gain_sum.reshape(width),
        joined_grad[:, :span],
        joined_grad[:, span : 2 * span],
        joined_grad[:, 2 * span : 3 * span],
        joined_grad[:, 3 * span :].T,
        table_sum,
        ffn_gain_sum.reshape(width),
        router_sum,
        w_in_grad[None],
        w_out_grad[None],
    )


def solution(mesh):
    return jax.shard_map(
        on_device,
        mesh=mesh,
        in_specs=(
            P(("dp", "mp"), None),
            P(),
            P("dp", "mp"),
            P("dp", "mp"),
            P("dp", "mp"),
            P("mp", "dp"),
            P(None, "mp"),
            P(),
            P(),
            P("dp", None, None),
            P("dp", None, None),
            P("dp", None),
            P(),
            P(("dp", "mp"), None),
            P(("dp", "mp"), None),
        ),
        out_specs=(
            P(("dp", "mp"), None),
            P(("dp", "mp"), None),
            P(),
            P("dp", "mp"),
            P("dp", "mp"),
            P("dp", "mp"),
            P("mp", "dp"),
            P(),
            P(),
            P(),
            P("dp", None, "mp"),
            P("dp", "mp", None),
        ),
        check_vma=False,
    )
```

time: 1380 us -> 396 us (0.29)
  local copies, waits for them, and re-layouts: 504 us -> 42.4 us
  blocking collectives: 331 us -> 0 us
  waiting for transfers between devices: 272 us -> 161 us
  matrix products: 120 us -> 38.8 us
  Pallas kernels: 0 us -> 70.3 us
  loops' own time: 61.4 us -> 0 us
  starting transfers between devices: 14.8 us -> 57 us
  other arithmetic: 51.3 us -> 19.4 us
  between operations: 15.5 us -> 1.69 us
    while x51 -> x0, local copies, waits for them, and re-layouts: 221 us -> none
    ppermute x0 -> x56, waiting for transfers between devices: none -> 161 us  [swap(): return lax.ppermute(values, axis, [(i, i ^ step) for i in range(count)])]
    all_to_all x3 -> x0, waiting for transfers between devices: 138 us -> none  [the longest x1 107 us: on_device(): lax.all_to_all(pre_grad, 'mp', split_axis=1, concat_axis=0, tiled=True)]
    all_gather x4 -> x0, blocking collectives: 129 us -> none  [the longest x1 33.2 us: on_device(): lax.all_gather(w_query, 'dp', axis=0, tiled=True)]
    all_to_all x3 -> x0, blocking collectives: 123 us -> none  [the longest x1 42.3 us: on_device(): lax.all_to_all(send_rows, 'dp', split_axis=0, concat_axis=0, tiled=True)]
    reshape x8 -> x5, local copies, waits for them, and re-layouts: 96.8 us -> 2.49 us  [the longest x2 0.89 us: on_device(): sums = sum_all(jnp.concatenate([item.reshape(-1) for item in pieces]))]
    unnamed x14 -> x0, waiting for transfers between devices: 83 us -> none
    psum x1 -> x0, blocking collectives: 79.5 us -> none  [on_device(): lax.psum((table_full, router_grad, norm_gain_grad, ffn_gain_grad), ('dp',...]
  transfers between devices with their start and end apart: 13 -> 56, of which waited for: 6 -> 28; matrix products, arithmetic and copies ran while one was open for 32% -> 18% of each run, Pallas kernels for 0% -> 8%
where the time goes in v1:
time: 396 us; the launch traced here: 391 us
  waiting for transfers between devices  161 us (41%)
  Pallas kernels  70.3 us (18%)
  starting transfers between devices  57 us (14%)
  local copies, waits for them, and re-layouts  42.4 us (11%)
  matrix products  38.8 us (10%)
  other arithmetic  19.4 us (5%)
    ppermute x56, waiting for transfers between devices, swap(): return lax.ppermute(values, axis, [(i, i ^ step) for i in range(count)])  161 us
    ppermute x56, starting transfers between devices, swap(): return lax.ppermute(values, axis, [(i, i ^ step) for i in range(count)])  57 us
    pallas_call x10, Pallas kernels, call(): pl.pallas_call(kernel, name=name, in_specs=in_specs, out_specs=[vmem] * l...  40 us
    dot_general x12, matrix products, dot(): lax.dot_general(left, right, (((left_dim,), (right_dim,)), ((), ())), pre...  37.1 us
    unnamed x169, local copies, waits for them, and re-layouts  33.5 us
    pallas_call x1, Pallas kernels, run_experts(): pl.pallas_call(functools.partial(experts_kernel, count, grads, experts),...  30.4 us
  transfers between devices with their start and end apart: 56, of which 28 were waited for; matrix products, arithmetic and copies ran while one was open for 18% of the time, Pallas kernels for 8%

profile of v1, /device:TPU:0, one launch (start us, length us, event | category | flops | bytes accessed | tf_op | source)
XLA Modules:
  0.0 390.9 jit_solution(6013891570219770288)
XLA Ops:
  1.2 2.6 collective-permute-start.1
  5.6 2.7 collective-permute-start.3
  20.6 2.1 collective-permute-start.14
  22.7 3.0 collective-permute-done.4.refs_5_
  25.7 2.5 collective-permute-done.5.refs_6_
  28.2 4.3 %collective-permute-done.6.refs_7_ = bf16[192,768]{1,0:T(8,128)(2,1)S(1)} collective-permute-done((bf16[192,768]{1,0:T(8,128)(2,1)S(1)}, bf16[192,768]{1,0:T(8,128)(2,1)S(1)}, u32[]{:S(2)}, u32[]{:S(2)}) %collective-permute-start.6) | collective-permute-done | bytes 294944 | tf_op jit(solution)/shard_map/ppermute | solution.py:36
  34.5 2.5 project.1
  47.7 9.7 %attend.1 = (bf16[256,192]{1,0:T(8,128)(2,1)S(1)}, bf16[256,192]{1,0:T(8,128)(2,1)S(1)}, bf16[256,192]{1,0:T(8,128)(2,1)S(1)}, bf16[256,192]{1,0:T(8,128)(2,1)S(1)}) custom-call(s32[2]{0:T(128)S(1)} %pad_add_fusion.2.place_ref.me_ref, bf16[1024,192]{1,0:T(8,128)(2,1)S(1)} %copy-done.30, bf16[1024,192]{1,0:T(8,128)(2,1)S(1)} %copy-done.33, ...), custom_call_target="tpu_custom_call" | custom-call | flops 2013265920 | bytes 1603592 | tf_op jit(solution)/shard_map/attend/pallas_call | solution.py:47
  59.9 2.6 collective-permute-start.21
  69.9 2.6 collective-permute-start.13
  74.0 15.6 %collective-permute-done.21.refs_2_ = bf16[256,768]{1,0:T(8,128)(2,1)S(1)} collective-permute-done((bf16[256,768]{1,0:T(8,128)(2,1)S(1)}, bf16[256,768]{1,0:T(8,128)(2,1)S(1)}, u32[]{:S(2)}, u32[]{:S(2)}) %collective-permute-start.21) | collective-permute-done | bytes 393248 | tf_op jit(solution)/shard_map/ppermute | solution.py:36
  94.6 3.0 collective-permute-done.13.refs_0_
  100.2 10.0 %collective-permute-done.17.refs_4_ = bf16[128,768]{1,0:T(8,128)(2,1)S(1)} collective-permute-done((bf16[128,768]{1,0:T(8,128)(2,1)S(1)}, bf16[128,768]{1,0:T(8,128)(2,1)S(1)}, u32[]{:S(2)}, u32[]{:S(2)}) %collective-permute-start.17) | collective-permute-done | bytes 196640 | tf_op jit(solution)/shard_map/ppermute | solution.py:36
  111.7 3.7 collective-permute-done.19.refs_6_
  117.4 6.4 %collective-permute-done.24.refs_11_ = bf16[256,768]{1,0:T(8,128)(2,1)S(1)} collective-permute-done((bf16[256,768]{1,0:T(8,128)(2,1)S(1)}, bf16[256,768]{1,0:T(8,128)(2,1)S(1)}, u32[]{:S(2)}, u32[]{:S(2)}) %collective-permute-start.24) | collective-permute-done | bytes 393248 | tf_op jit(solution)/shard_map/ppermute | solution.py:36
  123.8 4.1 %collective-permute-done.16.refs_3_ = bf16[128,768]{1,0:T(8,128)(2,1)S(1)} collective-permute-done((bf16[128,768]{1,0:T(8,128)(2,1)S(1)}, bf16[128,768]{1,0:T(8,128)(2,1)S(1)}, u32[]{:S(2)}, u32[]{:S(2)}) %collective-permute-start.16) | collective-permute-done | bytes 196640 | tf_op jit(solution)/shard_map/ppermute | solution.py:36
  127.9 4.2 %collective-permute-done.20.refs_7_ = bf16[128,768]{1,0:T(8,128)(2,1)S(1)} collective-permute-done((bf16[128,768]{1,0:T(8,128)(2,1)S(1)}, bf16[128,768]{1,0:T(8,128)(2,1)S(1)}, u32[]{:S(2)}, u32[]{:S(2)}) %collective-permute-start.20) | collective-permute-done | bytes 196640 | tf_op jit(solution)/shard_map/ppermute | solution.py:36
  132.8 30.4 %run_experts.1 = (bf16[128,896]{1,0:T(8,128)(2,1)}, bf16[128,896]{1,0:T(8,128)(2,1)}, bf16[128,896]{1,0:T(8,128)(2,1)}, bf16[128,896]{1,0:T(8,128)(2,1)}, bf16[1...) custom-call(s32[2]{0:T(128)} %copy-done.24, ...), custom_call_target="tpu_custom_call" | custom-call | flops 19327352832 | bytes 22020096 | tf_op jit(solution)/shard_map/run_experts/pallas_call | solution.py:445
  163.8 2.9 collective-permute-start.34
  167.3 5.6 %collective-permute-done.32.refs_1_ = bf16[128,896]{1,0:T(8,128)(2,1)S(1)} collective-permute-done((bf16[128,896]{1,0:T(8,128)(2,1)}, bf16[128,896]{1,0:T(8,128)(2,1)S(1)}, u32[]{:S(2)}, u32[]{:S(2)}) %collective-permute-start.32) | collective-permute-done | bytes 229408 | tf_op jit(solution)/shard_map/ppermute | solution.py:36
  173.0 5.5 %collective-permute-done.34.refs_3_ = bf16[128,896]{1,0:T(8,128)(2,1)} collective-permute-done((bf16[128,896]{1,0:T(8,128)(2,1)}, bf16[128,896]{1,0:T(8,128)(2,1)}, u32[]{:S(2)}, u32[]{:S(2)}) %collective-permute-start.34) | collective-permute-done | bytes 229408 | tf_op jit(solution)/shard_map/ppermute | solution.py:36
  183.2 4.5 %fusion.19 = bf16[768,768]{1,0:T(8,128)(2,1)} fusion(bf16[1024,768]{1,0:T(8,128)(2,1)} %get-tuple-element.138, bf16[1024,3072]{1,0:T(8,128)(2,1)} %get-tuple-element.139, s32[]{:T(128)S(6)} %select_n.84), kind=kOutput, calls=%fused_computation.24 | convolution fusion | flops 1208549376 | bytes 4325380 | tf_op jit(solution)/shard_map/dot_general | solution.py:25
  187.7 4.0 %fusion.16 = bf16[768,768]{1,0:T(8,128)(2,1)} fusion(bf16[1024,768]{1,0:T(8,128)(2,1)S(1)} %copy-done.52, bf16[1024,3072]{1,0:T(8,128)(2,1)} %get-tuple-element.139, s32[]{:T(128)S(6)} %select_n.83), kind=kOutput, calls=%fused_computation.23 | convolution fusion | flops 1208549376 | bytes 4325380 | tf_op jit(solution)/shard_map/dot_general | solution.py:25
  193.4 8.6 %collective-permute-done.35.refs_10_ = bf16[256,896]{1,0:T(8,128)(2,1)S(1)} collective-permute-done((bf16[256,896]{1,0:T(8,128)(2,1)S(1)}, bf16[256,896]{1,0:T(8,128)(2,1)S(1)}, u32[]{:S(2)}, u32[]{:S(2)}) %collective-permute-start.35) | collective-permute-done | bytes 458784 | tf_op jit(solution)/shard_map/ppermute | solution.py:36
  202.0 3.4 home.1
  207.4 4.0 %fusion.25 = bf16[768,768]{1,0:T(8,128)(2,1)} fusion(bf16[1024,768]{1,0:T(8,128)(2,1)S(1)} %copy-done.77, bf16[1024,3072]{1,0:T(8,128)(2,1)} %get-tuple-element.140, s32[]{:T(128)S(6)} %select_n.84), kind=kOutput, calls=%fused_computation.26 | convolution fusion | flops 1208549376 | bytes 4325380 | tf_op jit(solution)/shard_map/dot_general | solution.py:25
  218.5 2.0 fusion.33
  224.2 13.8 %attend_back.1 = (bf16[1024,192]{1,0:T(8,128)(2,1)S(1)}, bf16[1024,192]{1,0:T(8,128)(2,1)S(1)}, bf16[1024,192]{1,0:T(8,128)(2,1)S(1)}, f32[8,640]{1,0:T(8,128)S(1)}) custom-call(s32[2]{0:T(128)S(1)} %copy-done.25, bf16[1024,192]{1,0:T(8,128)(2,1)S(1)} %copy-done.31, bf16[1024,192]{1,0:T(8,128)(2,1)S(1)} %copy-done.34, bf16[1024,192]{1,0:T(8,128)(2,1)S(1)} %copy-done.37, ...), custom_call_target="tpu_custom_call" | custom-call | flops 5033164800 | bytes 2803720 | tf_op jit(solution)/shard_map/attend_back/pallas_call | solution.py:47
  247.8 5.4 %input_grads.1 = (bf16[512,768]{1,0:T(8,128)(2,1)S(1)}, f32[512,768]{1,0:T(8,128)}, f32[1,768]{1,0:T(1,128)S(1)}, f32[192,768]{1,0:T(8,128)S(1)}, bf16[192,768]{...) custom-call(s32[2]{0:T(128)S(1)} %copy-done.25, bf16[1024,192]{1,0:T(8,128)(2,1)S(1)} %copy-done.45, ...), custom_call_target="tpu_custom_call" | custom-call | flops 1811939328 | bytes 8067080 | tf_op jit(solution)/shard_map/input_grads/pallas_call | solution.py:47
  254.2 3.5 fusion.22
  259.0 2.3 collective-permute-start.27
  265.8 3.8 collective-permute-done.25.refs_1_
  270.3 8.6 %collective-permute-done.27.refs_3_ = bf16[256,768]{1,0:T(8,128)(2,1)S(1)} collective-permute-done((bf16[256,768]{1,0:T(8,128)(2,1)S(1)}, bf16[256,768]{1,0:T(8,128)(2,1)S(1)}, u32[]{:S(2)}, u32[]{:S(2)}) %collective-permute-start.27) | collective-permute-done | bytes 393248 | tf_op jit(solution)/shard_map/ppermute | solution.py:36
  279.9 2.4 collective-permute-start.28
  285.7 5.5 %collective-permute-done.46 = f32[8064]{0:T(1024)S(1)} collective-permute-done((f32[8064]{0:T(1024)S(1)}, f32[8064]{0:T(1024)S(1)}, u32[]{:S(2)}, u32[]{:S(2)}) %collective-permute-start.46) | collective-permute-done | bytes 32288 | tf_op jit(solution)/shard_map/ppermute | solution.py:36
  291.2 2.2 collective-permute-start.47
  293.4 4.3 %fusion.14 = f32[768,768]{1,0:T(8,128)} fusion(bf16[1024,768]{1,0:T(8,128)(2,1)S(1)} %copy-done.53, bf16[1024,3072]{1,0:T(8,128)(2,1)} %get-tuple-element.139, s32[]{:T(128)S(6)} %select_n.82), kind=kOutput, calls=%fused_computation.20 | convolution fusion | flops 1207959552 | bytes 5505028 | tf_op jit(solution)/shard_map/dot_general | solution.py:25
  298.1 2.6 collective-permute-done.28
  301.7 4.3 %fusion.6 = f32[768,768]{1,0:T(8,128)} fusion(bf16[1024,768]{1,0:T(8,128)(2,1)S(1)} %copy-done.78, bf16[1024,3072]{1,0:T(8,128)(2,1)} %get-tuple-element.140, s32[]{:T(128)S(6)} %select_n.82), kind=kOutput, calls=%fused_computation.12 | convolution fusion | flops 1207959552 | bytes 5505028 | tf_op jit(solution)/shard_map/dot_general | solution.py:25
  305.9 2.6 collective-permute-done.50
  311.2 2.6 collective-permute-done.49
  317.1 7.7 %collective-permute-done.51 = bf16[96,768]{1,0:T(8,128)(2,1)S(1)} collective-permute-done((bf16[96,768]{1,0:T(8,128)(2,1)S(1)}, bf16[96,768]{1,0:T(8,128)(2,1)S(1)}, u32[]{:S(2)}, u32[]{:S(2)}) %collective-permute-start.51) | collective-permute-done | bytes 147488 | tf_op jit(solution)/shard_map/ppermute | solution.py:36
  327.3 4.4 %add_convert_fusion.1 = bf16[768,768]{1,0:T(8,128)(2,1)} fusion(bf16[1024,768]{1,0:T(8,128)(2,1)S(1)} %copy-done.54, bf16[1024,3072]{1,0:T(8,128)(2,1)} %get-tuple-element.139, s32[]{:T(128)S(6)} %select_n.85, bf16[1536,768]{1,0:T(8,128)(2,1)} %collective-permute-done.52), kind=kOutput, calls=%fused_computation.5 | convolution fusion | flops 1209729024 | bytes 5505028 | tf_op jit(solution)/shard_map/dot_general | solution.py:25
  332.9 4.2 %add_convert_fusion = bf16[768,768]{1,0:T(8,128)(2,1)} fusion(bf16[1024,768]{1,0:T(8,128)(2,1)S(1)} %copy-done.79, bf16[1024,3072]{1,0:T(8,128)(2,1)} %get-tuple-element.140, s32[]{:T(128)S(6)} %select_n.85, bf16[1536,768]{1,0:T(8,128)(2,1)} %collective-permute-done.54), kind=kOutput, calls=%fused_computation.3 | convolution fusion | flops 1209729024 | bytes 5505028 | tf_op jit(solution)/shard_map/dot_general | solution.py:25
  341.8 22.1 %collective-permute-done.53 = bf16[768,768]{1,0:T(8,128)(2,1)} collective-permute-done((bf16[768,768]{1,0:T(8,128)(2,1)}, bf16[768,768]{1,0:T(8,128)(2,1)}, u32[]{:S(2)}, u32[]{:S(2)}) %collective-permute-start.53) | collective-permute-done | bytes 1179680 | tf_op jit(solution)/shard_map/ppermute | solution.py:36
  363.9 3.6 add_bitcast_fusion.1
  367.5 19.7 %collective-permute-done.55 = bf16[768,768]{1,0:T(8,128)(2,1)} collective-permute-done((bf16[768,768]{1,0:T(8,128)(2,1)}, bf16[768,768]{1,0:T(8,128)(2,1)}, u32[]{:S(2)}, u32[]{:S(2)}) %collective-permute-start.55) | collective-permute-done | bytes 1179680 | tf_op jit(solution)/shard_map/ppermute | solution.py:36
  387.2 3.5 add_bitcast_fusion
  (316 shorter events, 107.9 us)
Async XLA Ops:
  0.7 20.0 %collective-permute-start = (bf16[256,768]{1,0:T(8,128)(2,1)}, bf16[256,768]{1,0:T(8,128)(2,1)S(1)}, u32[]{:S(2)}, u32[]{:S(2)}) collective-permute-start(bf16[256,768]{1,0:T(8,128)(2,1)} %refs_0_.3), channel_id=1, source_target_pairs={{0,1},{1,0},{2,3},{3,2},{4,5},{5,4},{6,7},{7,6},{8,9},{9,8},{10,11... | collective-permute-start | bytes 1179656 | tf_op jit(solution)/shard_map/ppermute | solution.py:36
  1.2 12.6 %collective-permute-start.1 = (bf16[256,768]{1,0:T(8,128)(2,1)}, bf16[256,768]{1,0:T(8,128)(2,1)S(1)}, u32[]{:S(2)}, u32[]{:S(2)}) collective-permute-start(bf16[256,768]{1,0:T(8,128)(2,1)} %refs_0_.3), channel_id=1, source_target_pairs={{0,2},{1,3},{2,0},{3,1},{4,6},{5,7},{6,4},{7,5},{8,10},{9,11},{10,... | collective-permute-start | bytes 1179656 | tf_op jit(solution)/shard_map/ppermute | solution.py:36
  5.6 10.0 %collective-permute-start.3 = (bf16[96,768]{1,0:T(8,128)(2,1)S(1)}, bf16[96,768]{1,0:T(8,128)(2,1)S(1)}, u32[]{:S(2)}, u32[]{:S(2)}) collective-permute-start(bf16[96,768]{1,0:T(8,128)(2,1)S(1)} %pad_maximum_fusion.4), channel_id=1, source_target_pairs={{0,16},{4,20},{8,24},{12,28},{16,0},{20,4},{24,8},{28,12},{1,17},{... | collective-permute-start | bytes 442376 | tf_op jit(solution)/shard_map/ppermute | solution.py:36
  13.8 18.7 %collective-permute-start.2 = (bf16[256,768]{1,0:T(8,128)(2,1)S(1)}, bf16[256,768]{1,0:T(8,128)(2,1)S(1)}, u32[]{:S(2)}, u32[]{:S(2)}) collective-permute-start(bf16[256,768]{1,0:T(8,128)(2,1)S(1)} %collective-permute-done.1.refs_2_), channel_id=1, source_target_pairs={{0,1},{1,0},{2,3},{3,2},{4,5},{5,4},{6,7},{7,6},{8,9},{9,8},{10,11... | collective-permute-start | bytes 1179656 | tf_op jit(solution)/shard_map/ppermute | solution.py:36
  16.6 9.1 %collective-permute-start.4 = (bf16[192,768]{1,0:T(8,128)(2,1)S(1)}, bf16[192,768]{1,0:T(8,128)(2,1)S(1)}, u32[]{:S(2)}, u32[]{:S(2)}) collective-permute-start(bf16[192,768]{1,0:T(8,128)(2,1)S(1)} %pad_maximum_fusion.3.refs_4_), channel_id=1, source_target_pairs={{0,4},{4,0},{8,12},{12,8},{16,20},{20,16},{24,28},{28,24},{1,5},{5... | collective-permute-start | bytes 884744 | tf_op jit(solution)/shard_map/ppermute | solution.py:36
  18.2 10.0 %collective-permute-start.5 = (bf16[192,768]{1,0:T(8,128)(2,1)S(1)}, bf16[192,768]{1,0:T(8,128)(2,1)S(1)}, u32[]{:S(2)}, u32[]{:S(2)}) collective-permute-start(bf16[192,768]{1,0:T(8,128)(2,1)S(1)} %pad_maximum_fusion.3.refs_4_), channel_id=1, source_target_pairs={{0,8},{4,12},{8,0},{12,4},{16,24},{20,28},{24,16},{28,20},{1,9},{5... | collective-permute-start | bytes 884744 | tf_op jit(solution)/shard_map/ppermute | solution.py:36
  18.9 13.6 %collective-permute-start.6 = (bf16[192,768]{1,0:T(8,128)(2,1)S(1)}, bf16[192,768]{1,0:T(8,128)(2,1)S(1)}, u32[]{:S(2)}, u32[]{:S(2)}) collective-permute-start(bf16[192,768]{1,0:T(8,128)(2,1)S(1)} %pad_maximum_fusion.3.refs_4_), channel_id=1, source_target_pairs={{0,12},{4,8},{8,4},{12,0},{16,28},{20,24},{24,20},{28,16},{1,13},{... | collective-permute-start | bytes 884744 | tf_op jit(solution)/shard_map/ppermute | solution.py:36
  20.6 37.5 %collective-permute-start.14 = (s32[256,2]{0,1:T(2,128)}, s32[256,2]{0,1:T(2,128)S(1)}, u32[]{:S(2)}, u32[]{:S(2)}) collective-permute-start(s32[256,2]{0,1:T(2,128)} %param.28), channel_id=1, source_target_pairs={{0,16},{4,20},{8,24},{12,28},{16,0},{20,4},{24,8},{28,12},{1,17},{... | collective-permute-start | bytes 6152 | tf_op jit(solution)/shard_map/ppermute | solution.py:36
  42.1 15.9 %collective-permute-start.11 = (bf16[192,768]{1,0:T(8,128)(2,1)S(1)}, bf16[192,768]{1,0:T(8,128)(2,1)S(1)}, u32[]{:S(2)}, u32[]{:S(2)}) collective-permute-start(bf16[192,768]{1,0:T(8,128)(2,1)S(1)} %get-tuple-element.84.refs_8_.refs_11_), channel_id=1, source_target_pairs={{0,2},{1,3},{2,0},{3,1},{4,6},{5,7},{6,4},{7,5},{8,10},{9,11},{10,... | collective-permute-start | bytes 884744 | tf_op jit(solution)/shard_map/ppermute | solution.py:36
  44.5 21.8 %collective-permute-start.10 = (bf16[192,768]{1,0:T(8,128)(2,1)S(1)}, bf16[192,768]{1,0:T(8,128)(2,1)S(1)}, u32[]{:S(2)}, u32[]{:S(2)}) collective-permute-start(bf16[192,768]{1,0:T(8,128)(2,1)S(1)} %get-tuple-element.84.refs_8_.refs_11_), channel_id=1, source_target_pairs={{0,1},{1,0},{2,3},{3,2},{4,5},{5,4},{6,7},{7,6},{8,9},{9,8},{10,11... | collective-permute-start | bytes 884744 | tf_op jit(solution)/shard_map/ppermute | solution.py:36
  59.9 29.7 %collective-permute-start.21 = (bf16[256,768]{1,0:T(8,128)(2,1)S(1)}, bf16[256,768]{1,0:T(8,128)(2,1)S(1)}, u32[]{:S(2)}, u32[]{:S(2)}) collective-permute-start(bf16[256,768]{1,0:T(8,128)(2,1)S(1)} %get-tuple-element.95.refs_0_), channel_id=1, source_target_pairs={{0,16},{4,20},{8,24},{12,28},{16,0},{20,4},{24,8},{28,12},{1,17},{... | collective-permute-start | bytes 1179656 | tf_op jit(solution)/shard_map/ppermute | solution.py:36
  69.9 27.7 %collective-permute-start.13 = (bf16[256,768]{1,0:T(8,128)(2,1)S(1)}, bf16[256,768]{1,0:T(8,128)(2,1)S(1)}, u32[]{:S(2)}, u32[]{:S(2)}) collective-permute-start(bf16[256,768]{1,0:T(8,128)(2,1)S(1)} %get-tuple-element.87), channel_id=1, source_target_pairs={{0,16},{4,20},{8,24},{12,28},{16,0},{20,4},{24,8},{28,12},{1,17},{... | collective-permute-start | bytes 1179656 | tf_op jit(solution)/shard_map/ppermute | solution.py:36
  72.5 22.0 %collective-permute-start.15 = (bf16[128,768]{1,0:T(8,128)(2,1)S(1)}, bf16[128,768]{1,0:T(8,128)(2,1)S(1)}, u32[]{:S(2)}, u32[]{:S(2)}) collective-permute-start(bf16[128,768]{1,0:T(8,128)(2,1)S(1)} %get-tuple-element.89), channel_id=1, source_target_pairs={{0,4},{4,0},{8,12},{12,8},{16,20},{20,16},{24,28},{28,24},{1,5},{5... | collective-permute-start | bytes 589832 | tf_op jit(solution)/shard_map/ppermute | solution.py:36
  90.9 24.5 %collective-permute-start.22 = (bf16[256,768]{1,0:T(8,128)(2,1)S(1)}, bf16[256,768]{1,0:T(8,128)(2,1)S(1)}, u32[]{:S(2)}, u32[]{:S(2)}) collective-permute-start(bf16[256,768]{1,0:T(8,128)(2,1)S(1)} %get-tuple-element.97), channel_id=1, source_target_pairs={{0,4},{4,0},{8,12},{12,8},{16,20},{20,16},{24,28},{28,24},{1,5},{5... | collective-permute-start | bytes 1179656 | tf_op jit(solution)/shard_map/ppermute | solution.py:36
  92.4 25.0 %collective-permute-start.23 = (bf16[256,768]{1,0:T(8,128)(2,1)S(1)}, bf16[256,768]{1,0:T(8,128)(2,1)S(1)}, u32[]{:S(2)}, u32[]{:S(2)}) collective-permute-start(bf16[256,768]{1,0:T(8,128)(2,1)S(1)} %get-tuple-element.98), channel_id=1, source_target_pairs={{0,8},{4,12},{8,0},{12,4},{16,24},{20,28},{24,16},{28,20},{1,9},{5... | collective-permute-start | bytes 1179656 | tf_op jit(solution)/shard_map/ppermute | solution.py:36
  92.6 17.6 %collective-permute-start.17 = (bf16[128,768]{1,0:T(8,128)(2,1)S(1)}, bf16[128,768]{1,0:T(8,128)(2,1)S(1)}, u32[]{:S(2)}, u32[]{:S(2)}) collective-permute-start(bf16[128,768]{1,0:T(8,128)(2,1)S(1)} %get-tuple-element.91), channel_id=1, source_target_pairs={{0,8},{4,12},{8,0},{12,4},{16,24},{20,28},{24,16},{28,20},{1,9},{5... | collective-permute-start | bytes 589832 | tf_op jit(solution)/shard_map/ppermute | solution.py:36
  94.4 21.0 %collective-permute-start.19 = (bf16[128,768]{1,0:T(8,128)(2,1)S(1)}, bf16[128,768]{1,0:T(8,128)(2,1)S(1)}, u32[]{:S(2)}, u32[]{:S(2)}) collective-permute-start(bf16[128,768]{1,0:T(8,128)(2,1)S(1)} %get-tuple-element.93), channel_id=1, source_target_pairs={{0,12},{4,8},{8,4},{12,0},{16,28},{20,24},{24,20},{28,16},{1,13},{... | collective-permute-start | bytes 589832 | tf_op jit(solution)/shard_map/ppermute | solution.py:36
  97.6 26.2 %collective-permute-start.24 = (bf16[256,768]{1,0:T(8,128)(2,1)S(1)}, bf16[256,768]{1,0:T(8,128)(2,1)S(1)}, u32[]{:S(2)}, u32[]{:S(2)}) collective-permute-start(bf16[256,768]{1,0:T(8,128)(2,1)S(1)} %get-tuple-element.99), channel_id=1, source_target_pairs={{0,12},{4,8},{8,4},{12,0},{16,28},{20,24},{24,20},{28,16},{1,13},{... | collective-permute-start | bytes 1179656 | tf_op jit(solution)/shard_map/ppermute | solution.py:36
  110.2 17.7 %collective-permute-start.16 = (bf16[128,768]{1,0:T(8,128)(2,1)S(1)}, bf16[128,768]{1,0:T(8,128)(2,1)S(1)}, u32[]{:S(2)}, u32[]{:S(2)}) collective-permute-start(bf16[128,768]{1,0:T(8,128)(2,1)S(1)} %get-tuple-element.90), channel_id=1, source_target_pairs={{0,4},{4,0},{8,12},{12,8},{16,20},{20,16},{24,28},{28,24},{1,5},{5... | collective-permute-start | bytes 589832 | tf_op jit(solution)/shard_map/ppermute | solution.py:36
  115.4 12.5 %collective-permute-start.18 = (bf16[128,768]{1,0:T(8,128)(2,1)S(1)}, bf16[128,768]{1,0:T(8,128)(2,1)S(1)}, u32[]{:S(2)}, u32[]{:S(2)}) collective-permute-start(bf16[128,768]{1,0:T(8,128)(2,1)S(1)} %get-tuple-element.92), channel_id=1, source_target_pairs={{0,8},{4,12},{8,0},{12,4},{16,24},{20,28},{24,16},{28,20},{1,9},{5... | collective-permute-start | bytes 589832 | tf_op jit(solution)/shard_map/ppermute | solution.py:36
  115.4 16.7 %collective-permute-start.20 = (bf16[128,768]{1,0:T(8,128)(2,1)S(1)}, bf16[128,768]{1,0:T(8,128)(2,1)S(1)}, u32[]{:S(2)}, u32[]{:S(2)}) collective-permute-start(bf16[128,768]{1,0:T(8,128)(2,1)S(1)} %get-tuple-element.94), channel_id=1, source_target_pairs={{0,12},{4,8},{8,4},{12,0},{16,28},{20,24},{24,20},{28,16},{1,13},{... | collective-permute-start | bytes 589832 | tf_op jit(solution)/shard_map/ppermute | solution.py:36
  163.2 9.8 %collective-permute-start.32 = (bf16[128,896]{1,0:T(8,128)(2,1)}, bf16[128,896]{1,0:T(8,128)(2,1)S(1)}, u32[]{:S(2)}, u32[]{:S(2)}) collective-permute-start(bf16[128,896]{1,0:T(8,128)(2,1)} %get-tuple-element.112), channel_id=1, source_target_pairs={{0,4},{4,0},{8,12},{12,8},{16,20},{20,16},{24,28},{28,24},{1,5},{5... | collective-permute-start | bytes 688136 | tf_op jit(solution)/shard_map/ppermute | solution.py:36
  163.8 9.2 %collective-permute-start.33 = (bf16[128,896]{1,0:T(8,128)(2,1)}, bf16[128,896]{1,0:T(8,128)(2,1)}, u32[]{:S(2)}, u32[]{:S(2)}) collective-permute-start(bf16[128,896]{1,0:T(8,128)(2,1)} %get-tuple-element.113), channel_id=1, source_target_pairs={{0,8},{4,12},{8,0},{12,4},{16,24},{20,28},{24,16},{28,20},{1,9},{5... | collective-permute-start | bytes 688136 | tf_op jit(solution)/shard_map/ppermute | solution.py:36
  163.8 14.7 %collective-permute-start.34 = (bf16[128,896]{1,0:T(8,128)(2,1)}, bf16[128,896]{1,0:T(8,128)(2,1)}, u32[]{:S(2)}, u32[]{:S(2)}) collective-permute-start(bf16[128,896]{1,0:T(8,128)(2,1)} %get-tuple-element.114), channel_id=1, source_target_pairs={{0,12},{4,8},{8,4},{12,0},{16,28},{20,24},{24,20},{28,16},{1,13},{... | collective-permute-start | bytes 688136 | tf_op jit(solution)/shard_map/ppermute | solution.py:36
  166.7 24.9 %collective-permute-start.29 = (bf16[128,896]{1,0:T(8,128)(2,1)}, bf16[128,896]{1,0:T(8,128)(2,1)S(1)}, u32[]{:S(2)}, u32[]{:S(2)}) collective-permute-start(bf16[128,896]{1,0:T(8,128)(2,1)} %get-tuple-element.108), channel_id=1, source_target_pairs={{0,4},{4,0},{8,12},{12,8},{16,20},{20,16},{24,28},{28,24},{1,5},{5... | collective-permute-start | bytes 688136 | tf_op jit(solution)/shard_map/ppermute | solution.py:36
  167.3 24.4 %collective-permute-start.30 = (bf16[128,896]{1,0:T(8,128)(2,1)}, bf16[128,896]{1,0:T(8,128)(2,1)S(1)}, u32[]{:S(2)}, u32[]{:S(2)}) collective-permute-start(bf16[128,896]{1,0:T(8,128)(2,1)} %get-tuple-element.109), channel_id=1, source_target_pairs={{0,8},{4,12},{8,0},{12,4},{16,24},{20,28},{24,16},{28,20},{1,9},{5... | collective-permute-start | bytes 688136 | tf_op jit(solution)/shard_map/ppermute | solution.py:36
  173.0 20.5 %collective-permute-start.31 = (bf16[128,896]{1,0:T(8,128)(2,1)}, bf16[128,896]{1,0:T(8,128)(2,1)S(1)}, u32[]{:S(2)}, u32[]{:S(2)}) collective-permute-start(bf16[128,896]{1,0:T(8,128)(2,1)} %get-tuple-element.110), channel_id=1, source_target_pairs={{0,12},{4,8},{8,4},{12,0},{16,28},{20,24},{24,20},{28,16},{1,13},{... | collective-permute-start | bytes 688136 | tf_op jit(solution)/shard_map/ppermute | solution.py:36
  181.2 20.8 %collective-permute-start.35 = (bf16[256,896]{1,0:T(8,128)(2,1)S(1)}, bf16[256,896]{1,0:T(8,128)(2,1)S(1)}, u32[]{:S(2)}, u32[]{:S(2)}) collective-permute-start(bf16[256,896]{1,0:T(8,128)(2,1)S(1)} %back_from_slots.1), channel_id=1, source_target_pairs={{0,16},{4,20},{8,24},{12,28},{16,0},{20,4},{24,8},{28,12},{1,17},{... | collective-permute-start | bytes 1376264 | tf_op jit(solution)/shard_map/ppermute | solution.py:36
  211.3 10.7 %collective-permute-start.36 = (bf16[256,192]{1,0:T(8,128)(2,1)}, bf16[256,192]{1,0:T(8,128)(2,1)S(1)}, u32[]{:S(2)}, u32[]{:S(2)}) collective-permute-start(bf16[256,192]{1,0:T(8,128)(2,1)} %get-tuple-element.117), channel_id=1, source_target_pairs={{0,1},{1,0},{2,3},{3,2},{4,5},{5,4},{6,7},{7,6},{8,9},{9,8},{10,11... | collective-permute-start | bytes 294920 | tf_op jit(solution)/shard_map/ppermute | solution.py:36
  211.4 10.7 %collective-permute-start.37 = (bf16[256,192]{1,0:T(8,128)(2,1)}, bf16[256,192]{1,0:T(8,128)(2,1)S(1)}, u32[]{:S(2)}, u32[]{:S(2)}) collective-permute-start(bf16[256,192]{1,0:T(8,128)(2,1)} %get-tuple-element.118), channel_id=1, source_target_pairs={{0,2},{1,3},{2,0},{3,1},{4,6},{5,7},{6,4},{7,5},{8,10},{9,11},{10,... | collective-permute-start | bytes 294920 | tf_op jit(solution)/shard_map/ppermute | solution.py:36
  212.9 9.1 %collective-permute-start.38 = (bf16[256,192]{1,0:T(8,128)(2,1)}, bf16[256,192]{1,0:T(8,128)(2,1)S(1)}, u32[]{:S(2)}, u32[]{:S(2)}) collective-permute-start(bf16[256,192]{1,0:T(8,128)(2,1)} %get-tuple-element.119), channel_id=1, source_target_pairs={{0,3},{1,2},{2,1},{3,0},{4,7},{5,6},{6,5},{7,4},{8,11},{9,10},{10,... | collective-permute-start | bytes 294920 | tf_op jit(solution)/shard_map/ppermute | solution.py:36
  220.5 22.8 %collective-permute-start.40 = (bf16[768,192]{1,0:T(8,128)(2,1)}, bf16[768,192]{1,0:T(8,128)(2,1)}, u32[]{:S(2)}, u32[]{:S(2)}) collective-permute-start(bf16[768,192]{1,0:T(8,128)(2,1)} %fusion.33), channel_id=1, source_target_pairs={{0,2},{1,3},{2,0},{3,1},{4,6},{5,7},{6,4},{7,5},{8,10},{9,11},{10,... | collective-permute-start | bytes 884744 | tf_op jit(solution)/shard_map/ppermute | solution.py:36
  257.7 11.9 %collective-permute-start.25 = (bf16[256,768]{1,0:T(8,128)(2,1)S(1)}, bf16[256,768]{1,0:T(8,128)(2,1)S(1)}, u32[]{:S(2)}, u32[]{:S(2)}) collective-permute-start(bf16[256,768]{1,0:T(8,128)(2,1)S(1)} %copy-done.67), channel_id=1, source_target_pairs={{0,4},{4,0},{8,12},{12,8},{16,20},{20,16},{24,28},{28,24},{1,5},{5... | collective-permute-start | bytes 1179656 | tf_op jit(solution)/shard_map/ppermute | solution.py:36
  258.3 12.0 %collective-permute-start.26 = (bf16[256,768]{1,0:T(8,128)(2,1)S(1)}, bf16[256,768]{1,0:T(8,128)(2,1)S(1)}, u32[]{:S(2)}, u32[]{:S(2)}) collective-permute-start(bf16[256,768]{1,0:T(8,128)(2,1)S(1)} %copy-done.66), channel_id=1, source_target_pairs={{0,8},{4,12},{8,0},{12,4},{16,24},{20,28},{24,16},{28,20},{1,9},{5... | collective-permute-start | bytes 1179656 | tf_op jit(solution)/shard_map/ppermute | solution.py:36
  259.0 19.8 %collective-permute-start.27 = (bf16[256,768]{1,0:T(8,128)(2,1)S(1)}, bf16[256,768]{1,0:T(8,128)(2,1)S(1)}, u32[]{:S(2)}, u32[]{:S(2)}) collective-permute-start(bf16[256,768]{1,0:T(8,128)(2,1)S(1)} %copy-done.65), channel_id=1, source_target_pairs={{0,12},{4,8},{8,4},{12,0},{16,28},{20,24},{24,20},{28,16},{1,13},{... | collective-permute-start | bytes 1179656 | tf_op jit(solution)/shard_map/ppermute | solution.py:36
  263.5 63.8 %collective-permute-start.52 = (bf16[1536,768]{1,0:T(8,128)(2,1)}, bf16[1536,768]{1,0:T(8,128)(2,1)}, u32[]{:S(2)}, u32[]{:S(2)}) collective-permute-start(bf16[1536,768]{1,0:T(8,128)(2,1)} %pad_maximum_fusion), channel_id=1, source_target_pairs={{0,1},{1,0},{2,3},{3,2},{4,5},{5,4},{6,7},{7,6},{8,9},{9,8},{10,11... | collective-permute-start | bytes 7077896 | tf_op jit(solution)/shard_map/ppermute | solution.py:36
  265.3 16.9 %collective-permute-start.45 = (f32[8064]{0:T(1024)S(1)}, f32[8064]{0:T(1024)S(1)}, u32[]{:S(2)}, u32[]{:S(2)}) collective-permute-start(f32[8064]{0:T(1024)S(1)} %add.167), channel_id=1, source_target_pairs={{0,4},{4,0},{8,12},{12,8},{16,20},{20,16},{24,28},{28,24},{1,5},{5... | collective-permute-start | bytes 96776 | tf_op jit(solution)/shard_map/ppermute | solution.py:36
  279.9 20.9 %collective-permute-start.28 = (bf16[256,768]{1,0:T(8,128)(2,1)S(1)}, bf16[256,768]{1,0:T(8,128)(2,1)S(1)}, u32[]{:S(2)}, u32[]{:S(2)}) collective-permute-start(bf16[256,768]{1,0:T(8,128)(2,1)S(1)} %get-tuple-element.105), channel_id=1, source_target_pairs={{0,16},{4,20},{8,24},{12,28},{16,0},{20,4},{24,8},{28,12},{1,17},{... | collective-permute-start | bytes 1179656 | tf_op jit(solution)/shard_map/ppermute | solution.py:36
  285.7 47.2 %collective-permute-start.54 = (bf16[1536,768]{1,0:T(8,128)(2,1)}, bf16[1536,768]{1,0:T(8,128)(2,1)}, u32[]{:S(2)}, u32[]{:S(2)}) collective-permute-start(bf16[1536,768]{1,0:T(8,128)(2,1)} %pad_maximum_fusion.1), channel_id=1, source_target_pairs={{0,1},{1,0},{2,3},{3,2},{4,5},{5,4},{6,7},{7,6},{8,9},{9,8},{10,11... | collective-permute-start | bytes 7077896 | tf_op jit(solution)/shard_map/ppermute | solution.py:36
  291.2 10.0 %collective-permute-start.47 = (f32[8064]{0:T(1024)S(1)}, f32[8064]{0:T(1024)S(1)}, u32[]{:S(2)}, u32[]{:S(2)}) collective-permute-start(f32[8064]{0:T(1024)S(1)} %add.169), channel_id=1, source_target_pairs={{0,16},{4,20},{8,24},{12,28},{16,0},{20,4},{24,8},{28,12},{1,17},{... | collective-permute-start | bytes 96776 | tf_op jit(solution)/shard_map/ppermute | solution.py:36
  297.7 10.9 %collective-permute-start.50 = (bf16[192,768]{1,0:T(8,128)(2,1)S(1)}, bf16[192,768]{1,0:T(8,128)(2,1)S(1)}, u32[]{:S(2)}, u32[]{:S(2)}) collective-permute-start(bf16[192,768]{1,0:T(8,128)(2,1)S(1)} %copy-done.20), channel_id=1, source_target_pairs={{0,12},{4,8},{8,4},{12,0},{16,28},{20,24},{24,20},{28,16},{1,13},{... | collective-permute-start | bytes 884744 | tf_op jit(solution)/shard_map/ppermute | solution.py:36
  300.7 13.0 %collective-permute-start.49 = (bf16[192,768]{1,0:T(8,128)(2,1)S(1)}, bf16[192,768]{1,0:T(8,128)(2,1)}, u32[]{:S(2)}, u32[]{:S(2)}) collective-permute-start(bf16[192,768]{1,0:T(8,128)(2,1)S(1)} %get-tuple-element.136), channel_id=1, source_target_pairs={{0,8},{4,12},{8,0},{12,4},{16,24},{20,28},{24,16},{28,20},{1,9},{5... | collective-permute-start | bytes 884744 | tf_op jit(solution)/shard_map/ppermute | solution.py:36
  301.1 12.6 %collective-permute-start.48 = (bf16[192,768]{1,0:T(8,128)(2,1)S(1)}, bf16[192,768]{1,0:T(8,128)(2,1)}, u32[]{:S(2)}, u32[]{:S(2)}) collective-permute-start(bf16[192,768]{1,0:T(8,128)(2,1)S(1)} %get-tuple-element.135), channel_id=1, source_target_pairs={{0,4},{4,0},{8,12},{12,8},{16,20},{20,16},{24,28},{28,24},{1,5},{5... | collective-permute-start | bytes 884744 | tf_op jit(solution)/shard_map/ppermute | solution.py:36
  308.6 16.3 %collective-permute-start.41 = (bf16[512,768]{1,0:T(8,128)(2,1)S(1)}, bf16[512,768]{1,0:T(8,128)(2,1)}, u32[]{:S(2)}, u32[]{:S(2)}) collective-permute-start(bf16[512,768]{1,0:T(8,128)(2,1)S(1)} %get-tuple-element.129), channel_id=1, source_target_pairs={{0,1},{1,0},{2,3},{3,2},{4,5},{5,4},{6,7},{7,6},{8,9},{9,8},{10,11... | collective-permute-start | bytes 2359304 | tf_op jit(solution)/shard_map/ppermute | solution.py:36
  315.0 9.8 %collective-permute-start.51 = (bf16[96,768]{1,0:T(8,128)(2,1)S(1)}, bf16[96,768]{1,0:T(8,128)(2,1)S(1)}, u32[]{:S(2)}, u32[]{:S(2)}) collective-permute-start(bf16[96,768]{1,0:T(8,128)(2,1)S(1)} %slice.177), channel_id=1, source_target_pairs={{0,16},{4,20},{8,24},{12,28},{16,0},{20,4},{24,8},{28,12},{1,17},{... | collective-permute-start | bytes 442376 | tf_op jit(solution)/shard_map/ppermute | solution.py:36
  326.4 14.0 %collective-permute-start.42 = (bf16[256,768]{1,0:T(8,128)(2,1)S(1)}, bf16[256,768]{1,0:T(8,128)(2,1)S(1)}, u32[]{:S(2)}, u32[]{:S(2)}) collective-permute-start(bf16[256,768]{1,0:T(8,128)(2,1)S(1)} %slice.176), channel_id=1, source_target_pairs={{0,2},{1,3},{2,0},{3,1},{4,6},{5,7},{6,4},{7,5},{8,10},{9,11},{10,... | collective-permute-start | bytes 1179656 | tf_op jit(solution)/shard_map/ppermute | solution.py:36
  331.7 32.2 %collective-permute-start.53 = (bf16[768,768]{1,0:T(8,128)(2,1)}, bf16[768,768]{1,0:T(8,128)(2,1)}, u32[]{:S(2)}, u32[]{:S(2)}) collective-permute-start(bf16[768,768]{1,0:T(8,128)(2,1)} %add_convert_fusion.1), channel_id=1, source_target_pairs={{0,2},{1,3},{2,0},{3,1},{4,6},{5,7},{6,4},{7,5},{8,10},{9,11},{10,... | collective-permute-start | bytes 3538952 | tf_op jit(solution)/shard_map/ppermute | solution.py:36
  337.1 50.1 %collective-permute-start.55 = (bf16[768,768]{1,0:T(8,128)(2,1)}, bf16[768,768]{1,0:T(8,128)(2,1)}, u32[]{:S(2)}, u32[]{:S(2)}) collective-permute-start(bf16[768,768]{1,0:T(8,128)(2,1)} %add_convert_fusion), channel_id=1, source_target_pairs={{0,2},{1,3},{2,0},{3,1},{4,6},{5,7},{6,4},{7,5},{8,10},{9,11},{10,... | collective-permute-start | bytes 3538952 | tf_op jit(solution)/shard_map/ppermute | solution.py:36
  (88 other events, 672.6 us)

commit v2 on v1

--- a/solution.py
+++ b/solution.py
@@ -36,26 +36,41 @@
     return lax.ppermute(values, axis, [(i, i ^ step) for i in range(count)])
 
 
-def call(kernel, name, operands, outs, scratch=(), flops=0, limit=32, scalars=None):
-    vmem = pl.BlockSpec(memory_space=pltpu.VMEM)
-    in_specs = [vmem] * len(operands)
+def whole(dims):
+    return pl.BlockSpec(tuple(dims), lambda *_: (0,) * len(dims), pipeline_mode=pl.Buffered(1))
+
+
+def call(
+    kernel, name, operands, outs, scratch=(), flops=0, limit=32, scalars=None, after=(), through=()
+):
+    operands, outs = list(operands), list(outs)
+    moved = sum(math.prod(o.shape) * o.dtype.itemsize for o in operands + outs)
+    in_specs = [whole(o.shape) for o in operands]
+    out_specs = [whole(o.shape) for o in outs]
     if scalars is not None:
-        operands = [scalars] + list(operands)
+        operands = [scalars] + operands
         in_specs = [pl.BlockSpec(memory_space=pltpu.SMEM)] + in_specs
-    moved = sum(math.prod(o.shape) * o.dtype.itemsize for o in operands)
-    moved += sum(math.prod(o.shape) * o.dtype.itemsize for o in outs)
+    count, results = len(operands), len(outs)
+    extra = list(through) + list(after)
+
+    def body(*refs):
+        rest = refs[count + len(extra) :]
+        kernel(*refs[:count], *rest[:results], *rest[results + len(through) :])
+
     return pl.pallas_call(
-        kernel,
+        body,
         name=name,
-        in_specs=in_specs,
-        out_specs=[vmem] * len(outs),
-        out_shape=outs,
+        grid=(1,),
+        in_specs=in_specs + [pl.BlockSpec(memory_space=pl.ANY)] * len(extra),
+        out_specs=out_specs + [pl.BlockSpec(memory_space=pl.ANY)] * len(through),
+        out_shape=outs + [shape(o.shape, o.dtype) for o in through],
+        input_output_aliases={count + i: results + i for i in range(len(through))},
         scratch_shapes=list(scratch),
         compiler_params=pltpu.CompilerParams(vmem_limit_bytes=limit * 1024 * 1024),
         cost_estimate=pl.CostEstimate(
             flops=int(flops), bytes_accessed=int(moved), transcendentals=0
         ),
-    )(*operands)
+    )(*operands, *extra)
 
 
 def shape(dims, dtype):
@@ -135,7 +150,7 @@
         out_ref[...] = mixed[pl.ds(pl.multiple_of((place[1] ^ r) * rows, rows), rows), :]
 
 
-def attend(place, query, key_rows, value_rows, seg_q, seg_k, line, heads, members):
+def attend(place, query, key_rows, value_rows, seg_q, seg_k, line, heads, members, after):
     seq_len, span = query.shape
     window = reach + tile
 
@@ -155,6 +170,7 @@
         ],
         flops=4 * seq_len * window * heads * 256,
         scalars=place,
+        after=after,
     )
 
 
@@ -207,7 +223,7 @@
         line_grad_ref[head : head + 1, :] = jnp.sum(straight, axis=0, keepdims=True)
 
 
-def attend_back(place, query, key_rows, value_rows, seg_q, seg_k, line, grads, heads):
+def attend_back(place, query, key_rows, value_rows, seg_q, seg_k, line, grads, heads, after):
     seq_len, span = query.shape
     window = reach + tile
 
@@ -231,20 +247,51 @@
         flops=10 * seq_len * window * heads * 256,
         limit=48,
         scalars=place,
-    )
-
-
-def project(place, token_blocks, pack_blocks, gain, cotangent, span):
+        after=after,
+    )
+
+
+def pack_weights(w_query, w_key, w_value, w_output):
+    part, span = w_query.shape
+
+    def kernel(q_ref, k_ref, v_ref, o_ref, pack_ref):
+        for at, ref in enumerate((q_ref, k_ref, v_ref)):
+            pack_ref[:, at * span : (at + 1) * span] = ref[...]
+        pack_ref[:, 3 * span :] = o_ref[...].astype(f32).T.astype(bf16)
+
+    (pack,) = call(
+        kernel, "pack_weights", [w_query, w_key, w_value, w_output], [shape((part, 4 * span), bf16)]
+    )
+    return pack
+
+
+def pair_up(pack, far, cotangent):
+    part = pack.shape[0]
+
+    def kernel(near_ref, far_ref, both_ref):
+        both_ref[:part, :] = near_ref[...]
+        both_ref[part:, :] = far_ref[...]
+
+    return call(
+        kernel,
+        "pair_up",
+        [pack, far],
+        [shape((2 * part, pack.shape[1]), bf16)],
+        through=[cotangent],
+    )
+
+
+def project(place, token_blocks, pack_blocks, gain, span):
     rows, width = token_blocks[0].shape
     members = len(token_blocks)
     seq_len = rows * members
     parts = sum(len(held) for _, held in pack_blocks)
     part = width // parts
 
-    def kernel(place_ref, gain_ref, cot_ref, *refs):
+    def kernel(place_ref, gain_ref, *refs):
         token_refs = refs[:members]
         pack_refs = refs[members : members + len(pack_blocks)]
-        (normed_ref, q_ref, k_ref, v_ref, wq_ref, wk_ref, wv_ref, wo_ref, late_ref, pack) = refs[
+        (normed_ref, q_ref, k_ref, v_ref, wq_ref, wk_ref, wv_ref, wo_ref, pack) = refs[
             members + len(pack_blocks) :
         ]
         for (_, held), ref in zip(pack_blocks, pack_refs):
@@ -262,16 +309,15 @@
             q_ref[at, :] = dot(normed, wq_ref[...], 1, 0).astype(bf16)
             k_ref[at, :] = dot(normed, wk_ref[...], 1, 0).astype(bf16)
             v_ref[at, :] = dot(normed, wv_ref[...], 1, 0).astype(bf16)
-        late_ref[...] = cot_ref[...]
 
     return call(
         kernel,
         "project",
-        [gain, cotangent] + list(token_blocks) + [array for array, _ in pack_blocks],
+        [gain] + list(token_blocks) + [array for array, _ in pack_blocks],
         [shape((seq_len, width), bf16)]
         + [shape((seq_len, span), bf16)] * 3
         + [shape((width, span), bf16)] * 3
-        + [shape((span, width), bf16), shape((rows, width), bf16)],
+        + [shape((span, width), bf16)],
         scratch=[pltpu.VMEM((width, width), bf16)],
         flops=2 * seq_len * width * 4 * span,
         scalars=place,
@@ -306,7 +352,7 @@
     )
 
 
-def from_slots(name, blocks, slots, size, dtypes):
+def from_slots(name, blocks, slots, size, dtypes, after=(), through=()):
     count, sets = len(blocks), len(slots)
     width = blocks[0].shape[1]
     rows = slots[0].shape[1]
@@ -327,6 +373,8 @@
         list(blocks) + list(slots),
         [shape((rows, width), dtype) for dtype in dtypes],
         flops=2 * sets * count * size * rows * width,
+        after=after,
+        through=through,
     )
 
 
@@ -338,7 +386,7 @@
     return powers / jnp.sum(powers, axis=-1, keepdims=True)
 
 
-def middle(tokens, mixed, weight_o, gain, w_router, slots, experts, blocks, size):
+def middle(tokens, mixed, weight_o, gain, w_router, slots, experts, blocks, size, after):
     rows, width = tokens.shape
     members = len(mixed)
 
@@ -364,6 +412,7 @@
         [shape((rows, width), f32), shape((rows, width), bf16), shape((rows, 128), f32)]
         + [shape((size, width), bf16)] * blocks,
         flops=2 * rows * width * (width + blocks * size),
+        after=after,
     )
 
 
@@ -431,9 +480,6 @@
     size, each = x_blocks[0].shape[0], g_blocks[0].shape[0]
     total = size * count
     piece = 512
-
-    def whole(dims):
-        return pl.BlockSpec(tuple(dims), lambda i: (0, 0))
 
     columns = pl.BlockSpec((total, piece), lambda i: (0, i))
     outs = (
@@ -478,20 +524,35 @@
     )
 
 
-def home(own_back, far_sum, slots, hidden, probs, cotangent, gain, w_router, weight_o, size):
+def home(
+    own_back,
+    far_sum,
+    slots,
+    hidden,
+    probs,
+    cotangent,
+    gain,
+    w_router,
+    ffn_input,
+    weight_o,
+    mixed,
+    size,
+    experts,
+    after,
+):
     rows, width = hidden.shape
     count, members = len(own_back), len(weight_o)
     span = weight_o[0].shape[0]
     far = [] if far_sum is None else [far_sum]
 
     def kernel(*refs):
-        slots_ref, hidden_ref, probs_ref, cot_ref, gain_ref, router_ref = refs[:6]
-        back_refs = refs[6 : 6 + count]
-        far_refs = refs[6 + count : 6 + count + len(far)]
-        weight_refs = refs[6 + count + len(far) : 6 + count + len(far) + members]
-        outs = refs[6 + count + len(far) + members :]
-        grad_refs = outs[:members]
-        attn_ref, hidden_grad_ref, gain_grad_ref, logit_ref = outs[members:]
+        slots_ref, hidden_ref, probs_ref, cot_ref, gain_ref, router_ref, input_ref = refs[:7]
+        refs = refs[7:]
+        back_refs, refs = refs[:count], refs[count:]
+        far_refs, refs = refs[: len(far)], refs[len(far) :]
+        weight_refs, mixed_refs, refs = refs[:members], refs[members : 2 * members], refs[2 * members :]
+        grad_refs = refs[:members]
+        hidden_grad_ref, gain_grad_ref, router_grad_ref, near_ref, base_ref = refs[members:]
         total = None
         for b, ref in enumerate(back_refs):
             part = dot(hot(slots_ref, b * size, size), ref[...], 0, 0)
@@ -505,7 +566,7 @@
         logit_grad = router_probs * (
             prob_grad - jnp.sum(router_probs * prob_grad, axis=-1, keepdims=True)
         )
-        logit_ref[...] = logit_grad
+        router_grad_ref[...] = dot(logit_grad, input_ref[...].astype(f32), 0, 0, highest)[:experts, :]
         grad = total[:, :width] + dot(logit_grad, router_ref[...].astype(f32), 1, 1, highest)
         hidden_now = hidden_ref[...]
         inverse = lax.rsqrt(jnp.mean(hidden_now * hidden_now, axis=-1, keepdims=True) + eps)
@@ -519,35 +580,107 @@
         )
         hidden_grad_ref[...] = hidden_grad
         attn_grad = hidden_grad.astype(bf16)
-        attn_ref[...] = attn_grad
         for ref, weight in zip(grad_refs, weight_refs):
             ref[...] = dot(attn_grad, weight[...], 1, 1).astype(bf16)
+        for r, (ref, first) in enumerate(
+            ((base_ref, 0), (near_ref, 0), (base_ref, span), (near_ref, span))
+        ):
+            part = dot(attn_grad, mixed_refs[r][...], 0, 0)
+            ref[:, first : first + span] = part.astype(ref.dtype)
 
     return call(
         kernel,
         "home",
-        [slots, hidden, probs, cotangent, gain, w_router] + list(own_back) + far + weight_o,
+        [slots, hidden, probs, cotangent, gain, w_router, ffn_input]
+        + list(own_back)
+        + far
+        + weight_o
+        + mixed,
         [shape((rows, span), bf16)] * members
         + [
-            shape((rows, width), bf16),
             shape((rows, width), f32),
             shape((1, width), f32),
-            shape((rows, 128), f32),
+            shape((experts, width), f32),
+            shape((width, 2 * span), bf16),
+            shape((width, 2 * span), f32),
         ],
-        flops=2 * rows * width * (width + size * count),
-    )
-
-
-def input_grads(place, proj_grads, normed, weights, output_sum, gain, members, owners):
+        flops=2 * rows * width * (2 * width + size * count),
+        after=after,
+    )
+
+
+def expert_weight_grads(name, place, fixed, cut, cut_left, members):
+    total, width = fixed.shape
+    piece = cut.shape[1] // members
+    dims = (piece, width) if cut_left else (width, piece)
+
+    def kernel(place_ref, fixed_ref, cut_ref, near_ref, base_ref):
+        pair = (cut_ref, fixed_ref) if cut_left else (fixed_ref, cut_ref)
+        part = dot(pair[0][...], pair[1][...], 0, 0)
+
+        @pl.when(pl.program_id(0) < 2)
+        def _():
+            near_ref[...] = part.astype(bf16)
+
+        @pl.when(pl.program_id(0) >= 2)
+        def _():
+            base_ref[...] = part
+
+    def cut_map(i, place_ref):
+        return (0, place_ref[1] ^ jnp.where(i < 2, 2 * i + 1, 2 * i - 4))
+
+    return pl.pallas_call(
+        kernel,
+        name=name,
+        grid_spec=pltpu.PrefetchScalarGridSpec(
+            num_scalar_prefetch=1,
+            grid=(4,),
+            in_specs=[
+                pl.BlockSpec((total, width), lambda i, p: (0, 0)),
+                pl.BlockSpec((total, piece), cut_map),
+            ],
+            out_specs=[
+                pl.BlockSpec(dims, lambda i, p: (jnp.minimum(i, 1), 0)),
+                pl.BlockSpec(dims, lambda i, p: (jnp.maximum(i - 2, 0), 0)),
+            ],
+        ),
+        out_shape=[shape((2 * dims[0], dims[1]), bf16), shape((2 * dims[0], dims[1]), f32)],
+        compiler_params=pltpu.CompilerParams(vmem_limit_bytes=40 * 1024 * 1024),
+        cost_estimate=pl.CostEstimate(
+            flops=8 * total * width * piece,
+            bytes_accessed=2 * total * (width + 4 * piece) + 12 * width * piece,
+            transcendentals=0,
+        ),
+    )(place, fixed, cut)
+
+
+def input_grads(
+    place,
+    proj_grads,
+    normed,
+    weights,
+    output_sum,
+    gain,
+    line_grad,
+    bucket_hot,
+    ffn_gain_grad,
+    router_grad,
+    members,
+    owners,
+    heads,
+    after,
+):
     seq_len, width = normed.shape
     span = weights[0].shape[1]
     rows = seq_len // members
     part = width // owners
     few = owners == 8
+    experts = router_grad.shape[0]
 
     def kernel(place_ref, *refs):
         dq_ref, dk_ref, dv_ref, normed_ref, wq_ref, wk_ref, wv_ref, out_ref, gain_ref = refs[:9]
-        near_ref, base_ref, gain_grad_ref, *weight_refs, sums = refs[9:]
+        line_ref, hot_ref, ffn_gain_ref, router_ref = refs[9:13]
+        near_ref, base_ref, far_ref, small_ref, *weight_refs, sums = refs[13:]
         for at, ref in enumerate((dq_ref, dk_ref, dv_ref)):
             sums[:, at * span : (at + 1) * span] = dot(normed_ref[...], ref[...], 0, 0)
         sums[:, 3 * span :] = out_ref[...]
@@ -560,7 +693,7 @@
             weight_refs[0][...] = sums[...]
         gain_grad = jnp.zeros((1, width), f32)
         for r, (ref, first) in enumerate(
-            ((base_ref, 0), (near_ref, 0), (base_ref, rows), (near_ref, rows))
+            ((base_ref, 0), (near_ref, 0), (far_ref, 0), (near_ref, rows))
         ):
             at = pl.ds(pl.multiple_of((place_ref[1] ^ r) * rows, rows), rows)
             grad = (
@@ -572,7 +705,14 @@
                 grad * normed_ref[at, :].astype(f32), axis=0, keepdims=True
             )
             ref[first : first + rows, :] = grad.astype(ref.dtype)
-        gain_grad_ref[...] = gain_grad / gain_ref[...]
+        small_ref[...] = jnp.zeros_like(small_ref)
+        small_ref[0:1, :] = gain_grad / gain_ref[...]
+        small_ref[1:2, :] = ffn_gain_ref[...]
+        table = dot(line_ref[...], hot_ref[...], 1, 0, highest)
+        for m in range(members):
+            own = jnp.where(place_ref[1] == m, table[:heads, :], 0.0)
+            small_ref[2 + m * heads : 2 + (m + 1) * heads, :128] = own
+        small_ref[16:, :] = router_ref[...]
 
     if few:
         weight_outs = [shape((2 * part, 4 * span), f32)] + [shape((2 * part, 4 * span), bf16)] * 3
@@ -581,13 +721,61 @@
     return call(
         kernel,
         "input_grads",
-        list(proj_grads) + [normed] + list(weights) + [output_sum, gain],
-        [shape((2 * rows, width), bf16), shape((2 * rows, width), f32), shape((1, width), f32)]
+        list(proj_grads)
+        + [normed]
+        + list(weights)
+        + [output_sum, gain, line_grad, bucket_hot, ffn_gain_grad, router_grad],
+        [
+            shape((2 * rows, width), bf16),
+            shape((rows, width), f32),
+            shape((rows, width), f32),
+            shape((16 + experts, width), f32),
+        ]
         + weight_outs,
         scratch=[pltpu.VMEM((width, 4 * span), f32)],
         flops=4 * seq_len * width * 3 * span,
         limit=48,
         scalars=place,
+        after=after,
+    )
+
+
+def fold_weights(base, arrived):
+    part, width = base.shape[0] // 2, base.shape[1]
+
+    def kernel(base_ref, *refs):
+        own_ref, far_ref = refs[-2:]
+        total = base_ref[...]
+        for ref in refs[:-2]:
+            total = total + ref[...].astype(f32)
+        own_ref[...] = total[:part, :]
+        far_ref[...] = total[part:, :].astype(bf16)
+
+    return call(
+        kernel,
+        "fold_weights",
+        [base] + arrived,
+        [shape((part, width), f32), shape((part, width), bf16)],
+    )
+
+
+def split_weights(parts, span):
+    part = parts[0].shape[0]
+
+    def kernel(*refs):
+        q_ref, k_ref, v_ref, o_ref = refs[-4:]
+        total = refs[0][...]
+        for ref in refs[1:-4]:
+            total = total + ref[...].astype(f32)
+        for at, ref in enumerate((q_ref, k_ref, v_ref)):
+            ref[...] = total[:, at * span : (at + 1) * span]
+        o_ref[...] = total[:, 3 * span :].T
+
+    return call(
+        kernel,
+        "split_weights",
+        parts,
+        [shape((part, span), f32)] * 3 + [shape((span, part), f32)],
     )
 
 
@@ -596,12 +784,15 @@
     return [values, swap(values, "mp", 1), across, swap(across, "mp", 1)]
 
 
-def scatter_sum_mp(blocks):
-    near = swap(jnp.concatenate([blocks[1], blocks[3]], axis=0).astype(bf16), "mp", 1)
-    size = blocks[0].shape[0]
-    far = blocks[2].astype(f32) + near[size:].astype(f32)
-    far = swap(far.astype(bf16), "mp", 2)
-    return blocks[0].astype(f32) + near[:size].astype(f32) + far.astype(f32)
+def scatter_near(near, base, axis):
+    size = base.shape[axis] // 2
+    near = swap(near, "mp", 1)
+    own, far = [
+        lax.slice_in_dim(base, i * size, (i + 1) * size, axis=axis)
+        + lax.slice_in_dim(near, i * size, (i + 1) * size, axis=axis).astype(f32)
+        for i in (0, 1)
+    ]
+    return own, far.astype(bf16)
 
 
 def sum_all(values):
@@ -661,15 +852,16 @@
     few = owners == 8
 
     token_blocks = gather_mp(tokens)
-    pack = jnp.concatenate([w_query, w_key, w_value, w_output.T], axis=1)
+    pack = pack_weights(w_query, w_key, w_value, w_output)
     if few:
-        both = jnp.concatenate([pack, swap(pack, "dp", 4)], axis=0)
+        both, late_cotangent = pair_up(pack, swap(pack, "dp", 4), cotangent)
         pack_blocks = [(both, (0, 4))] + [(swap(both, "dp", r), (r, r ^ 4)) for r in (1, 2, 3)]
     else:
+        late_cotangent = cotangent
         pack_blocks = [(lax.all_gather(pack, "dp", axis=0, tiled=True), (0,))]
     gain_one, gain_two = norm_gain.reshape(1, width), ffn_gain.reshape(1, width)
-    normed, query, key_rows, value_rows, weight_q, weight_k, weight_v, w_o, late_cotangent = (
-        project(place, token_blocks, pack_blocks, gain_one, cotangent, span)
+    normed, query, key_rows, value_rows, weight_q, weight_k, weight_v, w_o = project(
+        place, token_blocks, pack_blocks, gain_one, span
     )
     weight_o = gather_mp(w_o)
 
@@ -696,18 +888,30 @@
 
     line_buckets = jnp.pad(jnp.flip(buckets[: reach + 1]), (0, window - reach - 1))
     bucket_hot = (
-        line_buckets[:, None] == jnp.arange(bias_table.shape[0], dtype=jnp.int32)[None, :]
+        line_buckets[:, None] == jnp.arange(128, dtype=jnp.int32)[None, :]
     ).astype(f32)
-    line = jnp.dot(bias_table.T, bucket_hot.T, precision=highest)
-    line = jnp.pad(line, ((0, 8 - heads), (0, 0)))
+    buckets_all = bias_table.shape[0]
+    table = jnp.pad(bias_table.T, ((0, 8 - heads), (0, 128 - buckets_all)))
+    line = jnp.dot(table, bucket_hot.T, precision=highest)
     seg_q = segments.reshape(seq_len, 1)
     seg_k = jnp.pad(segments.reshape(1, seq_len), ((0, 0), (reach, 0)), constant_values=-1)
-    mixed_out = attend(place, query, key_rows, value_rows, seg_q, seg_k, line, heads, members)
+    mixed_out = attend(
+        place, query, key_rows, value_rows, seg_q, seg_k, line, heads, members, held[:1]
+    )
     mixed_in = [mixed_out[0]] + [swap(mixed_out[r], "mp", r) for r in range(1, members)]
 
     router_wide = jnp.pad(w_router, ((0, 0), (0, 128 - experts)))
     hidden, ffn_input, router_probs, *send = middle(
-        tokens, mixed_in, weight_o, gain_two, router_wide, slots[0], experts, blocks, size
+        tokens,
+        mixed_in,
+        weight_o,
+        gain_two,
+        router_wide,
+        slots[0],
+        experts,
+        blocks,
+        size,
+        g_blocks[1:],
     )
     if few:
         far_input = swap(ffn_input, "dp", 4)
@@ -721,15 +925,29 @@
     back, result, active, pre_grad, arrived, slot_grad = run_experts(
         place, w_in[0], w_out[0], router_wide, x_blocks, g_blocks, experts
     )
+    near_in, base_in = expert_weight_grads(
+        "w_in_grads", place, arrived, pre_grad, False, members
+    )
+    near_out, base_out = expert_weight_grads(
+        "w_out_grads", place, slot_grad, active, True, members
+    )
     if few:
         far_back = [back[1]] + [swap(back[2 * r + 1], "dp", r) for r in (1, 2, 3)]
-        (far_total,) = from_slots("back_from_slots", far_back, [slots[1]], size, [bf16])
+        far_total, *own_back = from_slots(
+            "back_from_slots",
+            far_back,
+            [slots[1]],
+            size,
+            [bf16],
+            after=[near_in],
+            through=back[2::2],
+        )
         far_sum = swap(far_total, "dp", 4)
-        own_back = [back[0]] + [swap(back[2 * r], "dp", r) for r in (1, 2, 3)]
+        own_back = [back[0]] + [swap(own_back[r - 1], "dp", r) for r in (1, 2, 3)]
     else:
         own_back, far_sum = [all_to_all_dp(back[0])], None
 
-    *grad_out, attn_grad, hidden_grad, ffn_gain_grad, logit_grad = home(
+    *grad_out, hidden_grad, ffn_gain_grad, router_grad, near_o, base_o = home(
         own_back,
         far_sum,
         slots[0],
@@ -738,36 +956,68 @@
         cotangent,
         gain_two,
         router_wide,
+        ffn_input,
         weight_o,
+        mixed_in,
         size,
+        experts,
+        [near_out],
     )
     grad_in = [grad_out[0]] + [swap(grad_out[r], "mp", r) for r in range(1, members)]
+    own_in, far_in = scatter_near(near_in, base_in, 0)
+    own_out, far_out = scatter_near(near_out, base_out, 0)
+    own_o, far_o = scatter_near(near_o, base_o, 1)
 
     *proj_grads, line_grad = attend_back(
-        place, query, key_rows, value_rows, seg_q, seg_k, line, grad_in, heads
-    )
-    output_sum = scatter_sum_mp([dot(attn_grad, part, 0, 0) for part in mixed_in])
-    near, base, gain_part, *weight_sums = input_grads(
+        place,
+        query,
+        key_rows,
+        value_rows,
+        seg_q,
+        seg_k,
+        line,
+        grad_in,
+        heads,
+        [far_in, far_out],
+    )
+    output_sum = own_o + swap(far_o, "mp", 2).astype(f32)
+    far_in = swap(far_in, "mp", 2)
+    far_out = swap(far_out, "mp", 2)
+    if few:
+        result_in = [result[0]] + [swap(result[r], "dp", r) for r in (1, 2, 3)]
+        own_result, far_result = from_slots(
+            "result_from_slots", result_in, slots, size, [f32, bf16]
+        )
+    else:
+        (own_result,) = from_slots(
+            "result_from_slots", [all_to_all_dp(result[0])], slots, size, [f32]
+        )
+    near, base, base_far, small, *weight_sums = input_grads(
         place,
         proj_grads,
         normed,
         (weight_q, weight_k, weight_v),
         output_sum,
         gain_one,
+        line_grad,
+        bucket_hot,
+        ffn_gain_grad,
+        router_grad,
         members,
         owners,
+        heads,
+        [far_in, own_result],
     )
     if few:
-        total = weight_sums[0]
-        for r in (1, 2, 3):
-            total = total + swap(weight_sums[r], "dp", r).astype(f32)
-        part = width // owners
-        far_part = swap(total[part:].astype(bf16), "dp", 4)
-        joined_grad = total[:part] + far_part.astype(f32)
+        arrived_sums = [swap(weight_sums[r], "dp", r) for r in (1, 2, 3)]
+        own_sum, far_part = fold_weights(weight_sums[0], arrived_sums)
+        weight_grads = split_weights([own_sum, swap(far_part, "dp", 4)], span)
     else:
         joined_grad = lax.psum_scatter(weight_sums[0], "dp", scatter_dimension=0, tiled=True)
-    near = base + swap(near, "mp", 1).astype(f32)
-    normed_grad = near[:rows] + swap(near[rows:].astype(bf16), "mp", 2).astype(f32)
+        weight_grads = split_weights([joined_grad], span)
+    near = swap(near, "mp", 1)
+    far_normed = swap((base_far + near[rows:].astype(f32)).astype(bf16), "mp", 2)
+    normed_grad = base + near[:rows].astype(f32) + far_normed.astype(f32)
     resid = tokens.astype(f32)
     _, inverse_one = normalize(resid, norm_gain)
     scaled = normed_grad * norm_gain
@@ -776,53 +1026,21 @@
         hidden_grad + inverse_one * scaled - resid * inverse_one * inverse_one * inverse_one * inner
     ).astype(bf16)
 
+    block_out = hidden + own_result
     if few:
-        result_in = [result[0]] + [swap(result[r], "dp", r) for r in (1, 2, 3)]
-        own_result, far_result = from_slots(
-            "result_from_slots", result_in, slots, size, [f32, bf16]
-        )
-        block_out = hidden + own_result + swap(far_result, "dp", 4).astype(f32)
-    else:
-        (own_result,) = from_slots(
-            "result_from_slots", [all_to_all_dp(result[0])], slots, size, [f32]
-        )
-        block_out = hidden + own_result
+        block_out = block_out + swap(far_result, "dp", 4).astype(f32)
     block_out = block_out.astype(bf16)
-
-    piece = w_in.shape[2] // members
-
-    def hidden_cut(values, axis):
-        return [
-            lax.dynamic_slice_in_dim(values, (member ^ r) * piece, piece, axis)
-            for r in range(members)
-        ]
-
-    w_in_grad = scatter_sum_mp([dot(arrived, part, 0, 0) for part in hidden_cut(pre_grad, 1)])
-    w_out_grad = scatter_sum_mp([dot(part, slot_grad, 0, 0) for part in hidden_cut(active, 1)])
-
-    router_grad = jnp.dot(ffn_input.astype(f32).T, logit_grad[:, :experts], precision=highest)
-    table_local = jnp.dot(bucket_hot.T, line_grad[:heads].T, precision=highest)
-    table_full = jnp.zeros((bias_table.shape[0], heads * members), f32)
-    table_full = lax.dynamic_update_slice_in_dim(table_full, table_local, member * heads, 1)
-    pieces = [router_grad, table_full, gain_part, ffn_gain_grad]
-    sums = sum_all(jnp.concatenate([item.reshape(-1) for item in pieces]))
-    ends = [0]
-    for item in pieces:
-        ends.append(ends[-1] + item.size)
-    router_sum, table_sum, gain_sum, ffn_gain_sum = [
-        sums[ends[i] : ends[i + 1]].reshape(pieces[i].shape) for i in range(4)
-    ]
+    w_in_grad = own_in + far_in.astype(f32)
+    w_out_grad = own_out + far_out.astype(f32)
+    small = sum_all(small)
     return (
         block_out,
         tokens_grad,
-        gain_sum.reshape(width),
-        joined_grad[:, :span],
-        joined_grad[:, span : 2 * span],
-        joined_grad[:, 2 * span : 3 * span],
-        joined_grad[:, 3 * span :].T,
-        table_sum,
-        ffn_gain_sum.reshape(width),
-        router_sum,
+        small[0],
+        *weight_grads,
+        small[2 : 2 + heads * members, :buckets_all].T,
+        small[1],
+        small[16:].T,
         w_in_grad[None],
         w_out_grad[None],
     )

time: 396 us -> 328 us (0.83); the launches traced: 391 us -> 327 us
  matrix products: 38.8 us -> 1.43 us
  waiting for transfers between devices: 161 us -> 127 us
  Pallas kernels: 70.3 us -> 89.6 us
  local copies, waits for them, and re-layouts: 42.4 us -> 35.5 us
    dot_general x15 -> x1, matrix products: 38.4 us -> 1.04 us  [on_device(): line = jnp.dot(table, bucket_hot.T, precision=highest)]
    ppermute x56, waiting for transfers between devices: 161 us -> 127 us  [swap(): return lax.ppermute(values, axis, [(i, i ^ step) for i in range(count)])]
    pallas_call x10 -> x16, Pallas kernels: 40 us -> 59.5 us  [the longest x14 42.4 us: call(): pl.pallas_call(body, name=name, grid=(1,), in_specs=in_specs + [pl.BlockS...]
    concatenate x6 -> x0, other arithmetic: 5.93 us -> none  [the longest x3 4.02 us: scatter_sum_mp(): jnp.concatenate([blocks[1], blocks[3]], axis=0).astype(bf16)]
    convert_element_type x0 -> x5, other arithmetic: none -> 4.56 us  [the longest x3 4.34 us: scatter_near(): return (own, far.astype(bf16))]
    unnamed x169 -> x220, local copies, waits for them, and re-layouts: 33.5 us -> 29.7 us
  transfers between devices with their start and end apart: 56 -> 56, of which waited for: 28 -> 28; matrix products, arithmetic and copies ran while one was open for 18% -> 8% of each run, Pallas kernels for 8% -> 14%
where the time goes in v2:
time: 328 us; the launch traced here: 327 us
  waiting for transfers between devices  127 us (39%)
  Pallas kernels  89.6 us (27%)
  starting transfers between devices  54.4 us (17%)
  local copies, waits for them, and re-layouts  35.5 us (11%)
  other arithmetic  16.7 us (5%)
    ppermute x56, waiting for transfers between devices, swap(): return lax.ppermute(values, axis, [(i, i ^ step) for i in range(count)])  127 us
    ppermute x56, starting transfers between devices, swap(): return lax.ppermute(values, axis, [(i, i ^ step) for i in range(count)])  54.4 us
    pallas_call x14, Pallas kernels, call(): pl.pallas_call(body, name=name, grid=(1,), in_specs=in_specs + [pl.BlockS...  42.4 us
    pallas_call x1, Pallas kernels, run_experts(): pl.pallas_call(functools.partial(experts_kernel, count, grads, experts),...  30.1 us
    unnamed x220, local copies, waits for them, and re-layouts  29.7 us
    pallas_call x2, Pallas kernels, expert_weight_grads(): pl.pallas_call(kernel, name=name, grid_spec=pltpu.PrefetchScalarGridSpec(...  17.1 us
  transfers between devices with their start and end apart: 56, of which 28 were waited for; matrix products, arithmetic and copies ran while one was open for 8% of the time, Pallas kernels for 14%

profile of v2, /device:TPU:0, one launch (start us, length us, event | category | flops | bytes accessed | tf_op | source)
XLA Modules:
  0.0 326.9 jit_solution(6867662613213814672)
XLA Ops:
  1.2 2.6 collective-permute-start.1
  7.1 2.7 collective-permute-start.3
  14.8 2.5 collective-permute-done.3.refs_1_
  21.8 3.9 %collective-permute-start.5 = (bf16[192,768]{1,0:T(8,128)(2,1)S(1)}, bf16[192,768]{1,0:T(8,128)(2,1)S(1)}, u32[]{:S(2)}, u32[]{:S(2)}) collective-permute-start(bf16[192,768]{1,0:T(8,128)(2,1)S(1)} %get-tuple-element.94.refs_6_), channel_id=1, source_target_pairs={{0,8},{4,12},{8,0},{12,4},{16,24},{20,28},{24,16},{28,20},{1,9},{5... | collective-permute-start | bytes 884744 | tf_op jit(solution)/shard_map/ppermute | solution.py:36
  25.7 11.4 %collective-permute-done.7.refs_2_ = bf16[256,768]{1,0:T(8,128)(2,1)S(1)} collective-permute-done((bf16[256,768]{1,0:T(8,128)(2,1)S(1)}, bf16[256,768]{1,0:T(8,128)(2,1)S(1)}, u32[]{:S(2)}, u32[]{:S(2)}) %collective-permute-start.7) | collective-permute-done | bytes 393248 | tf_op jit(solution)/shard_map/ppermute | solution.py:36
  38.7 1.6 collective-permute-done.5.refs_8_
  40.2 5.9 %collective-permute-done.6.refs_9_ = bf16[192,768]{1,0:T(8,128)(2,1)S(1)} collective-permute-done((bf16[192,768]{1,0:T(8,128)(2,1)S(1)}, bf16[192,768]{1,0:T(8,128)(2,1)S(1)}, u32[]{:S(2)}, u32[]{:S(2)}) %collective-permute-start.6) | collective-permute-done | bytes 294944 | tf_op jit(solution)/shard_map/ppermute | solution.py:36
  47.1 2.5 project.1
  52.2 9.7 %attend.1 = (bf16[256,192]{1,0:T(8,128)(2,1)S(1)}, bf16[256,192]{1,0:T(8,128)(2,1)S(1)}, bf16[256,192]{1,0:T(8,128)(2,1)S(1)}, bf16[256,192]{1,0:T(8,128)(2,1)S(1)}) custom-call(s32[2]{0:T(128)S(1)} %pad_add_fusion.2.refs_0_.me_ref.place_ref, bf16[1024,192]{1,0:T(8,128)(2,1)S(1)} %get-tuple-element.95.refs_1_, ...), custom_call_target="tpu_custom_call" | custom-call | flops 2013265920 | bytes 1603584 | tf_op jit(solution)/shard_map/attend/pallas_call | solution.py:60
  62.1 1.6 collective-permute-start.10
  65.5 2.5 collective-permute-done.10.refs_6_.refs_18_
  68.2 2.8 collective-permute-done.11.refs_7_.refs_19_
  73.3 1.8 collective-permute-done.15.refs_12_.refs_9_
  78.1 6.6 %collective-permute-done.17.refs_14_.refs_11_ = bf16[256,768]{1,0:T(8,128)(2,1)S(1)} collective-permute-done((bf16[256,768]{1,0:T(8,128)(2,1)}, bf16[256,768]{1,0:T(8,128)(2,1)S(1)}, u32[]{:S(2)}, u32[]{:S(2)}) %collective-permute-start.17) | collective-permute-done | bytes 393248 | tf_op jit(solution)/shard_map/ppermute | solution.py:36
  92.1 1.6 collective-permute-start.18
  95.1 1.7 collective-permute-start.21
  97.1 14.4 %collective-permute-done.18.refs_0_ = bf16[256,768]{1,0:T(8,128)(2,1)S(1)} collective-permute-done((bf16[256,768]{1,0:T(8,128)(2,1)S(1)}, bf16[256,768]{1,0:T(8,128)(2,1)S(1)}, u32[]{:S(2)}, u32[]{:S(2)}) %collective-permute-start.18) | collective-permute-done | bytes 393248 | tf_op jit(solution)/shard_map/ppermute | solution.py:36
  114.2 2.0 collective-permute-start.24
  116.2 3.4 %collective-permute-done.20.refs_3_ = bf16[128,768]{1,0:T(8,128)(2,1)S(1)} collective-permute-done((bf16[128,768]{1,0:T(8,128)(2,1)S(1)}, bf16[128,768]{1,0:T(8,128)(2,1)S(1)}, u32[]{:S(2)}, u32[]{:S(2)}) %collective-permute-start.20) | collective-permute-done | bytes 196640 | tf_op jit(solution)/shard_map/ppermute | solution.py:36
  119.6 2.4 collective-permute-done.22.refs_5_
  122.0 2.7 collective-permute-done.24.refs_7_
  125.4 30.1 %run_experts.1 = (bf16[128,896]{1,0:T(8,128)(2,1)}, bf16[128,896]{1,0:T(8,128)(2,1)}, bf16[128,896]{1,0:T(8,128)(2,1)}, bf16[128,896]{1,0:T(8,128)(2,1)}, bf16[1...) custom-call(s32[2]{0:T(128)} %copy-done.68, ...), custom_call_target="tpu_custom_call" | custom-call | flops 19327352832 | bytes 22020096 | tf_op jit(solution)/shard_map/run_experts/pallas_call | solution.py:491
  157.0 8.6 %w_in_grads.1 = (bf16[1536,768]{1,0:T(8,128)(2,1)S(1)}, f32[1536,768]{1,0:T(8,128)S(1)}) custom-call(s32[2]{0:T(128)S(1)} %copy-done.69, bf16[1024,768]{1,0:T(8,128)(2,1)S(1)} %copy-done.86, bf16[1024,3072]{1,0:T(8,128)(2,1)} %get-tuple-element.134.cut_ref), custom_call_target="tpu_custom_call" | custom-call | flops 4831838208 | bytes 14942208 | tf_op jit(solution)/shard_map/w_in_grads/pallas_call | solution.py:632
  167.5 1.7 collective-permute-start.31
  169.3 8.5 %w_out_grads.1 = (bf16[1536,768]{1,0:T(8,128)(2,1)S(1)}, f32[1536,768]{1,0:T(8,128)S(1)}) custom-call(s32[2]{0:T(128)S(1)} %copy-done.70, bf16[1024,768]{1,0:T(8,128)(2,1)S(1)} %copy-done.85, bf16[1024,3072]{1,0:T(8,128)(2,1)} %get-tuple-element.141.cut_ref), custom_call_target="tpu_custom_call" | custom-call | flops 4831838208 | bytes 14942208 | tf_op jit(solution)/shard_map/w_out_grads/pallas_call | solution.py:632
  178.0 1.7 collective-permute-done.31.refs_3_
  182.0 1.6 collective-permute-start.35
  183.6 1.7 collective-permute-start.33
  185.4 2.0 collective-permute-done.32.refs_8_
  188.6 11.0 %collective-permute-done.33.refs_9_ = bf16[128,896]{1,0:T(8,128)(2,1)S(1)} collective-permute-done((bf16[128,896]{1,0:T(8,128)(2,1)S(1)}, bf16[128,896]{1,0:T(8,128)(2,1)S(1)}, u32[]{:S(2)}, u32[]{:S(2)}) %collective-permute-start.33) | collective-permute-done | bytes 229408 | tf_op jit(solution)/shard_map/ppermute | solution.py:36
  199.5 4.8 %collective-permute-done.34.refs_10_ = bf16[128,896]{1,0:T(8,128)(2,1)S(1)} collective-permute-done((bf16[128,896]{1,0:T(8,128)(2,1)S(1)}, bf16[128,896]{1,0:T(8,128)(2,1)S(1)}, u32[]{:S(2)}, u32[]{:S(2)}) %collective-permute-start.34) | collective-permute-done | bytes 229408 | tf_op jit(solution)/shard_map/ppermute | solution.py:36
  204.5 3.5 %home.1 = (bf16[256,192]{1,0:T(8,128)(2,1)S(1)}, bf16[256,192]{1,0:T(8,128)(2,1)S(1)}, bf16[256,192]{1,0:T(8,128)(2,1)S(1)}, bf16[256,192]{1,0:T(8,128)(2,1)S(1)...) custom-call(s32[8,256]{1,0:T(8,128)S(1)} %copy-done.51, ...), custom_call_target="tpu_custom_call" | custom-call | flops 805306368 | bytes 7837696 | tf_op jit(solution)/shard_map/home/pallas_call | solution.py:60
  214.0 2.6 add_convert_fusion.1.refs_11_
  216.6 4.1 %collective-permute-done.25.refs_1_ = bf16[256,768]{1,0:T(8,128)(2,1)S(1)} collective-permute-done((bf16[256,768]{1,0:T(8,128)(2,1)S(1)}, bf16[256,768]{1,0:T(8,128)(2,1)S(1)}, u32[]{:S(2)}, u32[]{:S(2)}) %collective-permute-start.25) | collective-permute-done | bytes 393248 | tf_op jit(solution)/shard_map/ppermute | solution.py:36
  222.7 7.6 %collective-permute-done.27.refs_3_ = bf16[256,768]{1,0:T(8,128)(2,1)S(1)} collective-permute-done((bf16[256,768]{1,0:T(8,128)(2,1)S(1)}, bf16[256,768]{1,0:T(8,128)(2,1)S(1)}, u32[]{:S(2)}, u32[]{:S(2)}) %collective-permute-start.27) | collective-permute-done | bytes 393248 | tf_op jit(solution)/shard_map/ppermute | solution.py:36
  230.4 1.7 result_from_slots.1
  239.1 13.9 %collective-permute-done.37.refs_9_ = bf16[256,192]{1,0:T(8,128)(2,1)S(1)} collective-permute-done((bf16[256,192]{1,0:T(8,128)(2,1)S(1)}, bf16[256,192]{1,0:T(8,128)(2,1)S(1)}, u32[]{:S(2)}, u32[]{:S(2)}) %collective-permute-start.37) | collective-permute-done | bytes 98336 | tf_op jit(solution)/shard_map/ppermute | solution.py:36
  254.3 14.1 %attend_back.1 = (bf16[1024,192]{1,0:T(8,128)(2,1)S(1)}, bf16[1024,192]{1,0:T(8,128)(2,1)S(1)}, bf16[1024,192]{1,0:T(8,128)(2,1)S(1)}, f32[8,640]{1,0:T(8,128)S(1)}) custom-call(s32[2]{0:T(128)S(1)} %copy-done.70, bf16[1024,192]{1,0:T(8,128)(2,1)S(1)} %copy-done.80, bf16[1024,192]{1,0:T(8,128)(2,1)S(1)} %copy-done.82, bf16[1024,192]{1,0:T(8,128)(2,1)S(1)} %copy-done.84, ...), custom_call_target="tpu_custom_call" | custom-call | flops 5033164800 | bytes 2803712 | tf_op jit(solution)/shard_map/attend_back/pallas_call | solution.py:60
  276.9 5.7 %input_grads.1 = (bf16[512,768]{1,0:T(8,128)(2,1)S(1)}, f32[256,768]{1,0:T(8,128)}, f32[256,768]{1,0:T(8,128)}, f32[24,768]{1,0:T(8,128)S(1)}, f32[192,768]{1,0:...) custom-call(s32[2]{0:T(128)S(1)} %copy-done.71, ...), custom_call_target="tpu_custom_call" | custom-call | flops 1811939328 | bytes 8513536 | tf_op jit(solution)/shard_map/input_grads/pallas_call | solution.py:60
  285.4 4.1 %collective-permute-done.47 = f32[24,768]{1,0:T(8,128)S(1)} collective-permute-done((f32[24,768]{1,0:T(8,128)S(1)}, f32[24,768]{1,0:T(8,128)S(1)}, u32[]{:S(2)}, u32[]{:S(2)}) %collective-permute-start.47) | collective-permute-done | bytes 73760 | tf_op jit(solution)/shard_map/ppermute | solution.py:36
  290.8 2.1 add_convert_fusion.4
  293.8 1.8 collective-permute-start.52
  295.9 3.5 %add_bitcast_fusion.1 = f32[1,768,768]{2,1,0:T(8,128)} fusion(bf16[768,768]{1,0:T(8,128)(2,1)} %collective-permute-done.43.refs_14_, f32[1536,768]{1,0:T(8,128)S(1)} %get-tuple-element.148, bf16[1536,768]{1,0:T(8,128)(2,1)} %collective-permute-done.39), kind=kLoop, calls=%fused_computation.1 | loop fusion | flops 2359296 | bytes 7077888 | tf_op jit(solution)/shard_map/broadcast_in_dim | solution.py:1044
  299.4 5.1 %collective-permute-done.49 = f32[24,768]{1,0:T(8,128)S(1)} collective-permute-done((f32[24,768]{1,0:T(8,128)S(1)}, f32[24,768]{1,0:T(8,128)S(1)}, u32[]{:S(2)}, u32[]{:S(2)}) %collective-permute-start.49) | collective-permute-done | bytes 73760 | tf_op jit(solution)/shard_map/ppermute | solution.py:36
  306.1 1.6 collective-permute-start.50
  307.6 3.1 add_bitcast_fusion
  310.7 4.7 %collective-permute-done.53.refs_3_ = bf16[192,768]{1,0:T(8,128)(2,1)S(1)} collective-permute-done((bf16[192,768]{1,0:T(8,128)(2,1)S(1)}, bf16[192,768]{1,0:T(8,128)(2,1)S(1)}, u32[]{:S(2)}, u32[]{:S(2)}) %collective-permute-start.53) | collective-permute-done | bytes 294944 | tf_op jit(solution)/shard_map/ppermute | solution.py:36
  319.1 4.4 %collective-permute-done.54.refs_1_ = bf16[96,768]{1,0:T(8,128)(2,1)S(1)} collective-permute-done((bf16[96,768]{1,0:T(8,128)(2,1)S(1)}, bf16[96,768]{1,0:T(8,128)(2,1)S(1)}, u32[]{:S(2)}, u32[]{:S(2)}) %collective-permute-start.54) | collective-permute-done | bytes 147488 | tf_op jit(solution)/shard_map/ppermute | solution.py:36
  (343 shorter events, 83.4 us)
Async XLA Ops:
  0.7 38.0 %collective-permute-start = (bf16[256,768]{1,0:T(8,128)(2,1)}, bf16[256,768]{1,0:T(8,128)(2,1)S(1)}, u32[]{:S(2)}, u32[]{:S(2)}) collective-permute-start(bf16[256,768]{1,0:T(8,128)(2,1)} %refs_0_.3), channel_id=1, source_target_pairs={{0,1},{1,0},{2,3},{3,2},{4,5},{5,4},{6,7},{7,6},{8,9},{9,8},{10,11... | collective-permute-start | bytes 1179656 | tf_op jit(solution)/shard_map/ppermute | solution.py:36
  1.2 18.7 %collective-permute-start.1 = (bf16[256,768]{1,0:T(8,128)(2,1)}, bf16[256,768]{1,0:T(8,128)(2,1)S(1)}, u32[]{:S(2)}, u32[]{:S(2)}) collective-permute-start(bf16[256,768]{1,0:T(8,128)(2,1)} %refs_0_.3), channel_id=1, source_target_pairs={{0,2},{1,3},{2,0},{3,1},{4,6},{5,7},{6,4},{7,5},{8,10},{9,11},{10,... | collective-permute-start | bytes 1179656 | tf_op jit(solution)/shard_map/ppermute | solution.py:36
  7.1 10.1 %collective-permute-start.3 = (bf16[96,768]{1,0:T(8,128)(2,1)S(1)}, bf16[96,768]{1,0:T(8,128)(2,1)S(1)}, u32[]{:S(2)}, u32[]{:S(2)}) collective-permute-start(bf16[96,768]{1,0:T(8,128)(2,1)S(1)} %pack_weights.1.refs_0_), channel_id=1, source_target_pairs={{0,16},{4,20},{8,24},{12,28},{16,0},{20,4},{24,8},{28,12},{1,17},{... | collective-permute-start | bytes 442376 | tf_op jit(solution)/shard_map/ppermute | solution.py:36
  9.8 10.1 %collective-permute-start.8 = (s32[256,2]{0,1:T(2,128)}, s32[256,2]{0,1:T(2,128)S(1)}, u32[]{:S(2)}, u32[]{:S(2)}) collective-permute-start(s32[256,2]{0,1:T(2,128)} %param.28), channel_id=1, source_target_pairs={{0,16},{4,20},{8,24},{12,28},{16,0},{20,4},{24,8},{28,12},{1,17},{... | collective-permute-start | bytes 6152 | tf_op jit(solution)/shard_map/ppermute | solution.py:36
  17.3 19.8 %collective-permute-start.7 = (bf16[256,768]{1,0:T(8,128)(2,1)S(1)}, bf16[256,768]{1,0:T(8,128)(2,1)S(1)}, u32[]{:S(2)}, u32[]{:S(2)}) collective-permute-start(bf16[256,768]{1,0:T(8,128)(2,1)S(1)} %get-tuple-element.98.refs_0_), channel_id=1, source_target_pairs={{0,16},{4,20},{8,24},{12,28},{16,0},{20,4},{24,8},{28,12},{1,17},{... | collective-permute-start | bytes 1179656 | tf_op jit(solution)/shard_map/ppermute | solution.py:36
  19.9 26.2 %collective-permute-start.2 = (bf16[256,768]{1,0:T(8,128)(2,1)S(1)}, bf16[256,768]{1,0:T(8,128)(2,1)S(1)}, u32[]{:S(2)}, u32[]{:S(2)}) collective-permute-start(bf16[256,768]{1,0:T(8,128)(2,1)S(1)} %collective-permute-done.1.refs_4_), channel_id=1, source_target_pairs={{0,1},{1,0},{2,3},{3,2},{4,5},{5,4},{6,7},{7,6},{8,9},{9,8},{10,11... | collective-permute-start | bytes 1179656 | tf_op jit(solution)/shard_map/ppermute | solution.py:36
  20.2 18.4 %collective-permute-start.4 = (bf16[192,768]{1,0:T(8,128)(2,1)S(1)}, bf16[192,768]{1,0:T(8,128)(2,1)S(1)}, u32[]{:S(2)}, u32[]{:S(2)}) collective-permute-start(bf16[192,768]{1,0:T(8,128)(2,1)S(1)} %get-tuple-element.94.refs_6_), channel_id=1, source_target_pairs={{0,4},{4,0},{8,12},{12,8},{16,20},{20,16},{24,28},{28,24},{1,5},{5... | collective-permute-start | bytes 884744 | tf_op jit(solution)/shard_map/ppermute | solution.py:36
  21.8 18.5 %collective-permute-start.5 = (bf16[192,768]{1,0:T(8,128)(2,1)S(1)}, bf16[192,768]{1,0:T(8,128)(2,1)S(1)}, u32[]{:S(2)}, u32[]{:S(2)}) collective-permute-start(bf16[192,768]{1,0:T(8,128)(2,1)S(1)} %get-tuple-element.94.refs_6_), channel_id=1, source_target_pairs={{0,8},{4,12},{8,0},{12,4},{16,24},{20,28},{24,16},{28,20},{1,9},{5... | collective-permute-start | bytes 884744 | tf_op jit(solution)/shard_map/ppermute | solution.py:36
  37.1 9.0 %collective-permute-start.6 = (bf16[192,768]{1,0:T(8,128)(2,1)S(1)}, bf16[192,768]{1,0:T(8,128)(2,1)S(1)}, u32[]{:S(2)}, u32[]{:S(2)}) collective-permute-start(bf16[192,768]{1,0:T(8,128)(2,1)S(1)} %get-tuple-element.94.refs_6_), channel_id=1, source_target_pairs={{0,12},{4,8},{8,4},{12,0},{16,28},{20,24},{24,20},{28,16},{1,13},{... | collective-permute-start | bytes 884744 | tf_op jit(solution)/shard_map/ppermute | solution.py:36
  51.6 19.6 %collective-permute-start.13 = (bf16[192,768]{1,0:T(8,128)(2,1)S(1)}, bf16[192,768]{1,0:T(8,128)(2,1)S(1)}, u32[]{:S(2)}, u32[]{:S(2)}) collective-permute-start(bf16[192,768]{1,0:T(8,128)(2,1)S(1)} %get-tuple-element.104.refs_8_.refs_12_), channel_id=1, source_target_pairs={{0,2},{1,3},{2,0},{3,1},{4,6},{5,7},{6,4},{7,5},{8,10},{9,11},{10,... | collective-permute-start | bytes 884744 | tf_op jit(solution)/shard_map/ppermute | solution.py:36
  63.7 11.4 %collective-permute-start.15 = (bf16[256,768]{1,0:T(8,128)(2,1)}, bf16[256,768]{1,0:T(8,128)(2,1)S(1)}, u32[]{:S(2)}, u32[]{:S(2)}) collective-permute-start(bf16[256,768]{1,0:T(8,128)(2,1)} %get-tuple-element.105), channel_id=1, source_target_pairs={{0,4},{4,0},{8,12},{12,8},{16,20},{20,16},{24,28},{28,24},{1,5},{5... | collective-permute-start | bytes 1179656 | tf_op jit(solution)/shard_map/ppermute | solution.py:36
  65.2 12.2 %collective-permute-start.16 = (bf16[256,768]{1,0:T(8,128)(2,1)}, bf16[256,768]{1,0:T(8,128)(2,1)S(1)}, u32[]{:S(2)}, u32[]{:S(2)}) collective-permute-start(bf16[256,768]{1,0:T(8,128)(2,1)} %get-tuple-element.106), channel_id=1, source_target_pairs={{0,8},{4,12},{8,0},{12,4},{16,24},{20,28},{24,16},{28,20},{1,9},{5... | collective-permute-start | bytes 1179656 | tf_op jit(solution)/shard_map/ppermute | solution.py:36
  68.0 16.7 %collective-permute-start.17 = (bf16[256,768]{1,0:T(8,128)(2,1)}, bf16[256,768]{1,0:T(8,128)(2,1)S(1)}, u32[]{:S(2)}, u32[]{:S(2)}) collective-permute-start(bf16[256,768]{1,0:T(8,128)(2,1)} %get-tuple-element.107), channel_id=1, source_target_pairs={{0,12},{4,8},{8,4},{12,0},{16,28},{20,24},{24,20},{28,16},{1,13},{... | collective-permute-start | bytes 1179656 | tf_op jit(solution)/shard_map/ppermute | solution.py:36
  71.0 14.5 %collective-permute-start.12 = (bf16[192,768]{1,0:T(8,128)(2,1)S(1)}, bf16[192,768]{1,0:T(8,128)(2,1)S(1)}, u32[]{:S(2)}, u32[]{:S(2)}) collective-permute-start(bf16[192,768]{1,0:T(8,128)(2,1)S(1)} %get-tuple-element.104.refs_8_.refs_12_), channel_id=1, source_target_pairs={{0,1},{1,0},{2,3},{3,2},{4,5},{5,4},{6,7},{7,6},{8,9},{9,8},{10,11... | collective-permute-start | bytes 884744 | tf_op jit(solution)/shard_map/ppermute | solution.py:36
  71.2 14.3 %collective-permute-start.14 = (bf16[192,768]{1,0:T(8,128)(2,1)S(1)}, bf16[192,768]{1,0:T(8,128)(2,1)S(1)}, u32[]{:S(2)}, u32[]{:S(2)}) collective-permute-start(bf16[192,768]{1,0:T(8,128)(2,1)S(1)} %collective-permute-done.13.refs_10_.refs_14_), channel_id=1, source_target_pairs={{0,1},{1,0},{2,3},{3,2},{4,5},{5,4},{6,7},{7,6},{8,9},{9,8},{10,11... | collective-permute-start | bytes 884744 | tf_op jit(solution)/shard_map/ppermute | solution.py:36
  92.1 19.5 %collective-permute-start.18 = (bf16[256,768]{1,0:T(8,128)(2,1)S(1)}, bf16[256,768]{1,0:T(8,128)(2,1)S(1)}, u32[]{:S(2)}, u32[]{:S(2)}) collective-permute-start(bf16[256,768]{1,0:T(8,128)(2,1)S(1)} %get-tuple-element.110.refs_6_), channel_id=1, source_target_pairs={{0,16},{4,20},{8,24},{12,28},{16,0},{20,4},{24,8},{28,12},{1,17},{... | collective-permute-start | bytes 1179656 | tf_op jit(solution)/shard_map/ppermute | solution.py:36
  93.6 20.5 %collective-permute-start.19 = (bf16[128,768]{1,0:T(8,128)(2,1)S(1)}, bf16[128,768]{1,0:T(8,128)(2,1)S(1)}, u32[]{:S(2)}, u32[]{:S(2)}) collective-permute-start(bf16[128,768]{1,0:T(8,128)(2,1)S(1)} %get-tuple-element.112), channel_id=1, source_target_pairs={{0,4},{4,0},{8,12},{12,8},{16,20},{20,16},{24,28},{28,24},{1,5},{5... | collective-permute-start | bytes 589832 | tf_op jit(solution)/shard_map/ppermute | solution.py:36
  95.1 21.0 %collective-permute-start.21 = (bf16[128,768]{1,0:T(8,128)(2,1)S(1)}, bf16[128,768]{1,0:T(8,128)(2,1)S(1)}, u32[]{:S(2)}, u32[]{:S(2)}) collective-permute-start(bf16[128,768]{1,0:T(8,128)(2,1)S(1)} %get-tuple-element.114), channel_id=1, source_target_pairs={{0,8},{4,12},{8,0},{12,4},{16,24},{20,28},{24,16},{28,20},{1,9},{5... | collective-permute-start | bytes 589832 | tf_op jit(solution)/shard_map/ppermute | solution.py:36
  96.9 19.3 %collective-permute-start.23 = (bf16[128,768]{1,0:T(8,128)(2,1)S(1)}, bf16[128,768]{1,0:T(8,128)(2,1)S(1)}, u32[]{:S(2)}, u32[]{:S(2)}) collective-permute-start(bf16[128,768]{1,0:T(8,128)(2,1)S(1)} %get-tuple-element.116), channel_id=1, source_target_pairs={{0,12},{4,8},{8,4},{12,0},{16,28},{20,24},{24,20},{28,16},{1,13},{... | collective-permute-start | bytes 589832 | tf_op jit(solution)/shard_map/ppermute | solution.py:36
  112.7 6.9 %collective-permute-start.20 = (bf16[128,768]{1,0:T(8,128)(2,1)S(1)}, bf16[128,768]{1,0:T(8,128)(2,1)S(1)}, u32[]{:S(2)}, u32[]{:S(2)}) collective-permute-start(bf16[128,768]{1,0:T(8,128)(2,1)S(1)} %get-tuple-element.113), channel_id=1, source_target_pairs={{0,4},{4,0},{8,12},{12,8},{16,20},{20,16},{24,28},{28,24},{1,5},{5... | collective-permute-start | bytes 589832 | tf_op jit(solution)/shard_map/ppermute | solution.py:36
  114.1 7.8 %collective-permute-start.22 = (bf16[128,768]{1,0:T(8,128)(2,1)S(1)}, bf16[128,768]{1,0:T(8,128)(2,1)S(1)}, u32[]{:S(2)}, u32[]{:S(2)}) collective-permute-start(bf16[128,768]{1,0:T(8,128)(2,1)S(1)} %get-tuple-element.115), channel_id=1, source_target_pairs={{0,8},{4,12},{8,0},{12,4},{16,24},{20,28},{24,16},{28,20},{1,9},{5... | collective-permute-start | bytes 589832 | tf_op jit(solution)/shard_map/ppermute | solution.py:36
  114.2 10.6 %collective-permute-start.24 = (bf16[128,768]{1,0:T(8,128)(2,1)S(1)}, bf16[128,768]{1,0:T(8,128)(2,1)S(1)}, u32[]{:S(2)}, u32[]{:S(2)}) collective-permute-start(bf16[128,768]{1,0:T(8,128)(2,1)S(1)} %get-tuple-element.117), channel_id=1, source_target_pairs={{0,12},{4,8},{8,4},{12,0},{16,28},{20,24},{24,20},{28,16},{1,13},{... | collective-permute-start | bytes 589832 | tf_op jit(solution)/shard_map/ppermute | solution.py:36
  165.6 47.7 %collective-permute-start.39 = (bf16[1536,768]{1,0:T(8,128)(2,1)S(1)}, bf16[1536,768]{1,0:T(8,128)(2,1)}, u32[]{:S(2)}, u32[]{:S(2)}) collective-permute-start(bf16[1536,768]{1,0:T(8,128)(2,1)S(1)} %get-tuple-element.135.refs_8_), channel_id=1, source_target_pairs={{0,1},{1,0},{2,3},{3,2},{4,5},{5,4},{6,7},{7,6},{8,9},{9,8},{10,11... | collective-permute-start | bytes 7077896 | tf_op jit(solution)/shard_map/ppermute | solution.py:36
  165.6 12.4 %collective-permute-start.29 = (bf16[128,896]{1,0:T(8,128)(2,1)S(1)}, bf16[128,896]{1,0:T(8,128)(2,1)S(1)}, u32[]{:S(2)}, u32[]{:S(2)}) collective-permute-start(bf16[128,896]{1,0:T(8,128)(2,1)S(1)} %copy-done.101), channel_id=1, source_target_pairs={{0,4},{4,0},{8,12},{12,8},{16,20},{20,16},{24,28},{28,24},{1,5},{5... | collective-permute-start | bytes 688136 | tf_op jit(solution)/shard_map/ppermute | solution.py:36
  167.2 10.8 %collective-permute-start.30 = (bf16[128,896]{1,0:T(8,128)(2,1)S(1)}, bf16[128,896]{1,0:T(8,128)(2,1)S(1)}, u32[]{:S(2)}, u32[]{:S(2)}) collective-permute-start(bf16[128,896]{1,0:T(8,128)(2,1)S(1)} %copy-done.100), channel_id=1, source_target_pairs={{0,8},{4,12},{8,0},{12,4},{16,24},{20,28},{24,16},{28,20},{1,9},{5... | collective-permute-start | bytes 688136 | tf_op jit(solution)/shard_map/ppermute | solution.py:36
  167.5 12.3 %collective-permute-start.31 = (bf16[128,896]{1,0:T(8,128)(2,1)S(1)}, bf16[128,896]{1,0:T(8,128)(2,1)S(1)}, u32[]{:S(2)}, u32[]{:S(2)}) collective-permute-start(bf16[128,896]{1,0:T(8,128)(2,1)S(1)} %copy-done.99), channel_id=1, source_target_pairs={{0,12},{4,8},{8,4},{12,0},{16,28},{20,24},{24,20},{28,16},{1,13},{... | collective-permute-start | bytes 688136 | tf_op jit(solution)/shard_map/ppermute | solution.py:36
  177.9 57.9 %collective-permute-start.40 = (bf16[1536,768]{1,0:T(8,128)(2,1)S(1)}, bf16[1536,768]{1,0:T(8,128)(2,1)S(1)}, u32[]{:S(2)}, u32[]{:S(2)}) collective-permute-start(bf16[1536,768]{1,0:T(8,128)(2,1)S(1)} %get-tuple-element.142.refs_20_), channel_id=1, source_target_pairs={{0,1},{1,0},{2,3},{3,2},{4,5},{5,4},{6,7},{7,6},{8,9},{9,8},{10,11... | collective-permute-start | bytes 7077896 | tf_op jit(solution)/shard_map/ppermute | solution.py:36
  180.5 6.9 %collective-permute-start.32 = (bf16[128,896]{1,0:T(8,128)(2,1)S(1)}, bf16[128,896]{1,0:T(8,128)(2,1)S(1)}, u32[]{:S(2)}, u32[]{:S(2)}) collective-permute-start(bf16[128,896]{1,0:T(8,128)(2,1)S(1)} %get-tuple-element.136), channel_id=1, source_target_pairs={{0,4},{4,0},{8,12},{12,8},{16,20},{20,16},{24,28},{28,24},{1,5},{5... | collective-permute-start | bytes 688136 | tf_op jit(solution)/shard_map/ppermute | solution.py:36
  182.0 22.4 %collective-permute-start.35 = (bf16[256,896]{1,0:T(8,128)(2,1)S(1)}, bf16[256,896]{1,0:T(8,128)(2,1)S(1)}, u32[]{:S(2)}, u32[]{:S(2)}) collective-permute-start(bf16[256,896]{1,0:T(8,128)(2,1)S(1)} %get-tuple-element.139), channel_id=1, source_target_pairs={{0,16},{4,20},{8,24},{12,28},{16,0},{20,4},{24,8},{28,12},{1,17},{... | collective-permute-start | bytes 1376264 | tf_op jit(solution)/shard_map/ppermute | solution.py:36
  183.6 15.9 %collective-permute-start.33 = (bf16[128,896]{1,0:T(8,128)(2,1)S(1)}, bf16[128,896]{1,0:T(8,128)(2,1)S(1)}, u32[]{:S(2)}, u32[]{:S(2)}) collective-permute-start(bf16[128,896]{1,0:T(8,128)(2,1)S(1)} %get-tuple-element.137), channel_id=1, source_target_pairs={{0,8},{4,12},{8,0},{12,4},{16,24},{20,28},{24,16},{28,20},{1,9},{5... | collective-permute-start | bytes 688136 | tf_op jit(solution)/shard_map/ppermute | solution.py:36
  187.4 17.0 %collective-permute-start.34 = (bf16[128,896]{1,0:T(8,128)(2,1)S(1)}, bf16[128,896]{1,0:T(8,128)(2,1)S(1)}, u32[]{:S(2)}, u32[]{:S(2)}) collective-permute-start(bf16[128,896]{1,0:T(8,128)(2,1)S(1)} %get-tuple-element.138), channel_id=1, source_target_pairs={{0,12},{4,8},{8,4},{12,0},{16,28},{20,24},{24,20},{28,16},{1,13},{... | collective-permute-start | bytes 688136 | tf_op jit(solution)/shard_map/ppermute | solution.py:36
  209.2 11.5 %collective-permute-start.25 = (bf16[256,768]{1,0:T(8,128)(2,1)S(1)}, bf16[256,768]{1,0:T(8,128)(2,1)S(1)}, u32[]{:S(2)}, u32[]{:S(2)}) collective-permute-start(bf16[256,768]{1,0:T(8,128)(2,1)S(1)} %copy-done.98), channel_id=1, source_target_pairs={{0,4},{4,0},{8,12},{12,8},{16,20},{20,16},{24,28},{28,24},{1,5},{5... | collective-permute-start | bytes 1179656 | tf_op jit(solution)/shard_map/ppermute | solution.py:36
  210.8 12.0 %collective-permute-start.26 = (bf16[256,768]{1,0:T(8,128)(2,1)S(1)}, bf16[256,768]{1,0:T(8,128)(2,1)S(1)}, u32[]{:S(2)}, u32[]{:S(2)}) collective-permute-start(bf16[256,768]{1,0:T(8,128)(2,1)S(1)} %copy-done.97), channel_id=1, source_target_pairs={{0,8},{4,12},{8,0},{12,4},{16,24},{20,28},{24,16},{28,20},{1,9},{5... | collective-permute-start | bytes 1179656 | tf_op jit(solution)/shard_map/ppermute | solution.py:36
  211.3 19.0 %collective-permute-start.27 = (bf16[256,768]{1,0:T(8,128)(2,1)S(1)}, bf16[256,768]{1,0:T(8,128)(2,1)S(1)}, u32[]{:S(2)}, u32[]{:S(2)}) collective-permute-start(bf16[256,768]{1,0:T(8,128)(2,1)S(1)} %copy-done.96), channel_id=1, source_target_pairs={{0,12},{4,8},{8,4},{12,0},{16,28},{20,24},{24,20},{28,16},{1,13},{... | collective-permute-start | bytes 1179656 | tf_op jit(solution)/shard_map/ppermute | solution.py:36
  213.2 21.0 %collective-permute-start.42 = (bf16[768,192]{1,0:T(8,128)(2,1)S(1)}, bf16[768,192]{1,0:T(8,128)(2,1)S(1)}, u32[]{:S(2)}, u32[]{:S(2)}) collective-permute-start(bf16[768,192]{1,0:T(8,128)(2,1)S(1)} %add_convert_fusion.3), channel_id=1, source_target_pairs={{0,2},{1,3},{2,0},{3,1},{4,6},{5,7},{6,4},{7,5},{8,10},{9,11},{10,... | collective-permute-start | bytes 884744 | tf_op jit(solution)/shard_map/ppermute | solution.py:36
  220.8 50.0 %collective-permute-start.43 = (bf16[768,768]{1,0:T(8,128)(2,1)}, bf16[768,768]{1,0:T(8,128)(2,1)}, u32[]{:S(2)}, u32[]{:S(2)}) collective-permute-start(bf16[768,768]{1,0:T(8,128)(2,1)} %add_convert_fusion.1.refs_11_), channel_id=1, source_target_pairs={{0,2},{1,3},{2,0},{3,1},{4,6},{5,7},{6,4},{7,5},{8,10},{9,11},{10,... | collective-permute-start | bytes 3538952 | tf_op jit(solution)/shard_map/ppermute | solution.py:36
  233.0 57.8 %collective-permute-start.28 = (bf16[256,768]{1,0:T(8,128)(2,1)}, bf16[256,768]{1,0:T(8,128)(2,1)}, u32[]{:S(2)}, u32[]{:S(2)}) collective-permute-start(bf16[256,768]{1,0:T(8,128)(2,1)} %get-tuple-element.123), channel_id=1, source_target_pairs={{0,16},{4,20},{8,24},{12,28},{16,0},{20,4},{24,8},{28,12},{1,17},{... | collective-permute-start | bytes 1179656 | tf_op jit(solution)/shard_map/ppermute | solution.py:36
  234.3 18.7 %collective-permute-start.37 = (bf16[256,192]{1,0:T(8,128)(2,1)S(1)}, bf16[256,192]{1,0:T(8,128)(2,1)S(1)}, u32[]{:S(2)}, u32[]{:S(2)}) collective-permute-start(bf16[256,192]{1,0:T(8,128)(2,1)S(1)} %get-tuple-element.146), channel_id=1, source_target_pairs={{0,2},{1,3},{2,0},{3,1},{4,6},{5,7},{6,4},{7,5},{8,10},{9,11},{10,... | collective-permute-start | bytes 294920 | tf_op jit(solution)/shard_map/ppermute | solution.py:36
  235.8 18.4 %collective-permute-start.38 = (bf16[256,192]{1,0:T(8,128)(2,1)S(1)}, bf16[256,192]{1,0:T(8,128)(2,1)S(1)}, u32[]{:S(2)}, u32[]{:S(2)}) collective-permute-start(bf16[256,192]{1,0:T(8,128)(2,1)S(1)} %get-tuple-element.147), channel_id=1, source_target_pairs={{0,3},{1,2},{2,1},{3,0},{4,7},{5,6},{6,5},{7,4},{8,11},{9,10},{10,... | collective-permute-start | bytes 294920 | tf_op jit(solution)/shard_map/ppermute | solution.py:36
  238.5 67.6 %collective-permute-start.55 = (bf16[768,768]{1,0:T(8,128)(2,1)}, bf16[768,768]{1,0:T(8,128)(2,1)}, u32[]{:S(2)}, u32[]{:S(2)}) collective-permute-start(bf16[768,768]{1,0:T(8,128)(2,1)} %add_convert_fusion.refs_12_), channel_id=1, source_target_pairs={{0,2},{1,3},{2,0},{3,1},{4,6},{5,7},{6,4},{7,5},{8,10},{9,11},{10,... | collective-permute-start | bytes 3538952 | tf_op jit(solution)/shard_map/ppermute | solution.py:36
  292.9 23.7 %collective-permute-start.44 = (bf16[512,768]{1,0:T(8,128)(2,1)S(1)}, bf16[512,768]{1,0:T(8,128)(2,1)S(1)}, u32[]{:S(2)}, u32[]{:S(2)}) collective-permute-start(bf16[512,768]{1,0:T(8,128)(2,1)S(1)} %get-tuple-element.163), channel_id=1, source_target_pairs={{0,1},{1,0},{2,3},{3,2},{4,5},{5,4},{6,7},{7,6},{8,9},{9,8},{10,11... | collective-permute-start | bytes 2359304 | tf_op jit(solution)/shard_map/ppermute | solution.py:36
  292.9 17.8 %collective-permute-start.51 = (bf16[192,768]{1,0:T(8,128)(2,1)S(1)}, bf16[192,768]{1,0:T(8,128)(2,1)S(1)}, u32[]{:S(2)}, u32[]{:S(2)}) collective-permute-start(bf16[192,768]{1,0:T(8,128)(2,1)S(1)} %get-tuple-element.167), channel_id=1, source_target_pairs={{0,4},{4,0},{8,12},{12,8},{16,20},{20,16},{24,28},{28,24},{1,5},{5... | collective-permute-start | bytes 884744 | tf_op jit(solution)/shard_map/ppermute | solution.py:36
  293.8 16.9 %collective-permute-start.52 = (bf16[192,768]{1,0:T(8,128)(2,1)S(1)}, bf16[192,768]{1,0:T(8,128)(2,1)S(1)}, u32[]{:S(2)}, u32[]{:S(2)}) collective-permute-start(bf16[192,768]{1,0:T(8,128)(2,1)S(1)} %get-tuple-element.168), channel_id=1, source_target_pairs={{0,8},{4,12},{8,0},{12,4},{16,24},{20,28},{24,16},{28,20},{1,9},{5... | collective-permute-start | bytes 884744 | tf_op jit(solution)/shard_map/ppermute | solution.py:36
  295.6 8.9 %collective-permute-start.49 = (f32[24,768]{1,0:T(8,128)S(1)}, f32[24,768]{1,0:T(8,128)S(1)}, u32[]{:S(2)}, u32[]{:S(2)}) collective-permute-start(f32[24,768]{1,0:T(8,128)S(1)} %add.142), channel_id=1, source_target_pairs={{0,8},{4,12},{8,0},{12,4},{16,24},{20,28},{24,16},{28,20},{1,9},{5... | collective-permute-start | bytes 221192 | tf_op jit(solution)/shard_map/ppermute | solution.py:36
  304.6 10.8 %collective-permute-start.53 = (bf16[192,768]{1,0:T(8,128)(2,1)S(1)}, bf16[192,768]{1,0:T(8,128)(2,1)S(1)}, u32[]{:S(2)}, u32[]{:S(2)}) collective-permute-start(bf16[192,768]{1,0:T(8,128)(2,1)S(1)} %get-tuple-element.169), channel_id=1, source_target_pairs={{0,12},{4,8},{8,4},{12,0},{16,28},{20,24},{24,20},{28,16},{1,13},{... | collective-permute-start | bytes 884744 | tf_op jit(solution)/shard_map/ppermute | solution.py:36
  306.1 10.5 %collective-permute-start.50 = (f32[24,768]{1,0:T(8,128)S(1)}, f32[24,768]{1,0:T(8,128)S(1)}, u32[]{:S(2)}, u32[]{:S(2)}) collective-permute-start(f32[24,768]{1,0:T(8,128)S(1)} %add.143), channel_id=1, source_target_pairs={{0,16},{4,20},{8,24},{12,28},{16,0},{20,4},{24,8},{28,12},{1,17},{... | collective-permute-start | bytes 221192 | tf_op jit(solution)/shard_map/ppermute | solution.py:36
  315.6 7.9 %collective-permute-start.54 = (bf16[96,768]{1,0:T(8,128)(2,1)S(1)}, bf16[96,768]{1,0:T(8,128)(2,1)S(1)}, u32[]{:S(2)}, u32[]{:S(2)}) collective-permute-start(bf16[96,768]{1,0:T(8,128)(2,1)S(1)} %get-tuple-element.171), channel_id=1, source_target_pairs={{0,16},{4,20},{8,24},{12,28},{16,0},{20,4},{24,8},{28,12},{1,17},{... | collective-permute-start | bytes 442376 | tf_op jit(solution)/shard_map/ppermute | solution.py:36
  316.7 8.7 %collective-permute-start.45 = (bf16[256,768]{1,0:T(8,128)(2,1)S(1)}, bf16[256,768]{1,0:T(8,128)(2,1)S(1)}, u32[]{:S(2)}, u32[]{:S(2)}) collective-permute-start(bf16[256,768]{1,0:T(8,128)(2,1)S(1)} %add_convert_fusion.2), channel_id=1, source_target_pairs={{0,2},{1,3},{2,0},{3,1},{4,6},{5,7},{6,4},{7,5},{8,10},{9,11},{10,... | collective-permute-start | bytes 1179656 | tf_op jit(solution)/shard_map/ppermute | solution.py:36
  (116 other events, 1828.0 us)

commit v3 on v2

--- a/solution.py
+++ b/solution.py
@@ -14,6 +14,9 @@
 excluded = -1e30
 reach = 512
 tile = 128
+params = pltpu.CompilerParams(vmem_limit_bytes=64 * 1024 * 1024)
+brief = pl.CostEstimate(flops=10**9, bytes_accessed=10**6, transcendentals=0)
+long = pl.CostEstimate(flops=2 * 10**10, bytes_accessed=10**7, transcendentals=0)
 
 
 def normalize(values, gain):
@@ -41,10 +44,9 @@
 
 
 def call(
-    kernel, name, operands, outs, scratch=(), flops=0, limit=32, scalars=None, after=(), through=()
+    kernel, name, operands, outs, scratch=(), scalars=None, after=(), through=()
 ):
     operands, outs = list(operands), list(outs)
-    moved = sum(math.prod(o.shape) * o.dtype.itemsize for o in operands + outs)
     in_specs = [whole(o.shape) for o in operands]
     out_specs = [whole(o.shape) for o in outs]
     if scalars is not None:
@@ -66,10 +68,8 @@
         out_shape=outs + [shape(o.shape, o.dtype) for o in through],
         input_output_aliases={count + i: results + i for i in range(len(through))},
         scratch_shapes=list(scratch),
-        compiler_params=pltpu.CompilerParams(vmem_limit_bytes=limit * 1024 * 1024),
-        cost_estimate=pl.CostEstimate(
-            flops=int(flops), bytes_accessed=int(moved), transcendentals=0
-        ),
+        compiler_params=params,
+        cost_estimate=brief,
     )(*operands, *extra)
 
 
@@ -168,7 +168,6 @@
             pltpu.VMEM((seq_len + reach, span), bf16),
             pltpu.VMEM((heads * tile, window), f32),
         ],
-        flops=4 * seq_len * window * heads * 256,
         scalars=place,
         after=after,
     )
@@ -244,8 +243,6 @@
             pltpu.VMEM((seq_len + reach, span), f32),
             pltpu.VMEM((heads * tile, window), f32),
         ],
-        flops=10 * seq_len * window * heads * 256,
-        limit=48,
         scalars=place,
         after=after,
     )
@@ -265,20 +262,17 @@
     return pack
 
 
-def pair_up(pack, far, cotangent):
+def pair_up(pack, far, after):
     part = pack.shape[0]
 
     def kernel(near_ref, far_ref, both_ref):
         both_ref[:part, :] = near_ref[...]
         both_ref[part:, :] = far_ref[...]
 
-    return call(
-        kernel,
-        "pair_up",
-        [pack, far],
-        [shape((2 * part, pack.shape[1]), bf16)],
-        through=[cotangent],
-    )
+    (both,) = call(
+        kernel, "pair_up", [pack, far], [shape((2 * part, pack.shape[1]), bf16)], after=after
+    )
+    return both
 
 
 def project(place, token_blocks, pack_blocks, gain, span):
@@ -319,7 +313,6 @@
         + [shape((width, span), bf16)] * 3
         + [shape((span, width), bf16)],
         scratch=[pltpu.VMEM((width, width), bf16)],
-        flops=2 * seq_len * width * 4 * span,
         scalars=place,
     )
 
@@ -331,7 +324,7 @@
     return jnp.where(taken, 1.0, 0.0).astype(bf16)
 
 
-def to_slots(name, sets, blocks, size):
+def to_slots(name, sets, blocks, size, after=(), through=()):
     width = sets[0][0].shape[1]
 
     def kernel(*refs):
@@ -348,7 +341,8 @@
         name,
         operands,
         [shape((size * len(sets), width), bf16)] * blocks,
-        flops=2 * len(sets) * blocks * size * sets[0][0].shape[0] * width,
+        after=after,
+        through=through,
     )
 
 
@@ -372,7 +366,6 @@
         name,
         list(blocks) + list(slots),
         [shape((rows, width), dtype) for dtype in dtypes],
-        flops=2 * sets * count * size * rows * width,
         after=after,
         through=through,
     )
@@ -411,86 +404,57 @@
         [tokens, gain, w_router, slots] + mixed + weight_o,
         [shape((rows, width), f32), shape((rows, width), bf16), shape((rows, 128), f32)]
         + [shape((size, width), bf16)] * blocks,
-        flops=2 * rows * width * (width + blocks * size),
         after=after,
     )
 
 
-def experts_kernel(count, grads, experts, me_ref, w_in_ref, w_out_ref, router_ref, *refs):
-    x_refs, g_refs = refs[:count], refs[count : count + grads]
-    refs = refs[count + grads :]
-    back_refs, result_refs = refs[:count], refs[count : count + grads]
-    active_ref, pre_grad_ref, x_all, s_all = refs[count + grads : count + grads + 4]
-    gates, result_sum, back_sum = refs[count + grads + 4 :]
-    step = pl.program_id(0)
-    total, width = x_all.shape
-    size = total // count
-    chunk = min(256, total)
-
-    def grad_rows():
-        return jnp.concatenate([ref[...] for ref in g_refs], axis=0)
-
-    @pl.when(step == 0)
-    def _():
-        for b, ref in enumerate(x_refs):
-            x_all[b * size : (b + 1) * size, :] = ref[...]
-        probs = router_softmax(x_all[...], router_ref[...], experts)
-        lane = lax.broadcasted_iota(jnp.int32, probs.shape, 1)
-        own = jnp.sum(jnp.where(lane == me_ref[0], probs, 0.0), axis=1, keepdims=True)
-        gates[...] = jnp.broadcast_to(own, gates.shape)
-        s_all[...] = (own * grad_rows().astype(f32)).astype(bf16)
-        result_sum[...] = jnp.zeros_like(result_sum)
-        back_sum[...] = jnp.zeros_like(back_sum)
-
-    for c in range(total // chunk):
-        at = slice(c * chunk, (c + 1) * chunk)
-        pre_act = dot(x_all[at, :], w_in_ref[...], 1, 0)
-        active_grad = dot(s_all[at, :], w_out_ref[...], 1, 1)
-        below = 0.5 + 0.5 * lax.erf(pre_act * math.sqrt(0.5))
-        active = (pre_act * below).astype(bf16)
-        bell = jnp.exp(-0.5 * pre_act * pre_act) * (1.0 / math.sqrt(2.0 * math.pi))
-        pre_grad = (active_grad * (below + pre_act * bell)).astype(bf16)
-        active_ref[at, :] = active
-        pre_grad_ref[at, :] = pre_grad
-        result_sum[at, :] += dot(active, w_out_ref[...], 1, 0)
-        back_sum[at, :] += dot(pre_grad, w_in_ref[...], 1, 1)
-
-    @pl.when(step == pl.num_programs(0) - 1)
-    def _():
-        result = result_sum[...].astype(bf16).astype(f32)
-        gate_grad = jnp.sum(grad_rows().astype(f32) * result, axis=1, keepdims=True)
-        upper = gate_grad.astype(bf16).astype(f32)
-        lane = lax.broadcasted_iota(jnp.int32, (total, 128), 1)
-        columns = jnp.where(
-            lane == me_ref[0], upper, jnp.where(lane == me_ref[0] + 64, gate_grad - upper, 0.0)
-        ).astype(bf16)
-        back = back_sum[...].astype(bf16)
-        for b, ref in enumerate(back_refs):
-            ref[:, :width] = back[b * size : (b + 1) * size, :]
-            ref[:, width:] = columns[b * size : (b + 1) * size, :]
-        gated = (gates[:, 0:1] * result).astype(bf16)
-        each = total // grads
-        for b, ref in enumerate(result_refs):
-            ref[...] = gated[b * each : (b + 1) * each, :]
-
-
-def run_experts(place, w_in, w_out, w_router, x_blocks, g_blocks, experts):
+def join_rows(refs):
+    return jnp.concatenate([ref[...] for ref in refs], axis=0)
+
+
+def experts_forward(place, w_in, w_out, w_router, x_blocks, experts, blocks):
     width, units = w_in.shape
-    count, grads = len(x_blocks), len(g_blocks)
-    size, each = x_blocks[0].shape[0], g_blocks[0].shape[0]
-    total = size * count
-    piece = 512
+    count, size = len(x_blocks), x_blocks[0].shape[0]
+    total, piece = size * count, 768
+    each, chunk = total // blocks, min(256, total)
+
+    def kernel(me_ref, w_in_ref, w_out_ref, router_ref, *refs):
+        x_refs, out_refs = refs[:count], refs[count : count + blocks]
+        active_ref, slope_ref, x_all, result_ref, gates_ref, result_sum = refs[count + blocks :]
+
+        @pl.when(pl.program_id(0) == 0)
+        def _():
+            x_all[...] = join_rows(x_refs)
+            probs = router_softmax(x_all[...], router_ref[...], experts)
+            lane = lax.broadcasted_iota(jnp.int32, probs.shape, 1)
+            own = jnp.sum(jnp.where(lane == me_ref[0], probs, 0.0), axis=1, keepdims=True)
+            gates_ref[...] = jnp.broadcast_to(own, gates_ref.shape)
+            result_sum[...] = jnp.zeros_like(result_sum)
+
+        for c in range(total // chunk):
+            at = slice(c * chunk, (c + 1) * chunk)
+            pre_act = dot(x_all[at, :], w_in_ref[...], 1, 0)
+            below = 0.5 + 0.5 * lax.erf(pre_act * math.sqrt(0.5))
+            bell = jnp.exp(-0.5 * pre_act * pre_act) * (1.0 / math.sqrt(2.0 * math.pi))
+            active = (pre_act * below).astype(bf16)
+            active_ref[at, :] = active
+            slope_ref[at, :] = (below + pre_act * bell).astype(bf16)
+            result_sum[at, :] += dot(active, w_out_ref[...], 1, 0)
+
+        @pl.when(pl.program_id(0) == pl.num_programs(0) - 1)
+        def _():
+            result = result_sum[...].astype(bf16)
+            result_ref[...] = result
+            gated = (gates_ref[:, 0:1] * result.astype(f32)).astype(bf16)
+            for b, ref in enumerate(out_refs):
+                ref[...] = gated[b * each : (b + 1) * each, :]
 
     columns = pl.BlockSpec((total, piece), lambda i: (0, i))
-    outs = (
-        [shape((size, width + 128), bf16)] * count
-        + [shape((each, width), bf16)] * grads
-        + [shape((total, units), bf16)] * 2
-        + [shape((total, width), bf16)] * 2
-    )
+    outs = [shape((each, width), bf16)] * blocks
+    kept = [shape((total, width), bf16)] * 2 + [shape((total, 128), f32)]
     flat = pl.pallas_call(
-        functools.partial(experts_kernel, count, grads, experts),
-        name="run_experts",
+        kernel,
+        name="experts_forward",
         grid=(units // piece,),
         in_specs=[
             pl.BlockSpec(memory_space=pltpu.SMEM),
@@ -498,30 +462,77 @@
             pl.BlockSpec((piece, width), lambda i: (i, 0)),
             whole(w_router.shape),
         ]
-        + [whole((size, width))] * count
-        + [whole((each, width))] * grads,
-        out_specs=[whole((size, width + 128))] * count
-        + [whole((each, width))] * grads
+        + [whole(o.shape) for o in x_blocks],
+        out_specs=[whole(o.shape) for o in outs]
         + [columns] * 2
-        + [whole((total, width))] * 2,
-        out_shape=outs,
-        scratch_shapes=[
-            pltpu.VMEM((total, 128), f32),
-            pltpu.VMEM((total, width), f32),
-            pltpu.VMEM((total, width), f32),
-        ],
-        compiler_params=pltpu.CompilerParams(vmem_limit_bytes=56 * 1024 * 1024),
-        cost_estimate=pl.CostEstimate(
-            flops=8 * total * width * units,
-            bytes_accessed=4 * width * units + 4 * total * units,
-            transcendentals=2 * total * units,
-        ),
-    )(place, w_in, w_out, w_router, *x_blocks, *g_blocks)
-    return (
-        flat[:count],
-        flat[count : count + grads],
-        *flat[count + grads :],
-    )
+        + [whole(o.shape) for o in kept],
+        out_shape=outs + [shape((total, units), bf16)] * 2 + kept,
+        scratch_shapes=[pltpu.VMEM((total, width), f32)],
+        compiler_params=params,
+        cost_estimate=brief,
+    )(place, w_in, w_out, w_router, *x_blocks)
+    return (flat[:blocks], *flat[blocks:])
+
+
+def experts_backward(place, w_in, w_out, slope, result, gates, g_blocks, count):
+    width, units = w_in.shape
+    total, piece = slope.shape[0], 768
+    size, chunk = total // count, min(256, total)
+
+    def kernel(me_ref, w_in_ref, w_out_ref, slope_ref, result_ref, gates_ref, *refs):
+        g_refs, back_refs = refs[: len(g_blocks)], refs[len(g_blocks) : len(g_blocks) + count]
+        pre_grad_ref, s_all, back_sum = refs[len(g_blocks) + count :]
+
+        @pl.when(pl.program_id(0) == 0)
+        def _():
+            s_all[...] = (gates_ref[:, 0:1] * join_rows(g_refs).astype(f32)).astype(bf16)
+            back_sum[...] = jnp.zeros_like(back_sum)
+
+        for c in range(total // chunk):
+            at = slice(c * chunk, (c + 1) * chunk)
+            active_grad = dot(s_all[at, :], w_out_ref[...], 1, 1)
+            pre_grad = (active_grad * slope_ref[at, :].astype(f32)).astype(bf16)
+            pre_grad_ref[at, :] = pre_grad
+            back_sum[at, :] += dot(pre_grad, w_in_ref[...], 1, 1)
+
+        @pl.when(pl.program_id(0) == pl.num_programs(0) - 1)
+        def _():
+            products = join_rows(g_refs).astype(f32) * result_ref[...].astype(f32)
+            gate_grad = jnp.sum(products, axis=1, keepdims=True)
+            upper = gate_grad.astype(bf16).astype(f32)
+            lane = lax.broadcasted_iota(jnp.int32, (total, 128), 1)
+            columns = jnp.where(
+                lane == me_ref[0],
+                upper,
+                jnp.where(lane == me_ref[0] + 64, gate_grad - upper, 0.0),
+            ).astype(bf16)
+            back = back_sum[...].astype(bf16)
+            for b, ref in enumerate(back_refs):
+                ref[:, :width] = back[b * size : (b + 1) * size, :]
+                ref[:, width:] = columns[b * size : (b + 1) * size, :]
+
+    by_units = pl.BlockSpec((total, piece), lambda i: (0, i))
+    outs = [shape((size, width + 128), bf16)] * count
+    flat = pl.pallas_call(
+        kernel,
+        name="experts_backward",
+        grid=(units // piece,),
+        in_specs=[
+            pl.BlockSpec(memory_space=pltpu.SMEM),
+            pl.BlockSpec((width, piece), lambda i: (0, i)),
+            pl.BlockSpec((piece, width), lambda i: (i, 0)),
+            by_units,
+            whole(result.shape),
+            whole(gates.shape),
+        ]
+        + [whole(o.shape) for o in g_blocks],
+        out_specs=[whole(o.shape) for o in outs] + [by_units, whole((total, width))],
+        out_shape=outs + [shape((total, units), bf16), shape((total, width), bf16)],
+        scratch_shapes=[pltpu.VMEM((total, width), f32)],
+        compiler_params=params,
+        cost_estimate=brief,
+    )(place, w_in, w_out, slope, result, gates, *g_blocks)
+    return (flat[:count], *flat[count:])
 
 
 def home(
@@ -539,6 +550,7 @@
     size,
     experts,
     after,
+    through,
 ):
     rows, width = hidden.shape
     count, members = len(own_back), len(weight_o)
@@ -604,8 +616,8 @@
             shape((width, 2 * span), bf16),
             shape((width, 2 * span), f32),
         ],
-        flops=2 * rows * width * (2 * width + size * count),
         after=after,
+        through=through,
     )
 
 
@@ -645,12 +657,8 @@
             ],
         ),
         out_shape=[shape((2 * dims[0], dims[1]), bf16), shape((2 * dims[0], dims[1]), f32)],
-        compiler_params=pltpu.CompilerParams(vmem_limit_bytes=40 * 1024 * 1024),
-        cost_estimate=pl.CostEstimate(
-            flops=8 * total * width * piece,
-            bytes_accessed=2 * total * (width + 4 * piece) + 12 * width * piece,
-            transcendentals=0,
-        ),
+        compiler_params=params,
+        cost_estimate=long,
     )(place, fixed, cut)
 
 
@@ -733,14 +741,12 @@
         ]
         + weight_outs,
         scratch=[pltpu.VMEM((width, 4 * span), f32)],
-        flops=4 * seq_len * width * 3 * span,
-        limit=48,
         scalars=place,
         after=after,
     )
 
 
-def fold_weights(base, arrived):
+def fold_weights(base, arrived, after):
     part, width = base.shape[0] // 2, base.shape[1]
 
     def kernel(base_ref, *refs):
@@ -756,6 +762,7 @@
         "fold_weights",
         [base] + arrived,
         [shape((part, width), f32), shape((part, width), bf16)],
+        after=after,
     )
 
 
@@ -854,10 +861,9 @@
     token_blocks = gather_mp(tokens)
     pack = pack_weights(w_query, w_key, w_value, w_output)
     if few:
-        both, late_cotangent = pair_up(pack, swap(pack, "dp", 4), cotangent)
+        both = pair_up(pack, swap(pack, "dp", 4), token_blocks[1:3])
         pack_blocks = [(both, (0, 4))] + [(swap(both, "dp", r), (r, r ^ 4)) for r in (1, 2, 3)]
     else:
-        late_cotangent = cotangent
         pack_blocks = [(lax.all_gather(pack, "dp", axis=0, tiled=True), (0,))]
     gain_one, gain_two = norm_gain.reshape(1, width), ffn_gain.reshape(1, width)
     normed, query, key_rows, value_rows, weight_q, weight_k, weight_v, w_o = project(
@@ -874,17 +880,16 @@
         slots = [slots_of(routes, 0, capacity, experts, experts)]
 
     if few:
-        far_cotangent = swap(late_cotangent, "dp", 4)
+        far_cotangent = swap(cotangent, "dp", 4)
         held = to_slots(
             "grads_to_slots",
-            [(late_cotangent, slots[0]), (far_cotangent, slots[1])],
+            [(cotangent, slots[0]), (far_cotangent, slots[1])],
             blocks,
             size,
+            [query],
         )
-        g_blocks = [held[0]] + [swap(held[r], "dp", r) for r in (1, 2, 3)]
     else:
-        held = to_slots("grads_to_slots", [(late_cotangent, slots[0])], blocks, size)
-        g_blocks = [all_to_all_dp(held[0])]
+        held = to_slots("grads_to_slots", [(cotangent, slots[0])], blocks, size, [query])
 
     line_buckets = jnp.pad(jnp.flip(buckets[: reach + 1]), (0, window - reach - 1))
     bucket_hot = (
@@ -911,19 +916,26 @@
         experts,
         blocks,
         size,
-        g_blocks[1:],
+        [],
     )
     if few:
         far_input = swap(ffn_input, "dp", 4)
         own = [send[0]] + [swap(send[r], "dp", r) for r in (1, 2, 3)]
-        far = to_slots("far_to_slots", [(far_input, slots[1])], blocks, size)
+        far = to_slots(
+            "far_to_slots", [(far_input, slots[1])], blocks, size, through=held[1:]
+        )
+        g_blocks = [held[0]] + [swap(far[blocks + r - 1], "dp", r) for r in (1, 2, 3)]
         far = [far[0]] + [swap(far[r], "dp", r) for r in (1, 2, 3)]
         x_blocks = [item for pair in zip(own, far) for item in pair]
     else:
         x_blocks = [all_to_all_dp(send[0])]
-
-    back, result, active, pre_grad, arrived, slot_grad = run_experts(
-        place, w_in[0], w_out[0], router_wide, x_blocks, g_blocks, experts
+        g_blocks = [all_to_all_dp(held[0])]
+
+    result, active, slope, arrived, plain_result, slot_gates = experts_forward(
+        place, w_in[0], w_out[0], router_wide, x_blocks, experts, blocks
+    )
+    back, pre_grad, slot_grad = experts_backward(
+        place, w_in[0], w_out[0], slope, plain_result, slot_gates, g_blocks, len(x_blocks)
     )
     near_in, base_in = expert_weight_grads(
         "w_in_grads", place, arrived, pre_grad, False, members
@@ -932,6 +944,11 @@
         "w_out_grads", place, slot_grad, active, True, members
     )
     if few:
+        result_in = [result[0]] + [swap(result[r], "dp", r) for r in (1, 2, 3)]
+        own_result, far_result = from_slots(
+            "result_from_slots", result_in, slots, size, [f32, bf16]
+        )
+        far_result = swap(far_result, "dp", 4)
         far_back = [back[1]] + [swap(back[2 * r + 1], "dp", r) for r in (1, 2, 3)]
         far_total, *own_back = from_slots(
             "back_from_slots",
@@ -939,15 +956,20 @@
             [slots[1]],
             size,
             [bf16],
-            after=[near_in],
-            through=back[2::2],
+            after=[own_result],
+            through=list(back[2::2]) + [near_in],
         )
+        near_in = own_back.pop()
         far_sum = swap(far_total, "dp", 4)
         own_back = [back[0]] + [swap(own_back[r - 1], "dp", r) for r in (1, 2, 3)]
     else:
+        (own_result,) = from_slots(
+            "result_from_slots", [all_to_all_dp(result[0])], slots, size, [f32]
+        )
         own_back, far_sum = [all_to_all_dp(back[0])], None
-
-    *grad_out, hidden_grad, ffn_gain_grad, router_grad, near_o, base_o = home(
+    own_in, far_in = scatter_near(near_in, base_in, 0)
+
+    *grad_out, hidden_grad, ffn_gain_grad, router_grad, near_o, base_o, near_out = home(
         own_back,
         far_sum,
         slots[0],
@@ -961,10 +983,10 @@
         mixed_in,
         size,
         experts,
+        [far_in],
         [near_out],
     )
     grad_in = [grad_out[0]] + [swap(grad_out[r], "mp", r) for r in range(1, members)]
-    own_in, far_in = scatter_near(near_in, base_in, 0)
     own_out, far_out = scatter_near(near_out, base_out, 0)
     own_o, far_o = scatter_near(near_o, base_o, 1)
 
@@ -978,20 +1000,11 @@
         line,
         grad_in,
         heads,
-        [far_in, far_out],
+        [far_out],
     )
     output_sum = own_o + swap(far_o, "mp", 2).astype(f32)
     far_in = swap(far_in, "mp", 2)
     far_out = swap(far_out, "mp", 2)
-    if few:
-        result_in = [result[0]] + [swap(result[r], "dp", r) for r in (1, 2, 3)]
-        own_result, far_result = from_slots(
-            "result_from_slots", result_in, slots, size, [f32, bf16]
-        )
-    else:
-        (own_result,) = from_slots(
-            "result_from_slots", [all_to_all_dp(result[0])], slots, size, [f32]
-        )
     near, base, base_far, small, *weight_sums = input_grads(
         place,
         proj_grads,
@@ -1006,11 +1019,11 @@
         members,
         owners,
         heads,
-        [far_in, own_result],
+        [far_in],
     )
     if few:
         arrived_sums = [swap(weight_sums[r], "dp", r) for r in (1, 2, 3)]
-        own_sum, far_part = fold_weights(weight_sums[0], arrived_sums)
+        own_sum, far_part = fold_weights(weight_sums[0], arrived_sums, [far_out])
         weight_grads = split_weights([own_sum, swap(far_part, "dp", 4)], span)
     else:
         joined_grad = lax.psum_scatter(weight_sums[0], "dp", scatter_dimension=0, tiled=True)
@@ -1028,7 +1041,7 @@
 
     block_out = hidden + own_result
     if few:
-        block_out = block_out + swap(far_result, "dp", 4).astype(f32)
+        block_out = block_out + far_result.astype(f32)
     block_out = block_out.astype(bf16)
     w_in_grad = own_in + far_in.astype(f32)
     w_out_grad = own_out + far_out.astype(f32)

time: 328 us -> 347 us (1.058)
  Pallas kernels: 89.6 us -> 129 us
  local copies, waits for them, and re-layouts: 35.5 us -> 17.4 us
  other arithmetic: 16.7 us -> 29.8 us
  waiting for transfers between devices: 127 us -> 114 us
    pallas_call x14, Pallas kernels: 42.4 us -> 68.9 us  [call(): pl.pallas_call(body, name=name, grid=(1,), in_specs=in_specs + [pl.BlockS...]
    unnamed x220 -> x49, local copies, waits for them, and re-layouts: 29.7 us -> 5.4 us
    ppermute x56, waiting for transfers between devices: 127 us -> 114 us  [swap(): return lax.ppermute(values, axis, [(i, i ^ step) for i in range(count)])]
    pallas_call x1 -> x2, Pallas kernels: 30.1 us -> 37.9 us  [the longest x1 19.5 us: experts_forward(): pl.pallas_call(kernel, name='experts_forward', grid=(units // piece,), in...]
    pallas_call x2, Pallas kernels: 17.1 us -> 22 us  [expert_weight_grads(): pl.pallas_call(kernel, name=name, grid_spec=pltpu.PrefetchScalarGridSpec(...]
    convert_element_type x3, other arithmetic: 4.34 us -> 8.59 us  [scatter_near(): return (own, far.astype(bf16))]
  transfers between devices with their start and end apart: 56 -> 56, of which waited for: 28 -> 23; matrix products, arithmetic and copies ran while one was open for 8% -> 13% of each run, Pallas kernels for 14% -> 33%
where the time goes in v3:
time: 347 us; the launch traced here: 346 us
  Pallas kernels  129 us (37%)
  waiting for transfers between devices  114 us (33%)
  starting transfers between devices  52.5 us (15%)
  other arithmetic  29.8 us (9%)
  local copies, waits for them, and re-layouts  17.4 us (5%)
    ppermute x56, waiting for transfers between devices, swap(): return lax.ppermute(values, axis, [(i, i ^ step) for i in range(count)])  114 us
    pallas_call x14, Pallas kernels, call(): pl.pallas_call(body, name=name, grid=(1,), in_specs=in_specs + [pl.BlockS...  68.9 us
    ppermute x56, starting transfers between devices, swap(): return lax.ppermute(values, axis, [(i, i ^ step) for i in range(count)])  52.5 us
    pallas_call x2, Pallas kernels, expert_weight_grads(): pl.pallas_call(kernel, name=name, grid_spec=pltpu.PrefetchScalarGridSpec(...  22 us
    pallas_call x1, Pallas kernels, experts_forward(): pl.pallas_call(kernel, name='experts_forward', grid=(units // piece,), in...  19.5 us
    pallas_call x1, Pallas kernels, experts_backward(): pl.pallas_call(kernel, name='experts_backward', grid=(units // piece,), i...  18.3 us
    convert_element_type x3, other arithmetic, scatter_near(): return (own, far.astype(bf16))  8.59 us
  transfers between devices with their start and end apart: 56, of which 23 were waited for; matrix products, arithmetic and copies ran while one was open for 13% of the time, Pallas kernels for 33%

profile of v3, /device:TPU:0, one launch (start us, length us, event | category | flops | bytes accessed | tf_op | source)
XLA Modules:
  0.0 346.0 jit_solution(3519243945389553835)
XLA Ops:
  1.2 2.6 collective-permute-start.1
  5.5 2.6 collective-permute-start.3
  13.8 2.0 collective-permute-done.3.refs_1_
  27.2 2.1 collective-permute-start.7
  30.6 8.3 %collective-permute-done.6.refs_9_ = bf16[192,768]{1,0:T(8,128)(2,1)} collective-permute-done((bf16[192,768]{1,0:T(8,128)(2,1)}, bf16[192,768]{1,0:T(8,128)(2,1)}, u32[]{:S(2)}, u32[]{:S(2)}) %collective-permute-start.6) | collective-permute-done | bytes 294944 | tf_op jit(solution)/shard_map/ppermute | solution.py:39
  38.9 5.2 %project.1 = (bf16[1024,768]{1,0:T(8,128)(2,1)}, bf16[1024,192]{1,0:T(8,128)(2,1)}, bf16[1024,192]{1,0:T(8,128)(2,1)}, bf16[1024,192]{1,0:T(8,128)(2,1)}, bf16[7...) custom-call(s32[2]{0:T(128)} %pad_add_fusion.2.refs_0_.me_ref.place_ref, ...), custom_call_target="tpu_custom_call" | custom-call | flops 1000000000 | bytes 1000000 | tf_op jit(solution)/shard_map/project/pallas_call | solution.py:62
  46.8 4.4 %collective-permute-done.13.refs_10_.refs_14_ = bf16[192,768]{1,0:T(8,128)(2,1)} collective-permute-done((bf16[192,768]{1,0:T(8,128)(2,1)}, bf16[192,768]{1,0:T(8,128)(2,1)}, u32[]{:S(2)}, u32[]{:S(2)}) %collective-permute-start.13) | collective-permute-done | bytes 294944 | tf_op jit(solution)/shard_map/ppermute | solution.py:39
  51.7 2.8 grads_to_slots.1
  54.5 11.5 %attend.1 = (bf16[256,192]{1,0:T(8,128)(2,1)}, bf16[256,192]{1,0:T(8,128)(2,1)}, bf16[256,192]{1,0:T(8,128)(2,1)}, bf16[256,192]{1,0:T(8,128)(2,1)}) custom-call(s32[2]{0:T(128)} %pad_add_fusion.2.refs_0_.me_ref.place_ref, bf16[1024,192]{1,0:T(8,128)(2,1)} %get-tuple-element.100.refs_4_.refs_1_, bf16[1024,192]{1,0:T(8,128)(2,1)} %get-tuple-element.101.refs_2_, ...), custom_call_target="tpu_custom_call" | custom-call | flops 1000000000 | bytes 1000000 | tf_op jit(solution)/shard_map/attend/pallas_call | solution.py:62
  71.1 2.0 collective-permute-done.10.refs_6_.refs_18_
  74.3 3.8 %middle.1 = (f32[256,768]{1,0:T(8,128)}, bf16[256,768]{1,0:T(8,128)(2,1)}, f32[256,128]{1,0:T(8,128)}, bf16[128,768]{1,0:T(8,128)(2,1)}, bf16[128,768]{1,0:T(8,1...) custom-call(bf16[256,768]{1,0:T(8,128)(2,1)} %refs_0_.5, f32[1,768]{1,0:T(1,128)} %reshape.191.refs_1_.refs_4_, ...), custom_call_target="tpu_custom_call" | custom-call | flops 1000000000 | bytes 1000000 | tf_op jit(solution)/shard_map/middle/pallas_call | solution.py:62
  80.8 2.3 collective-permute-start.18
  83.1 16.4 %collective-permute-done.15.refs_0_ = bf16[256,768]{1,0:T(8,128)(2,1)} collective-permute-done((bf16[256,768]{1,0:T(8,128)(2,1)}, bf16[256,768]{1,0:T(8,128)(2,1)}, u32[]{:S(2)}, u32[]{:S(2)}) %collective-permute-start.15) | collective-permute-done | bytes 393248 | tf_op jit(solution)/shard_map/ppermute | solution.py:39
  99.5 2.2 far_to_slots.1
  101.7 1.9 collective-permute-start.17
  105.2 1.9 collective-permute-start.26
  107.1 3.4 collective-permute-done.17.refs_3_
  111.7 3.8 %collective-permute-done.21.refs_7_ = bf16[128,768]{1,0:T(8,128)(2,1)} collective-permute-done((bf16[128,768]{1,0:T(8,128)(2,1)}, bf16[128,768]{1,0:T(8,128)(2,1)}, u32[]{:S(2)}, u32[]{:S(2)}) %collective-permute-start.21) | collective-permute-done | bytes 196640 | tf_op jit(solution)/shard_map/ppermute | solution.py:39
  115.5 19.5 %experts_forward.1 = (bf16[256,768]{1,0:T(8,128)(2,1)}, bf16[256,768]{1,0:T(8,128)(2,1)}, bf16[256,768]{1,0:T(8,128)(2,1)}, bf16[256,768]{1,0:T(8,128)(2,1)}, bf...) custom-call(s32[2]{0:T(128)} %pad_add_fusion.2.refs_0_.me_ref.place_, ...), custom_call_target="tpu_custom_call" | custom-call | flops 1000000000 | bytes 1000000 | tf_op jit(solution)/shard_map/experts_forward/pallas_call | solution.py:455
  135.1 1.9 collective-permute-start.22
  138.7 18.3 %experts_backward.1 = (bf16[128,896]{1,0:T(8,128)(2,1)}, bf16[128,896]{1,0:T(8,128)(2,1)}, bf16[128,896]{1,0:T(8,128)(2,1)}, bf16[128,896]{1,0:T(8,128)(2,1)}, b...) custom-call(s32[2]{0:T(128)} %pad_add_fusion.2.refs_0_.me_ref.place_, ...), custom_call_target="tpu_custom_call" | custom-call | flops 1000000000 | bytes 1000000 | tf_op jit(solution)/shard_map/experts_backward/pallas_call | solution.py:516
  157.0 1.9 collective-permute-start.29
  160.6 11.0 %w_in_grads.1 = (bf16[1536,768]{1,0:T(8,128)(2,1)}, f32[1536,768]{1,0:T(8,128)}) custom-call(s32[2]{0:T(128)} %pad_add_fusion.2.refs_0_.me_ref.place_ref, bf16[1024,768]{1,0:T(8,128)(2,1)} %get-tuple-element.143.fixed_ref, bf16[1024,3072]{1,0:T(8,128)(2,1)} %get-tuple-element.144.cut_ref), custom_call_target="tpu_custom_call" | custom-call | flops 20000000000 | bytes 10000000 | tf_op jit(solution)/shard_map/w_in_grads/pallas_call | solution.py:644
  171.5 3.4 result_from_slots.1
  175.0 2.7 back_from_slots.1
  178.7 11.0 %w_out_grads.1 = (bf16[1536,768]{1,0:T(8,128)(2,1)}, f32[1536,768]{1,0:T(8,128)}) custom-call(s32[2]{0:T(128)} %pad_add_fusion.2.refs_0_.me_ref.place_ref, bf16[1024,768]{1,0:T(8,128)(2,1)} %get-tuple-element.150.fixed_ref, bf16[1024,3072]{1,0:T(8,128)(2,1)} %get-tuple-element.151.cut_ref), custom_call_target="tpu_custom_call" | custom-call | flops 20000000000 | bytes 10000000 | tf_op jit(solution)/shard_map/w_out_grads/pallas_call | solution.py:644
  191.1 2.0 collective-permute-start.33
  193.1 3.2 add_convert_fusion.1.refs_21_
  197.7 8.8 %collective-permute-done.33.refs_9_ = bf16[128,896]{1,0:T(8,128)(2,1)} collective-permute-done((bf16[128,896]{1,0:T(8,128)(2,1)}, bf16[128,896]{1,0:T(8,128)(2,1)}, u32[]{:S(2)}, u32[]{:S(2)}) %collective-permute-start.33) | collective-permute-done | bytes 229408 | tf_op jit(solution)/shard_map/ppermute | solution.py:39
  206.5 5.7 %collective-permute-done.34.refs_10_ = bf16[128,896]{1,0:T(8,128)(2,1)} collective-permute-done((bf16[128,896]{1,0:T(8,128)(2,1)}, bf16[128,896]{1,0:T(8,128)(2,1)}, u32[]{:S(2)}, u32[]{:S(2)}) %collective-permute-start.34) | collective-permute-done | bytes 229408 | tf_op jit(solution)/shard_map/ppermute | solution.py:39
  212.3 7.2 %home.1 = (bf16[256,192]{1,0:T(8,128)(2,1)}, bf16[256,192]{1,0:T(8,128)(2,1)}, bf16[256,192]{1,0:T(8,128)(2,1)}, bf16[256,192]{1,0:T(8,128)(2,1)}, f32[256,768]{...) custom-call(s32[8,256]{1,0:T(8,128)} %pad.24.refs_1_.refs_3_.refs_4_, ...), custom_call_target="tpu_custom_call", output_to_operand_aliasing={{9}: (20, {})} | custom-call | flops 1000000000 | bytes 1000000 | tf_op jit(solution)/shard_map/home/pallas_call | solution.py:62
  221.3 3.8 %collective-permute-done.41 = bf16[768,384]{1,0:T(8,128)(2,1)S(1)} collective-permute-done((bf16[768,384]{1,0:T(8,128)(2,1)}, bf16[768,384]{1,0:T(8,128)(2,1)S(1)}, u32[]{:S(2)}, u32[]{:S(2)}) %collective-permute-start.41) | collective-permute-done | bytes 589856 | tf_op jit(solution)/shard_map/ppermute | solution.py:39
  229.5 27.1 %collective-permute-done.42 = bf16[768,192]{1,0:T(8,128)(2,1)S(1)} collective-permute-done((bf16[768,192]{1,0:T(8,128)(2,1)S(1)}, bf16[768,192]{1,0:T(8,128)(2,1)S(1)}, u32[]{:S(2)}, u32[]{:S(2)}) %collective-permute-start.42) | collective-permute-done | bytes 294944 | tf_op jit(solution)/shard_map/ppermute | solution.py:39
  259.0 3.8 %add_convert_fusion.refs_11_ = bf16[768,768]{1,0:T(8,128)(2,1)} fusion(f32[1536,768]{1,0:T(8,128)} %get-tuple-element.160, bf16[1536,768]{1,0:T(8,128)(2,1)S(1)} %collective-permute-done.40), kind=kLoop, calls=%fused_computation.2 | loop fusion | flops 1769472 | bytes 4718592 | tf_op jit(solution)/shard_map/convert_element_type | solution.py:802
  265.3 16.1 %attend_back.1 = (bf16[1024,192]{1,0:T(8,128)(2,1)}, bf16[1024,192]{1,0:T(8,128)(2,1)}, bf16[1024,192]{1,0:T(8,128)(2,1)}, f32[8,640]{1,0:T(8,128)}) custom-call(s32[2]{0:T(128)} %pad_add_fusion.2.refs_0_.me_ref.place_ref, bf16[1024,192]{1,0:T(8,128)(2,1)} %get-tuple-element.100.refs_4_.refs_1_, bf16[1024,192]{1,0:T(8,128)(2,1)} %get-tuple-element.101.refs_2_, ...), custom_call_target="tpu_custom_call" | custom-call | flops 1000000000 | bytes 1000000 | tf_op jit(solution)/shard_map/attend_back/pallas_call | solution.py:62
  281.4 6.6 %input_grads.1 = (bf16[512,768]{1,0:T(8,128)(2,1)}, f32[256,768]{1,0:T(8,128)}, f32[256,768]{1,0:T(8,128)}, f32[24,768]{1,0:T(8,128)}, f32[192,768]{1,0:T(8,128)...) custom-call(s32[2]{0:T(128)} %pad_add_fusion.2.refs_0_.me_ref.place_ref, ...), custom_call_target="tpu_custom_call" | custom-call | flops 1000000000 | bytes 1000000 | tf_op jit(solution)/shard_map/input_grads/pallas_call | solution.py:62
  291.4 3.4 collective-permute-done.47
  295.5 3.8 %collective-permute-done.48 = f32[24,768]{1,0:T(8,128)S(1)} collective-permute-done((f32[24,768]{1,0:T(8,128)S(1)}, f32[24,768]{1,0:T(8,128)S(1)}, u32[]{:S(2)}, u32[]{:S(2)}) %collective-permute-start.48) | collective-permute-done | bytes 73760 | tf_op jit(solution)/shard_map/ppermute | solution.py:39
  299.4 2.4 add_convert_fusion.4
  305.4 4.1 %add_bitcast_fusion.1 = f32[1,768,768]{2,1,0:T(8,128)} fusion(bf16[768,768]{1,0:T(8,128)(2,1)} %collective-permute-done.43.refs_14_, f32[1536,768]{1,0:T(8,128)} %get-tuple-element.153, bf16[1536,768]{1,0:T(8,128)(2,1)} %collective-permute-done.36), kind=kLoop, calls=%fused_computation.1 | loop fusion | flops 2359296 | bytes 7077888 | tf_op jit(solution)/shard_map/broadcast_in_dim | solution.py:1057
  311.0 1.9 collective-permute-start.53
  316.7 1.8 collective-permute-done.51.refs_1_
  319.9 6.2 %collective-permute-done.53.refs_3_ = bf16[192,768]{1,0:T(8,128)(2,1)S(1)} collective-permute-done((bf16[192,768]{1,0:T(8,128)(2,1)S(1)}, bf16[192,768]{1,0:T(8,128)(2,1)S(1)}, u32[]{:S(2)}, u32[]{:S(2)}) %collective-permute-start.53) | collective-permute-done | bytes 294944 | tf_op jit(solution)/shard_map/ppermute | solution.py:39
  326.1 4.6 %collective-permute-done.54.refs_4_ = bf16[768,768]{1,0:T(8,128)(2,1)S(1)} collective-permute-done((bf16[768,768]{1,0:T(8,128)(2,1)S(1)}, bf16[768,768]{1,0:T(8,128)(2,1)S(1)}, u32[]{:S(2)}, u32[]{:S(2)}) %collective-permute-start.54) | collective-permute-done | bytes 1179680 | tf_op jit(solution)/shard_map/ppermute | solution.py:39
  331.7 2.2 fold_weights.1
  333.9 2.6 collective-permute-start.55
  336.5 4.0 %add_bitcast_fusion = f32[1,768,768]{2,1,0:T(8,128)} fusion(bf16[768,768]{1,0:T(8,128)(2,1)} %copy-done.7, f32[1536,768]{1,0:T(8,128)} %get-tuple-element.160, bf16[1536,768]{1,0:T(8,128)(2,1)} %copy-done.2), kind=kLoop, calls=%fused_computation | loop fusion | flops 2359296 | bytes 7077888 | tf_op jit(solution)/shard_map/broadcast_in_dim | solution.py:1058
  342.0 2.1 fusion.5
  (173 shorter events, 72.7 us)
Async XLA Ops:
  0.6 15.2 %collective-permute-start = (bf16[256,768]{1,0:T(8,128)(2,1)}, bf16[256,768]{1,0:T(8,128)(2,1)}, u32[]{:S(2)}, u32[]{:S(2)}) collective-permute-start(bf16[256,768]{1,0:T(8,128)(2,1)} %refs_0_.5), channel_id=1, source_target_pairs={{0,1},{1,0},{2,3},{3,2},{4,5},{5,4},{6,7},{7,6},{8,9},{9,8},{10,11... | collective-permute-start | bytes 1179656 | tf_op jit(solution)/shard_map/ppermute | solution.py:39
  1.2 12.7 %collective-permute-start.1 = (bf16[256,768]{1,0:T(8,128)(2,1)}, bf16[256,768]{1,0:T(8,128)(2,1)}, u32[]{:S(2)}, u32[]{:S(2)}) collective-permute-start(bf16[256,768]{1,0:T(8,128)(2,1)} %refs_0_.5), channel_id=1, source_target_pairs={{0,2},{1,3},{2,0},{3,1},{4,6},{5,7},{6,4},{7,5},{8,10},{9,11},{10,... | collective-permute-start | bytes 1179656 | tf_op jit(solution)/shard_map/ppermute | solution.py:39
  5.5 10.4 %collective-permute-start.3 = (bf16[96,768]{1,0:T(8,128)(2,1)}, bf16[96,768]{1,0:T(8,128)(2,1)}, u32[]{:S(2)}, u32[]{:S(2)}) collective-permute-start(bf16[96,768]{1,0:T(8,128)(2,1)} %pack_weights.1.refs_0_), channel_id=1, source_target_pairs={{0,16},{4,20},{8,24},{12,28},{16,0},{20,4},{24,8},{28,12},{1,17},{... | collective-permute-start | bytes 442376 | tf_op jit(solution)/shard_map/ppermute | solution.py:39
  8.0 19.2 %collective-permute-start.8 = (s32[256,2]{0,1:T(2,128)}, s32[256,2]{0,1:T(2,128)}, u32[]{:S(2)}, u32[]{:S(2)}) collective-permute-start(s32[256,2]{0,1:T(2,128)} %param.28), channel_id=1, source_target_pairs={{0,16},{4,20},{8,24},{12,28},{16,0},{20,4},{24,8},{28,12},{1,17},{... | collective-permute-start | bytes 6152 | tf_op jit(solution)/shard_map/ppermute | solution.py:39
  13.8 25.1 %collective-permute-start.2 = (bf16[256,768]{1,0:T(8,128)(2,1)}, bf16[256,768]{1,0:T(8,128)(2,1)}, u32[]{:S(2)}, u32[]{:S(2)}) collective-permute-start(bf16[256,768]{1,0:T(8,128)(2,1)} %collective-permute-done.1.refs_3_.refs_4_), channel_id=1, source_target_pairs={{0,1},{1,0},{2,3},{3,2},{4,5},{5,4},{6,7},{7,6},{8,9},{9,8},{10,11... | collective-permute-start | bytes 1179656 | tf_op jit(solution)/shard_map/ppermute | solution.py:39
  17.5 13.1 %collective-permute-start.4 = (bf16[192,768]{1,0:T(8,128)(2,1)}, bf16[192,768]{1,0:T(8,128)(2,1)}, u32[]{:S(2)}, u32[]{:S(2)}) collective-permute-start(bf16[192,768]{1,0:T(8,128)(2,1)} %pair_up.1.refs_6_), channel_id=1, source_target_pairs={{0,4},{4,0},{8,12},{12,8},{16,20},{20,16},{24,28},{28,24},{1,5},{5... | collective-permute-start | bytes 884744 | tf_op jit(solution)/shard_map/ppermute | solution.py:39
  19.0 11.6 %collective-permute-start.5 = (bf16[192,768]{1,0:T(8,128)(2,1)}, bf16[192,768]{1,0:T(8,128)(2,1)}, u32[]{:S(2)}, u32[]{:S(2)}) collective-permute-start(bf16[192,768]{1,0:T(8,128)(2,1)} %pair_up.1.refs_6_), channel_id=1, source_target_pairs={{0,8},{4,12},{8,0},{12,4},{16,24},{20,28},{24,16},{28,20},{1,9},{5... | collective-permute-start | bytes 884744 | tf_op jit(solution)/shard_map/ppermute | solution.py:39
  19.7 19.2 %collective-permute-start.6 = (bf16[192,768]{1,0:T(8,128)(2,1)}, bf16[192,768]{1,0:T(8,128)(2,1)}, u32[]{:S(2)}, u32[]{:S(2)}) collective-permute-start(bf16[192,768]{1,0:T(8,128)(2,1)} %pair_up.1.refs_6_), channel_id=1, source_target_pairs={{0,12},{4,8},{8,4},{12,0},{16,28},{20,24},{24,20},{28,16},{1,13},{... | collective-permute-start | bytes 884744 | tf_op jit(solution)/shard_map/ppermute | solution.py:39
  27.2 24.5 %collective-permute-start.7 = (bf16[256,768]{1,0:T(8,128)(2,1)}, bf16[256,768]{1,0:T(8,128)(2,1)}, u32[]{:S(2)}, u32[]{:S(2)}) collective-permute-start(bf16[256,768]{1,0:T(8,128)(2,1)} %refs_3_.3), channel_id=1, source_target_pairs={{0,16},{4,20},{8,24},{12,28},{16,0},{20,4},{24,8},{28,12},{1,17},{... | collective-permute-start | bytes 1179656 | tf_op jit(solution)/shard_map/ppermute | solution.py:39
  44.1 7.0 %collective-permute-start.13 = (bf16[192,768]{1,0:T(8,128)(2,1)}, bf16[192,768]{1,0:T(8,128)(2,1)}, u32[]{:S(2)}, u32[]{:S(2)}) collective-permute-start(bf16[192,768]{1,0:T(8,128)(2,1)} %get-tuple-element.108.refs_8_.refs_12_), channel_id=1, source_target_pairs={{0,2},{1,3},{2,0},{3,1},{4,6},{5,7},{6,4},{7,5},{8,10},{9,11},{10,... | collective-permute-start | bytes 884744 | tf_op jit(solution)/shard_map/ppermute | solution.py:39
  46.7 27.6 %collective-permute-start.12 = (bf16[192,768]{1,0:T(8,128)(2,1)}, bf16[192,768]{1,0:T(8,128)(2,1)}, u32[]{:S(2)}, u32[]{:S(2)}) collective-permute-start(bf16[192,768]{1,0:T(8,128)(2,1)} %get-tuple-element.108.refs_8_.refs_12_), channel_id=1, source_target_pairs={{0,1},{1,0},{2,3},{3,2},{4,5},{5,4},{6,7},{7,6},{8,9},{9,8},{10,11... | collective-permute-start | bytes 884744 | tf_op jit(solution)/shard_map/ppermute | solution.py:39
  51.1 23.2 %collective-permute-start.14 = (bf16[192,768]{1,0:T(8,128)(2,1)}, bf16[192,768]{1,0:T(8,128)(2,1)}, u32[]{:S(2)}, u32[]{:S(2)}) collective-permute-start(bf16[192,768]{1,0:T(8,128)(2,1)} %collective-permute-done.13.refs_10_.refs_14_), channel_id=1, source_target_pairs={{0,1},{1,0},{2,3},{3,2},{4,5},{5,4},{6,7},{7,6},{8,9},{9,8},{10,11... | collective-permute-start | bytes 884744 | tf_op jit(solution)/shard_map/ppermute | solution.py:39
  66.5 6.5 %collective-permute-start.10 = (bf16[256,192]{1,0:T(8,128)(2,1)}, bf16[256,192]{1,0:T(8,128)(2,1)}, u32[]{:S(2)}, u32[]{:S(2)}) collective-permute-start(bf16[256,192]{1,0:T(8,128)(2,1)} %get-tuple-element.106), channel_id=1, source_target_pairs={{0,2},{1,3},{2,0},{3,1},{4,6},{5,7},{6,4},{7,5},{8,10},{9,11},{10,... | collective-permute-start | bytes 294920 | tf_op jit(solution)/shard_map/ppermute | solution.py:39
  78.1 21.4 %collective-permute-start.15 = (bf16[256,768]{1,0:T(8,128)(2,1)}, bf16[256,768]{1,0:T(8,128)(2,1)}, u32[]{:S(2)}, u32[]{:S(2)}) collective-permute-start(bf16[256,768]{1,0:T(8,128)(2,1)} %get-tuple-element.111.refs_6_), channel_id=1, source_target_pairs={{0,16},{4,20},{8,24},{12,28},{16,0},{20,4},{24,8},{28,12},{1,17},{... | collective-permute-start | bytes 1179656 | tf_op jit(solution)/shard_map/ppermute | solution.py:39
  79.2 24.4 %collective-permute-start.16 = (bf16[128,768]{1,0:T(8,128)(2,1)}, bf16[128,768]{1,0:T(8,128)(2,1)}, u32[]{:S(2)}, u32[]{:S(2)}) collective-permute-start(bf16[128,768]{1,0:T(8,128)(2,1)} %get-tuple-element.116), channel_id=1, source_target_pairs={{0,4},{4,0},{8,12},{12,8},{16,20},{20,16},{24,28},{28,24},{1,5},{5... | collective-permute-start | bytes 589832 | tf_op jit(solution)/shard_map/ppermute | solution.py:39
  80.8 24.4 %collective-permute-start.18 = (bf16[128,768]{1,0:T(8,128)(2,1)}, bf16[128,768]{1,0:T(8,128)(2,1)}, u32[]{:S(2)}, u32[]{:S(2)}) collective-permute-start(bf16[128,768]{1,0:T(8,128)(2,1)} %get-tuple-element.118), channel_id=1, source_target_pairs={{0,8},{4,12},{8,0},{12,4},{16,24},{20,28},{24,16},{28,20},{1,9},{5... | collective-permute-start | bytes 589832 | tf_op jit(solution)/shard_map/ppermute | solution.py:39
  83.1 23.9 %collective-permute-start.20 = (bf16[128,768]{1,0:T(8,128)(2,1)}, bf16[128,768]{1,0:T(8,128)(2,1)}, u32[]{:S(2)}, u32[]{:S(2)}) collective-permute-start(bf16[128,768]{1,0:T(8,128)(2,1)} %get-tuple-element.120), channel_id=1, source_target_pairs={{0,12},{4,8},{8,4},{12,0},{16,28},{20,24},{24,20},{28,16},{1,13},{... | collective-permute-start | bytes 589832 | tf_op jit(solution)/shard_map/ppermute | solution.py:39
  101.7 8.8 %collective-permute-start.17 = (bf16[128,768]{1,0:T(8,128)(2,1)}, bf16[128,768]{1,0:T(8,128)(2,1)}, u32[]{:S(2)}, u32[]{:S(2)}) collective-permute-start(bf16[128,768]{1,0:T(8,128)(2,1)} %get-tuple-element.117), channel_id=1, source_target_pairs={{0,4},{4,0},{8,12},{12,8},{16,20},{20,16},{24,28},{28,24},{1,5},{5... | collective-permute-start | bytes 589832 | tf_op jit(solution)/shard_map/ppermute | solution.py:39
  103.6 8.1 %collective-permute-start.19 = (bf16[128,768]{1,0:T(8,128)(2,1)}, bf16[128,768]{1,0:T(8,128)(2,1)}, u32[]{:S(2)}, u32[]{:S(2)}) collective-permute-start(bf16[128,768]{1,0:T(8,128)(2,1)} %get-tuple-element.119), channel_id=1, source_target_pairs={{0,8},{4,12},{8,0},{12,4},{16,24},{20,28},{24,16},{28,20},{1,9},{5... | collective-permute-start | bytes 589832 | tf_op jit(solution)/shard_map/ppermute | solution.py:39
  103.6 11.9 %collective-permute-start.21 = (bf16[128,768]{1,0:T(8,128)(2,1)}, bf16[128,768]{1,0:T(8,128)(2,1)}, u32[]{:S(2)}, u32[]{:S(2)}) collective-permute-start(bf16[128,768]{1,0:T(8,128)(2,1)} %get-tuple-element.121), channel_id=1, source_target_pairs={{0,12},{4,8},{8,4},{12,0},{16,28},{20,24},{24,20},{28,16},{1,13},{... | collective-permute-start | bytes 589832 | tf_op jit(solution)/shard_map/ppermute | solution.py:39
  105.2 31.8 %collective-permute-start.26 = (bf16[256,768]{1,0:T(8,128)(2,1)}, bf16[256,768]{1,0:T(8,128)(2,1)}, u32[]{:S(2)}, u32[]{:S(2)}) collective-permute-start(bf16[256,768]{1,0:T(8,128)(2,1)} %get-tuple-element.132), channel_id=1, source_target_pairs={{0,4},{4,0},{8,12},{12,8},{16,20},{20,16},{24,28},{28,24},{1,5},{5... | collective-permute-start | bytes 1179656 | tf_op jit(solution)/shard_map/ppermute | solution.py:39
  107.1 31.6 %collective-permute-start.27 = (bf16[256,768]{1,0:T(8,128)(2,1)}, bf16[256,768]{1,0:T(8,128)(2,1)}, u32[]{:S(2)}, u32[]{:S(2)}) collective-permute-start(bf16[256,768]{1,0:T(8,128)(2,1)} %get-tuple-element.133), channel_id=1, source_target_pairs={{0,8},{4,12},{8,0},{12,4},{16,24},{20,28},{24,16},{28,20},{1,9},{5... | collective-permute-start | bytes 1179656 | tf_op jit(solution)/shard_map/ppermute | solution.py:39
  110.5 28.2 %collective-permute-start.28 = (bf16[256,768]{1,0:T(8,128)(2,1)}, bf16[256,768]{1,0:T(8,128)(2,1)}, u32[]{:S(2)}, u32[]{:S(2)}) collective-permute-start(bf16[256,768]{1,0:T(8,128)(2,1)} %get-tuple-element.134), channel_id=1, source_target_pairs={{0,12},{4,8},{8,4},{12,0},{16,28},{20,24},{24,20},{28,16},{1,13},{... | collective-permute-start | bytes 1179656 | tf_op jit(solution)/shard_map/ppermute | solution.py:39
  135.1 23.9 %collective-permute-start.22 = (bf16[256,768]{1,0:T(8,128)(2,1)}, bf16[256,768]{1,0:T(8,128)(2,1)}, u32[]{:S(2)}, u32[]{:S(2)}) collective-permute-start(bf16[256,768]{1,0:T(8,128)(2,1)} %get-tuple-element.123), channel_id=1, source_target_pairs={{0,4},{4,0},{8,12},{12,8},{16,20},{20,16},{24,28},{28,24},{1,5},{5... | collective-permute-start | bytes 1179656 | tf_op jit(solution)/shard_map/ppermute | solution.py:39
  137.0 34.5 %collective-permute-start.23 = (bf16[256,768]{1,0:T(8,128)(2,1)}, bf16[256,768]{1,0:T(8,128)(2,1)}, u32[]{:S(2)}, u32[]{:S(2)}) collective-permute-start(bf16[256,768]{1,0:T(8,128)(2,1)} %get-tuple-element.124), channel_id=1, source_target_pairs={{0,8},{4,12},{8,0},{12,4},{16,24},{20,28},{24,16},{28,20},{1,9},{5... | collective-permute-start | bytes 1179656 | tf_op jit(solution)/shard_map/ppermute | solution.py:39
  137.0 34.5 %collective-permute-start.24 = (bf16[256,768]{1,0:T(8,128)(2,1)}, bf16[256,768]{1,0:T(8,128)(2,1)}, u32[]{:S(2)}, u32[]{:S(2)}) collective-permute-start(bf16[256,768]{1,0:T(8,128)(2,1)} %get-tuple-element.125), channel_id=1, source_target_pairs={{0,12},{4,8},{8,4},{12,0},{16,28},{20,24},{24,20},{28,16},{1,13},{... | collective-permute-start | bytes 1179656 | tf_op jit(solution)/shard_map/ppermute | solution.py:39
  157.0 17.9 %collective-permute-start.29 = (bf16[128,896]{1,0:T(8,128)(2,1)}, bf16[128,896]{1,0:T(8,128)(2,1)}, u32[]{:S(2)}, u32[]{:S(2)}) collective-permute-start(bf16[128,896]{1,0:T(8,128)(2,1)} %get-tuple-element.137), channel_id=1, source_target_pairs={{0,4},{4,0},{8,12},{12,8},{16,20},{20,16},{24,28},{28,24},{1,5},{5... | collective-permute-start | bytes 688136 | tf_op jit(solution)/shard_map/ppermute | solution.py:39
  158.9 16.0 %collective-permute-start.30 = (bf16[128,896]{1,0:T(8,128)(2,1)}, bf16[128,896]{1,0:T(8,128)(2,1)}, u32[]{:S(2)}, u32[]{:S(2)}) collective-permute-start(bf16[128,896]{1,0:T(8,128)(2,1)} %get-tuple-element.138), channel_id=1, source_target_pairs={{0,8},{4,12},{8,0},{12,4},{16,24},{20,28},{24,16},{28,20},{1,9},{5... | collective-permute-start | bytes 688136 | tf_op jit(solution)/shard_map/ppermute | solution.py:39
  158.9 16.0 %collective-permute-start.31 = (bf16[128,896]{1,0:T(8,128)(2,1)}, bf16[128,896]{1,0:T(8,128)(2,1)}, u32[]{:S(2)}, u32[]{:S(2)}) collective-permute-start(bf16[128,896]{1,0:T(8,128)(2,1)} %get-tuple-element.139), channel_id=1, source_target_pairs={{0,12},{4,8},{8,4},{12,0},{16,28},{20,24},{24,20},{28,16},{1,13},{... | collective-permute-start | bytes 688136 | tf_op jit(solution)/shard_map/ppermute | solution.py:39
  177.7 15.5 %collective-permute-start.36 = (bf16[1536,768]{1,0:T(8,128)(2,1)}, bf16[1536,768]{1,0:T(8,128)(2,1)}, u32[]{:S(2)}, u32[]{:S(2)}) collective-permute-start(bf16[1536,768]{1,0:T(8,128)(2,1)} %get-tuple-element.154), channel_id=1, source_target_pairs={{0,1},{1,0},{2,3},{3,2},{4,5},{5,4},{6,7},{7,6},{8,9},{9,8},{10,11... | collective-permute-start | bytes 7077896 | tf_op jit(solution)/shard_map/ppermute | solution.py:39
  177.7 34.6 %collective-permute-start.35 = (bf16[256,896]{1,0:T(8,128)(2,1)}, bf16[256,896]{1,0:T(8,128)(2,1)}, u32[]{:S(2)}, u32[]{:S(2)}) collective-permute-start(bf16[256,896]{1,0:T(8,128)(2,1)} %get-tuple-element.149), channel_id=1, source_target_pairs={{0,16},{4,20},{8,24},{12,28},{16,0},{20,4},{24,8},{28,12},{1,17},{... | collective-permute-start | bytes 1376264 | tf_op jit(solution)/shard_map/ppermute | solution.py:39
  189.7 8.1 %collective-permute-start.32 = (bf16[128,896]{1,0:T(8,128)(2,1)}, bf16[128,896]{1,0:T(8,128)(2,1)}, u32[]{:S(2)}, u32[]{:S(2)}) collective-permute-start(bf16[128,896]{1,0:T(8,128)(2,1)} %get-tuple-element.146), channel_id=1, source_target_pairs={{0,4},{4,0},{8,12},{12,8},{16,20},{20,16},{24,28},{28,24},{1,5},{5... | collective-permute-start | bytes 688136 | tf_op jit(solution)/shard_map/ppermute | solution.py:39
  191.1 15.4 %collective-permute-start.33 = (bf16[128,896]{1,0:T(8,128)(2,1)}, bf16[128,896]{1,0:T(8,128)(2,1)}, u32[]{:S(2)}, u32[]{:S(2)}) collective-permute-start(bf16[128,896]{1,0:T(8,128)(2,1)} %get-tuple-element.147), channel_id=1, source_target_pairs={{0,8},{4,12},{8,0},{12,4},{16,24},{20,28},{24,16},{28,20},{1,9},{5... | collective-permute-start | bytes 688136 | tf_op jit(solution)/shard_map/ppermute | solution.py:39
  193.1 19.2 %collective-permute-start.34 = (bf16[128,896]{1,0:T(8,128)(2,1)}, bf16[128,896]{1,0:T(8,128)(2,1)}, u32[]{:S(2)}, u32[]{:S(2)}) collective-permute-start(bf16[128,896]{1,0:T(8,128)(2,1)} %get-tuple-element.148), channel_id=1, source_target_pairs={{0,12},{4,8},{8,4},{12,0},{16,28},{20,24},{24,20},{28,16},{1,13},{... | collective-permute-start | bytes 688136 | tf_op jit(solution)/shard_map/ppermute | solution.py:39
  219.5 39.4 %collective-permute-start.40 = (bf16[1536,768]{1,0:T(8,128)(2,1)}, bf16[1536,768]{1,0:T(8,128)(2,1)S(1)}, u32[]{:S(2)}, u32[]{:S(2)}) collective-permute-start(bf16[1536,768]{1,0:T(8,128)(2,1)} %get-tuple-element.161), channel_id=1, source_target_pairs={{0,1},{1,0},{2,3},{3,2},{4,5},{5,4},{6,7},{7,6},{8,9},{9,8},{10,11... | collective-permute-start | bytes 7077896 | tf_op jit(solution)/shard_map/ppermute | solution.py:39
  220.0 61.3 %collective-permute-start.43 = (bf16[768,768]{1,0:T(8,128)(2,1)}, bf16[768,768]{1,0:T(8,128)(2,1)}, u32[]{:S(2)}, u32[]{:S(2)}) collective-permute-start(bf16[768,768]{1,0:T(8,128)(2,1)} %add_convert_fusion.1.refs_21_), channel_id=1, source_target_pairs={{0,2},{1,3},{2,0},{3,1},{4,6},{5,7},{6,4},{7,5},{8,10},{9,11},{10,... | collective-permute-start | bytes 3538952 | tf_op jit(solution)/shard_map/ppermute | solution.py:39
  226.7 30.0 %collective-permute-start.42 = (bf16[768,192]{1,0:T(8,128)(2,1)S(1)}, bf16[768,192]{1,0:T(8,128)(2,1)S(1)}, u32[]{:S(2)}, u32[]{:S(2)}) collective-permute-start(bf16[768,192]{1,0:T(8,128)(2,1)S(1)} %add_convert_fusion.3), channel_id=1, source_target_pairs={{0,2},{1,3},{2,0},{3,1},{4,6},{5,7},{6,4},{7,5},{8,10},{9,11},{10,... | collective-permute-start | bytes 884744 | tf_op jit(solution)/shard_map/ppermute | solution.py:39
  229.5 69.8 %collective-permute-start.25 = (bf16[256,768]{1,0:T(8,128)(2,1)}, bf16[256,768]{1,0:T(8,128)(2,1)}, u32[]{:S(2)}, u32[]{:S(2)}) collective-permute-start(bf16[256,768]{1,0:T(8,128)(2,1)} %get-tuple-element.127), channel_id=1, source_target_pairs={{0,16},{4,20},{8,24},{12,28},{16,0},{20,4},{24,8},{28,12},{1,17},{... | collective-permute-start | bytes 1179656 | tf_op jit(solution)/shard_map/ppermute | solution.py:39
  229.5 33.3 %collective-permute-start.37 = (bf16[256,192]{1,0:T(8,128)(2,1)}, bf16[256,192]{1,0:T(8,128)(2,1)S(1)}, u32[]{:S(2)}, u32[]{:S(2)}) collective-permute-start(bf16[256,192]{1,0:T(8,128)(2,1)} %get-tuple-element.157), channel_id=1, source_target_pairs={{0,1},{1,0},{2,3},{3,2},{4,5},{5,4},{6,7},{7,6},{8,9},{9,8},{10,11... | collective-permute-start | bytes 294920 | tf_op jit(solution)/shard_map/ppermute | solution.py:39
  256.6 6.8 %collective-permute-start.38 = (bf16[256,192]{1,0:T(8,128)(2,1)}, bf16[256,192]{1,0:T(8,128)(2,1)S(1)}, u32[]{:S(2)}, u32[]{:S(2)}) collective-permute-start(bf16[256,192]{1,0:T(8,128)(2,1)} %get-tuple-element.158), channel_id=1, source_target_pairs={{0,2},{1,3},{2,0},{3,1},{4,6},{5,7},{6,4},{7,5},{8,10},{9,11},{10,... | collective-permute-start | bytes 294920 | tf_op jit(solution)/shard_map/ppermute | solution.py:39
  301.7 28.9 %collective-permute-start.54 = (bf16[768,768]{1,0:T(8,128)(2,1)S(1)}, bf16[768,768]{1,0:T(8,128)(2,1)S(1)}, u32[]{:S(2)}, u32[]{:S(2)}) collective-permute-start(bf16[768,768]{1,0:T(8,128)(2,1)S(1)} %copy-done), channel_id=1, source_target_pairs={{0,2},{1,3},{2,0},{3,1},{4,6},{5,7},{6,4},{7,5},{8,10},{9,11},{10,... | collective-permute-start | bytes 3538952 | tf_op jit(solution)/shard_map/ppermute | solution.py:39
  302.6 12.1 %collective-permute-start.44 = (bf16[512,768]{1,0:T(8,128)(2,1)S(1)}, bf16[512,768]{1,0:T(8,128)(2,1)S(1)}, u32[]{:S(2)}, u32[]{:S(2)}) collective-permute-start(bf16[512,768]{1,0:T(8,128)(2,1)S(1)} %copy-done.15), channel_id=1, source_target_pairs={{0,1},{1,0},{2,3},{3,2},{4,5},{5,4},{6,7},{7,6},{8,9},{9,8},{10,11... | collective-permute-start | bytes 2359304 | tf_op jit(solution)/shard_map/ppermute | solution.py:39
  303.8 7.3 %collective-permute-start.50 = (f32[24,768]{1,0:T(8,128)S(1)}, f32[24,768]{1,0:T(8,128)S(1)}, u32[]{:S(2)}, u32[]{:S(2)}) collective-permute-start(f32[24,768]{1,0:T(8,128)S(1)} %add.143), channel_id=1, source_target_pairs={{0,16},{4,20},{8,24},{12,28},{16,0},{20,4},{24,8},{28,12},{1,17},{... | collective-permute-start | bytes 221192 | tf_op jit(solution)/shard_map/ppermute | solution.py:39
  309.4 9.1 %collective-permute-start.51 = (bf16[192,768]{1,0:T(8,128)(2,1)S(1)}, bf16[192,768]{1,0:T(8,128)(2,1)S(1)}, u32[]{:S(2)}, u32[]{:S(2)}) collective-permute-start(bf16[192,768]{1,0:T(8,128)(2,1)S(1)} %copy-done.18), channel_id=1, source_target_pairs={{0,4},{4,0},{8,12},{12,8},{16,20},{20,16},{24,28},{28,24},{1,5},{5... | collective-permute-start | bytes 884744 | tf_op jit(solution)/shard_map/ppermute | solution.py:39
  310.0 9.9 %collective-permute-start.52 = (bf16[192,768]{1,0:T(8,128)(2,1)S(1)}, bf16[192,768]{1,0:T(8,128)(2,1)S(1)}, u32[]{:S(2)}, u32[]{:S(2)}) collective-permute-start(bf16[192,768]{1,0:T(8,128)(2,1)S(1)} %copy-done.17), channel_id=1, source_target_pairs={{0,8},{4,12},{8,0},{12,4},{16,24},{20,28},{24,16},{28,20},{1,9},{5... | collective-permute-start | bytes 884744 | tf_op jit(solution)/shard_map/ppermute | solution.py:39
  311.0 15.0 %collective-permute-start.53 = (bf16[192,768]{1,0:T(8,128)(2,1)S(1)}, bf16[192,768]{1,0:T(8,128)(2,1)S(1)}, u32[]{:S(2)}, u32[]{:S(2)}) collective-permute-start(bf16[192,768]{1,0:T(8,128)(2,1)S(1)} %copy-done.16), channel_id=1, source_target_pairs={{0,12},{4,8},{8,4},{12,0},{16,28},{20,24},{24,20},{28,16},{1,13},{... | collective-permute-start | bytes 884744 | tf_op jit(solution)/shard_map/ppermute | solution.py:39
  315.7 24.9 %collective-permute-start.45 = (bf16[256,768]{1,0:T(8,128)(2,1)}, bf16[256,768]{1,0:T(8,128)(2,1)}, u32[]{:S(2)}, u32[]{:S(2)}) collective-permute-start(bf16[256,768]{1,0:T(8,128)(2,1)} %add_convert_fusion.2), channel_id=1, source_target_pairs={{0,2},{1,3},{2,0},{3,1},{4,6},{5,7},{6,4},{7,5},{8,10},{9,11},{10,... | collective-permute-start | bytes 1179656 | tf_op jit(solution)/shard_map/ppermute | solution.py:39
  333.9 10.3 %collective-permute-start.55 = (bf16[96,768]{1,0:T(8,128)(2,1)}, bf16[96,768]{1,0:T(8,128)(2,1)}, u32[]{:S(2)}, u32[]{:S(2)}) collective-permute-start(bf16[96,768]{1,0:T(8,128)(2,1)} %get-tuple-element.183), channel_id=1, source_target_pairs={{0,16},{4,20},{8,24},{12,28},{16,0},{20,4},{24,8},{28,12},{1,17},{... | collective-permute-start | bytes 442376 | tf_op jit(solution)/shard_map/ppermute | solution.py:39
  (31 other events, 252.8 us)

commit v4 on v3

--- a/solution.py
+++ b/solution.py
@@ -14,7 +14,12 @@
 excluded = -1e30
 reach = 512
 tile = 128
-params = pltpu.CompilerParams(vmem_limit_bytes=64 * 1024 * 1024)
+
+
+def limit(mebibytes):
+    return pltpu.CompilerParams(vmem_limit_bytes=mebibytes * 1024 * 1024)
+
+
 brief = pl.CostEstimate(flops=10**9, bytes_accessed=10**6, transcendentals=0)
 long = pl.CostEstimate(flops=2 * 10**10, bytes_accessed=10**7, transcendentals=0)
 
@@ -44,7 +49,7 @@
 
 
 def call(
-    kernel, name, operands, outs, scratch=(), scalars=None, after=(), through=()
+    kernel, name, operands, outs, scratch=(), scalars=None, after=(), through=(), room=64
 ):
     operands, outs = list(operands), list(outs)
     in_specs = [whole(o.shape) for o in operands]
@@ -68,7 +73,7 @@
         out_shape=outs + [shape(o.shape, o.dtype) for o in through],
         input_output_aliases={count + i: results + i for i in range(len(through))},
         scratch_shapes=list(scratch),
-        compiler_params=params,
+        compiler_params=limit(room),
         cost_estimate=brief,
     )(*operands, *extra)
 
@@ -412,15 +417,20 @@
     return jnp.concatenate([ref[...] for ref in refs], axis=0)
 
 
-def experts_forward(place, w_in, w_out, w_router, x_blocks, experts, blocks):
+def experts_forward(name, place, w_in, w_out, w_router, x_blocks, experts, before, cost):
     width, units = w_in.shape
     count, size = len(x_blocks), x_blocks[0].shape[0]
     total, piece = size * count, 768
-    each, chunk = total // blocks, min(256, total)
+    chunk = min(256, total)
+    sets = 1 if before is None else 1 + len(before) // 2
+    blocks = 0 if before is None else count
+    before = [] if before is None else list(before)
 
     def kernel(me_ref, w_in_ref, w_out_ref, router_ref, *refs):
-        x_refs, out_refs = refs[:count], refs[count : count + blocks]
-        active_ref, slope_ref, x_all, result_ref, gates_ref, result_sum = refs[count + blocks :]
+        x_refs, refs = refs[:count], refs[count:]
+        before_refs, refs = refs[: len(before)], refs[len(before) :]
+        out_refs = refs[:blocks]
+        active_ref, slope_ref, x_all, result_ref, gates_ref, result_sum = refs[blocks:]
 
         @pl.when(pl.program_id(0) == 0)
         def _():
@@ -445,16 +455,20 @@
         def _():
             result = result_sum[...].astype(bf16)
             result_ref[...] = result
-            gated = (gates_ref[:, 0:1] * result.astype(f32)).astype(bf16)
-            for b, ref in enumerate(out_refs):
-                ref[...] = gated[b * each : (b + 1) * each, :]
+            if blocks:
+                held = [(before_refs[i], before_refs[i + 1]) for i in range(0, len(before), 2)]
+                held.append((result_ref, gates_ref))
+                for at, (rows_ref, gate_ref) in enumerate(held):
+                    gated = (gate_ref[:, 0:1] * rows_ref[...].astype(f32)).astype(bf16)
+                    for b, ref in enumerate(out_refs):
+                        ref[at * size : (at + 1) * size, :] = gated[b * size : (b + 1) * size, :]
 
     columns = pl.BlockSpec((total, piece), lambda i: (0, i))
-    outs = [shape((each, width), bf16)] * blocks
+    outs = [shape((size * sets, width), bf16)] * blocks
     kept = [shape((total, width), bf16)] * 2 + [shape((total, 128), f32)]
     flat = pl.pallas_call(
         kernel,
-        name="experts_forward",
+        name=name,
         grid=(units // piece,),
         in_specs=[
             pl.BlockSpec(memory_space=pltpu.SMEM),
@@ -462,60 +476,75 @@
             pl.BlockSpec((piece, width), lambda i: (i, 0)),
             whole(w_router.shape),
         ]
-        + [whole(o.shape) for o in x_blocks],
+        + [whole(o.shape) for o in x_blocks]
+        + [whole(o.shape) for o in before],
         out_specs=[whole(o.shape) for o in outs]
         + [columns] * 2
         + [whole(o.shape) for o in kept],
         out_shape=outs + [shape((total, units), bf16)] * 2 + kept,
         scratch_shapes=[pltpu.VMEM((total, width), f32)],
-        compiler_params=params,
-        cost_estimate=brief,
-    )(place, w_in, w_out, w_router, *x_blocks)
-    return (flat[:blocks], *flat[blocks:])
-
-
-def experts_backward(place, w_in, w_out, slope, result, gates, g_blocks, count):
+        compiler_params=limit(64),
+        cost_estimate=cost,
+    )(place, w_in, w_out, w_router, *x_blocks, *before)
+    return (list(flat[:blocks]), *flat[blocks:])
+
+
+def experts_backward(name, place, w_in, w_out, sets, at_set, slot_grad, g_blocks, count, cost):
     width, units = w_in.shape
+    slope, result, _ = sets[at_set]
     total, piece = slope.shape[0], 768
     size, chunk = total // count, min(256, total)
-
-    def kernel(me_ref, w_in_ref, w_out_ref, slope_ref, result_ref, gates_ref, *refs):
-        g_refs, back_refs = refs[: len(g_blocks)], refs[len(g_blocks) : len(g_blocks) + count]
-        pre_grad_ref, s_all, back_sum = refs[len(g_blocks) + count :]
+    number = len(sets)
+    first = slot_grad is None
+    given = [gates for _, _, gates in sets] if first else [slot_grad]
+    made = number if first else 0
+
+    def kernel(me_ref, w_in_ref, w_out_ref, slope_ref, result_ref, *refs):
+        given_refs, refs = refs[: len(given)], refs[len(given) :]
+        g_refs, refs = refs[: len(g_blocks)], refs[len(g_blocks) :]
+        back_refs, refs = refs[:count], refs[count:]
+        s_refs, pre_grad_ref, back_sum = refs[:made], refs[made], refs[made + 1]
+        s_ref = s_refs[at_set] if first else given_refs[0]
 
         @pl.when(pl.program_id(0) == 0)
         def _():
-            s_all[...] = (gates_ref[:, 0:1] * join_rows(g_refs).astype(f32)).astype(bf16)
             back_sum[...] = jnp.zeros_like(back_sum)
+            if first:
+                for at in range(number):
+                    for b, ref in enumerate(g_refs):
+                        rows = slice(b * size, (b + 1) * size)
+                        grad = ref[at * size : (at + 1) * size, :].astype(f32)
+                        s_refs[at][rows, :] = (given_refs[at][rows, 0:1] * grad).astype(bf16)
 
         for c in range(total // chunk):
             at = slice(c * chunk, (c + 1) * chunk)
-            active_grad = dot(s_all[at, :], w_out_ref[...], 1, 1)
+            active_grad = dot(s_ref[at, :], w_out_ref[...], 1, 1)
             pre_grad = (active_grad * slope_ref[at, :].astype(f32)).astype(bf16)
             pre_grad_ref[at, :] = pre_grad
             back_sum[at, :] += dot(pre_grad, w_in_ref[...], 1, 1)
 
         @pl.when(pl.program_id(0) == pl.num_programs(0) - 1)
         def _():
-            products = join_rows(g_refs).astype(f32) * result_ref[...].astype(f32)
-            gate_grad = jnp.sum(products, axis=1, keepdims=True)
-            upper = gate_grad.astype(bf16).astype(f32)
-            lane = lax.broadcasted_iota(jnp.int32, (total, 128), 1)
-            columns = jnp.where(
-                lane == me_ref[0],
-                upper,
-                jnp.where(lane == me_ref[0] + 64, gate_grad - upper, 0.0),
-            ).astype(bf16)
-            back = back_sum[...].astype(bf16)
-            for b, ref in enumerate(back_refs):
-                ref[:, :width] = back[b * size : (b + 1) * size, :]
-                ref[:, width:] = columns[b * size : (b + 1) * size, :]
+            lane = lax.broadcasted_iota(jnp.int32, (size, 128), 1)
+            for b, (ref, g_ref) in enumerate(zip(back_refs, g_refs)):
+                rows = slice(b * size, (b + 1) * size)
+                grad = g_ref[at_set * size : (at_set + 1) * size, :].astype(f32)
+                gate_grad = jnp.sum(
+                    grad * result_ref[rows, :].astype(f32), axis=1, keepdims=True
+                )
+                upper = gate_grad.astype(bf16).astype(f32)
+                ref[:, :width] = back_sum[rows, :].astype(bf16)
+                ref[:, width:] = jnp.where(
+                    lane == me_ref[0],
+                    upper,
+                    jnp.where(lane == me_ref[0] + 64, gate_grad - upper, 0.0),
+                ).astype(bf16)
 
     by_units = pl.BlockSpec((total, piece), lambda i: (0, i))
-    outs = [shape((size, width + 128), bf16)] * count
+    outs = [shape((size, width + 128), bf16)] * count + [shape((total, width), bf16)] * made
     flat = pl.pallas_call(
         kernel,
-        name="experts_backward",
+        name=name,
         grid=(units // piece,),
         in_specs=[
             pl.BlockSpec(memory_space=pltpu.SMEM),
@@ -523,16 +552,16 @@
             pl.BlockSpec((piece, width), lambda i: (i, 0)),
             by_units,
             whole(result.shape),
-            whole(gates.shape),
         ]
+        + [whole(o.shape) for o in given]
         + [whole(o.shape) for o in g_blocks],
-        out_specs=[whole(o.shape) for o in outs] + [by_units, whole((total, width))],
-        out_shape=outs + [shape((total, units), bf16), shape((total, width), bf16)],
+        out_specs=[whole(o.shape) for o in outs] + [by_units],
+        out_shape=outs + [shape((total, units), bf16)],
         scratch_shapes=[pltpu.VMEM((total, width), f32)],
-        compiler_params=params,
-        cost_estimate=brief,
-    )(place, w_in, w_out, slope, result, gates, *g_blocks)
-    return (flat[:count], *flat[count:])
+        compiler_params=limit(64),
+        cost_estimate=cost,
+    )(place, w_in, w_out, slope, result, *given, *g_blocks)
+    return list(flat[:count]), list(flat[count : count + made]), flat[-1]
 
 
 def home(
@@ -621,45 +650,96 @@
     )
 
 
-def expert_weight_grads(name, place, fixed, cut, cut_left, members):
-    total, width = fixed.shape
-    piece = cut.shape[1] // members
-    dims = (piece, width) if cut_left else (width, piece)
-
-    def kernel(place_ref, fixed_ref, cut_ref, near_ref, base_ref):
-        pair = (cut_ref, fixed_ref) if cut_left else (fixed_ref, cut_ref)
-        part = dot(pair[0][...], pair[1][...], 0, 0)
-
-        @pl.when(pl.program_id(0) < 2)
+def expert_weight_grads(place, rows_in, pre_grads, actives, slot_grads, members):
+    sets = len(rows_in)
+    total, width = rows_in[0].shape
+    piece = pre_grads[0].shape[1] // members
+
+    def kernel(place_ref, *refs):
+        x_refs, p_refs, a_refs, s_refs = [refs[i * sets : (i + 1) * sets] for i in range(4)]
+        near_ref, base_ref, out = refs[4 * sets :]
+        step = pl.program_id(0)
+
+        def total_of(lefts, rights):
+            held = dot(lefts[0][...], rights[0][...], 0, 0)
+            for left, right in zip(lefts[1:], rights[1:]):
+                held = held + dot(left[...], right[...], 0, 0)
+            return held
+
+        @pl.when(step < 4)
         def _():
-            near_ref[...] = part.astype(bf16)
-
-        @pl.when(pl.program_id(0) >= 2)
+            out[...] = total_of(x_refs, p_refs)
+
+        @pl.when(step >= 4)
         def _():
-            base_ref[...] = part
-
-    def cut_map(i, place_ref):
-        return (0, place_ref[1] ^ jnp.where(i < 2, 2 * i + 1, 2 * i - 4))
-
+            out[...] = total_of(a_refs, s_refs)
+
+        @pl.when(step % 4 < 2)
+        def _():
+            near_ref[...] = out[...].astype(bf16)
+
+        @pl.when(step % 4 >= 2)
+        def _():
+            base_ref[...] = out[...]
+
+    def partner(i):
+        return jnp.where(i < 2, 2 * i + 1, 2 * i - 4)
+
+    fixed = pl.BlockSpec((total, width), lambda i, p: (0, 0))
+    pre_cut = pl.BlockSpec((total, piece), lambda i, p: (0, p[1] ^ partner(jnp.minimum(i, 3))))
+    act_cut = pl.BlockSpec((total, piece), lambda i, p: (0, p[1] ^ partner(jnp.maximum(i - 4, 0))))
     return pl.pallas_call(
         kernel,
-        name=name,
+        name="expert_weight_grads",
         grid_spec=pltpu.PrefetchScalarGridSpec(
             num_scalar_prefetch=1,
-            grid=(4,),
-            in_specs=[
-                pl.BlockSpec((total, width), lambda i, p: (0, 0)),
-                pl.BlockSpec((total, piece), cut_map),
+            grid=(8,),
+            in_specs=[fixed] * sets + [pre_cut] * sets + [act_cut] * sets + [fixed] * sets,
+            out_specs=[
+                pl.BlockSpec(
+                    (piece, width), lambda i, p: (2 * (i // 4) + jnp.minimum(i % 4, 1), 0)
+                ),
+                pl.BlockSpec(
+                    (piece, width), lambda i, p: (2 * (i // 4) + jnp.maximum(i % 4 - 2, 0), 0)
+                ),
             ],
-            out_specs=[
-                pl.BlockSpec(dims, lambda i, p: (jnp.minimum(i, 1), 0)),
-                pl.BlockSpec(dims, lambda i, p: (jnp.maximum(i - 2, 0), 0)),
-            ],
+            scratch_shapes=[pltpu.VMEM((piece, width), f32)],
         ),
-        out_shape=[shape((2 * dims[0], dims[1]), bf16), shape((2 * dims[0], dims[1]), f32)],
-        compiler_params=params,
+        out_shape=[shape((4 * piece, width), bf16), shape((4 * piece, width), f32)],
+        compiler_params=limit(64),
         cost_estimate=long,
-    )(place, fixed, cut)
+    )(place, *rows_in, *pre_grads, *actives, *slot_grads)
+
+
+def far_sums(near, base, cut, after, through):
+    size, width = base.shape[0] // 4, base.shape[1]
+    count = len(through)
+
+    def block(at):
+        return pl.BlockSpec(
+            (size, width), lambda *_: (2 * at + 1, 0), pipeline_mode=pl.Buffered(1)
+        )
+
+    def kernel(near_in, near_out, base_in, base_out, *refs):
+        first_ref, rest_ref = refs[count + len(after) : count + len(after) + 2]
+        held = (base_in[...] + near_in[...].astype(f32)).astype(bf16)
+        first_ref[...] = held[:cut, :]
+        rest_ref[: size - cut, :] = held[cut:, :]
+        rest_ref[size - cut :, :] = (base_out[...] + near_out[...].astype(f32)).astype(bf16)
+
+    anywhere = pl.BlockSpec(memory_space=pl.ANY)
+    return pl.pallas_call(
+        kernel,
+        name="far_sums",
+        grid=(1,),
+        in_specs=[block(0), block(1), block(0), block(1)] + [anywhere] * (count + len(after)),
+        out_specs=[whole((cut, width)), whole((2 * size - cut, width))] + [anywhere] * count,
+        out_shape=[shape((cut, width), bf16), shape((2 * size - cut, width), bf16)]
+        + [shape(o.shape, o.dtype) for o in through],
+        input_output_aliases={4 + i: 2 + i for i in range(count)},
+        compiler_params=limit(64),
+        cost_estimate=brief,
+    )(near, near, base, base, *through, *after)
 
 
 def input_grads(
@@ -746,7 +826,7 @@
     )
 
 
-def fold_weights(base, arrived, after):
+def fold_weights(base, arrived, after, through):
     part, width = base.shape[0] // 2, base.shape[1]
 
     def kernel(base_ref, *refs):
@@ -763,6 +843,7 @@
         [base] + arrived,
         [shape((part, width), f32), shape((part, width), bf16)],
         after=after,
+        through=through,
     )
 
 
@@ -791,23 +872,11 @@
     return [values, swap(values, "mp", 1), across, swap(across, "mp", 1)]
 
 
-def scatter_near(near, base, axis):
-    size = base.shape[axis] // 2
-    near = swap(near, "mp", 1)
-    own, far = [
-        lax.slice_in_dim(base, i * size, (i + 1) * size, axis=axis)
-        + lax.slice_in_dim(near, i * size, (i + 1) * size, axis=axis).astype(f32)
-        for i in (0, 1)
-    ]
-    return own, far.astype(bf16)
-
-
-def sum_all(values):
-    for axis in ("mp", "dp"):
-        step = 1
-        while step < lax.axis_size(axis):
-            values = values + swap(values, axis, step)
-            step = 2 * step
+def sum_over(values, axis):
+    step = 1
+    while step < lax.axis_size(axis):
+        values = values + swap(values, axis, step)
+        step = 2 * step
     return values
 
 
@@ -869,7 +938,6 @@
     normed, query, key_rows, value_rows, weight_q, weight_k, weight_v, w_o = project(
         place, token_blocks, pack_blocks, gain_one, span
     )
-    weight_o = gather_mp(w_o)
 
     if few:
         blocks, size = 4, capacity
@@ -903,6 +971,7 @@
     mixed_out = attend(
         place, query, key_rows, value_rows, seg_q, seg_k, line, heads, members, held[:1]
     )
+    weight_o = gather_mp(w_o)
     mixed_in = [mixed_out[0]] + [swap(mixed_out[r], "mp", r) for r in range(1, members)]
 
     router_wide = jnp.pad(w_router, ((0, 0), (0, 128 - experts)))
@@ -926,50 +995,67 @@
         )
         g_blocks = [held[0]] + [swap(far[blocks + r - 1], "dp", r) for r in (1, 2, 3)]
         far = [far[0]] + [swap(far[r], "dp", r) for r in (1, 2, 3)]
-        x_blocks = [item for pair in zip(own, far) for item in pair]
+        x_sets = [own, far]
     else:
-        x_blocks = [all_to_all_dp(send[0])]
+        x_sets = [[all_to_all_dp(send[0])]]
         g_blocks = [all_to_all_dp(held[0])]
 
-    result, active, slope, arrived, plain_result, slot_gates = experts_forward(
-        place, w_in[0], w_out[0], router_wide, x_blocks, experts, blocks
-    )
-    back, pre_grad, slot_grad = experts_backward(
-        place, w_in[0], w_out[0], slope, plain_result, slot_gates, g_blocks, len(x_blocks)
-    )
-    near_in, base_in = expert_weight_grads(
-        "w_in_grads", place, arrived, pre_grad, False, members
-    )
-    near_out, base_out = expert_weight_grads(
-        "w_out_grads", place, slot_grad, active, True, members
-    )
+    kept, before = [], []
+    for at, x_blocks in enumerate(x_sets):
+        last = at == len(x_sets) - 1
+        result, *held = experts_forward(
+            "experts_forward" + str(at),
+            place,
+            w_in[0],
+            w_out[0],
+            router_wide,
+            x_blocks,
+            experts,
+            before if last else None,
+            brief if last else long,
+        )
+        kept.append(held)
+        before = before + held[3:]
+    actives, slopes, arrived, plain, slot_gates = zip(*kept)
+    sets = list(zip(slopes, plain, slot_gates))
+    back, slot_grads, pre_grad = experts_backward(
+        "experts_backward" + str(len(sets) - 1),
+        place,
+        w_in[0],
+        w_out[0],
+        sets,
+        len(sets) - 1,
+        None,
+        g_blocks,
+        blocks,
+        brief,
+    )
+    pre_grads = [pre_grad]
     if few:
-        result_in = [result[0]] + [swap(result[r], "dp", r) for r in (1, 2, 3)]
-        own_result, far_result = from_slots(
-            "result_from_slots", result_in, slots, size, [f32, bf16]
+        own_back, _, pre_grad = experts_backward(
+            "experts_backward0",
+            place,
+            w_in[0],
+            w_out[0],
+            sets,
+            0,
+            slot_grads[0],
+            g_blocks,
+            blocks,
+            long,
         )
-        far_result = swap(far_result, "dp", 4)
-        far_back = [back[1]] + [swap(back[2 * r + 1], "dp", r) for r in (1, 2, 3)]
-        far_total, *own_back = from_slots(
-            "back_from_slots",
-            far_back,
-            [slots[1]],
-            size,
-            [bf16],
-            after=[own_result],
-            through=list(back[2::2]) + [near_in],
+        pre_grads = [pre_grad] + pre_grads
+        far_back = [back[0]] + [swap(back[r], "dp", r) for r in (1, 2, 3)]
+        far_total, *passed = from_slots(
+            "back_from_slots", far_back, [slots[1]], size, [bf16], through=own_back[1:]
         )
-        near_in = own_back.pop()
         far_sum = swap(far_total, "dp", 4)
-        own_back = [back[0]] + [swap(own_back[r - 1], "dp", r) for r in (1, 2, 3)]
+        own_back = [own_back[0]] + [swap(passed[r - 1], "dp", r) for r in (1, 2, 3)]
     else:
-        (own_result,) = from_slots(
-            "result_from_slots", [all_to_all_dp(result[0])], slots, size, [f32]
-        )
         own_back, far_sum = [all_to_all_dp(back[0])], None
-    own_in, far_in = scatter_near(near_in, base_in, 0)
-
-    *grad_out, hidden_grad, ffn_gain_grad, router_grad, near_o, base_o, near_out = home(
+    near_w, base_w = expert_weight_grads(place, arrived, pre_grads, actives, slot_grads, members)
+
+    homed = home(
         own_back,
         far_sum,
         slots[0],
@@ -983,12 +1069,20 @@
         mixed_in,
         size,
         experts,
-        [far_in],
-        [near_out],
-    )
+        [],
+        [near_w],
+    )
+    grad_out, homed = homed[:members], homed[members:]
+    hidden_grad, ffn_gain_grad, router_grad, near_o, base_o, near_w = homed
     grad_in = [grad_out[0]] + [swap(grad_out[r], "mp", r) for r in range(1, members)]
-    own_out, far_out = scatter_near(near_out, base_out, 0)
-    own_o, far_o = scatter_near(near_o, base_o, 1)
+    near_o = swap(near_o, "mp", 1)
+    sum_o = base_o + near_o.astype(f32)
+    output_sum = sum_o[:, :span] + swap(sum_o[:, span:].astype(bf16), "mp", 2).astype(f32)
+    near_w = swap(near_w, "mp", 1)
+    far_first, far_rest, *passed = far_sums(
+        near_w, base_w, 2 * rows, grad_in[1:] + [output_sum], result[1:]
+    )
+    result = result[:1] + passed
 
     *proj_grads, line_grad = attend_back(
         place,
@@ -1000,11 +1094,14 @@
         line,
         grad_in,
         heads,
-        [far_out],
-    )
-    output_sum = own_o + swap(far_o, "mp", 2).astype(f32)
-    far_in = swap(far_in, "mp", 2)
-    far_out = swap(far_out, "mp", 2)
+        [far_first],
+    )
+    far_first = swap(far_first, "mp", 2)
+    far_rest = swap(far_rest, "mp", 2)
+    if few:
+        result_in = [result[0]] + [swap(result[r], "dp", r) for r in (1, 2, 3)]
+    else:
+        result_in = [all_to_all_dp(result[0])]
     near, base, base_far, small, *weight_sums = input_grads(
         place,
         proj_grads,
@@ -1019,11 +1116,13 @@
         members,
         owners,
         heads,
-        [far_in],
+        [far_first] + result_in[1:],
     )
     if few:
         arrived_sums = [swap(weight_sums[r], "dp", r) for r in (1, 2, 3)]
-        own_sum, far_part = fold_weights(weight_sums[0], arrived_sums, [far_out])
+        own_sum, far_part, small = fold_weights(
+            weight_sums[0], arrived_sums, [], [small]
+        )
         weight_grads = split_weights([own_sum, swap(far_part, "dp", 4)], span)
     else:
         joined_grad = lax.psum_scatter(weight_sums[0], "dp", scatter_dimension=0, tiled=True)
@@ -1039,13 +1138,23 @@
         hidden_grad + inverse_one * scaled - resid * inverse_one * inverse_one * inverse_one * inner
     ).astype(bf16)
 
-    block_out = hidden + own_result
     if few:
-        block_out = block_out + far_result.astype(f32)
+        own_result, far_result = from_slots(
+            "result_from_slots", result_in, slots, size, [f32, bf16], after=[own_sum]
+        )
+        block_out = hidden + own_result + swap(far_result, "dp", 4).astype(f32)
+    else:
+        (own_result,) = from_slots("result_from_slots", result_in, slots, size, [f32])
+        block_out = hidden + own_result
     block_out = block_out.astype(bf16)
-    w_in_grad = own_in + far_in.astype(f32)
-    w_out_grad = own_out + far_out.astype(f32)
-    small = sum_all(small)
+    piece = w_in.shape[2] // members
+    own_w = base_w[:piece] + near_w[:piece].astype(f32)
+    w_in_grad = own_w + jnp.concatenate(
+        [far_first, far_rest[: piece - far_first.shape[0]]], axis=0
+    ).astype(f32)
+    own_w = base_w[2 * piece : 3 * piece] + near_w[2 * piece : 3 * piece].astype(f32)
+    w_out_grad = own_w + far_rest[piece - far_first.shape[0] :].astype(f32)
+    small = sum_over(sum_over(small, "mp"), "dp")
     return (
         block_out,
         tokens_grad,

time: 347 us -> 355 us (1.023)
  Pallas kernels: 129 us -> 143 us
  other arithmetic: 29.8 us -> 24 us
    pallas_call x4 -> x6, Pallas kernels: 59.8 us -> 73.7 us  [the longest x2 24.8 us: experts_forward(): pl.pallas_call(kernel, name=name, grid=(units // piece,), in_specs=[pl.Bl...]
    convert_element_type x3 -> x0, other arithmetic: 8.59 us -> none  [scatter_near(): return (own, far.astype(bf16))]
    add x6 -> x7, other arithmetic: 1.97 us -> 6.36 us  [the longest x5 4.03 us: sum_over(): values = values + swap(values, axis, step)]
    broadcast_in_dim x1 -> x0, other arithmetic: 4.05 us -> none  [on_device(): w_in_grad[None]]
    ppermute x56 -> x55, starting transfers between devices: 52.5 us -> 55.1 us  [swap(): return lax.ppermute(values, axis, [(i, i ^ step) for i in range(count)])]
    ppermute x56 -> x55, waiting for transfers between devices: 114 us -> 112 us  [swap(): return lax.ppermute(values, axis, [(i, i ^ step) for i in range(count)])]
  transfers between devices with their start and end apart: 56 -> 55, of which waited for: 23 -> 19; matrix products, arithmetic and copies ran while one was open for 13% -> 11% of each run, Pallas kernels for 33% -> 30%
where the time goes in v4:
time: 355 us; the launch traced here: 353 us
  Pallas kernels  143 us (40%)
  waiting for transfers between devices  112 us (32%)
  starting transfers between devices  55.1 us (16%)
  other arithmetic  24 us (7%)
  local copies, waits for them, and re-layouts  15.6 us (4%)
    ppermute x55, waiting for transfers between devices, swap(): return lax.ppermute(values, axis, [(i, i ^ step) for i in range(count)])  112 us
    pallas_call x14, Pallas kernels, call(): pl.pallas_call(body, name=name, grid=(1,), in_specs=in_specs + [pl.BlockS...  68.9 us
    ppermute x55, starting transfers between devices, swap(): return lax.ppermute(values, axis, [(i, i ^ step) for i in range(count)])  55.1 us
    pallas_call x2, Pallas kernels, experts_forward(): pl.pallas_call(kernel, name=name, grid=(units // piece,), in_specs=[pl.Bl...  24.8 us
    pallas_call x2, Pallas kernels, experts_backward(): pl.pallas_call(kernel, name=name, grid=(units // piece,), in_specs=[pl.Bl...  24.4 us
    pallas_call x1, Pallas kernels, expert_weight_grads(): pl.pallas_call(kernel, name='expert_weight_grads', grid_spec=pltpu.Prefet...  19.8 us
  transfers between devices with their start and end apart: 55, of which 19 were waited for; matrix products, arithmetic and copies ran while one was open for 11% of the time, Pallas kernels for 30%

profile of v4, /device:TPU:0, one launch (start us, length us, event | category | flops | bytes accessed | tf_op | source)
XLA Modules:
  0.0 353.1 jit_solution(5955683189550926587)
XLA Ops:
  1.2 2.6 collective-permute-start.1
  5.5 2.6 collective-permute-start.3
  13.8 2.0 collective-permute-done.3.refs_1_
  15.8 1.7 pair_up.1.refs_6_
  27.2 2.1 collective-permute-start.7
  30.6 8.3 %collective-permute-done.6.refs_9_ = bf16[192,768]{1,0:T(8,128)(2,1)} collective-permute-done((bf16[192,768]{1,0:T(8,128)(2,1)}, bf16[192,768]{1,0:T(8,128)(2,1)}, u32[]{:S(2)}, u32[]{:S(2)}) %collective-permute-start.6) | collective-permute-done | bytes 294944 | tf_op jit(solution)/shard_map/ppermute | solution.py:44
  38.9 5.2 %project.1 = (bf16[1024,768]{1,0:T(8,128)(2,1)}, bf16[1024,192]{1,0:T(8,128)(2,1)}, bf16[1024,192]{1,0:T(8,128)(2,1)}, bf16[1024,192]{1,0:T(8,128)(2,1)}, bf16[7...) custom-call(s32[2]{0:T(128)} %pad_add_fusion.2.refs_0_.me_ref.place_ref, ...), custom_call_target="tpu_custom_call" | custom-call | flops 1000000000 | bytes 1000000 | tf_op jit(solution)/shard_map/project/pallas_call | solution.py:67
  46.7 4.4 %collective-permute-done.13.refs_10_.refs_14_ = bf16[192,768]{1,0:T(8,128)(2,1)} collective-permute-done((bf16[192,768]{1,0:T(8,128)(2,1)}, bf16[192,768]{1,0:T(8,128)(2,1)}, u32[]{:S(2)}, u32[]{:S(2)}) %collective-permute-start.13) | collective-permute-done | bytes 294944 | tf_op jit(solution)/shard_map/ppermute | solution.py:44
  51.7 2.8 grads_to_slots.1
  54.5 11.5 %attend.1 = (bf16[256,192]{1,0:T(8,128)(2,1)}, bf16[256,192]{1,0:T(8,128)(2,1)}, bf16[256,192]{1,0:T(8,128)(2,1)}, bf16[256,192]{1,0:T(8,128)(2,1)}) custom-call(s32[2]{0:T(128)} %pad_add_fusion.2.refs_0_.me_ref.place_ref, bf16[1024,192]{1,0:T(8,128)(2,1)} %get-tuple-element.110.refs_4_.refs_1_, bf16[1024,192]{1,0:T(8,128)(2,1)} %get-tuple-element.111.refs_2_, ...), custom_call_target="tpu_custom_call" | custom-call | flops 1000000000 | bytes 1000000 | tf_op jit(solution)/shard_map/attend/pallas_call | solution.py:67
  71.1 2.0 collective-permute-done.10.refs_6_.refs_18_
  74.4 3.8 %middle.1 = (f32[256,768]{1,0:T(8,128)}, bf16[256,768]{1,0:T(8,128)(2,1)}, f32[256,128]{1,0:T(8,128)}, bf16[128,768]{1,0:T(8,128)(2,1)}, bf16[128,768]{1,0:T(8,1...) custom-call(bf16[256,768]{1,0:T(8,128)(2,1)} %refs_0_.5, f32[1,768]{1,0:T(1,128)} %reshape.191.refs_1_.refs_4_, ...), custom_call_target="tpu_custom_call" | custom-call | flops 1000000000 | bytes 1000000 | tf_op jit(solution)/shard_map/middle/pallas_call | solution.py:67
  80.9 2.3 collective-permute-start.20
  83.2 16.4 %collective-permute-done.15.refs_0_ = bf16[256,768]{1,0:T(8,128)(2,1)} collective-permute-done((bf16[256,768]{1,0:T(8,128)(2,1)}, bf16[256,768]{1,0:T(8,128)(2,1)}, u32[]{:S(2)}, u32[]{:S(2)}) %collective-permute-start.15) | collective-permute-done | bytes 393248 | tf_op jit(solution)/shard_map/ppermute | solution.py:44
  99.6 2.1 far_to_slots.1
  101.7 1.9 collective-permute-start.16
  105.2 1.9 collective-permute-start.22
  107.1 3.4 collective-permute-done.16.refs_1_
  110.5 11.8 %experts_forward0.1 = (bf16[512,3072]{1,0:T(8,128)(2,1)}, bf16[512,3072]{1,0:T(8,128)(2,1)}, bf16[512,768]{1,0:T(8,128)(2,1)}, bf16[512,768]{1,0:T(8,128)(2,1)}, f32[512,128]{1,0:T(8,128)}) custom-call(s32[2]{0:T(128)} %pad_add_fusion.2.refs_0_.me_ref.place_ref, bf16[768,3072]{1,0:T(8,128)(2,1)} %bitcast.48, bf16[3072,768]{1,0:T(8,128)(2,1)} %bitcast.52, ...), custom_call_target="tpu_custom_call" | custom-call | flops 20000000000 | bytes 10000000 | tf_op jit(solution)/shard_map/experts_forward0/pallas_call | solution.py:469
  122.3 13.0 %experts_forward1.1 = (bf16[256,768]{1,0:T(8,128)(2,1)}, bf16[256,768]{1,0:T(8,128)(2,1)}, bf16[256,768]{1,0:T(8,128)(2,1)}, bf16[256,768]{1,0:T(8,128)(2,1)}, b...) custom-call(s32[2]{0:T(128)} %pad_add_fusion.2.refs_0_.me_ref.place_, ...), custom_call_target="tpu_custom_call" | custom-call | flops 1000000000 | bytes 1000000 | tf_op jit(solution)/shard_map/experts_forward1/pallas_call | solution.py:469
  135.4 12.6 %experts_backward1.1 = (bf16[128,896]{1,0:T(8,128)(2,1)}, bf16[128,896]{1,0:T(8,128)(2,1)}, bf16[128,896]{1,0:T(8,128)(2,1)}, bf16[128,896]{1,0:T(8,128)(2,1)}, ...) custom-call(s32[2]{0:T(128)} %pad_add_fusion.2.refs_0_.me_ref.place_ref, ...), custom_call_target="tpu_custom_call" | custom-call | flops 1000000000 | bytes 1000000 | tf_op jit(solution)/shard_map/experts_backward1/pallas_call | solution.py:545
  147.9 2.2 collective-permute-start.25
  153.1 11.8 %experts_backward0.1 = (bf16[128,896]{1,0:T(8,128)(2,1)}, bf16[128,896]{1,0:T(8,128)(2,1)}, bf16[128,896]{1,0:T(8,128)(2,1)}, bf16[128,896]{1,0:T(8,128)(2,1)}, bf16[512,3072]{1,0:T(8,128)(2,1)}) custom-call(s32[2]{0:T(128)} %pad_add_fusion.2.refs_0_.me_ref.place_ref, bf16[768,3072]{1,0:T(8,128)(2,1)} %bitcast.51, bf16[3072,768]{1,0:T(8,128)(2,1)} %bitcast.55, ...), custom_call_target="tpu_custom_call" | custom-call | flops 20000000000 | bytes 10000000 | tf_op jit(solution)/shard_map/experts_backward0/pallas_call | solution.py:545
  164.9 2.7 back_from_slots.1
  171.1 2.5 collective-permute-start.31
  173.6 19.8 %expert_weight_grads.1 = (bf16[3072,768]{1,0:T(8,128)(2,1)}, f32[3072,768]{1,0:T(8,128)}) custom-call(s32[2]{0:T(128)} %pad_add_fusion.2.refs_0_.me_ref.place_ref, bf16[512,768]{1,0:T(8,128)(2,1)} %get-tuple-element.156.refs_0_, bf16[512,768]{1,0:T(8,128)(2,1)} %get-tuple-element.157.refs_1_, bf16[512,3072]{1,0:T(8,128)(2,1)} %get-tuple-element.158.refs_2_, ...), custom_call_target="tpu_custom_call" | custom-call | flops 20000000000 | bytes 10000000 | tf_op jit(solution)/shard_map/expert_weight_grads/pallas_call | solution.py:691
  193.5 7.2 %home.1 = (bf16[256,192]{1,0:T(8,128)(2,1)}, bf16[256,192]{1,0:T(8,128)(2,1)}, bf16[256,192]{1,0:T(8,128)(2,1)}, bf16[256,192]{1,0:T(8,128)(2,1)}, f32[256,768]{...) custom-call(s32[8,256]{1,0:T(8,128)} %pad.24.refs_1_.refs_3_.refs_0_, ...), custom_call_target="tpu_custom_call", output_to_operand_aliasing={{9}: (20, {})} | custom-call | flops 1000000000 | bytes 1000000 | tf_op jit(solution)/shard_map/home/pallas_call | solution.py:67
  201.3 7.2 %collective-permute-done.36 = bf16[768,384]{1,0:T(8,128)(2,1)S(1)} collective-permute-done((bf16[768,384]{1,0:T(8,128)(2,1)}, bf16[768,384]{1,0:T(8,128)(2,1)S(1)}, u32[]{:S(2)}, u32[]{:S(2)}) %collective-permute-start.36) | collective-permute-done | bytes 589856 | tf_op jit(solution)/shard_map/ppermute | solution.py:44
  213.4 8.7 %collective-permute-done.37 = bf16[768,192]{1,0:T(8,128)(2,1)S(1)} collective-permute-done((bf16[768,192]{1,0:T(8,128)(2,1)S(1)}, bf16[768,192]{1,0:T(8,128)(2,1)S(1)}, u32[]{:S(2)}, u32[]{:S(2)}) %collective-permute-start.37) | collective-permute-done | bytes 294944 | tf_op jit(solution)/shard_map/ppermute | solution.py:44
  223.1 2.0 collective-permute-done.34.refs_4_.refs_9_
  226.7 4.6 %far_sums.1 = (bf16[512,768]{1,0:T(8,128)(2,1)}, bf16[1024,768]{1,0:T(8,128)(2,1)}, bf16[256,768]{1,0:T(8,128)(2,1)}, bf16[256,768]{1,0:T(8,128)(2,1)}, bf16[256,768]{1,0:T(8,128)(2,1)}) custom-call(bf16[3072,768]{1,0:T(8,128)(2,1)} %collective-permute-done.32.near_in.near_out, ...), custom_call_target="tpu_custom_call", output_to_operand_aliasing={{2}: (4, {}), {3}: (5, {}), {4}: (6, {})} | custom-call | flops 1000000000 | bytes 1000000 | tf_op jit(solution)/shard_map/far_sums/pallas_call | solution.py:731
  233.5 2.7 collective-permute-start.40
  237.8 16.1 %attend_back.1 = (bf16[1024,192]{1,0:T(8,128)(2,1)}, bf16[1024,192]{1,0:T(8,128)(2,1)}, bf16[1024,192]{1,0:T(8,128)(2,1)}, f32[8,640]{1,0:T(8,128)}) custom-call(s32[2]{0:T(128)} %pad_add_fusion.2.refs_0_.me_ref.place_ref, bf16[1024,192]{1,0:T(8,128)(2,1)} %get-tuple-element.110.refs_4_.refs_1_, bf16[1024,192]{1,0:T(8,128)(2,1)} %get-tuple-element.111.refs_2_, ...), custom_call_target="tpu_custom_call" | custom-call | flops 1000000000 | bytes 1000000 | tf_op jit(solution)/shard_map/attend_back/pallas_call | solution.py:67
  253.9 6.6 %input_grads.1 = (bf16[512,768]{1,0:T(8,128)(2,1)}, f32[256,768]{1,0:T(8,128)}, f32[256,768]{1,0:T(8,128)}, f32[24,768]{1,0:T(8,128)}, f32[192,768]{1,0:T(8,128)...) custom-call(s32[2]{0:T(128)} %pad_add_fusion.2.refs_0_.me_ref.place_ref, ...), custom_call_target="tpu_custom_call" | custom-call | flops 1000000000 | bytes 1000000 | tf_op jit(solution)/shard_map/input_grads/pallas_call | solution.py:67
  261.4 2.7 collective-permute-start.44
  264.8 5.2 %collective-permute-done.42.refs_1_ = bf16[192,768]{1,0:T(8,128)(2,1)} collective-permute-done((bf16[192,768]{1,0:T(8,128)(2,1)}, bf16[192,768]{1,0:T(8,128)(2,1)}, u32[]{:S(2)}, u32[]{:S(2)}) %collective-permute-start.42) | collective-permute-done | bytes 294944 | tf_op jit(solution)/shard_map/ppermute | solution.py:44
  270.9 5.6 %collective-permute-done.44.refs_3_ = bf16[192,768]{1,0:T(8,128)(2,1)} collective-permute-done((bf16[192,768]{1,0:T(8,128)(2,1)}, bf16[192,768]{1,0:T(8,128)(2,1)}, u32[]{:S(2)}, u32[]{:S(2)}) %collective-permute-start.44) | collective-permute-done | bytes 294944 | tf_op jit(solution)/shard_map/ppermute | solution.py:44
  276.6 2.1 fold_weights.1
  281.9 18.7 %collective-permute-done.49 = f32[24,768]{1,0:T(8,128)S(1)} collective-permute-done((f32[24,768]{1,0:T(8,128)S(1)}, f32[24,768]{1,0:T(8,128)S(1)}, u32[]{:S(2)}, u32[]{:S(2)}) %collective-permute-start.49) | collective-permute-done | bytes 73760 | tf_op jit(solution)/shard_map/ppermute | solution.py:44
  301.7 3.3 collective-permute-done.50
  305.9 3.4 result_from_slots.1
  309.3 2.0 collective-permute-start.45
  313.8 1.8 split_weights.1
  315.6 15.7 %collective-permute-done.52 = f32[24,768]{1,0:T(8,128)} collective-permute-done((f32[24,768]{1,0:T(8,128)}, f32[24,768]{1,0:T(8,128)}, u32[]{:S(2)}, u32[]{:S(2)}) %collective-permute-start.52) | collective-permute-done | bytes 73760 | tf_op jit(solution)/shard_map/ppermute | solution.py:44
  334.0 2.4 add_convert_fusion.1
  339.4 6.4 %add_bitcast_fusion = (f32[1,768,768]{2,1,0:T(8,128)}, f32[1,768,768]{2,1,0:T(8,128)}) fusion(f32[3072,768]{1,0:T(8,128)} %get-tuple-element.165.base_in.base_out, bf16[1024,768]{1,0:T(8,128)(2,1)} %collective-permute-done.54, bf16[3072,768]{1,0:T(8,128)(2,1)} %collective-permute-done.32.near_in.near_out, bf16[256,768]{1,0:T(8,128)(2,1)S(1)} %slice.96, ...), kind=kLoop, calls=%fused_computation | loop fusion | flops 6488064 | bytes 14155776 | tf_op jit(solution)/shard_map/broadcast_in_dim | solution.py:1167
  345.8 3.8 %collective-permute-done.47 = bf16[256,768]{1,0:T(8,128)(2,1)S(1)} collective-permute-done((bf16[256,768]{1,0:T(8,128)(2,1)S(1)}, bf16[256,768]{1,0:T(8,128)(2,1)S(1)}, u32[]{:S(2)}, u32[]{:S(2)}) %collective-permute-start.47) | collective-permute-done | bytes 393248 | tf_op jit(solution)/shard_map/ppermute | solution.py:44
  351.0 2.1 fusion.5
  (144 shorter events, 68.5 us)
Async XLA Ops:
  0.6 15.2 %collective-permute-start = (bf16[256,768]{1,0:T(8,128)(2,1)}, bf16[256,768]{1,0:T(8,128)(2,1)}, u32[]{:S(2)}, u32[]{:S(2)}) collective-permute-start(bf16[256,768]{1,0:T(8,128)(2,1)} %refs_0_.5), channel_id=1, source_target_pairs={{0,1},{1,0},{2,3},{3,2},{4,5},{5,4},{6,7},{7,6},{8,9},{9,8},{10,11... | collective-permute-start | bytes 1179656 | tf_op jit(solution)/shard_map/ppermute | solution.py:44
  1.2 12.7 %collective-permute-start.1 = (bf16[256,768]{1,0:T(8,128)(2,1)}, bf16[256,768]{1,0:T(8,128)(2,1)}, u32[]{:S(2)}, u32[]{:S(2)}) collective-permute-start(bf16[256,768]{1,0:T(8,128)(2,1)} %refs_0_.5), channel_id=1, source_target_pairs={{0,2},{1,3},{2,0},{3,1},{4,6},{5,7},{6,4},{7,5},{8,10},{9,11},{10,... | collective-permute-start | bytes 1179656 | tf_op jit(solution)/shard_map/ppermute | solution.py:44
  5.5 10.4 %collective-permute-start.3 = (bf16[96,768]{1,0:T(8,128)(2,1)}, bf16[96,768]{1,0:T(8,128)(2,1)}, u32[]{:S(2)}, u32[]{:S(2)}) collective-permute-start(bf16[96,768]{1,0:T(8,128)(2,1)} %pack_weights.1.refs_0_), channel_id=1, source_target_pairs={{0,16},{4,20},{8,24},{12,28},{16,0},{20,4},{24,8},{28,12},{1,17},{... | collective-permute-start | bytes 442376 | tf_op jit(solution)/shard_map/ppermute | solution.py:44
  8.0 19.2 %collective-permute-start.8 = (s32[256,2]{0,1:T(2,128)}, s32[256,2]{0,1:T(2,128)}, u32[]{:S(2)}, u32[]{:S(2)}) collective-permute-start(s32[256,2]{0,1:T(2,128)} %param.28), channel_id=1, source_target_pairs={{0,16},{4,20},{8,24},{12,28},{16,0},{20,4},{24,8},{28,12},{1,17},{... | collective-permute-start | bytes 6152 | tf_op jit(solution)/shard_map/ppermute | solution.py:44
  13.8 25.0 %collective-permute-start.2 = (bf16[256,768]{1,0:T(8,128)(2,1)}, bf16[256,768]{1,0:T(8,128)(2,1)}, u32[]{:S(2)}, u32[]{:S(2)}) collective-permute-start(bf16[256,768]{1,0:T(8,128)(2,1)} %collective-permute-done.1.refs_3_.refs_4_), channel_id=1, source_target_pairs={{0,1},{1,0},{2,3},{3,2},{4,5},{5,4},{6,7},{7,6},{8,9},{9,8},{10,11... | collective-permute-start | bytes 1179656 | tf_op jit(solution)/shard_map/ppermute | solution.py:44
  17.5 13.1 %collective-permute-start.4 = (bf16[192,768]{1,0:T(8,128)(2,1)}, bf16[192,768]{1,0:T(8,128)(2,1)}, u32[]{:S(2)}, u32[]{:S(2)}) collective-permute-start(bf16[192,768]{1,0:T(8,128)(2,1)} %pair_up.1.refs_6_), channel_id=1, source_target_pairs={{0,4},{4,0},{8,12},{12,8},{16,20},{20,16},{24,28},{28,24},{1,5},{5... | collective-permute-start | bytes 884744 | tf_op jit(solution)/shard_map/ppermute | solution.py:44
  19.0 11.6 %collective-permute-start.5 = (bf16[192,768]{1,0:T(8,128)(2,1)}, bf16[192,768]{1,0:T(8,128)(2,1)}, u32[]{:S(2)}, u32[]{:S(2)}) collective-permute-start(bf16[192,768]{1,0:T(8,128)(2,1)} %pair_up.1.refs_6_), channel_id=1, source_target_pairs={{0,8},{4,12},{8,0},{12,4},{16,24},{20,28},{24,16},{28,20},{1,9},{5... | collective-permute-start | bytes 884744 | tf_op jit(solution)/shard_map/ppermute | solution.py:44
  19.7 19.2 %collective-permute-start.6 = (bf16[192,768]{1,0:T(8,128)(2,1)}, bf16[192,768]{1,0:T(8,128)(2,1)}, u32[]{:S(2)}, u32[]{:S(2)}) collective-permute-start(bf16[192,768]{1,0:T(8,128)(2,1)} %pair_up.1.refs_6_), channel_id=1, source_target_pairs={{0,12},{4,8},{8,4},{12,0},{16,28},{20,24},{24,20},{28,16},{1,13},{... | collective-permute-start | bytes 884744 | tf_op jit(solution)/shard_map/ppermute | solution.py:44
  27.2 24.5 %collective-permute-start.7 = (bf16[256,768]{1,0:T(8,128)(2,1)}, bf16[256,768]{1,0:T(8,128)(2,1)}, u32[]{:S(2)}, u32[]{:S(2)}) collective-permute-start(bf16[256,768]{1,0:T(8,128)(2,1)} %refs_3_.3), channel_id=1, source_target_pairs={{0,16},{4,20},{8,24},{12,28},{16,0},{20,4},{24,8},{28,12},{1,17},{... | collective-permute-start | bytes 1179656 | tf_op jit(solution)/shard_map/ppermute | solution.py:44
  46.7 27.7 %collective-permute-start.12 = (bf16[192,768]{1,0:T(8,128)(2,1)}, bf16[192,768]{1,0:T(8,128)(2,1)}, u32[]{:S(2)}, u32[]{:S(2)}) collective-permute-start(bf16[192,768]{1,0:T(8,128)(2,1)} %get-tuple-element.118.refs_8_.refs_12_), channel_id=1, source_target_pairs={{0,1},{1,0},{2,3},{3,2},{4,5},{5,4},{6,7},{7,6},{8,9},{9,8},{10,11... | collective-permute-start | bytes 884744 | tf_op jit(solution)/shard_map/ppermute | solution.py:44
  51.1 23.3 %collective-permute-start.14 = (bf16[192,768]{1,0:T(8,128)(2,1)}, bf16[192,768]{1,0:T(8,128)(2,1)}, u32[]{:S(2)}, u32[]{:S(2)}) collective-permute-start(bf16[192,768]{1,0:T(8,128)(2,1)} %collective-permute-done.13.refs_10_.refs_14_), channel_id=1, source_target_pairs={{0,1},{1,0},{2,3},{3,2},{4,5},{5,4},{6,7},{7,6},{8,9},{9,8},{10,11... | collective-permute-start | bytes 884744 | tf_op jit(solution)/shard_map/ppermute | solution.py:44
  78.2 21.4 %collective-permute-start.15 = (bf16[256,768]{1,0:T(8,128)(2,1)}, bf16[256,768]{1,0:T(8,128)(2,1)}, u32[]{:S(2)}, u32[]{:S(2)}) collective-permute-start(bf16[256,768]{1,0:T(8,128)(2,1)} %get-tuple-element.120.refs_6_), channel_id=1, source_target_pairs={{0,16},{4,20},{8,24},{12,28},{16,0},{20,4},{24,8},{28,12},{1,17},{... | collective-permute-start | bytes 1179656 | tf_op jit(solution)/shard_map/ppermute | solution.py:44
  79.3 24.3 %collective-permute-start.19 = (bf16[128,768]{1,0:T(8,128)(2,1)}, bf16[128,768]{1,0:T(8,128)(2,1)}, u32[]{:S(2)}, u32[]{:S(2)}) collective-permute-start(bf16[128,768]{1,0:T(8,128)(2,1)} %get-tuple-element.129), channel_id=1, source_target_pairs={{0,4},{4,0},{8,12},{12,8},{16,20},{20,16},{24,28},{28,24},{1,5},{5... | collective-permute-start | bytes 589832 | tf_op jit(solution)/shard_map/ppermute | solution.py:44
  80.9 24.3 %collective-permute-start.20 = (bf16[128,768]{1,0:T(8,128)(2,1)}, bf16[128,768]{1,0:T(8,128)(2,1)}, u32[]{:S(2)}, u32[]{:S(2)}) collective-permute-start(bf16[128,768]{1,0:T(8,128)(2,1)} %get-tuple-element.130), channel_id=1, source_target_pairs={{0,8},{4,12},{8,0},{12,4},{16,24},{20,28},{24,16},{28,20},{1,9},{5... | collective-permute-start | bytes 589832 | tf_op jit(solution)/shard_map/ppermute | solution.py:44
  83.2 23.9 %collective-permute-start.21 = (bf16[128,768]{1,0:T(8,128)(2,1)}, bf16[128,768]{1,0:T(8,128)(2,1)}, u32[]{:S(2)}, u32[]{:S(2)}) collective-permute-start(bf16[128,768]{1,0:T(8,128)(2,1)} %get-tuple-element.131), channel_id=1, source_target_pairs={{0,12},{4,8},{8,4},{12,0},{16,28},{20,24},{24,20},{28,16},{1,13},{... | collective-permute-start | bytes 589832 | tf_op jit(solution)/shard_map/ppermute | solution.py:44
  101.7 8.8 %collective-permute-start.16 = (bf16[128,768]{1,0:T(8,128)(2,1)}, bf16[128,768]{1,0:T(8,128)(2,1)}, u32[]{:S(2)}, u32[]{:S(2)}) collective-permute-start(bf16[128,768]{1,0:T(8,128)(2,1)} %get-tuple-element.125), channel_id=1, source_target_pairs={{0,4},{4,0},{8,12},{12,8},{16,20},{20,16},{24,28},{28,24},{1,5},{5... | collective-permute-start | bytes 589832 | tf_op jit(solution)/shard_map/ppermute | solution.py:44
  103.6 18.7 %collective-permute-start.17 = (bf16[128,768]{1,0:T(8,128)(2,1)}, bf16[128,768]{1,0:T(8,128)(2,1)}, u32[]{:S(2)}, u32[]{:S(2)}) collective-permute-start(bf16[128,768]{1,0:T(8,128)(2,1)} %get-tuple-element.126), channel_id=1, source_target_pairs={{0,8},{4,12},{8,0},{12,4},{16,24},{20,28},{24,16},{28,20},{1,9},{5... | collective-permute-start | bytes 589832 | tf_op jit(solution)/shard_map/ppermute | solution.py:44
  103.6 18.8 %collective-permute-start.18 = (bf16[128,768]{1,0:T(8,128)(2,1)}, bf16[128,768]{1,0:T(8,128)(2,1)}, u32[]{:S(2)}, u32[]{:S(2)}) collective-permute-start(bf16[128,768]{1,0:T(8,128)(2,1)} %get-tuple-element.127), channel_id=1, source_target_pairs={{0,12},{4,8},{8,4},{12,0},{16,28},{20,24},{24,20},{28,16},{1,13},{... | collective-permute-start | bytes 589832 | tf_op jit(solution)/shard_map/ppermute | solution.py:44
  105.2 30.1 %collective-permute-start.22 = (bf16[256,768]{1,0:T(8,128)(2,1)}, bf16[256,768]{1,0:T(8,128)(2,1)}, u32[]{:S(2)}, u32[]{:S(2)}) collective-permute-start(bf16[256,768]{1,0:T(8,128)(2,1)} %get-tuple-element.140), channel_id=1, source_target_pairs={{0,4},{4,0},{8,12},{12,8},{16,20},{20,16},{24,28},{28,24},{1,5},{5... | collective-permute-start | bytes 1179656 | tf_op jit(solution)/shard_map/ppermute | solution.py:44
  107.1 28.3 %collective-permute-start.23 = (bf16[256,768]{1,0:T(8,128)(2,1)}, bf16[256,768]{1,0:T(8,128)(2,1)}, u32[]{:S(2)}, u32[]{:S(2)}) collective-permute-start(bf16[256,768]{1,0:T(8,128)(2,1)} %get-tuple-element.141), channel_id=1, source_target_pairs={{0,8},{4,12},{8,0},{12,4},{16,24},{20,28},{24,16},{28,20},{1,9},{5... | collective-permute-start | bytes 1179656 | tf_op jit(solution)/shard_map/ppermute | solution.py:44
  110.5 24.9 %collective-permute-start.24 = (bf16[256,768]{1,0:T(8,128)(2,1)}, bf16[256,768]{1,0:T(8,128)(2,1)}, u32[]{:S(2)}, u32[]{:S(2)}) collective-permute-start(bf16[256,768]{1,0:T(8,128)(2,1)} %get-tuple-element.142), channel_id=1, source_target_pairs={{0,12},{4,8},{8,4},{12,0},{16,28},{20,24},{24,20},{28,16},{1,13},{... | collective-permute-start | bytes 1179656 | tf_op jit(solution)/shard_map/ppermute | solution.py:44
  147.9 16.9 %collective-permute-start.25 = (bf16[128,896]{1,0:T(8,128)(2,1)}, bf16[128,896]{1,0:T(8,128)(2,1)}, u32[]{:S(2)}, u32[]{:S(2)}) collective-permute-start(bf16[128,896]{1,0:T(8,128)(2,1)} %get-tuple-element.146), channel_id=1, source_target_pairs={{0,4},{4,0},{8,12},{12,8},{16,20},{20,16},{24,28},{28,24},{1,5},{5... | collective-permute-start | bytes 688136 | tf_op jit(solution)/shard_map/ppermute | solution.py:44
  150.1 14.7 %collective-permute-start.26 = (bf16[128,896]{1,0:T(8,128)(2,1)}, bf16[128,896]{1,0:T(8,128)(2,1)}, u32[]{:S(2)}, u32[]{:S(2)}) collective-permute-start(bf16[128,896]{1,0:T(8,128)(2,1)} %get-tuple-element.147), channel_id=1, source_target_pairs={{0,8},{4,12},{8,0},{12,4},{16,24},{20,28},{24,16},{28,20},{1,9},{5... | collective-permute-start | bytes 688136 | tf_op jit(solution)/shard_map/ppermute | solution.py:44
  151.7 13.2 %collective-permute-start.27 = (bf16[128,896]{1,0:T(8,128)(2,1)}, bf16[128,896]{1,0:T(8,128)(2,1)}, u32[]{:S(2)}, u32[]{:S(2)}) collective-permute-start(bf16[128,896]{1,0:T(8,128)(2,1)} %get-tuple-element.148), channel_id=1, source_target_pairs={{0,12},{4,8},{8,4},{12,0},{16,28},{20,24},{24,20},{28,16},{1,13},{... | collective-permute-start | bytes 688136 | tf_op jit(solution)/shard_map/ppermute | solution.py:44
  167.6 25.9 %collective-permute-start.28 = (bf16[128,896]{1,0:T(8,128)(2,1)}, bf16[128,896]{1,0:T(8,128)(2,1)}, u32[]{:S(2)}, u32[]{:S(2)}) collective-permute-start(bf16[128,896]{1,0:T(8,128)(2,1)} %get-tuple-element.152), channel_id=1, source_target_pairs={{0,4},{4,0},{8,12},{12,8},{16,20},{20,16},{24,28},{28,24},{1,5},{5... | collective-permute-start | bytes 688136 | tf_op jit(solution)/shard_map/ppermute | solution.py:44
  168.4 25.1 %collective-permute-start.29 = (bf16[128,896]{1,0:T(8,128)(2,1)}, bf16[128,896]{1,0:T(8,128)(2,1)}, u32[]{:S(2)}, u32[]{:S(2)}) collective-permute-start(bf16[128,896]{1,0:T(8,128)(2,1)} %get-tuple-element.153), channel_id=1, source_target_pairs={{0,8},{4,12},{8,0},{12,4},{16,24},{20,28},{24,16},{28,20},{1,9},{5... | collective-permute-start | bytes 688136 | tf_op jit(solution)/shard_map/ppermute | solution.py:44
  169.7 23.8 %collective-permute-start.30 = (bf16[128,896]{1,0:T(8,128)(2,1)}, bf16[128,896]{1,0:T(8,128)(2,1)}, u32[]{:S(2)}, u32[]{:S(2)}) collective-permute-start(bf16[128,896]{1,0:T(8,128)(2,1)} %get-tuple-element.154), channel_id=1, source_target_pairs={{0,12},{4,8},{8,4},{12,0},{16,28},{20,24},{24,20},{28,16},{1,13},{... | collective-permute-start | bytes 688136 | tf_op jit(solution)/shard_map/ppermute | solution.py:44
  171.1 22.4 %collective-permute-start.31 = (bf16[256,896]{1,0:T(8,128)(2,1)}, bf16[256,896]{1,0:T(8,128)(2,1)}, u32[]{:S(2)}, u32[]{:S(2)}) collective-permute-start(bf16[256,896]{1,0:T(8,128)(2,1)} %get-tuple-element.155), channel_id=1, source_target_pairs={{0,16},{4,20},{8,24},{12,28},{16,0},{20,4},{24,8},{28,12},{1,17},{... | collective-permute-start | bytes 1376264 | tf_op jit(solution)/shard_map/ppermute | solution.py:44
  200.8 26.0 %collective-permute-start.32 = (bf16[3072,768]{1,0:T(8,128)(2,1)}, bf16[3072,768]{1,0:T(8,128)(2,1)}, u32[]{:S(2)}, u32[]{:S(2)}) collective-permute-start(bf16[3072,768]{1,0:T(8,128)(2,1)} %get-tuple-element.164), channel_id=1, source_target_pairs={{0,1},{1,0},{2,3},{3,2},{4,5},{5,4},{6,7},{7,6},{8,9},{9,8},{10,11... | collective-permute-start | bytes 14155784 | tf_op jit(solution)/shard_map/ppermute | solution.py:44
  200.8 7.7 %collective-permute-start.36 = (bf16[768,384]{1,0:T(8,128)(2,1)}, bf16[768,384]{1,0:T(8,128)(2,1)S(1)}, u32[]{:S(2)}, u32[]{:S(2)}) collective-permute-start(bf16[768,384]{1,0:T(8,128)(2,1)} %get-tuple-element.173), channel_id=1, source_target_pairs={{0,1},{1,0},{2,3},{3,2},{4,5},{5,4},{6,7},{7,6},{8,9},{9,8},{10,11... | collective-permute-start | bytes 1769480 | tf_op jit(solution)/shard_map/ppermute | solution.py:44
  210.1 12.0 %collective-permute-start.37 = (bf16[768,192]{1,0:T(8,128)(2,1)S(1)}, bf16[768,192]{1,0:T(8,128)(2,1)S(1)}, u32[]{:S(2)}, u32[]{:S(2)}) collective-permute-start(bf16[768,192]{1,0:T(8,128)(2,1)S(1)} %slice.121), channel_id=1, source_target_pairs={{0,2},{1,3},{2,0},{3,1},{4,6},{5,7},{6,4},{7,5},{8,10},{9,11},{10,... | collective-permute-start | bytes 884744 | tf_op jit(solution)/shard_map/ppermute | solution.py:44
  211.5 11.6 %collective-permute-start.33 = (bf16[256,192]{1,0:T(8,128)(2,1)S(1)}, bf16[256,192]{1,0:T(8,128)(2,1)}, u32[]{:S(2)}, u32[]{:S(2)}) collective-permute-start(bf16[256,192]{1,0:T(8,128)(2,1)S(1)} %copy-done.8), channel_id=1, source_target_pairs={{0,1},{1,0},{2,3},{3,2},{4,5},{5,4},{6,7},{7,6},{8,9},{9,8},{10,11... | collective-permute-start | bytes 294920 | tf_op jit(solution)/shard_map/ppermute | solution.py:44
  211.6 13.5 %collective-permute-start.34 = (bf16[256,192]{1,0:T(8,128)(2,1)S(1)}, bf16[256,192]{1,0:T(8,128)(2,1)}, u32[]{:S(2)}, u32[]{:S(2)}) collective-permute-start(bf16[256,192]{1,0:T(8,128)(2,1)S(1)} %copy-done.7), channel_id=1, source_target_pairs={{0,2},{1,3},{2,0},{3,1},{4,6},{5,7},{6,4},{7,5},{8,10},{9,11},{10,... | collective-permute-start | bytes 294920 | tf_op jit(solution)/shard_map/ppermute | solution.py:44
  212.3 14.4 %collective-permute-start.35 = (bf16[256,192]{1,0:T(8,128)(2,1)S(1)}, bf16[256,192]{1,0:T(8,128)(2,1)}, u32[]{:S(2)}, u32[]{:S(2)}) collective-permute-start(bf16[256,192]{1,0:T(8,128)(2,1)S(1)} %copy-done.6), channel_id=1, source_target_pairs={{0,3},{1,2},{2,1},{3,0},{4,7},{5,6},{6,5},{7,4},{8,11},{9,10},{10,... | collective-permute-start | bytes 294920 | tf_op jit(solution)/shard_map/ppermute | solution.py:44
  231.4 22.6 %collective-permute-start.41 = (bf16[512,768]{1,0:T(8,128)(2,1)}, bf16[512,768]{1,0:T(8,128)(2,1)}, u32[]{:S(2)}, u32[]{:S(2)}) collective-permute-start(bf16[512,768]{1,0:T(8,128)(2,1)} %get-tuple-element.178.refs_11_), channel_id=1, source_target_pairs={{0,2},{1,3},{2,0},{3,1},{4,6},{5,7},{6,4},{7,5},{8,10},{9,11},{10,... | collective-permute-start | bytes 2359304 | tf_op jit(solution)/shard_map/ppermute | solution.py:44
  232.7 21.2 %collective-permute-start.38 = (bf16[256,768]{1,0:T(8,128)(2,1)}, bf16[256,768]{1,0:T(8,128)(2,1)}, u32[]{:S(2)}, u32[]{:S(2)}) collective-permute-start(bf16[256,768]{1,0:T(8,128)(2,1)} %get-tuple-element.174), channel_id=1, source_target_pairs={{0,4},{4,0},{8,12},{12,8},{16,20},{20,16},{24,28},{28,24},{1,5},{5... | collective-permute-start | bytes 1179656 | tf_op jit(solution)/shard_map/ppermute | solution.py:44
  232.8 21.2 %collective-permute-start.39 = (bf16[256,768]{1,0:T(8,128)(2,1)}, bf16[256,768]{1,0:T(8,128)(2,1)}, u32[]{:S(2)}, u32[]{:S(2)}) collective-permute-start(bf16[256,768]{1,0:T(8,128)(2,1)} %get-tuple-element.175), channel_id=1, source_target_pairs={{0,8},{4,12},{8,0},{12,4},{16,24},{20,28},{24,16},{28,20},{1,9},{5... | collective-permute-start | bytes 1179656 | tf_op jit(solution)/shard_map/ppermute | solution.py:44
  233.5 20.4 %collective-permute-start.40 = (bf16[256,768]{1,0:T(8,128)(2,1)}, bf16[256,768]{1,0:T(8,128)(2,1)}, u32[]{:S(2)}, u32[]{:S(2)}) collective-permute-start(bf16[256,768]{1,0:T(8,128)(2,1)} %get-tuple-element.176), channel_id=1, source_target_pairs={{0,12},{4,8},{8,4},{12,0},{16,28},{20,24},{24,20},{28,16},{1,13},{... | collective-permute-start | bytes 1179656 | tf_op jit(solution)/shard_map/ppermute | solution.py:44
  260.5 9.4 %collective-permute-start.42 = (bf16[192,768]{1,0:T(8,128)(2,1)}, bf16[192,768]{1,0:T(8,128)(2,1)}, u32[]{:S(2)}, u32[]{:S(2)}) collective-permute-start(bf16[192,768]{1,0:T(8,128)(2,1)} %get-tuple-element.190), channel_id=1, source_target_pairs={{0,4},{4,0},{8,12},{12,8},{16,20},{20,16},{24,28},{28,24},{1,5},{5... | collective-permute-start | bytes 884744 | tf_op jit(solution)/shard_map/ppermute | solution.py:44
  260.7 10.3 %collective-permute-start.43 = (bf16[192,768]{1,0:T(8,128)(2,1)}, bf16[192,768]{1,0:T(8,128)(2,1)}, u32[]{:S(2)}, u32[]{:S(2)}) collective-permute-start(bf16[192,768]{1,0:T(8,128)(2,1)} %get-tuple-element.191), channel_id=1, source_target_pairs={{0,8},{4,12},{8,0},{12,4},{16,24},{20,28},{24,16},{28,20},{1,9},{5... | collective-permute-start | bytes 884744 | tf_op jit(solution)/shard_map/ppermute | solution.py:44
  261.4 15.2 %collective-permute-start.44 = (bf16[192,768]{1,0:T(8,128)(2,1)}, bf16[192,768]{1,0:T(8,128)(2,1)}, u32[]{:S(2)}, u32[]{:S(2)}) collective-permute-start(bf16[192,768]{1,0:T(8,128)(2,1)} %get-tuple-element.192), channel_id=1, source_target_pairs={{0,12},{4,8},{8,4},{12,0},{16,28},{20,24},{24,20},{28,16},{1,13},{... | collective-permute-start | bytes 884744 | tf_op jit(solution)/shard_map/ppermute | solution.py:44
  264.1 72.3 %collective-permute-start.54 = (bf16[1024,768]{1,0:T(8,128)(2,1)}, bf16[1024,768]{1,0:T(8,128)(2,1)}, u32[]{:S(2)}, u32[]{:S(2)}) collective-permute-start(bf16[1024,768]{1,0:T(8,128)(2,1)} %get-tuple-element.207), channel_id=1, source_target_pairs={{0,2},{1,3},{2,0},{3,1},{4,6},{5,7},{6,4},{7,5},{8,10},{9,11},{10,... | collective-permute-start | bytes 4718600 | tf_op jit(solution)/shard_map/ppermute | solution.py:44
  281.1 19.5 %collective-permute-start.49 = (f32[24,768]{1,0:T(8,128)S(1)}, f32[24,768]{1,0:T(8,128)S(1)}, u32[]{:S(2)}, u32[]{:S(2)}) collective-permute-start(f32[24,768]{1,0:T(8,128)S(1)} %add.128), channel_id=1, source_target_pairs={{0,2},{1,3},{2,0},{3,1},{4,6},{5,7},{6,4},{7,5},{8,10},{9,11},{10,... | collective-permute-start | bytes 221192 | tf_op jit(solution)/shard_map/ppermute | solution.py:44
  301.0 12.8 %collective-permute-start.53 = (bf16[96,768]{1,0:T(8,128)(2,1)}, bf16[96,768]{1,0:T(8,128)(2,1)}, u32[]{:S(2)}, u32[]{:S(2)}) collective-permute-start(bf16[96,768]{1,0:T(8,128)(2,1)} %get-tuple-element.202), channel_id=1, source_target_pairs={{0,16},{4,20},{8,24},{12,28},{16,0},{20,4},{24,8},{28,12},{1,17},{... | collective-permute-start | bytes 442376 | tf_op jit(solution)/shard_map/ppermute | solution.py:44
  301.7 35.7 %collective-permute-start.46 = (bf16[512,768]{1,0:T(8,128)(2,1)}, bf16[512,768]{1,0:T(8,128)(2,1)}, u32[]{:S(2)}, u32[]{:S(2)}) collective-permute-start(bf16[512,768]{1,0:T(8,128)(2,1)} %get-tuple-element.199), channel_id=1, source_target_pairs={{0,1},{1,0},{2,3},{3,2},{4,5},{5,4},{6,7},{7,6},{8,9},{9,8},{10,11... | collective-permute-start | bytes 2359304 | tf_op jit(solution)/shard_map/ppermute | solution.py:44
  309.3 24.7 %collective-permute-start.45 = (bf16[256,768]{1,0:T(8,128)(2,1)}, bf16[256,768]{1,0:T(8,128)(2,1)}, u32[]{:S(2)}, u32[]{:S(2)}) collective-permute-start(bf16[256,768]{1,0:T(8,128)(2,1)} %get-tuple-element.196), channel_id=1, source_target_pairs={{0,16},{4,20},{8,24},{12,28},{16,0},{20,4},{24,8},{28,12},{1,17},{... | collective-permute-start | bytes 1179656 | tf_op jit(solution)/shard_map/ppermute | solution.py:44
  312.8 18.5 %collective-permute-start.52 = (f32[24,768]{1,0:T(8,128)}, f32[24,768]{1,0:T(8,128)}, u32[]{:S(2)}, u32[]{:S(2)}) collective-permute-start(f32[24,768]{1,0:T(8,128)} %add.131), channel_id=1, source_target_pairs={{0,16},{4,20},{8,24},{12,28},{16,0},{20,4},{24,8},{28,12},{1,17},{... | collective-permute-start | bytes 221192 | tf_op jit(solution)/shard_map/ppermute | solution.py:44
  338.5 11.1 %collective-permute-start.47 = (bf16[256,768]{1,0:T(8,128)(2,1)S(1)}, bf16[256,768]{1,0:T(8,128)(2,1)S(1)}, u32[]{:S(2)}, u32[]{:S(2)}) collective-permute-start(bf16[256,768]{1,0:T(8,128)(2,1)S(1)} %add_convert_fusion), channel_id=1, source_target_pairs={{0,2},{1,3},{2,0},{3,1},{4,6},{5,7},{6,4},{7,5},{8,10},{9,11},{10,... | collective-permute-start | bytes 1179656 | tf_op jit(solution)/shard_map/ppermute | solution.py:44
  (16 other events, 130.4 us)

commit v5 on v4

--- a/solution.py
+++ b/solution.py
@@ -20,7 +20,7 @@
     return pltpu.CompilerParams(vmem_limit_bytes=mebibytes * 1024 * 1024)
 
 
-brief = pl.CostEstimate(flops=10**9, bytes_accessed=10**6, transcendentals=0)
+brief = pl.CostEstimate(flops=10**7, bytes_accessed=10**4, transcendentals=0)
 long = pl.CostEstimate(flops=2 * 10**10, bytes_accessed=10**7, transcendentals=0)
 
 
@@ -49,7 +49,7 @@
 
 
 def call(
-    kernel, name, operands, outs, scratch=(), scalars=None, after=(), through=(), room=64
+    kernel, name, operands, outs, scratch=(), scalars=None, after=(), through=(), cost=None
 ):
     operands, outs = list(operands), list(outs)
     in_specs = [whole(o.shape) for o in operands]
@@ -73,8 +73,8 @@
         out_shape=outs + [shape(o.shape, o.dtype) for o in through],
         input_output_aliases={count + i: results + i for i in range(len(through))},
         scratch_shapes=list(scratch),
-        compiler_params=limit(room),
-        cost_estimate=brief,
+        compiler_params=limit(64),
+        cost_estimate=cost or brief,
     )(*operands, *extra)
 
 
@@ -280,7 +280,7 @@
     return both
 
 
-def project(place, token_blocks, pack_blocks, gain, span):
+def project(place, token_blocks, pack_blocks, gain, cotangent, span):
     rows, width = token_blocks[0].shape
     members = len(token_blocks)
     seq_len = rows * members
@@ -319,6 +319,7 @@
         + [shape((span, width), bf16)],
         scratch=[pltpu.VMEM((width, width), bf16)],
         scalars=place,
+        through=[cotangent],
     )
 
 
@@ -329,7 +330,7 @@
     return jnp.where(taken, 1.0, 0.0).astype(bf16)
 
 
-def to_slots(name, sets, blocks, size, after=(), through=()):
+def to_slots(name, sets, blocks, size, through=(), cost=None):
     width = sets[0][0].shape[1]
 
     def kernel(*refs):
@@ -346,8 +347,8 @@
         name,
         operands,
         [shape((size * len(sets), width), bf16)] * blocks,
-        after=after,
         through=through,
+        cost=cost,
     )
 
 
@@ -420,8 +421,7 @@
 def experts_forward(name, place, w_in, w_out, w_router, x_blocks, experts, before, cost):
     width, units = w_in.shape
     count, size = len(x_blocks), x_blocks[0].shape[0]
-    total, piece = size * count, 768
-    chunk = min(256, total)
+    total, piece, chunk = size * count, 768, 256
     sets = 1 if before is None else 1 + len(before) // 2
     blocks = 0 if before is None else count
     before = [] if before is None else list(before)
@@ -441,15 +441,14 @@
             gates_ref[...] = jnp.broadcast_to(own, gates_ref.shape)
             result_sum[...] = jnp.zeros_like(result_sum)
 
-        for c in range(total // chunk):
+        for c in range(piece // chunk):
             at = slice(c * chunk, (c + 1) * chunk)
-            pre_act = dot(x_all[at, :], w_in_ref[...], 1, 0)
+            pre_act = dot(x_all[...], w_in_ref[:, at], 1, 0)
             below = 0.5 + 0.5 * lax.erf(pre_act * math.sqrt(0.5))
             bell = jnp.exp(-0.5 * pre_act * pre_act) * (1.0 / math.sqrt(2.0 * math.pi))
-            active = (pre_act * below).astype(bf16)
-            active_ref[at, :] = active
-            slope_ref[at, :] = (below + pre_act * bell).astype(bf16)
-            result_sum[at, :] += dot(active, w_out_ref[...], 1, 0)
+            active_ref[:, at] = (pre_act * below).astype(bf16)
+            slope_ref[:, at] = (below + pre_act * bell).astype(bf16)
+        result_sum[...] += dot(active_ref[...], w_out_ref[...], 1, 0)
 
         @pl.when(pl.program_id(0) == pl.num_programs(0) - 1)
         def _():
@@ -492,8 +491,8 @@
 def experts_backward(name, place, w_in, w_out, sets, at_set, slot_grad, g_blocks, count, cost):
     width, units = w_in.shape
     slope, result, _ = sets[at_set]
-    total, piece = slope.shape[0], 768
-    size, chunk = total // count, min(256, total)
+    total, piece, chunk = slope.shape[0], 768, 256
+    size = total // count
     number = len(sets)
     first = slot_grad is None
     given = [gates for _, _, gates in sets] if first else [slot_grad]
@@ -516,12 +515,11 @@
                         grad = ref[at * size : (at + 1) * size, :].astype(f32)
                         s_refs[at][rows, :] = (given_refs[at][rows, 0:1] * grad).astype(bf16)
 
-        for c in range(total // chunk):
+        for c in range(piece // chunk):
             at = slice(c * chunk, (c + 1) * chunk)
-            active_grad = dot(s_ref[at, :], w_out_ref[...], 1, 1)
-            pre_grad = (active_grad * slope_ref[at, :].astype(f32)).astype(bf16)
-            pre_grad_ref[at, :] = pre_grad
-            back_sum[at, :] += dot(pre_grad, w_in_ref[...], 1, 1)
+            active_grad = dot(s_ref[...], w_out_ref[at, :], 1, 1)
+            pre_grad_ref[:, at] = (active_grad * slope_ref[:, at].astype(f32)).astype(bf16)
+        back_sum[...] += dot(pre_grad_ref[...], w_in_ref[...], 1, 1)
 
         @pl.when(pl.program_id(0) == pl.num_programs(0) - 1)
         def _():
@@ -626,8 +624,8 @@
         for r, (ref, first) in enumerate(
             ((base_ref, 0), (near_ref, 0), (base_ref, span), (near_ref, span))
         ):
-            part = dot(attn_grad, mixed_refs[r][...], 0, 0)
-            ref[:, first : first + span] = part.astype(ref.dtype)
+            part = dot(mixed_refs[r][...], attn_grad, 0, 0)
+            ref[first : first + span, :] = part.astype(ref.dtype)
 
     return call(
         kernel,
@@ -642,8 +640,8 @@
             shape((rows, width), f32),
             shape((1, width), f32),
             shape((experts, width), f32),
-            shape((width, 2 * span), bf16),
-            shape((width, 2 * span), f32),
+            shape((2 * span, width), bf16),
+            shape((2 * span, width), f32),
         ],
         after=after,
         through=through,
@@ -711,35 +709,41 @@
     )(place, *rows_in, *pre_grads, *actives, *slot_grads)
 
 
-def far_sums(near, base, cut, after, through):
+def far_sums(near, base, near_o, base_o, cuts, after):
     size, width = base.shape[0] // 4, base.shape[1]
-    count = len(through)
-
-    def block(at):
-        return pl.BlockSpec(
-            (size, width), lambda *_: (2 * at + 1, 0), pipeline_mode=pl.Buffered(1)
-        )
-
-    def kernel(near_in, near_out, base_in, base_out, *refs):
-        first_ref, rest_ref = refs[count + len(after) : count + len(after) + 2]
-        held = (base_in[...] + near_in[...].astype(f32)).astype(bf16)
-        first_ref[...] = held[:cut, :]
-        rest_ref[: size - cut, :] = held[cut:, :]
-        rest_ref[size - cut :, :] = (base_out[...] + near_out[...].astype(f32)).astype(bf16)
-
-    anywhere = pl.BlockSpec(memory_space=pl.ANY)
+    span = near_o.shape[0] // 2
+
+    def block(rows, at):
+        return pl.BlockSpec((rows, width), lambda *_: (at, 0), pipeline_mode=pl.Buffered(1))
+
+    def kernel(near_in, near_out, base_in, base_out, near_o_ref, base_o_ref, *refs):
+        out_refs = refs[len(after) :]
+        out_refs[0][:span, :] = (base_o_ref[...] + near_o_ref[...].astype(f32)).astype(bf16)
+        starts = [0] + cuts
+        for i, ref in enumerate(out_refs):
+            low, high = starts[i], starts[i + 1]
+            at = span if i == 0 else 0
+            for near_ref, base_ref, shift in ((near_in, base_in, 0), (near_out, base_out, size)):
+                first, last = max(low, shift), min(high, shift + size)
+                if first < last:
+                    rows = slice(first - shift, last - shift)
+                    held = base_ref[rows, :] + near_ref[rows, :].astype(f32)
+                    ref[at + first - low : at + last - low, :] = held.astype(bf16)
+
+    rows = [high - low for low, high in zip([0] + cuts, cuts)]
+    rows[0] = rows[0] + span
     return pl.pallas_call(
         kernel,
         name="far_sums",
         grid=(1,),
-        in_specs=[block(0), block(1), block(0), block(1)] + [anywhere] * (count + len(after)),
-        out_specs=[whole((cut, width)), whole((2 * size - cut, width))] + [anywhere] * count,
-        out_shape=[shape((cut, width), bf16), shape((2 * size - cut, width), bf16)]
-        + [shape(o.shape, o.dtype) for o in through],
-        input_output_aliases={4 + i: 2 + i for i in range(count)},
+        in_specs=[block(size, 1), block(size, 3), block(size, 1), block(size, 3)]
+        + [block(span, 1), block(span, 1)]
+        + [pl.BlockSpec(memory_space=pl.ANY)] * len(after),
+        out_specs=[whole((count, width)) for count in rows],
+        out_shape=[shape((count, width), bf16) for count in rows],
         compiler_params=limit(64),
         cost_estimate=brief,
-    )(near, near, base, base, *through, *after)
+    )(near, near, base, base, near_o, base_o, *after)
 
 
 def input_grads(
@@ -771,7 +775,7 @@
         near_ref, base_ref, far_ref, small_ref, *weight_refs, sums = refs[13:]
         for at, ref in enumerate((dq_ref, dk_ref, dv_ref)):
             sums[:, at * span : (at + 1) * span] = dot(normed_ref[...], ref[...], 0, 0)
-        sums[:, 3 * span :] = out_ref[...]
+        sums[:, 3 * span :] = out_ref[...].T
         if few:
             for r, ref in enumerate(weight_refs):
                 for i, far in enumerate((0, 4)):
@@ -935,8 +939,8 @@
     else:
         pack_blocks = [(lax.all_gather(pack, "dp", axis=0, tiled=True), (0,))]
     gain_one, gain_two = norm_gain.reshape(1, width), ffn_gain.reshape(1, width)
-    normed, query, key_rows, value_rows, weight_q, weight_k, weight_v, w_o = project(
-        place, token_blocks, pack_blocks, gain_one, span
+    normed, query, key_rows, value_rows, weight_q, weight_k, weight_v, w_o, late_cotangent = (
+        project(place, token_blocks, pack_blocks, gain_one, cotangent, span)
     )
 
     if few:
@@ -948,16 +952,16 @@
         slots = [slots_of(routes, 0, capacity, experts, experts)]
 
     if few:
-        far_cotangent = swap(cotangent, "dp", 4)
+        far_cotangent = swap(late_cotangent, "dp", 4)
         held = to_slots(
             "grads_to_slots",
             [(cotangent, slots[0]), (far_cotangent, slots[1])],
             blocks,
             size,
-            [query],
+            cost=long,
         )
     else:
-        held = to_slots("grads_to_slots", [(cotangent, slots[0])], blocks, size, [query])
+        held = to_slots("grads_to_slots", [(cotangent, slots[0])], blocks, size)
 
     line_buckets = jnp.pad(jnp.flip(buckets[: reach + 1]), (0, window - reach - 1))
     bucket_hot = (
@@ -969,7 +973,7 @@
     seg_q = segments.reshape(seq_len, 1)
     seg_k = jnp.pad(segments.reshape(1, seq_len), ((0, 0), (reach, 0)), constant_values=-1)
     mixed_out = attend(
-        place, query, key_rows, value_rows, seg_q, seg_k, line, heads, members, held[:1]
+        place, query, key_rows, value_rows, seg_q, seg_k, line, heads, members, []
     )
     weight_o = gather_mp(w_o)
     mixed_in = [mixed_out[0]] + [swap(mixed_out[r], "mp", r) for r in range(1, members)]
@@ -985,7 +989,7 @@
         experts,
         blocks,
         size,
-        [],
+        [far_cotangent] if few else [],
     )
     if few:
         far_input = swap(ffn_input, "dp", 4)
@@ -1046,13 +1050,21 @@
         )
         pre_grads = [pre_grad] + pre_grads
         far_back = [back[0]] + [swap(back[r], "dp", r) for r in (1, 2, 3)]
+        result_in = [result[0]] + [swap(result[r], "dp", r) for r in (1, 2, 3)]
         far_total, *passed = from_slots(
-            "back_from_slots", far_back, [slots[1]], size, [bf16], through=own_back[1:]
+            "back_from_slots",
+            far_back,
+            [slots[1]],
+            size,
+            [bf16],
+            after=result_in[1:],
+            through=own_back[1:],
         )
         far_sum = swap(far_total, "dp", 4)
         own_back = [own_back[0]] + [swap(passed[r - 1], "dp", r) for r in (1, 2, 3)]
     else:
         own_back, far_sum = [all_to_all_dp(back[0])], None
+        result_in = [all_to_all_dp(result[0])]
     near_w, base_w = expert_weight_grads(place, arrived, pre_grads, actives, slot_grads, members)
 
     homed = home(
@@ -1075,14 +1087,11 @@
     grad_out, homed = homed[:members], homed[members:]
     hidden_grad, ffn_gain_grad, router_grad, near_o, base_o, near_w = homed
     grad_in = [grad_out[0]] + [swap(grad_out[r], "mp", r) for r in range(1, members)]
-    near_o = swap(near_o, "mp", 1)
-    sum_o = base_o + near_o.astype(f32)
-    output_sum = sum_o[:, :span] + swap(sum_o[:, span:].astype(bf16), "mp", 2).astype(f32)
-    near_w = swap(near_w, "mp", 1)
-    far_first, far_rest, *passed = far_sums(
-        near_w, base_w, 2 * rows, grad_in[1:] + [output_sum], result[1:]
-    )
-    result = result[:1] + passed
+    near_o, near_w = swap(near_o, "mp", 1), swap(near_w, "mp", 1)
+    piece = w_in.shape[2] // members
+    far_first, far_next, far_last = far_sums(
+        near_w, base_w, near_o, base_o, [rows, piece, 2 * piece], grad_in[2:]
+    )
 
     *proj_grads, line_grad = attend_back(
         place,
@@ -1097,11 +1106,9 @@
         [far_first],
     )
     far_first = swap(far_first, "mp", 2)
-    far_rest = swap(far_rest, "mp", 2)
-    if few:
-        result_in = [result[0]] + [swap(result[r], "dp", r) for r in (1, 2, 3)]
-    else:
-        result_in = [all_to_all_dp(result[0])]
+    far_next = swap(far_next, "mp", 2)
+    far_last = swap(far_last, "mp", 2)
+    output_sum = base_o[:span] + near_o[:span].astype(f32) + far_first[:span].astype(f32)
     near, base, base_far, small, *weight_sums = input_grads(
         place,
         proj_grads,
@@ -1116,12 +1123,12 @@
         members,
         owners,
         heads,
-        [far_first] + result_in[1:],
+        [],
     )
     if few:
         arrived_sums = [swap(weight_sums[r], "dp", r) for r in (1, 2, 3)]
         own_sum, far_part, small = fold_weights(
-            weight_sums[0], arrived_sums, [], [small]
+            weight_sums[0], arrived_sums, [far_next], [small]
         )
         weight_grads = split_weights([own_sum, swap(far_part, "dp", 4)], span)
     else:
@@ -1140,21 +1147,18 @@
 
     if few:
         own_result, far_result = from_slots(
-            "result_from_slots", result_in, slots, size, [f32, bf16], after=[own_sum]
+            "result_from_slots", result_in, slots, size, [f32, bf16], after=[base]
         )
         block_out = hidden + own_result + swap(far_result, "dp", 4).astype(f32)
     else:
         (own_result,) = from_slots("result_from_slots", result_in, slots, size, [f32])
         block_out = hidden + own_result
     block_out = block_out.astype(bf16)
-    piece = w_in.shape[2] // members
-    own_w = base_w[:piece] + near_w[:piece].astype(f32)
-    w_in_grad = own_w + jnp.concatenate(
-        [far_first, far_rest[: piece - far_first.shape[0]]], axis=0
-    ).astype(f32)
-    own_w = base_w[2 * piece : 3 * piece] + near_w[2 * piece : 3 * piece].astype(f32)
-    w_out_grad = own_w + far_rest[piece - far_first.shape[0] :].astype(f32)
-    small = sum_over(sum_over(small, "mp"), "dp")
+    far_in = jnp.concatenate([far_first[span:], far_next], axis=0).astype(f32)
+    w_in_grad = base_w[:piece] + near_w[:piece].astype(f32) + far_in
+    own_out = base_w[2 * piece : 3 * piece] + near_w[2 * piece : 3 * piece].astype(f32)
+    w_out_grad = own_out + far_last.astype(f32)
+    small = sum_over(sum_over(small, "dp"), "mp")
     return (
         block_out,
         tokens_grad,

time: 355 us -> 319 us (0.90)
  waiting for transfers between devices: 112 us -> 76.5 us
    ppermute x55, waiting for transfers between devices: 112 us -> 76.5 us  [swap(): return lax.ppermute(values, axis, [(i, i ^ step) for i in range(count)])]
  transfers between devices with their start and end apart: 55 -> 55, of which waited for: 19 -> 16; matrix products, arithmetic and copies ran while one was open for 11% -> 12% of each run, Pallas kernels for 30% -> 39%
where the time goes in v5:
time: 319 us; the launch traced here: 317 us
  Pallas kernels  144 us (45%)
  waiting for transfers between devices  76.5 us (24%)
  starting transfers between devices  53 us (17%)
  other arithmetic  23.7 us (7%)
  local copies, waits for them, and re-layouts  17.4 us (5%)
    ppermute x55, waiting for transfers between devices, swap(): return lax.ppermute(values, axis, [(i, i ^ step) for i in range(count)])  76.5 us
    pallas_call x14, Pallas kernels, call(): pl.pallas_call(body, name=name, grid=(1,), in_specs=in_specs + [pl.BlockS...  68.6 us
    ppermute x55, starting transfers between devices, swap(): return lax.ppermute(values, axis, [(i, i ^ step) for i in range(count)])  53 us
    pallas_call x2, Pallas kernels, experts_forward(): pl.pallas_call(kernel, name=name, grid=(units // piece,), in_specs=[pl.Bl...  26 us
    pallas_call x2, Pallas kernels, experts_backward(): pl.pallas_call(kernel, name=name, grid=(units // piece,), in_specs=[pl.Bl...  24.2 us
    pallas_call x1, Pallas kernels, expert_weight_grads(): pl.pallas_call(kernel, name='expert_weight_grads', grid_spec=pltpu.Prefet...  19.8 us
    broadcast_in_dim x1, other arithmetic, on_device(): w_out_grad[None]  6.61 us
  transfers between devices with their start and end apart: 55, of which 16 were waited for; matrix products, arithmetic and copies ran while one was open for 12% of the time, Pallas kernels for 39%

profile of v5, /device:TPU:0, one launch (start us, length us, event | category | flops | bytes accessed | tf_op | source)
XLA Modules:
  0.0 317.2 jit_solution(17062894882355908152)
XLA Ops:
  1.2 2.6 collective-permute-start.1
  5.5 2.6 collective-permute-start.3
  10.1 3.6 %collective-permute-done.1.refs_3_.refs_4_ = bf16[256,768]{1,0:T(8,128)(2,1)} collective-permute-done((bf16[256,768]{1,0:T(8,128)(2,1)}, bf16[256,768]{1,0:T(8,128)(2,1)}, u32[]{:S(2)}, u32[]{:S(2)}) %collective-permute-start.1) | collective-permute-done | bytes 393248 | tf_op jit(solution)/shard_map/ppermute | solution.py:44
  15.8 1.7 pair_up.1.refs_6_
  17.5 1.7 collective-permute-start.4
  26.8 1.8 copy.40.refs_10_
  34.9 5.2 %project.1 = (bf16[1024,768]{1,0:T(8,128)(2,1)}, bf16[1024,192]{1,0:T(8,128)(2,1)}, bf16[1024,192]{1,0:T(8,128)(2,1)}, bf16[1024,192]{1,0:T(8,128)(2,1)}, bf16[7...) custom-call(s32[2]{0:T(128)} %pad_add_fusion.2.refs_0_.me_ref.place_, ...), custom_call_target="tpu_custom_call", output_to_operand_aliasing={{8}: (10, {})} | custom-call | flops 10000000 | bytes 10000 | tf_op jit(solution)/shard_map/project/pallas_call | solution.py:67
  42.5 2.6 collective-permute-start.13
  46.4 11.5 %attend.1 = (bf16[256,192]{1,0:T(8,128)(2,1)}, bf16[256,192]{1,0:T(8,128)(2,1)}, bf16[256,192]{1,0:T(8,128)(2,1)}, bf16[256,192]{1,0:T(8,128)(2,1)}) custom-call(s32[2]{0:T(128)} %pad_add_fusion.2.refs_0_.me_ref.place_ref, bf16[1024,192]{1,0:T(8,128)(2,1)} %get-tuple-element.109.refs_1_, bf16[1024,192]{1,0:T(8,128)(2,1)} %get-tuple-element.110.refs_2_, ...), custom_call_target="tpu_custom_call" | custom-call | flops 10000000 | bytes 10000 | tf_op jit(solution)/shard_map/attend/pallas_call | solution.py:67
  61.7 4.2 %collective-permute-done.8.refs_6_.refs_18_ = bf16[256,192]{1,0:T(8,128)(2,1)} collective-permute-done((bf16[256,192]{1,0:T(8,128)(2,1)}, bf16[256,192]{1,0:T(8,128)(2,1)}, u32[]{:S(2)}, u32[]{:S(2)}) %collective-permute-start.8) | collective-permute-done | bytes 98336 | tf_op jit(solution)/shard_map/ppermute | solution.py:44
  65.9 1.9 collective-permute-done.9.refs_7_.refs_19_
  67.8 3.9 %middle.1 = (f32[256,768]{1,0:T(8,128)}, bf16[256,768]{1,0:T(8,128)(2,1)}, f32[256,128]{1,0:T(8,128)}, bf16[128,768]{1,0:T(8,128)(2,1)}, bf16[128,768]{1,0:T(8,1...) custom-call(bf16[256,768]{1,0:T(8,128)(2,1)} %refs_0_.4, f32[1,768]{1,0:T(1,128)} %reshape.191.refs_1_.refs_4_, ...), custom_call_target="tpu_custom_call" | custom-call | flops 10000000 | bytes 10000 | tf_op jit(solution)/shard_map/middle/pallas_call | solution.py:67
  72.0 2.8 grads_to_slots.1
  78.3 14.4 %collective-permute-done.14.refs_0_ = bf16[256,768]{1,0:T(8,128)(2,1)} collective-permute-done((bf16[256,768]{1,0:T(8,128)(2,1)}, bf16[256,768]{1,0:T(8,128)(2,1)}, u32[]{:S(2)}, u32[]{:S(2)}) %collective-permute-start.14) | collective-permute-done | bytes 393248 | tf_op jit(solution)/shard_map/ppermute | solution.py:44
  92.8 2.1 far_to_slots.1
  96.4 2.0 collective-permute-start.18
  99.9 5.8 %collective-permute-done.16.refs_1_ = bf16[128,768]{1,0:T(8,128)(2,1)} collective-permute-done((bf16[128,768]{1,0:T(8,128)(2,1)}, bf16[128,768]{1,0:T(8,128)(2,1)}, u32[]{:S(2)}, u32[]{:S(2)}) %collective-permute-start.16) | collective-permute-done | bytes 196640 | tf_op jit(solution)/shard_map/ppermute | solution.py:44
  105.7 12.4 %experts_forward0.1 = (bf16[512,3072]{1,0:T(8,128)(2,1)}, bf16[512,3072]{1,0:T(8,128)(2,1)}, bf16[512,768]{1,0:T(8,128)(2,1)}, bf16[512,768]{1,0:T(8,128)(2,1)}, f32[512,128]{1,0:T(8,128)}) custom-call(s32[2]{0:T(128)} %pad_add_fusion.2.refs_0_.me_ref.place_ref, bf16[768,3072]{1,0:T(8,128)(2,1)} %bitcast.48, bf16[3072,768]{1,0:T(8,128)(2,1)} %bitcast.52, ...), custom_call_target="tpu_custom_call" | custom-call | flops 20000000000 | bytes 10000000 | tf_op jit(solution)/shard_map/experts_forward0/pallas_call | solution.py:468
  118.1 13.6 %experts_forward1.1 = (bf16[256,768]{1,0:T(8,128)(2,1)}, bf16[256,768]{1,0:T(8,128)(2,1)}, bf16[256,768]{1,0:T(8,128)(2,1)}, bf16[256,768]{1,0:T(8,128)(2,1)}, b...) custom-call(s32[2]{0:T(128)} %pad_add_fusion.2.refs_0_.me_ref.place_, ...), custom_call_target="tpu_custom_call" | custom-call | flops 10000000 | bytes 10000 | tf_op jit(solution)/shard_map/experts_forward1/pallas_call | solution.py:468
  133.2 2.0 collective-permute-start.23
  136.1 12.5 %experts_backward1.1 = (bf16[128,896]{1,0:T(8,128)(2,1)}, bf16[128,896]{1,0:T(8,128)(2,1)}, bf16[128,896]{1,0:T(8,128)(2,1)}, bf16[128,896]{1,0:T(8,128)(2,1)}, ...) custom-call(s32[2]{0:T(128)} %pad_add_fusion.2.refs_0_.me_ref.place_ref, ...), custom_call_target="tpu_custom_call" | custom-call | flops 10000000 | bytes 10000 | tf_op jit(solution)/shard_map/experts_backward1/pallas_call | solution.py:543
  149.3 2.0 collective-permute-start.29
  152.2 11.7 %experts_backward0.1 = (bf16[128,896]{1,0:T(8,128)(2,1)}, bf16[128,896]{1,0:T(8,128)(2,1)}, bf16[128,896]{1,0:T(8,128)(2,1)}, bf16[128,896]{1,0:T(8,128)(2,1)}, bf16[512,3072]{1,0:T(8,128)(2,1)}) custom-call(s32[2]{0:T(128)} %pad_add_fusion.2.refs_0_.me_ref.place_ref, bf16[768,3072]{1,0:T(8,128)(2,1)} %bitcast.51, bf16[3072,768]{1,0:T(8,128)(2,1)} %bitcast.55, ...), custom_call_target="tpu_custom_call" | custom-call | flops 20000000000 | bytes 10000000 | tf_op jit(solution)/shard_map/experts_backward0/pallas_call | solution.py:543
  164.0 2.7 back_from_slots.1
  167.5 1.8 collective-permute-start.32
  170.4 19.8 %expert_weight_grads.1 = (bf16[3072,768]{1,0:T(8,128)(2,1)}, f32[3072,768]{1,0:T(8,128)}) custom-call(s32[2]{0:T(128)} %pad_add_fusion.2.refs_0_.me_ref.place_ref, bf16[512,768]{1,0:T(8,128)(2,1)} %get-tuple-element.159.refs_0_, bf16[512,768]{1,0:T(8,128)(2,1)} %get-tuple-element.160.refs_1_, bf16[512,3072]{1,0:T(8,128)(2,1)} %get-tuple-element.161.refs_2_, ...), custom_call_target="tpu_custom_call" | custom-call | flops 20000000000 | bytes 10000000 | tf_op jit(solution)/shard_map/expert_weight_grads/pallas_call | solution.py:689
  190.2 6.9 %home.1 = (bf16[256,192]{1,0:T(8,128)(2,1)}, bf16[256,192]{1,0:T(8,128)(2,1)}, bf16[256,192]{1,0:T(8,128)(2,1)}, bf16[256,192]{1,0:T(8,128)(2,1)}, f32[256,768]{...) custom-call(s32[8,256]{1,0:T(8,128)} %pad.24.refs_3_.refs_1_.refs_0_, ...), custom_call_target="tpu_custom_call", output_to_operand_aliasing={{9}: (20, {})} | custom-call | flops 10000000 | bytes 10000 | tf_op jit(solution)/shard_map/home/pallas_call | solution.py:67
  199.2 5.2 %collective-permute-done.36.refs_0_.refs_9_ = bf16[256,192]{1,0:T(8,128)(2,1)} collective-permute-done((bf16[256,192]{1,0:T(8,128)(2,1)}, bf16[256,192]{1,0:T(8,128)(2,1)}, u32[]{:S(2)}, u32[]{:S(2)}) %collective-permute-start.36) | collective-permute-done | bytes 98336 | tf_op jit(solution)/shard_map/ppermute | solution.py:44
  206.4 4.9 %far_sums.1 = (bf16[448,768]{1,0:T(8,128)(2,1)}, bf16[512,768]{1,0:T(8,128)(2,1)}, bf16[768,768]{1,0:T(8,128)(2,1)}) custom-call(bf16[3072,768]{1,0:T(8,128)(2,1)} %collective-permute-done.38.near_in.near_out, bf16[3072,768]{1,0:T(8,128)(2,1)} %collective-permute-done.38.near_in.near_out, f32[3072,768]{1,0:T(8,128)} %get-tuple-element.172.base_in.base_out, ...), custom_call_target="tpu_custom_call" | custom-call | flops 10000000 | bytes 10000 | tf_op jit(solution)/shard_map/far_sums/pallas_call | solution.py:735
  215.4 16.1 %attend_back.1 = (bf16[1024,192]{1,0:T(8,128)(2,1)}, bf16[1024,192]{1,0:T(8,128)(2,1)}, bf16[1024,192]{1,0:T(8,128)(2,1)}, f32[8,640]{1,0:T(8,128)}) custom-call(s32[2]{0:T(128)} %pad_add_fusion.2.refs_0_.me_ref.place_ref, bf16[1024,192]{1,0:T(8,128)(2,1)} %get-tuple-element.109.refs_1_, bf16[1024,192]{1,0:T(8,128)(2,1)} %get-tuple-element.110.refs_2_, ...), custom_call_target="tpu_custom_call" | custom-call | flops 10000000 | bytes 10000 | tf_op jit(solution)/shard_map/attend_back/pallas_call | solution.py:67
  231.5 2.2 convert_add_fusion.refs_8_
  233.7 6.5 %input_grads.1 = (bf16[512,768]{1,0:T(8,128)(2,1)}, f32[256,768]{1,0:T(8,128)}, f32[256,768]{1,0:T(8,128)}, f32[24,768]{1,0:T(8,128)}, f32[192,768]{1,0:T(8,128)...) custom-call(s32[2]{0:T(128)} %pad_add_fusion.2.refs_0_.me_ref.place_ref, ...), custom_call_target="tpu_custom_call" | custom-call | flops 10000000 | bytes 10000 | tf_op jit(solution)/shard_map/input_grads/pallas_call | solution.py:67
  240.9 1.8 collective-permute-start.45
  243.8 3.4 %result_from_slots.1 = (f32[256,768]{1,0:T(8,128)}, bf16[256,768]{1,0:T(8,128)(2,1)}) custom-call(bf16[256,768]{1,0:T(8,128)(2,1)} %get-tuple-element.133.refs_0_, bf16[256,768]{1,0:T(8,128)(2,1)} %collective-permute-done.22.refs_8_.refs_1_, bf16[256,768]{1,0:T(8,128)(2,1)} %collective-permute-done.23.refs_9_.refs_2_, ...), custom_call_target="tpu_custom_call" | custom-call | flops 10000000 | bytes 10000 | tf_op jit(solution)/shard_map/result_from_slots/pallas_call | solution.py:67
  247.1 2.7 collective-permute-start.41
  249.8 8.5 %collective-permute-done.45.refs_2_ = bf16[192,768]{1,0:T(8,128)(2,1)} collective-permute-done((bf16[192,768]{1,0:T(8,128)(2,1)}, bf16[192,768]{1,0:T(8,128)(2,1)}, u32[]{:S(2)}, u32[]{:S(2)}) %collective-permute-start.45) | collective-permute-done | bytes 294944 | tf_op jit(solution)/shard_map/ppermute | solution.py:44
  258.4 7.3 %collective-permute-done.46.refs_3_ = bf16[192,768]{1,0:T(8,128)(2,1)} collective-permute-done((bf16[192,768]{1,0:T(8,128)(2,1)}, bf16[192,768]{1,0:T(8,128)(2,1)}, u32[]{:S(2)}, u32[]{:S(2)}) %collective-permute-start.46) | collective-permute-done | bytes 294944 | tf_op jit(solution)/shard_map/ppermute | solution.py:44
  265.7 2.2 fold_weights.1
  268.1 4.3 %collective-permute-done.48 = f32[24,768]{1,0:T(8,128)S(1)} collective-permute-done((f32[24,768]{1,0:T(8,128)}, f32[24,768]{1,0:T(8,128)S(1)}, u32[]{:S(2)}, u32[]{:S(2)}) %collective-permute-start.48) | collective-permute-done | bytes 73760 | tf_op jit(solution)/shard_map/ppermute | solution.py:44
  273.4 4.3 %collective-permute-done.49 = f32[24,768]{1,0:T(8,128)S(1)} collective-permute-done((f32[24,768]{1,0:T(8,128)S(1)}, f32[24,768]{1,0:T(8,128)S(1)}, u32[]{:S(2)}, u32[]{:S(2)}) %collective-permute-start.49) | collective-permute-done | bytes 73760 | tf_op jit(solution)/shard_map/ppermute | solution.py:44
  278.5 1.8 slice.95
  280.3 2.3 collective-permute-start.53
  284.0 2.4 add_convert_fusion.1
  286.3 4.6 %collective-permute-done.53.refs_1_ = bf16[96,768]{1,0:T(8,128)(2,1)} collective-permute-done((bf16[96,768]{1,0:T(8,128)(2,1)}, bf16[96,768]{1,0:T(8,128)(2,1)}, u32[]{:S(2)}, u32[]{:S(2)}) %collective-permute-start.53) | collective-permute-done | bytes 147488 | tf_op jit(solution)/shard_map/ppermute | solution.py:44
  290.9 1.8 split_weights.1
  295.3 6.6 %add_bitcast_fusion = (f32[1,768,768]{2,1,0:T(8,128)}, f32[1,768,768]{2,1,0:T(8,128)}) fusion(bf16[768,768]{1,0:T(8,128)(2,1)} %collective-permute-done.54, f32[3072,768]{1,0:T(8,128)} %get-tuple-element.172.base_in.base_out, bf16[3072,768]{1,0:T(8,128)(2,1)} %collective-permute-done.38.near_in.near_out, bf16[512,768]{1,0:T(8,128)(2,1)} %collective-permute-done.47.refs_5_, ...), kind=kLoop, calls=%fused_computation | loop fusion | flops 6488064 | bytes 14155776 | tf_op jit(solution)/shard_map/broadcast_in_dim | solution.py:1171
  305.5 8.1 %collective-permute-done.43 = bf16[256,768]{1,0:T(8,128)(2,1)S(1)} collective-permute-done((bf16[256,768]{1,0:T(8,128)(2,1)S(1)}, bf16[256,768]{1,0:T(8,128)(2,1)S(1)}, u32[]{:S(2)}, u32[]{:S(2)}) %collective-permute-start.43) | collective-permute-done | bytes 393248 | tf_op jit(solution)/shard_map/ppermute | solution.py:44
  315.0 2.1 fusion.5
  (135 shorter events, 61.2 us)
Async XLA Ops:
  0.6 15.2 %collective-permute-start = (bf16[256,768]{1,0:T(8,128)(2,1)}, bf16[256,768]{1,0:T(8,128)(2,1)}, u32[]{:S(2)}, u32[]{:S(2)}) collective-permute-start(bf16[256,768]{1,0:T(8,128)(2,1)} %refs_0_.4), channel_id=1, source_target_pairs={{0,1},{1,0},{2,3},{3,2},{4,5},{5,4},{6,7},{7,6},{8,9},{9,8},{10,11... | collective-permute-start | bytes 1179656 | tf_op jit(solution)/shard_map/ppermute | solution.py:44
  1.2 12.6 %collective-permute-start.1 = (bf16[256,768]{1,0:T(8,128)(2,1)}, bf16[256,768]{1,0:T(8,128)(2,1)}, u32[]{:S(2)}, u32[]{:S(2)}) collective-permute-start(bf16[256,768]{1,0:T(8,128)(2,1)} %refs_0_.4), channel_id=1, source_target_pairs={{0,2},{1,3},{2,0},{3,1},{4,6},{5,7},{6,4},{7,5},{8,10},{9,11},{10,... | collective-permute-start | bytes 1179656 | tf_op jit(solution)/shard_map/ppermute | solution.py:44
  5.5 10.4 %collective-permute-start.3 = (bf16[96,768]{1,0:T(8,128)(2,1)}, bf16[96,768]{1,0:T(8,128)(2,1)}, u32[]{:S(2)}, u32[]{:S(2)}) collective-permute-start(bf16[96,768]{1,0:T(8,128)(2,1)} %pack_weights.1.refs_0_), channel_id=1, source_target_pairs={{0,16},{4,20},{8,24},{12,28},{16,0},{20,4},{24,8},{28,12},{1,17},{... | collective-permute-start | bytes 442376 | tf_op jit(solution)/shard_map/ppermute | solution.py:44
  8.0 33.7 %collective-permute-start.15 = (s32[256,2]{0,1:T(2,128)}, s32[256,2]{0,1:T(2,128)}, u32[]{:S(2)}, u32[]{:S(2)}) collective-permute-start(s32[256,2]{0,1:T(2,128)} %param.28), channel_id=1, source_target_pairs={{0,16},{4,20},{8,24},{12,28},{16,0},{20,4},{24,8},{28,12},{1,17},{... | collective-permute-start | bytes 6152 | tf_op jit(solution)/shard_map/ppermute | solution.py:44
  13.8 21.1 %collective-permute-start.2 = (bf16[256,768]{1,0:T(8,128)(2,1)}, bf16[256,768]{1,0:T(8,128)(2,1)}, u32[]{:S(2)}, u32[]{:S(2)}) collective-permute-start(bf16[256,768]{1,0:T(8,128)(2,1)} %collective-permute-done.1.refs_3_.refs_4_), channel_id=1, source_target_pairs={{0,1},{1,0},{2,3},{3,2},{4,5},{5,4},{6,7},{7,6},{8,9},{9,8},{10,11... | collective-permute-start | bytes 1179656 | tf_op jit(solution)/shard_map/ppermute | solution.py:44
  17.5 16.0 %collective-permute-start.4 = (bf16[192,768]{1,0:T(8,128)(2,1)}, bf16[192,768]{1,0:T(8,128)(2,1)}, u32[]{:S(2)}, u32[]{:S(2)}) collective-permute-start(bf16[192,768]{1,0:T(8,128)(2,1)} %pair_up.1.refs_6_), channel_id=1, source_target_pairs={{0,4},{4,0},{8,12},{12,8},{16,20},{20,16},{24,28},{28,24},{1,5},{5... | collective-permute-start | bytes 884744 | tf_op jit(solution)/shard_map/ppermute | solution.py:44
  19.3 14.3 %collective-permute-start.5 = (bf16[192,768]{1,0:T(8,128)(2,1)}, bf16[192,768]{1,0:T(8,128)(2,1)}, u32[]{:S(2)}, u32[]{:S(2)}) collective-permute-start(bf16[192,768]{1,0:T(8,128)(2,1)} %pair_up.1.refs_6_), channel_id=1, source_target_pairs={{0,8},{4,12},{8,0},{12,4},{16,24},{20,28},{24,16},{28,20},{1,9},{5... | collective-permute-start | bytes 884744 | tf_op jit(solution)/shard_map/ppermute | solution.py:44
  20.8 14.0 %collective-permute-start.6 = (bf16[192,768]{1,0:T(8,128)(2,1)}, bf16[192,768]{1,0:T(8,128)(2,1)}, u32[]{:S(2)}, u32[]{:S(2)}) collective-permute-start(bf16[192,768]{1,0:T(8,128)(2,1)} %pair_up.1.refs_6_), channel_id=1, source_target_pairs={{0,12},{4,8},{8,4},{12,0},{16,28},{20,24},{24,20},{28,16},{1,13},{... | collective-permute-start | bytes 884744 | tf_op jit(solution)/shard_map/ppermute | solution.py:44
  40.1 18.3 %collective-permute-start.11 = (bf16[192,768]{1,0:T(8,128)(2,1)}, bf16[192,768]{1,0:T(8,128)(2,1)}, u32[]{:S(2)}, u32[]{:S(2)}) collective-permute-start(bf16[192,768]{1,0:T(8,128)(2,1)} %get-tuple-element.116.refs_8_.refs_12_), channel_id=1, source_target_pairs={{0,2},{1,3},{2,0},{3,1},{4,6},{5,7},{6,4},{7,5},{8,10},{9,11},{10,... | collective-permute-start | bytes 884744 | tf_op jit(solution)/shard_map/ppermute | solution.py:44
  42.5 25.3 %collective-permute-start.13 = (bf16[256,768]{1,0:T(8,128)(2,1)}, bf16[256,768]{1,0:T(8,128)(2,1)}, u32[]{:S(2)}, u32[]{:S(2)}) collective-permute-start(bf16[256,768]{1,0:T(8,128)(2,1)} %get-tuple-element.117), channel_id=1, source_target_pairs={{0,16},{4,20},{8,24},{12,28},{16,0},{20,4},{24,8},{28,12},{1,17},{... | collective-permute-start | bytes 1179656 | tf_op jit(solution)/shard_map/ppermute | solution.py:44
  46.4 21.4 %collective-permute-start.10 = (bf16[192,768]{1,0:T(8,128)(2,1)}, bf16[192,768]{1,0:T(8,128)(2,1)}, u32[]{:S(2)}, u32[]{:S(2)}) collective-permute-start(bf16[192,768]{1,0:T(8,128)(2,1)} %get-tuple-element.116.refs_8_.refs_12_), channel_id=1, source_target_pairs={{0,1},{1,0},{2,3},{3,2},{4,5},{5,4},{6,7},{7,6},{8,9},{9,8},{10,11... | collective-permute-start | bytes 884744 | tf_op jit(solution)/shard_map/ppermute | solution.py:44
  58.4 9.4 %collective-permute-start.12 = (bf16[192,768]{1,0:T(8,128)(2,1)}, bf16[192,768]{1,0:T(8,128)(2,1)}, u32[]{:S(2)}, u32[]{:S(2)}) collective-permute-start(bf16[192,768]{1,0:T(8,128)(2,1)} %collective-permute-done.11.refs_10_.refs_14_), channel_id=1, source_target_pairs={{0,1},{1,0},{2,3},{3,2},{4,5},{5,4},{6,7},{7,6},{8,9},{9,8},{10,11... | collective-permute-start | bytes 884744 | tf_op jit(solution)/shard_map/ppermute | solution.py:44
  59.8 8.0 %collective-permute-start.9 = (bf16[256,192]{1,0:T(8,128)(2,1)}, bf16[256,192]{1,0:T(8,128)(2,1)}, u32[]{:S(2)}, u32[]{:S(2)}) collective-permute-start(bf16[256,192]{1,0:T(8,128)(2,1)} %get-tuple-element.115), channel_id=1, source_target_pairs={{0,3},{1,2},{2,1},{3,0},{4,7},{5,6},{6,5},{7,4},{8,11},{9,10},{10,... | collective-permute-start | bytes 294920 | tf_op jit(solution)/shard_map/ppermute | solution.py:44
  71.7 21.1 %collective-permute-start.14 = (bf16[256,768]{1,0:T(8,128)(2,1)}, bf16[256,768]{1,0:T(8,128)(2,1)}, u32[]{:S(2)}, u32[]{:S(2)}) collective-permute-start(bf16[256,768]{1,0:T(8,128)(2,1)} %get-tuple-element.119.refs_6_), channel_id=1, source_target_pairs={{0,16},{4,20},{8,24},{12,28},{16,0},{20,4},{24,8},{28,12},{1,17},{... | collective-permute-start | bytes 1179656 | tf_op jit(solution)/shard_map/ppermute | solution.py:44
  74.8 21.6 %collective-permute-start.19 = (bf16[128,768]{1,0:T(8,128)(2,1)}, bf16[128,768]{1,0:T(8,128)(2,1)}, u32[]{:S(2)}, u32[]{:S(2)}) collective-permute-start(bf16[128,768]{1,0:T(8,128)(2,1)} %get-tuple-element.128), channel_id=1, source_target_pairs={{0,4},{4,0},{8,12},{12,8},{16,20},{20,16},{24,28},{28,24},{1,5},{5... | collective-permute-start | bytes 589832 | tf_op jit(solution)/shard_map/ppermute | solution.py:44
  76.3 22.1 %collective-permute-start.20 = (bf16[128,768]{1,0:T(8,128)(2,1)}, bf16[128,768]{1,0:T(8,128)(2,1)}, u32[]{:S(2)}, u32[]{:S(2)}) collective-permute-start(bf16[128,768]{1,0:T(8,128)(2,1)} %get-tuple-element.129), channel_id=1, source_target_pairs={{0,8},{4,12},{8,0},{12,4},{16,24},{20,28},{24,16},{28,20},{1,9},{5... | collective-permute-start | bytes 589832 | tf_op jit(solution)/shard_map/ppermute | solution.py:44
  77.9 22.0 %collective-permute-start.21 = (bf16[128,768]{1,0:T(8,128)(2,1)}, bf16[128,768]{1,0:T(8,128)(2,1)}, u32[]{:S(2)}, u32[]{:S(2)}) collective-permute-start(bf16[128,768]{1,0:T(8,128)(2,1)} %get-tuple-element.130), channel_id=1, source_target_pairs={{0,12},{4,8},{8,4},{12,0},{16,28},{20,24},{24,20},{28,16},{1,13},{... | collective-permute-start | bytes 589832 | tf_op jit(solution)/shard_map/ppermute | solution.py:44
  94.9 10.8 %collective-permute-start.16 = (bf16[128,768]{1,0:T(8,128)(2,1)}, bf16[128,768]{1,0:T(8,128)(2,1)}, u32[]{:S(2)}, u32[]{:S(2)}) collective-permute-start(bf16[128,768]{1,0:T(8,128)(2,1)} %get-tuple-element.124), channel_id=1, source_target_pairs={{0,4},{4,0},{8,12},{12,8},{16,20},{20,16},{24,28},{28,24},{1,5},{5... | collective-permute-start | bytes 589832 | tf_op jit(solution)/shard_map/ppermute | solution.py:44
  96.4 21.7 %collective-permute-start.17 = (bf16[128,768]{1,0:T(8,128)(2,1)}, bf16[128,768]{1,0:T(8,128)(2,1)}, u32[]{:S(2)}, u32[]{:S(2)}) collective-permute-start(bf16[128,768]{1,0:T(8,128)(2,1)} %get-tuple-element.125), channel_id=1, source_target_pairs={{0,8},{4,12},{8,0},{12,4},{16,24},{20,28},{24,16},{28,20},{1,9},{5... | collective-permute-start | bytes 589832 | tf_op jit(solution)/shard_map/ppermute | solution.py:44
  96.4 21.7 %collective-permute-start.18 = (bf16[128,768]{1,0:T(8,128)(2,1)}, bf16[128,768]{1,0:T(8,128)(2,1)}, u32[]{:S(2)}, u32[]{:S(2)}) collective-permute-start(bf16[128,768]{1,0:T(8,128)(2,1)} %get-tuple-element.126), channel_id=1, source_target_pairs={{0,12},{4,8},{8,4},{12,0},{16,28},{20,24},{24,20},{28,16},{1,13},{... | collective-permute-start | bytes 589832 | tf_op jit(solution)/shard_map/ppermute | solution.py:44
  98.4 36.8 %collective-permute-start.25 = (bf16[256,768]{1,0:T(8,128)(2,1)}, bf16[256,768]{1,0:T(8,128)(2,1)}, u32[]{:S(2)}, u32[]{:S(2)}) collective-permute-start(bf16[256,768]{1,0:T(8,128)(2,1)} %get-tuple-element.143), channel_id=1, source_target_pairs={{0,4},{4,0},{8,12},{12,8},{16,20},{20,16},{24,28},{28,24},{1,5},{5... | collective-permute-start | bytes 1179656 | tf_op jit(solution)/shard_map/ppermute | solution.py:44
  99.9 36.3 %collective-permute-start.26 = (bf16[256,768]{1,0:T(8,128)(2,1)}, bf16[256,768]{1,0:T(8,128)(2,1)}, u32[]{:S(2)}, u32[]{:S(2)}) collective-permute-start(bf16[256,768]{1,0:T(8,128)(2,1)} %get-tuple-element.144), channel_id=1, source_target_pairs={{0,8},{4,12},{8,0},{12,4},{16,24},{20,28},{24,16},{28,20},{1,9},{5... | collective-permute-start | bytes 1179656 | tf_op jit(solution)/shard_map/ppermute | solution.py:44
  105.7 30.5 %collective-permute-start.27 = (bf16[256,768]{1,0:T(8,128)(2,1)}, bf16[256,768]{1,0:T(8,128)(2,1)}, u32[]{:S(2)}, u32[]{:S(2)}) collective-permute-start(bf16[256,768]{1,0:T(8,128)(2,1)} %get-tuple-element.145), channel_id=1, source_target_pairs={{0,12},{4,8},{8,4},{12,0},{16,28},{20,24},{24,20},{28,16},{1,13},{... | collective-permute-start | bytes 1179656 | tf_op jit(solution)/shard_map/ppermute | solution.py:44
  131.7 19.6 %collective-permute-start.22 = (bf16[256,768]{1,0:T(8,128)(2,1)}, bf16[256,768]{1,0:T(8,128)(2,1)}, u32[]{:S(2)}, u32[]{:S(2)}) collective-permute-start(bf16[256,768]{1,0:T(8,128)(2,1)} %get-tuple-element.134), channel_id=1, source_target_pairs={{0,4},{4,0},{8,12},{12,8},{16,20},{20,16},{24,28},{28,24},{1,5},{5... | collective-permute-start | bytes 1179656 | tf_op jit(solution)/shard_map/ppermute | solution.py:44
  133.2 30.7 %collective-permute-start.23 = (bf16[256,768]{1,0:T(8,128)(2,1)}, bf16[256,768]{1,0:T(8,128)(2,1)}, u32[]{:S(2)}, u32[]{:S(2)}) collective-permute-start(bf16[256,768]{1,0:T(8,128)(2,1)} %get-tuple-element.135), channel_id=1, source_target_pairs={{0,8},{4,12},{8,0},{12,4},{16,24},{20,28},{24,16},{28,20},{1,9},{5... | collective-permute-start | bytes 1179656 | tf_op jit(solution)/shard_map/ppermute | solution.py:44
  135.2 28.7 %collective-permute-start.24 = (bf16[256,768]{1,0:T(8,128)(2,1)}, bf16[256,768]{1,0:T(8,128)(2,1)}, u32[]{:S(2)}, u32[]{:S(2)}) collective-permute-start(bf16[256,768]{1,0:T(8,128)(2,1)} %get-tuple-element.136), channel_id=1, source_target_pairs={{0,12},{4,8},{8,4},{12,0},{16,28},{20,24},{24,20},{28,16},{1,13},{... | collective-permute-start | bytes 1179656 | tf_op jit(solution)/shard_map/ppermute | solution.py:44
  148.7 15.3 %collective-permute-start.28 = (bf16[128,896]{1,0:T(8,128)(2,1)}, bf16[128,896]{1,0:T(8,128)(2,1)}, u32[]{:S(2)}, u32[]{:S(2)}) collective-permute-start(bf16[128,896]{1,0:T(8,128)(2,1)} %get-tuple-element.149), channel_id=1, source_target_pairs={{0,4},{4,0},{8,12},{12,8},{16,20},{20,16},{24,28},{28,24},{1,5},{5... | collective-permute-start | bytes 688136 | tf_op jit(solution)/shard_map/ppermute | solution.py:44
  149.3 14.7 %collective-permute-start.29 = (bf16[128,896]{1,0:T(8,128)(2,1)}, bf16[128,896]{1,0:T(8,128)(2,1)}, u32[]{:S(2)}, u32[]{:S(2)}) collective-permute-start(bf16[128,896]{1,0:T(8,128)(2,1)} %get-tuple-element.150), channel_id=1, source_target_pairs={{0,8},{4,12},{8,0},{12,4},{16,24},{20,28},{24,16},{28,20},{1,9},{5... | collective-permute-start | bytes 688136 | tf_op jit(solution)/shard_map/ppermute | solution.py:44
  151.3 12.7 %collective-permute-start.30 = (bf16[128,896]{1,0:T(8,128)(2,1)}, bf16[128,896]{1,0:T(8,128)(2,1)}, u32[]{:S(2)}, u32[]{:S(2)}) collective-permute-start(bf16[128,896]{1,0:T(8,128)(2,1)} %get-tuple-element.151), channel_id=1, source_target_pairs={{0,12},{4,8},{8,4},{12,0},{16,28},{20,24},{24,20},{28,16},{1,13},{... | collective-permute-start | bytes 688136 | tf_op jit(solution)/shard_map/ppermute | solution.py:44
  166.7 23.5 %collective-permute-start.31 = (bf16[128,896]{1,0:T(8,128)(2,1)}, bf16[128,896]{1,0:T(8,128)(2,1)}, u32[]{:S(2)}, u32[]{:S(2)}) collective-permute-start(bf16[128,896]{1,0:T(8,128)(2,1)} %get-tuple-element.155), channel_id=1, source_target_pairs={{0,4},{4,0},{8,12},{12,8},{16,20},{20,16},{24,28},{28,24},{1,5},{5... | collective-permute-start | bytes 688136 | tf_op jit(solution)/shard_map/ppermute | solution.py:44
  167.5 22.7 %collective-permute-start.32 = (bf16[128,896]{1,0:T(8,128)(2,1)}, bf16[128,896]{1,0:T(8,128)(2,1)}, u32[]{:S(2)}, u32[]{:S(2)}) collective-permute-start(bf16[128,896]{1,0:T(8,128)(2,1)} %get-tuple-element.156), channel_id=1, source_target_pairs={{0,8},{4,12},{8,0},{12,4},{16,24},{20,28},{24,16},{28,20},{1,9},{5... | collective-permute-start | bytes 688136 | tf_op jit(solution)/shard_map/ppermute | solution.py:44
  169.3 20.9 %collective-permute-start.33 = (bf16[128,896]{1,0:T(8,128)(2,1)}, bf16[128,896]{1,0:T(8,128)(2,1)}, u32[]{:S(2)}, u32[]{:S(2)}) collective-permute-start(bf16[128,896]{1,0:T(8,128)(2,1)} %get-tuple-element.157), channel_id=1, source_target_pairs={{0,12},{4,8},{8,4},{12,0},{16,28},{20,24},{24,20},{28,16},{1,13},{... | collective-permute-start | bytes 688136 | tf_op jit(solution)/shard_map/ppermute | solution.py:44
  170.2 20.0 %collective-permute-start.34 = (bf16[256,896]{1,0:T(8,128)(2,1)}, bf16[256,896]{1,0:T(8,128)(2,1)}, u32[]{:S(2)}, u32[]{:S(2)}) collective-permute-start(bf16[256,896]{1,0:T(8,128)(2,1)} %get-tuple-element.158), channel_id=1, source_target_pairs={{0,16},{4,20},{8,24},{12,28},{16,0},{20,4},{24,8},{28,12},{1,17},{... | collective-permute-start | bytes 1376264 | tf_op jit(solution)/shard_map/ppermute | solution.py:44
  197.2 9.2 %collective-permute-start.38 = (bf16[3072,768]{1,0:T(8,128)(2,1)}, bf16[3072,768]{1,0:T(8,128)(2,1)}, u32[]{:S(2)}, u32[]{:S(2)}) collective-permute-start(bf16[3072,768]{1,0:T(8,128)(2,1)} %get-tuple-element.171), channel_id=1, source_target_pairs={{0,1},{1,0},{2,3},{3,2},{4,5},{5,4},{6,7},{7,6},{8,9},{9,8},{10,11... | collective-permute-start | bytes 14155784 | tf_op jit(solution)/shard_map/ppermute | solution.py:44
  197.3 9.1 %collective-permute-start.39 = (bf16[384,768]{1,0:T(8,128)(2,1)}, bf16[384,768]{1,0:T(8,128)(2,1)}, u32[]{:S(2)}, u32[]{:S(2)}) collective-permute-start(bf16[384,768]{1,0:T(8,128)(2,1)} %get-tuple-element.173), channel_id=1, source_target_pairs={{0,1},{1,0},{2,3},{3,2},{4,5},{5,4},{6,7},{7,6},{8,9},{9,8},{10,11... | collective-permute-start | bytes 1769480 | tf_op jit(solution)/shard_map/ppermute | solution.py:44
  198.3 7.2 %collective-permute-start.37 = (bf16[256,192]{1,0:T(8,128)(2,1)}, bf16[256,192]{1,0:T(8,128)(2,1)}, u32[]{:S(2)}, u32[]{:S(2)}) collective-permute-start(bf16[256,192]{1,0:T(8,128)(2,1)} %get-tuple-element.170), channel_id=1, source_target_pairs={{0,3},{1,2},{2,1},{3,0},{4,7},{5,6},{6,5},{7,4},{8,11},{9,10},{10,... | collective-permute-start | bytes 294920 | tf_op jit(solution)/shard_map/ppermute | solution.py:44
  211.2 20.2 %collective-permute-start.40 = (bf16[448,768]{1,0:T(8,128)(2,1)}, bf16[448,768]{1,0:T(8,128)(2,1)}, u32[]{:S(2)}, u32[]{:S(2)}) collective-permute-start(bf16[448,768]{1,0:T(8,128)(2,1)} %get-tuple-element.175.refs_11_), channel_id=1, source_target_pairs={{0,2},{1,3},{2,0},{3,1},{4,6},{5,7},{6,4},{7,5},{8,10},{9,11},{10,... | collective-permute-start | bytes 2064392 | tf_op jit(solution)/shard_map/ppermute | solution.py:44
  211.8 35.3 %collective-permute-start.47 = (bf16[512,768]{1,0:T(8,128)(2,1)}, bf16[512,768]{1,0:T(8,128)(2,1)}, u32[]{:S(2)}, u32[]{:S(2)}) collective-permute-start(bf16[512,768]{1,0:T(8,128)(2,1)} %get-tuple-element.197), channel_id=1, source_target_pairs={{0,2},{1,3},{2,0},{3,1},{4,6},{5,7},{6,4},{7,5},{8,10},{9,11},{10,... | collective-permute-start | bytes 2359304 | tf_op jit(solution)/shard_map/ppermute | solution.py:44
  213.3 82.0 %collective-permute-start.54 = (bf16[768,768]{1,0:T(8,128)(2,1)}, bf16[768,768]{1,0:T(8,128)(2,1)}, u32[]{:S(2)}, u32[]{:S(2)}) collective-permute-start(bf16[768,768]{1,0:T(8,128)(2,1)} %get-tuple-element.205), channel_id=1, source_target_pairs={{0,2},{1,3},{2,0},{3,1},{4,6},{5,7},{6,4},{7,5},{8,10},{9,11},{10,... | collective-permute-start | bytes 3538952 | tf_op jit(solution)/shard_map/ppermute | solution.py:44
  240.2 9.6 %collective-permute-start.44 = (bf16[192,768]{1,0:T(8,128)(2,1)}, bf16[192,768]{1,0:T(8,128)(2,1)}, u32[]{:S(2)}, u32[]{:S(2)}) collective-permute-start(bf16[192,768]{1,0:T(8,128)(2,1)} %get-tuple-element.193), channel_id=1, source_target_pairs={{0,4},{4,0},{8,12},{12,8},{16,20},{20,16},{24,28},{28,24},{1,5},{5... | collective-permute-start | bytes 884744 | tf_op jit(solution)/shard_map/ppermute | solution.py:44
  240.9 17.5 %collective-permute-start.45 = (bf16[192,768]{1,0:T(8,128)(2,1)}, bf16[192,768]{1,0:T(8,128)(2,1)}, u32[]{:S(2)}, u32[]{:S(2)}) collective-permute-start(bf16[192,768]{1,0:T(8,128)(2,1)} %get-tuple-element.194), channel_id=1, source_target_pairs={{0,8},{4,12},{8,0},{12,4},{16,24},{20,28},{24,16},{28,20},{1,9},{5... | collective-permute-start | bytes 884744 | tf_op jit(solution)/shard_map/ppermute | solution.py:44
  242.6 23.1 %collective-permute-start.46 = (bf16[192,768]{1,0:T(8,128)(2,1)}, bf16[192,768]{1,0:T(8,128)(2,1)}, u32[]{:S(2)}, u32[]{:S(2)}) collective-permute-start(bf16[192,768]{1,0:T(8,128)(2,1)} %get-tuple-element.195), channel_id=1, source_target_pairs={{0,12},{4,8},{8,4},{12,0},{16,28},{20,24},{24,20},{28,16},{1,13},{... | collective-permute-start | bytes 884744 | tf_op jit(solution)/shard_map/ppermute | solution.py:44
  247.1 36.8 %collective-permute-start.41 = (bf16[256,768]{1,0:T(8,128)(2,1)}, bf16[256,768]{1,0:T(8,128)(2,1)}, u32[]{:S(2)}, u32[]{:S(2)}) collective-permute-start(bf16[256,768]{1,0:T(8,128)(2,1)} %get-tuple-element.188), channel_id=1, source_target_pairs={{0,16},{4,20},{8,24},{12,28},{16,0},{20,4},{24,8},{28,12},{1,17},{... | collective-permute-start | bytes 1179656 | tf_op jit(solution)/shard_map/ppermute | solution.py:44
  278.5 23.4 %collective-permute-start.42 = (bf16[512,768]{1,0:T(8,128)(2,1)}, bf16[512,768]{1,0:T(8,128)(2,1)}, u32[]{:S(2)}, u32[]{:S(2)}) collective-permute-start(bf16[512,768]{1,0:T(8,128)(2,1)} %get-tuple-element.190), channel_id=1, source_target_pairs={{0,1},{1,0},{2,3},{3,2},{4,5},{5,4},{6,7},{7,6},{8,9},{9,8},{10,11... | collective-permute-start | bytes 2359304 | tf_op jit(solution)/shard_map/ppermute | solution.py:44
  280.3 10.6 %collective-permute-start.53 = (bf16[96,768]{1,0:T(8,128)(2,1)}, bf16[96,768]{1,0:T(8,128)(2,1)}, u32[]{:S(2)}, u32[]{:S(2)}) collective-permute-start(bf16[96,768]{1,0:T(8,128)(2,1)} %get-tuple-element.200), channel_id=1, source_target_pairs={{0,16},{4,20},{8,24},{12,28},{16,0},{20,4},{24,8},{28,12},{1,17},{... | collective-permute-start | bytes 442376 | tf_op jit(solution)/shard_map/ppermute | solution.py:44
  284.0 8.8 %collective-permute-start.51 = (f32[24,768]{1,0:T(8,128)}, f32[24,768]{1,0:T(8,128)}, u32[]{:S(2)}, u32[]{:S(2)}) collective-permute-start(f32[24,768]{1,0:T(8,128)} %add.130), channel_id=1, source_target_pairs={{0,1},{1,0},{2,3},{3,2},{4,5},{5,4},{6,7},{7,6},{8,9},{9,8},{10,11... | collective-permute-start | bytes 221192 | tf_op jit(solution)/shard_map/ppermute | solution.py:44
  293.7 8.2 %collective-permute-start.52 = (f32[24,768]{1,0:T(8,128)S(1)}, f32[24,768]{1,0:T(8,128)S(1)}, u32[]{:S(2)}, u32[]{:S(2)}) collective-permute-start(f32[24,768]{1,0:T(8,128)S(1)} %add.131), channel_id=1, source_target_pairs={{0,2},{1,3},{2,0},{3,1},{4,6},{5,7},{6,4},{7,5},{8,10},{9,11},{10,... | collective-permute-start | bytes 221192 | tf_op jit(solution)/shard_map/ppermute | solution.py:44
  303.1 10.5 %collective-permute-start.43 = (bf16[256,768]{1,0:T(8,128)(2,1)S(1)}, bf16[256,768]{1,0:T(8,128)(2,1)S(1)}, u32[]{:S(2)}, u32[]{:S(2)}) collective-permute-start(bf16[256,768]{1,0:T(8,128)(2,1)S(1)} %add_convert_fusion), channel_id=1, source_target_pairs={{0,2},{1,3},{2,0},{3,1},{4,6},{5,7},{6,4},{7,5},{8,10},{9,11},{10,... | collective-permute-start | bytes 1179656 | tf_op jit(solution)/shard_map/ppermute | solution.py:44
  (12 other events, 105.1 us)

commit v6 on v5

--- a/solution.py
+++ b/solution.py
@@ -51,8 +51,10 @@
 def call(
     kernel, name, operands, outs, scratch=(), scalars=None, after=(), through=(), cost=None
 ):
-    operands, outs = list(operands), list(outs)
-    in_specs = [whole(o.shape) for o in operands]
+    outs = list(outs)
+    pairs = [o if isinstance(o, tuple) else (o, o.shape[0]) for o in operands]
+    operands = [array for array, _ in pairs]
+    in_specs = [whole((rows,) + array.shape[1:]) for array, rows in pairs]
     out_specs = [whole(o.shape) for o in outs]
     if scalars is not None:
         operands = [scalars] + operands
@@ -352,7 +354,7 @@
     )
 
 
-def from_slots(name, blocks, slots, size, dtypes, after=(), through=()):
+def from_slots(name, blocks, slots, size, dtypes, after=(), through=(), cost=None):
     count, sets = len(blocks), len(slots)
     width = blocks[0].shape[1]
     rows = slots[0].shape[1]
@@ -374,6 +376,7 @@
         [shape((rows, width), dtype) for dtype in dtypes],
         after=after,
         through=through,
+        cost=cost,
     )
 
 
@@ -418,19 +421,22 @@
     return jnp.concatenate([ref[...] for ref in refs], axis=0)
 
 
-def experts_forward(name, place, w_in, w_out, w_router, x_blocks, experts, before, cost):
+def experts_forward(
+    name, place, w_in, w_out, w_router, x_blocks, experts, before, cost, through=()
+):
     width, units = w_in.shape
     count, size = len(x_blocks), x_blocks[0].shape[0]
     total, piece, chunk = size * count, 768, 256
     sets = 1 if before is None else 1 + len(before) // 2
     blocks = 0 if before is None else count
-    before = [] if before is None else list(before)
+    before, through = [] if before is None else list(before), list(through)
 
     def kernel(me_ref, w_in_ref, w_out_ref, router_ref, *refs):
         x_refs, refs = refs[:count], refs[count:]
-        before_refs, refs = refs[: len(before)], refs[len(before) :]
-        out_refs = refs[:blocks]
-        active_ref, slope_ref, x_all, result_ref, gates_ref, result_sum = refs[blocks:]
+        before_refs, refs = refs[: len(before)], refs[len(before) + len(through) :]
+        out_refs, refs = refs[:blocks], refs[blocks:]
+        active_ref, slope_ref, x_all, result_ref, gates_ref = refs[:5]
+        result_sum = refs[-1]
 
         @pl.when(pl.program_id(0) == 0)
         def _():
@@ -476,15 +482,23 @@
             whole(w_router.shape),
         ]
         + [whole(o.shape) for o in x_blocks]
-        + [whole(o.shape) for o in before],
+        + [whole(o.shape) for o in before]
+        + [pl.BlockSpec(memory_space=pl.ANY)] * len(through),
         out_specs=[whole(o.shape) for o in outs]
         + [columns] * 2
-        + [whole(o.shape) for o in kept],
-        out_shape=outs + [shape((total, units), bf16)] * 2 + kept,
+        + [whole(o.shape) for o in kept]
+        + [pl.BlockSpec(memory_space=pl.ANY)] * len(through),
+        out_shape=outs
+        + [shape((total, units), bf16)] * 2
+        + kept
+        + [shape(o.shape, o.dtype) for o in through],
+        input_output_aliases={
+            4 + count + len(before) + i: blocks + 5 + i for i in range(len(through))
+        },
         scratch_shapes=[pltpu.VMEM((total, width), f32)],
         compiler_params=limit(64),
         cost_estimate=cost,
-    )(place, w_in, w_out, w_router, *x_blocks, *before)
+    )(place, w_in, w_out, w_router, *x_blocks, *before, *through)
     return (list(flat[:blocks]), *flat[blocks:])
 
 
@@ -751,7 +765,7 @@
     proj_grads,
     normed,
     weights,
-    output_sum,
+    output_parts,
     gain,
     line_grad,
     bucket_hot,
@@ -770,12 +784,14 @@
     experts = router_grad.shape[0]
 
     def kernel(place_ref, *refs):
-        dq_ref, dk_ref, dv_ref, normed_ref, wq_ref, wk_ref, wv_ref, out_ref, gain_ref = refs[:9]
-        line_ref, hot_ref, ffn_gain_ref, router_ref = refs[9:13]
-        near_ref, base_ref, far_ref, small_ref, *weight_refs, sums = refs[13:]
+        dq_ref, dk_ref, dv_ref, normed_ref, wq_ref, wk_ref, wv_ref, gain_ref = refs[:8]
+        line_ref, hot_ref, ffn_gain_ref, router_ref = refs[8:12]
+        base_o_ref, near_o_ref, far_o_ref = refs[12:15]
+        near_ref, base_ref, far_ref, small_ref, *weight_refs, sums = refs[15:]
         for at, ref in enumerate((dq_ref, dk_ref, dv_ref)):
             sums[:, at * span : (at + 1) * span] = dot(normed_ref[...], ref[...], 0, 0)
-        sums[:, 3 * span :] = out_ref[...].T
+        output_sum = base_o_ref[...] + near_o_ref[...].astype(f32) + far_o_ref[...].astype(f32)
+        sums[:, 3 * span :] = output_sum.T
         if few:
             for r, ref in enumerate(weight_refs):
                 for i, far in enumerate((0, 4)):
@@ -816,7 +832,8 @@
         list(proj_grads)
         + [normed]
         + list(weights)
-        + [output_sum, gain, line_grad, bucket_hot, ffn_gain_grad, router_grad],
+        + [gain, line_grad, bucket_hot, ffn_gain_grad, router_grad]
+        + [(part, span) for part in output_parts],
         [
             shape((2 * rows, width), bf16),
             shape((rows, width), f32),
@@ -851,7 +868,7 @@
     )
 
 
-def split_weights(parts, span):
+def split_weights(parts, span, after):
     part = parts[0].shape[0]
 
     def kernel(*refs):
@@ -868,6 +885,7 @@
         "split_weights",
         parts,
         [shape((part, span), f32)] * 3 + [shape((span, part), f32)],
+        after=after,
     )
 
 
@@ -997,17 +1015,17 @@
         far = to_slots(
             "far_to_slots", [(far_input, slots[1])], blocks, size, through=held[1:]
         )
-        g_blocks = [held[0]] + [swap(far[blocks + r - 1], "dp", r) for r in (1, 2, 3)]
+        held = [held[0]] + list(far[blocks:])
         far = [far[0]] + [swap(far[r], "dp", r) for r in (1, 2, 3)]
         x_sets = [own, far]
     else:
         x_sets = [[all_to_all_dp(send[0])]]
         g_blocks = [all_to_all_dp(held[0])]
 
-    kept, before = [], []
+    kept, before, passed = [], [], list(held[1:])
     for at, x_blocks in enumerate(x_sets):
         last = at == len(x_sets) - 1
-        result, *held = experts_forward(
+        result, *state = experts_forward(
             "experts_forward" + str(at),
             place,
             w_in[0],
@@ -1017,9 +1035,13 @@
             experts,
             before if last else None,
             brief if last else long,
+            [] if last else passed,
         )
-        kept.append(held)
-        before = before + held[3:]
+        passed = passed if last else state[5:]
+        kept.append(state[:5])
+        before = before + list(state[3:5])
+    if few:
+        g_blocks = [held[0]] + [swap(passed[r - 1], "dp", r) for r in (1, 2, 3)]
     actives, slopes, arrived, plain, slot_gates = zip(*kept)
     sets = list(zip(slopes, plain, slot_gates))
     back, slot_grads, pre_grad = experts_backward(
@@ -1087,10 +1109,24 @@
     grad_out, homed = homed[:members], homed[members:]
     hidden_grad, ffn_gain_grad, router_grad, near_o, base_o, near_w = homed
     grad_in = [grad_out[0]] + [swap(grad_out[r], "mp", r) for r in range(1, members)]
+    if few:
+        own_result, far_result = from_slots(
+            "result_from_slots",
+            result_in,
+            slots,
+            size,
+            [f32, bf16],
+            after=[hidden_grad],
+            cost=long,
+        )
+        far_result = swap(far_result, "dp", 4)
+    else:
+        (own_result,) = from_slots("result_from_slots", result_in, slots, size, [f32])
+        far_result = own_result
     near_o, near_w = swap(near_o, "mp", 1), swap(near_w, "mp", 1)
     piece = w_in.shape[2] // members
     far_first, far_next, far_last = far_sums(
-        near_w, base_w, near_o, base_o, [rows, piece, 2 * piece], grad_in[2:]
+        near_w, base_w, near_o, base_o, [rows, piece, 2 * piece], grad_in[2:] + [own_result]
     )
 
     *proj_grads, line_grad = attend_back(
@@ -1108,13 +1144,12 @@
     far_first = swap(far_first, "mp", 2)
     far_next = swap(far_next, "mp", 2)
     far_last = swap(far_last, "mp", 2)
-    output_sum = base_o[:span] + near_o[:span].astype(f32) + far_first[:span].astype(f32)
     near, base, base_far, small, *weight_sums = input_grads(
         place,
         proj_grads,
         normed,
         (weight_q, weight_k, weight_v),
-        output_sum,
+        (base_o, near_o, far_first),
         gain_one,
         line_grad,
         bucket_hot,
@@ -1123,19 +1158,19 @@
         members,
         owners,
         heads,
-        [],
-    )
+        [far_result],
+    )
+    near = swap(near, "mp", 1)
+    far_normed = swap((base_far + near[rows:].astype(f32)).astype(bf16), "mp", 2)
     if few:
         arrived_sums = [swap(weight_sums[r], "dp", r) for r in (1, 2, 3)]
         own_sum, far_part, small = fold_weights(
-            weight_sums[0], arrived_sums, [far_next], [small]
+            weight_sums[0], arrived_sums, [far_next, near], [small]
         )
-        weight_grads = split_weights([own_sum, swap(far_part, "dp", 4)], span)
+        weight_grads = split_weights([own_sum, swap(far_part, "dp", 4)], span, [far_normed])
     else:
         joined_grad = lax.psum_scatter(weight_sums[0], "dp", scatter_dimension=0, tiled=True)
-        weight_grads = split_weights([joined_grad], span)
-    near = swap(near, "mp", 1)
-    far_normed = swap((base_far + near[rows:].astype(f32)).astype(bf16), "mp", 2)
+        weight_grads = split_weights([joined_grad], span, [far_normed])
     normed_grad = base + near[:rows].astype(f32) + far_normed.astype(f32)
     resid = tokens.astype(f32)
     _, inverse_one = normalize(resid, norm_gain)
@@ -1145,14 +1180,9 @@
         hidden_grad + inverse_one * scaled - resid * inverse_one * inverse_one * inverse_one * inner
     ).astype(bf16)
 
+    block_out = hidden + own_result
     if few:
-        own_result, far_result = from_slots(
-            "result_from_slots", result_in, slots, size, [f32, bf16], after=[base]
-        )
-        block_out = hidden + own_result + swap(far_result, "dp", 4).astype(f32)
-    else:
-        (own_result,) = from_slots("result_from_slots", result_in, slots, size, [f32])
-        block_out = hidden + own_result
+        block_out = block_out + far_result.astype(f32)
     block_out = block_out.astype(bf16)
     far_in = jnp.concatenate([far_first[span:], far_next], axis=0).astype(f32)
     w_in_grad = base_w[:piece] + near_w[:piece].astype(f32) + far_in

time: 319 us -> 300 us (0.940)
  waiting for transfers between devices: 76.5 us -> 58.8 us
  other arithmetic: 23.7 us -> 19.8 us
    ppermute x55, waiting for transfers between devices: 76.5 us -> 58.8 us  [swap(): return lax.ppermute(values, axis, [(i, i ^ step) for i in range(count)])]
  transfers between devices with their start and end apart: 55 -> 55, of which waited for: 16 -> 18; matrix products, arithmetic and copies ran while one was open for 12% -> 13% of each run, Pallas kernels for 39% -> 41%
where the time goes in v6:
time: 300 us; the launch traced here: 299 us
  Pallas kernels  144 us (48%)
  waiting for transfers between devices  58.8 us (20%)
  starting transfers between devices  55.6 us (19%)
  other arithmetic  19.8 us (7%)
  local copies, waits for them, and re-layouts  17.3 us (6%)
    pallas_call x14, Pallas kernels, call(): pl.pallas_call(body, name=name, grid=(1,), in_specs=in_specs + [pl.BlockS...  68.7 us
    ppermute x55, waiting for transfers between devices, swap(): return lax.ppermute(values, axis, [(i, i ^ step) for i in range(count)])  58.8 us
    ppermute x55, starting transfers between devices, swap(): return lax.ppermute(values, axis, [(i, i ^ step) for i in range(count)])  55.6 us
    pallas_call x2, Pallas kernels, experts_forward(): pl.pallas_call(kernel, name=name, grid=(units // piece,), in_specs=[pl.Bl...  26.2 us
    pallas_call x2, Pallas kernels, experts_backward(): pl.pallas_call(kernel, name=name, grid=(units // piece,), in_specs=[pl.Bl...  24.4 us
    pallas_call x1, Pallas kernels, expert_weight_grads(): pl.pallas_call(kernel, name='expert_weight_grads', grid_spec=pltpu.Prefet...  19.8 us
    broadcast_in_dim x1, other arithmetic, on_device(): w_out_grad[None]  6.42 us
  transfers between devices with their start and end apart: 55, of which 18 were waited for; matrix products, arithmetic and copies ran while one was open for 13% of the time, Pallas kernels for 41%

profile of v6, /device:TPU:0, one launch (start us, length us, event | category | flops | bytes accessed | tf_op | source)
XLA Modules:
  0.0 298.7 jit_solution(6547699286047493163)
XLA Ops:
  1.2 2.6 collective-permute-start.1
  5.5 2.6 collective-permute-start.3
  10.1 3.6 %collective-permute-done.1.refs_3_.refs_4_ = bf16[256,768]{1,0:T(8,128)(2,1)} collective-permute-done((bf16[256,768]{1,0:T(8,128)(2,1)}, bf16[256,768]{1,0:T(8,128)(2,1)}, u32[]{:S(2)}, u32[]{:S(2)}) %collective-permute-start.1) | collective-permute-done | bytes 393248 | tf_op jit(solution)/shard_map/ppermute | solution.py:44
  15.8 1.7 pair_up.1.refs_6_
  17.5 1.7 collective-permute-start.4
  26.7 1.8 copy.43.refs_10_
  31.0 1.7 copy.41.refs_4_
  34.9 5.2 %project.1 = (bf16[1024,768]{1,0:T(8,128)(2,1)}, bf16[1024,192]{1,0:T(8,128)(2,1)}, bf16[1024,192]{1,0:T(8,128)(2,1)}, bf16[1024,192]{1,0:T(8,128)(2,1)}, bf16[7...) custom-call(s32[2]{0:T(128)} %pad_add_fusion.2.refs_0_.me_ref.place_, ...), custom_call_target="tpu_custom_call", output_to_operand_aliasing={{8}: (10, {})} | custom-call | flops 10000000 | bytes 10000 | tf_op jit(solution)/shard_map/project/pallas_call | solution.py:69
  42.5 2.6 collective-permute-start.13
  46.4 11.5 %attend.1 = (bf16[256,192]{1,0:T(8,128)(2,1)}, bf16[256,192]{1,0:T(8,128)(2,1)}, bf16[256,192]{1,0:T(8,128)(2,1)}, bf16[256,192]{1,0:T(8,128)(2,1)}) custom-call(s32[2]{0:T(128)} %pad_add_fusion.2.refs_0_.me_ref.place_ref, bf16[1024,192]{1,0:T(8,128)(2,1)} %get-tuple-element.112.refs_1_, bf16[1024,192]{1,0:T(8,128)(2,1)} %get-tuple-element.113.refs_2_, ...), custom_call_target="tpu_custom_call" | custom-call | flops 10000000 | bytes 10000 | tf_op jit(solution)/shard_map/attend/pallas_call | solution.py:69
  61.8 4.2 %collective-permute-done.8.refs_6_.refs_18_ = bf16[256,192]{1,0:T(8,128)(2,1)} collective-permute-done((bf16[256,192]{1,0:T(8,128)(2,1)}, bf16[256,192]{1,0:T(8,128)(2,1)}, u32[]{:S(2)}, u32[]{:S(2)}) %collective-permute-start.8) | collective-permute-done | bytes 98336 | tf_op jit(solution)/shard_map/ppermute | solution.py:44
  66.0 1.9 collective-permute-done.9.refs_7_.refs_19_
  67.9 3.9 %middle.1 = (f32[256,768]{1,0:T(8,128)}, bf16[256,768]{1,0:T(8,128)(2,1)}, f32[256,128]{1,0:T(8,128)}, bf16[128,768]{1,0:T(8,128)(2,1)}, bf16[128,768]{1,0:T(8,1...) custom-call(bf16[256,768]{1,0:T(8,128)(2,1)} %refs_0_.4, f32[1,768]{1,0:T(1,128)} %reshape.191.refs_1_.refs_4_, ...), custom_call_target="tpu_custom_call" | custom-call | flops 10000000 | bytes 10000 | tf_op jit(solution)/shard_map/middle/pallas_call | solution.py:69
  75.6 2.8 grads_to_slots.1
  78.3 14.3 %collective-permute-done.14.refs_0_ = bf16[256,768]{1,0:T(8,128)(2,1)} collective-permute-done((bf16[256,768]{1,0:T(8,128)(2,1)}, bf16[256,768]{1,0:T(8,128)(2,1)}, u32[]{:S(2)}, u32[]{:S(2)}) %collective-permute-start.14) | collective-permute-done | bytes 393248 | tf_op jit(solution)/shard_map/ppermute | solution.py:44
  92.7 2.1 far_to_slots.1
  96.4 1.9 collective-permute-start.18
  98.3 12.4 %experts_forward0.1 = (bf16[512,3072]{1,0:T(8,128)(2,1)}, bf16[512,3072]{1,0:T(8,128)(2,1)}, bf16[512,768]{1,0:T(8,128)(2,1)}, bf16[512,768]{1,0:T(8,128)(2,1)},...) custom-call(s32[2]{0:T(128)} %pad_add_fusion.2.refs_0_.me_ref.place_, ...), custom_call_target="tpu_custom_call", output_to_operand_aliasing={{5}: (8, {}), {6}: (9, {}), {7}: (10, {})} | custom-call | flops 20000000000 | bytes 10000000 | tf_op jit(solution)/shard_map/experts_forward0/pallas_call | solution.py:474
  112.4 1.9 collective-permute-start.27
  114.3 13.8 %experts_forward1.1 = (bf16[256,768]{1,0:T(8,128)(2,1)}, bf16[256,768]{1,0:T(8,128)(2,1)}, bf16[256,768]{1,0:T(8,128)(2,1)}, bf16[256,768]{1,0:T(8,128)(2,1)}, b...) custom-call(s32[2]{0:T(128)} %pad_add_fusion.2.refs_0_.me_ref.place_, ...), custom_call_target="tpu_custom_call" | custom-call | flops 10000000 | bytes 10000 | tf_op jit(solution)/shard_map/experts_forward1/pallas_call | solution.py:474
  129.7 1.9 collective-permute-start.24
  131.6 12.5 %experts_backward1.1 = (bf16[128,896]{1,0:T(8,128)(2,1)}, bf16[128,896]{1,0:T(8,128)(2,1)}, bf16[128,896]{1,0:T(8,128)(2,1)}, bf16[128,896]{1,0:T(8,128)(2,1)}, ...) custom-call(s32[2]{0:T(128)} %pad_add_fusion.2.refs_0_.me_ref.place_ref, ...), custom_call_target="tpu_custom_call" | custom-call | flops 10000000 | bytes 10000 | tf_op jit(solution)/shard_map/experts_backward1/pallas_call | solution.py:557
  145.8 1.9 collective-permute-start.30
  147.7 11.9 %experts_backward0.1 = (bf16[128,896]{1,0:T(8,128)(2,1)}, bf16[128,896]{1,0:T(8,128)(2,1)}, bf16[128,896]{1,0:T(8,128)(2,1)}, bf16[128,896]{1,0:T(8,128)(2,1)}, bf16[512,3072]{1,0:T(8,128)(2,1)}) custom-call(s32[2]{0:T(128)} %pad_add_fusion.2.refs_0_.me_ref.place_ref, bf16[768,3072]{1,0:T(8,128)(2,1)} %bitcast.51, bf16[3072,768]{1,0:T(8,128)(2,1)} %bitcast.55, ...), custom_call_target="tpu_custom_call" | custom-call | flops 20000000000 | bytes 10000000 | tf_op jit(solution)/shard_map/experts_backward0/pallas_call | solution.py:557
  159.7 2.7 back_from_slots.1
  163.9 1.9 collective-permute-start.33
  166.0 19.8 %expert_weight_grads.1 = (bf16[3072,768]{1,0:T(8,128)(2,1)}, f32[3072,768]{1,0:T(8,128)}) custom-call(s32[2]{0:T(128)} %pad_add_fusion.2.refs_0_.me_ref.place_ref, bf16[512,768]{1,0:T(8,128)(2,1)} %get-tuple-element.165.refs_0_, bf16[512,768]{1,0:T(8,128)(2,1)} %get-tuple-element.166.refs_1_, bf16[512,3072]{1,0:T(8,128)(2,1)} %get-tuple-element.167.refs_2_, ...), custom_call_target="tpu_custom_call" | custom-call | flops 20000000000 | bytes 10000000 | tf_op jit(solution)/shard_map/expert_weight_grads/pallas_call | solution.py:703
  185.9 6.9 %home.1 = (bf16[256,192]{1,0:T(8,128)(2,1)}, bf16[256,192]{1,0:T(8,128)(2,1)}, bf16[256,192]{1,0:T(8,128)(2,1)}, bf16[256,192]{1,0:T(8,128)(2,1)}, f32[256,768]{...) custom-call(s32[8,256]{1,0:T(8,128)} %pad.24.refs_3_.refs_1_.refs_0_, ...), custom_call_target="tpu_custom_call", output_to_operand_aliasing={{9}: (20, {})} | custom-call | flops 10000000 | bytes 10000 | tf_op jit(solution)/shard_map/home/pallas_call | solution.py:69
  195.1 3.4 %result_from_slots.1 = (f32[256,768]{1,0:T(8,128)}, bf16[256,768]{1,0:T(8,128)(2,1)}) custom-call(bf16[256,768]{1,0:T(8,128)(2,1)} %get-tuple-element.139.refs_0_, bf16[256,768]{1,0:T(8,128)(2,1)} %collective-permute-done.22.refs_8_.refs_1_, bf16[256,768]{1,0:T(8,128)(2,1)} %collective-permute-done.23.refs_9_.refs_2_, ...), custom_call_target="tpu_custom_call" | custom-call | flops 20000000000 | bytes 10000000 | tf_op jit(solution)/shard_map/result_from_slots/pallas_call | solution.py:69
  199.6 1.9 collective-permute-done.38.refs_1_.refs_10_
  202.0 5.0 %far_sums.1 = (bf16[448,768]{1,0:T(8,128)(2,1)}, bf16[512,768]{1,0:T(8,128)(2,1)}, bf16[768,768]{1,0:T(8,128)(2,1)}) custom-call(bf16[3072,768]{1,0:T(8,128)(2,1)} %collective-permute-done.39.near_in.near_out, bf16[3072,768]{1,0:T(8,128)(2,1)} %collective-permute-done.39.near_in.near_out, f32[3072,768]{1,0:T(8,128)} %get-tuple-element.181.base_in.base_out, ...), custom_call_target="tpu_custom_call" | custom-call | flops 10000000 | bytes 10000 | tf_op jit(solution)/shard_map/far_sums/pallas_call | solution.py:749
  207.6 2.8 collective-permute-start.35
  213.5 16.1 %attend_back.1 = (bf16[1024,192]{1,0:T(8,128)(2,1)}, bf16[1024,192]{1,0:T(8,128)(2,1)}, bf16[1024,192]{1,0:T(8,128)(2,1)}, f32[8,640]{1,0:T(8,128)}) custom-call(s32[2]{0:T(128)} %pad_add_fusion.2.refs_0_.me_ref.place_ref, bf16[1024,192]{1,0:T(8,128)(2,1)} %get-tuple-element.112.refs_1_, bf16[1024,192]{1,0:T(8,128)(2,1)} %get-tuple-element.113.refs_2_, ...), custom_call_target="tpu_custom_call" | custom-call | flops 10000000 | bytes 10000 | tf_op jit(solution)/shard_map/attend_back/pallas_call | solution.py:69
  229.6 6.8 %input_grads.1 = (bf16[512,768]{1,0:T(8,128)(2,1)}, f32[256,768]{1,0:T(8,128)}, f32[256,768]{1,0:T(8,128)}, f32[24,768]{1,0:T(8,128)}, f32[192,768]{1,0:T(8,128)...) custom-call(s32[2]{0:T(128)} %pad_add_fusion.2.refs_0_.me_ref.place_ref, ...), custom_call_target="tpu_custom_call" | custom-call | flops 10000000 | bytes 10000 | tf_op jit(solution)/shard_map/input_grads/pallas_call | solution.py:69
  238.9 3.5 %collective-permute-done.47.refs_5_ = bf16[512,768]{1,0:T(8,128)(2,1)} collective-permute-done((bf16[512,768]{1,0:T(8,128)(2,1)}, bf16[512,768]{1,0:T(8,128)(2,1)}, u32[]{:S(2)}, u32[]{:S(2)}) %collective-permute-start.47) | collective-permute-done | bytes 786464 | tf_op jit(solution)/shard_map/ppermute | solution.py:44
  242.4 2.7 collective-permute-start.46
  246.8 2.4 collective-permute-done.45.refs_2_
  249.2 4.8 %collective-permute-done.46.refs_3_ = bf16[192,768]{1,0:T(8,128)(2,1)} collective-permute-done((bf16[192,768]{1,0:T(8,128)(2,1)}, bf16[192,768]{1,0:T(8,128)(2,1)}, u32[]{:S(2)}, u32[]{:S(2)}) %collective-permute-start.46) | collective-permute-done | bytes 294944 | tf_op jit(solution)/shard_map/ppermute | solution.py:44
  254.0 2.1 fold_weights.1
  257.6 3.0 %collective-permute-done.48 = f32[24,768]{1,0:T(8,128)S(1)} collective-permute-done((f32[24,768]{1,0:T(8,128)}, f32[24,768]{1,0:T(8,128)S(1)}, u32[]{:S(2)}, u32[]{:S(2)}) %collective-permute-start.48) | collective-permute-done | bytes 73760 | tf_op jit(solution)/shard_map/ppermute | solution.py:44
  262.0 4.0 %collective-permute-done.49 = f32[24,768]{1,0:T(8,128)S(1)} collective-permute-done((f32[24,768]{1,0:T(8,128)S(1)}, f32[24,768]{1,0:T(8,128)S(1)}, u32[]{:S(2)}, u32[]{:S(2)}) %collective-permute-start.49) | collective-permute-done | bytes 73760 | tf_op jit(solution)/shard_map/ppermute | solution.py:44
  266.8 2.3 add_convert_fusion.1
  270.2 1.7 collective-permute-done.50
  272.0 6.4 %add_bitcast_fusion = (f32[1,768,768]{2,1,0:T(8,128)}, f32[1,768,768]{2,1,0:T(8,128)}) fusion(bf16[768,768]{1,0:T(8,128)(2,1)} %collective-permute-done.54, f32[3072,768]{1,0:T(8,128)} %get-tuple-element.181.base_in.base_out, bf16[3072,768]{1,0:T(8,128)(2,1)} %collective-permute-done.39.near_in.near_out, bf16[512,768]{1,0:T(8,128)(2,1)} %collective-permute-done.47.refs_5_, ...), kind=kLoop, calls=%fused_computation | loop fusion | flops 6488064 | bytes 14155776 | tf_op jit(solution)/shard_map/broadcast_in_dim | solution.py:1201
  278.5 1.7 collective-permute-start.52
  285.0 7.5 %collective-permute-done.43.refs_2_ = bf16[256,768]{1,0:T(8,128)(2,1)S(1)} collective-permute-done((bf16[256,768]{1,0:T(8,128)(2,1)S(1)}, bf16[256,768]{1,0:T(8,128)(2,1)S(1)}, u32[]{:S(2)}, u32[]{:S(2)}) %collective-permute-start.43) | collective-permute-done | bytes 393248 | tf_op jit(solution)/shard_map/ppermute | solution.py:44
  294.1 2.1 fusion.5
  296.8 1.8 split_weights.1
  (140 shorter events, 61.5 us)
Async XLA Ops:
  0.6 15.2 %collective-permute-start = (bf16[256,768]{1,0:T(8,128)(2,1)}, bf16[256,768]{1,0:T(8,128)(2,1)}, u32[]{:S(2)}, u32[]{:S(2)}) collective-permute-start(bf16[256,768]{1,0:T(8,128)(2,1)} %refs_0_.4), channel_id=1, source_target_pairs={{0,1},{1,0},{2,3},{3,2},{4,5},{5,4},{6,7},{7,6},{8,9},{9,8},{10,11... | collective-permute-start | bytes 1179656 | tf_op jit(solution)/shard_map/ppermute | solution.py:44
  1.2 12.6 %collective-permute-start.1 = (bf16[256,768]{1,0:T(8,128)(2,1)}, bf16[256,768]{1,0:T(8,128)(2,1)}, u32[]{:S(2)}, u32[]{:S(2)}) collective-permute-start(bf16[256,768]{1,0:T(8,128)(2,1)} %refs_0_.4), channel_id=1, source_target_pairs={{0,2},{1,3},{2,0},{3,1},{4,6},{5,7},{6,4},{7,5},{8,10},{9,11},{10,... | collective-permute-start | bytes 1179656 | tf_op jit(solution)/shard_map/ppermute | solution.py:44
  5.5 10.4 %collective-permute-start.3 = (bf16[96,768]{1,0:T(8,128)(2,1)}, bf16[96,768]{1,0:T(8,128)(2,1)}, u32[]{:S(2)}, u32[]{:S(2)}) collective-permute-start(bf16[96,768]{1,0:T(8,128)(2,1)} %pack_weights.1.refs_0_), channel_id=1, source_target_pairs={{0,16},{4,20},{8,24},{12,28},{16,0},{20,4},{24,8},{28,12},{1,17},{... | collective-permute-start | bytes 442376 | tf_op jit(solution)/shard_map/ppermute | solution.py:44
  8.0 33.7 %collective-permute-start.15 = (s32[256,2]{0,1:T(2,128)}, s32[256,2]{0,1:T(2,128)}, u32[]{:S(2)}, u32[]{:S(2)}) collective-permute-start(s32[256,2]{0,1:T(2,128)} %param.28), channel_id=1, source_target_pairs={{0,16},{4,20},{8,24},{12,28},{16,0},{20,4},{24,8},{28,12},{1,17},{... | collective-permute-start | bytes 6152 | tf_op jit(solution)/shard_map/ppermute | solution.py:44
  13.8 21.1 %collective-permute-start.2 = (bf16[256,768]{1,0:T(8,128)(2,1)}, bf16[256,768]{1,0:T(8,128)(2,1)}, u32[]{:S(2)}, u32[]{:S(2)}) collective-permute-start(bf16[256,768]{1,0:T(8,128)(2,1)} %collective-permute-done.1.refs_3_.refs_4_), channel_id=1, source_target_pairs={{0,1},{1,0},{2,3},{3,2},{4,5},{5,4},{6,7},{7,6},{8,9},{9,8},{10,11... | collective-permute-start | bytes 1179656 | tf_op jit(solution)/shard_map/ppermute | solution.py:44
  17.5 15.9 %collective-permute-start.4 = (bf16[192,768]{1,0:T(8,128)(2,1)}, bf16[192,768]{1,0:T(8,128)(2,1)}, u32[]{:S(2)}, u32[]{:S(2)}) collective-permute-start(bf16[192,768]{1,0:T(8,128)(2,1)} %pair_up.1.refs_6_), channel_id=1, source_target_pairs={{0,4},{4,0},{8,12},{12,8},{16,20},{20,16},{24,28},{28,24},{1,5},{5... | collective-permute-start | bytes 884744 | tf_op jit(solution)/shard_map/ppermute | solution.py:44
  19.3 14.2 %collective-permute-start.5 = (bf16[192,768]{1,0:T(8,128)(2,1)}, bf16[192,768]{1,0:T(8,128)(2,1)}, u32[]{:S(2)}, u32[]{:S(2)}) collective-permute-start(bf16[192,768]{1,0:T(8,128)(2,1)} %pair_up.1.refs_6_), channel_id=1, source_target_pairs={{0,8},{4,12},{8,0},{12,4},{16,24},{20,28},{24,16},{28,20},{1,9},{5... | collective-permute-start | bytes 884744 | tf_op jit(solution)/shard_map/ppermute | solution.py:44
  20.8 14.0 %collective-permute-start.6 = (bf16[192,768]{1,0:T(8,128)(2,1)}, bf16[192,768]{1,0:T(8,128)(2,1)}, u32[]{:S(2)}, u32[]{:S(2)}) collective-permute-start(bf16[192,768]{1,0:T(8,128)(2,1)} %pair_up.1.refs_6_), channel_id=1, source_target_pairs={{0,12},{4,8},{8,4},{12,0},{16,28},{20,24},{24,20},{28,16},{1,13},{... | collective-permute-start | bytes 884744 | tf_op jit(solution)/shard_map/ppermute | solution.py:44
  40.1 18.4 %collective-permute-start.11 = (bf16[192,768]{1,0:T(8,128)(2,1)}, bf16[192,768]{1,0:T(8,128)(2,1)}, u32[]{:S(2)}, u32[]{:S(2)}) collective-permute-start(bf16[192,768]{1,0:T(8,128)(2,1)} %get-tuple-element.119.refs_8_.refs_12_), channel_id=1, source_target_pairs={{0,2},{1,3},{2,0},{3,1},{4,6},{5,7},{6,4},{7,5},{8,10},{9,11},{10,... | collective-permute-start | bytes 884744 | tf_op jit(solution)/shard_map/ppermute | solution.py:44
  42.5 25.4 %collective-permute-start.13 = (bf16[256,768]{1,0:T(8,128)(2,1)}, bf16[256,768]{1,0:T(8,128)(2,1)}, u32[]{:S(2)}, u32[]{:S(2)}) collective-permute-start(bf16[256,768]{1,0:T(8,128)(2,1)} %get-tuple-element.120), channel_id=1, source_target_pairs={{0,16},{4,20},{8,24},{12,28},{16,0},{20,4},{24,8},{28,12},{1,17},{... | collective-permute-start | bytes 1179656 | tf_op jit(solution)/shard_map/ppermute | solution.py:44
  46.4 21.4 %collective-permute-start.10 = (bf16[192,768]{1,0:T(8,128)(2,1)}, bf16[192,768]{1,0:T(8,128)(2,1)}, u32[]{:S(2)}, u32[]{:S(2)}) collective-permute-start(bf16[192,768]{1,0:T(8,128)(2,1)} %get-tuple-element.119.refs_8_.refs_12_), channel_id=1, source_target_pairs={{0,1},{1,0},{2,3},{3,2},{4,5},{5,4},{6,7},{7,6},{8,9},{9,8},{10,11... | collective-permute-start | bytes 884744 | tf_op jit(solution)/shard_map/ppermute | solution.py:44
  58.5 9.4 %collective-permute-start.12 = (bf16[192,768]{1,0:T(8,128)(2,1)}, bf16[192,768]{1,0:T(8,128)(2,1)}, u32[]{:S(2)}, u32[]{:S(2)}) collective-permute-start(bf16[192,768]{1,0:T(8,128)(2,1)} %collective-permute-done.11.refs_10_.refs_14_), channel_id=1, source_target_pairs={{0,1},{1,0},{2,3},{3,2},{4,5},{5,4},{6,7},{7,6},{8,9},{9,8},{10,11... | collective-permute-start | bytes 884744 | tf_op jit(solution)/shard_map/ppermute | solution.py:44
  59.3 6.7 %collective-permute-start.8 = (bf16[256,192]{1,0:T(8,128)(2,1)}, bf16[256,192]{1,0:T(8,128)(2,1)}, u32[]{:S(2)}, u32[]{:S(2)}) collective-permute-start(bf16[256,192]{1,0:T(8,128)(2,1)} %get-tuple-element.117), channel_id=1, source_target_pairs={{0,2},{1,3},{2,0},{3,1},{4,6},{5,7},{6,4},{7,5},{8,10},{9,11},{10,... | collective-permute-start | bytes 294920 | tf_op jit(solution)/shard_map/ppermute | solution.py:44
  59.9 8.0 %collective-permute-start.9 = (bf16[256,192]{1,0:T(8,128)(2,1)}, bf16[256,192]{1,0:T(8,128)(2,1)}, u32[]{:S(2)}, u32[]{:S(2)}) collective-permute-start(bf16[256,192]{1,0:T(8,128)(2,1)} %get-tuple-element.118), channel_id=1, source_target_pairs={{0,3},{1,2},{2,1},{3,0},{4,7},{5,6},{6,5},{7,4},{8,11},{9,10},{10,... | collective-permute-start | bytes 294920 | tf_op jit(solution)/shard_map/ppermute | solution.py:44
  71.7 21.0 %collective-permute-start.14 = (bf16[256,768]{1,0:T(8,128)(2,1)}, bf16[256,768]{1,0:T(8,128)(2,1)}, u32[]{:S(2)}, u32[]{:S(2)}) collective-permute-start(bf16[256,768]{1,0:T(8,128)(2,1)} %get-tuple-element.122.refs_6_), channel_id=1, source_target_pairs={{0,16},{4,20},{8,24},{12,28},{16,0},{20,4},{24,8},{28,12},{1,17},{... | collective-permute-start | bytes 1179656 | tf_op jit(solution)/shard_map/ppermute | solution.py:44
  72.1 24.3 %collective-permute-start.19 = (bf16[128,768]{1,0:T(8,128)(2,1)}, bf16[128,768]{1,0:T(8,128)(2,1)}, u32[]{:S(2)}, u32[]{:S(2)}) collective-permute-start(bf16[128,768]{1,0:T(8,128)(2,1)} %get-tuple-element.131), channel_id=1, source_target_pairs={{0,4},{4,0},{8,12},{12,8},{16,20},{20,16},{24,28},{28,24},{1,5},{5... | collective-permute-start | bytes 589832 | tf_op jit(solution)/shard_map/ppermute | solution.py:44
  73.6 24.7 %collective-permute-start.20 = (bf16[128,768]{1,0:T(8,128)(2,1)}, bf16[128,768]{1,0:T(8,128)(2,1)}, u32[]{:S(2)}, u32[]{:S(2)}) collective-permute-start(bf16[128,768]{1,0:T(8,128)(2,1)} %get-tuple-element.132), channel_id=1, source_target_pairs={{0,8},{4,12},{8,0},{12,4},{16,24},{20,28},{24,16},{28,20},{1,9},{5... | collective-permute-start | bytes 589832 | tf_op jit(solution)/shard_map/ppermute | solution.py:44
  75.1 23.2 %collective-permute-start.21 = (bf16[128,768]{1,0:T(8,128)(2,1)}, bf16[128,768]{1,0:T(8,128)(2,1)}, u32[]{:S(2)}, u32[]{:S(2)}) collective-permute-start(bf16[128,768]{1,0:T(8,128)(2,1)} %get-tuple-element.133), channel_id=1, source_target_pairs={{0,12},{4,8},{8,4},{12,0},{16,28},{20,24},{24,20},{28,16},{1,13},{... | collective-permute-start | bytes 589832 | tf_op jit(solution)/shard_map/ppermute | solution.py:44
  94.8 17.6 %collective-permute-start.16 = (bf16[128,768]{1,0:T(8,128)(2,1)}, bf16[128,768]{1,0:T(8,128)(2,1)}, u32[]{:S(2)}, u32[]{:S(2)}) collective-permute-start(bf16[128,768]{1,0:T(8,128)(2,1)} %get-tuple-element.127), channel_id=1, source_target_pairs={{0,4},{4,0},{8,12},{12,8},{16,20},{20,16},{24,28},{28,24},{1,5},{5... | collective-permute-start | bytes 589832 | tf_op jit(solution)/shard_map/ppermute | solution.py:44
  96.4 18.0 %collective-permute-start.17 = (bf16[128,768]{1,0:T(8,128)(2,1)}, bf16[128,768]{1,0:T(8,128)(2,1)}, u32[]{:S(2)}, u32[]{:S(2)}) collective-permute-start(bf16[128,768]{1,0:T(8,128)(2,1)} %get-tuple-element.128), channel_id=1, source_target_pairs={{0,8},{4,12},{8,0},{12,4},{16,24},{20,28},{24,16},{28,20},{1,9},{5... | collective-permute-start | bytes 589832 | tf_op jit(solution)/shard_map/ppermute | solution.py:44
  96.4 17.9 %collective-permute-start.18 = (bf16[128,768]{1,0:T(8,128)(2,1)}, bf16[128,768]{1,0:T(8,128)(2,1)}, u32[]{:S(2)}, u32[]{:S(2)}) collective-permute-start(bf16[128,768]{1,0:T(8,128)(2,1)} %get-tuple-element.129), channel_id=1, source_target_pairs={{0,12},{4,8},{8,4},{12,0},{16,28},{20,24},{24,20},{28,16},{1,13},{... | collective-permute-start | bytes 589832 | tf_op jit(solution)/shard_map/ppermute | solution.py:44
  110.7 18.9 %collective-permute-start.25 = (bf16[256,768]{1,0:T(8,128)(2,1)}, bf16[256,768]{1,0:T(8,128)(2,1)}, u32[]{:S(2)}, u32[]{:S(2)}) collective-permute-start(bf16[256,768]{1,0:T(8,128)(2,1)} %get-tuple-element.149), channel_id=1, source_target_pairs={{0,4},{4,0},{8,12},{12,8},{16,20},{20,16},{24,28},{28,24},{1,5},{5... | collective-permute-start | bytes 1179656 | tf_op jit(solution)/shard_map/ppermute | solution.py:44
  112.4 19.3 %collective-permute-start.26 = (bf16[256,768]{1,0:T(8,128)(2,1)}, bf16[256,768]{1,0:T(8,128)(2,1)}, u32[]{:S(2)}, u32[]{:S(2)}) collective-permute-start(bf16[256,768]{1,0:T(8,128)(2,1)} %get-tuple-element.150), channel_id=1, source_target_pairs={{0,8},{4,12},{8,0},{12,4},{16,24},{20,28},{24,16},{28,20},{1,9},{5... | collective-permute-start | bytes 1179656 | tf_op jit(solution)/shard_map/ppermute | solution.py:44
  112.4 19.3 %collective-permute-start.27 = (bf16[256,768]{1,0:T(8,128)(2,1)}, bf16[256,768]{1,0:T(8,128)(2,1)}, u32[]{:S(2)}, u32[]{:S(2)}) collective-permute-start(bf16[256,768]{1,0:T(8,128)(2,1)} %get-tuple-element.151), channel_id=1, source_target_pairs={{0,12},{4,8},{8,4},{12,0},{16,28},{20,24},{24,20},{28,16},{1,13},{... | collective-permute-start | bytes 1179656 | tf_op jit(solution)/shard_map/ppermute | solution.py:44
  128.1 17.7 %collective-permute-start.22 = (bf16[256,768]{1,0:T(8,128)(2,1)}, bf16[256,768]{1,0:T(8,128)(2,1)}, u32[]{:S(2)}, u32[]{:S(2)}) collective-permute-start(bf16[256,768]{1,0:T(8,128)(2,1)} %get-tuple-element.140), channel_id=1, source_target_pairs={{0,4},{4,0},{8,12},{12,8},{16,20},{20,16},{24,28},{28,24},{1,5},{5... | collective-permute-start | bytes 1179656 | tf_op jit(solution)/shard_map/ppermute | solution.py:44
  129.7 29.9 %collective-permute-start.23 = (bf16[256,768]{1,0:T(8,128)(2,1)}, bf16[256,768]{1,0:T(8,128)(2,1)}, u32[]{:S(2)}, u32[]{:S(2)}) collective-permute-start(bf16[256,768]{1,0:T(8,128)(2,1)} %get-tuple-element.141), channel_id=1, source_target_pairs={{0,8},{4,12},{8,0},{12,4},{16,24},{20,28},{24,16},{28,20},{1,9},{5... | collective-permute-start | bytes 1179656 | tf_op jit(solution)/shard_map/ppermute | solution.py:44
  129.7 29.9 %collective-permute-start.24 = (bf16[256,768]{1,0:T(8,128)(2,1)}, bf16[256,768]{1,0:T(8,128)(2,1)}, u32[]{:S(2)}, u32[]{:S(2)}) collective-permute-start(bf16[256,768]{1,0:T(8,128)(2,1)} %get-tuple-element.142), channel_id=1, source_target_pairs={{0,12},{4,8},{8,4},{12,0},{16,28},{20,24},{24,20},{28,16},{1,13},{... | collective-permute-start | bytes 1179656 | tf_op jit(solution)/shard_map/ppermute | solution.py:44
  144.2 15.5 %collective-permute-start.28 = (bf16[128,896]{1,0:T(8,128)(2,1)}, bf16[128,896]{1,0:T(8,128)(2,1)}, u32[]{:S(2)}, u32[]{:S(2)}) collective-permute-start(bf16[128,896]{1,0:T(8,128)(2,1)} %get-tuple-element.155), channel_id=1, source_target_pairs={{0,4},{4,0},{8,12},{12,8},{16,20},{20,16},{24,28},{28,24},{1,5},{5... | collective-permute-start | bytes 688136 | tf_op jit(solution)/shard_map/ppermute | solution.py:44
  145.8 13.9 %collective-permute-start.29 = (bf16[128,896]{1,0:T(8,128)(2,1)}, bf16[128,896]{1,0:T(8,128)(2,1)}, u32[]{:S(2)}, u32[]{:S(2)}) collective-permute-start(bf16[128,896]{1,0:T(8,128)(2,1)} %get-tuple-element.156), channel_id=1, source_target_pairs={{0,8},{4,12},{8,0},{12,4},{16,24},{20,28},{24,16},{28,20},{1,9},{5... | collective-permute-start | bytes 688136 | tf_op jit(solution)/shard_map/ppermute | solution.py:44
  145.8 13.9 %collective-permute-start.30 = (bf16[128,896]{1,0:T(8,128)(2,1)}, bf16[128,896]{1,0:T(8,128)(2,1)}, u32[]{:S(2)}, u32[]{:S(2)}) collective-permute-start(bf16[128,896]{1,0:T(8,128)(2,1)} %get-tuple-element.157), channel_id=1, source_target_pairs={{0,12},{4,8},{8,4},{12,0},{16,28},{20,24},{24,20},{28,16},{1,13},{... | collective-permute-start | bytes 688136 | tf_op jit(solution)/shard_map/ppermute | solution.py:44
  162.4 23.5 %collective-permute-start.31 = (bf16[128,896]{1,0:T(8,128)(2,1)}, bf16[128,896]{1,0:T(8,128)(2,1)}, u32[]{:S(2)}, u32[]{:S(2)}) collective-permute-start(bf16[128,896]{1,0:T(8,128)(2,1)} %get-tuple-element.161), channel_id=1, source_target_pairs={{0,4},{4,0},{8,12},{12,8},{16,20},{20,16},{24,28},{28,24},{1,5},{5... | collective-permute-start | bytes 688136 | tf_op jit(solution)/shard_map/ppermute | solution.py:44
  163.9 21.9 %collective-permute-start.32 = (bf16[128,896]{1,0:T(8,128)(2,1)}, bf16[128,896]{1,0:T(8,128)(2,1)}, u32[]{:S(2)}, u32[]{:S(2)}) collective-permute-start(bf16[128,896]{1,0:T(8,128)(2,1)} %get-tuple-element.162), channel_id=1, source_target_pairs={{0,8},{4,12},{8,0},{12,4},{16,24},{20,28},{24,16},{28,20},{1,9},{5... | collective-permute-start | bytes 688136 | tf_op jit(solution)/shard_map/ppermute | solution.py:44
  163.9 21.9 %collective-permute-start.33 = (bf16[128,896]{1,0:T(8,128)(2,1)}, bf16[128,896]{1,0:T(8,128)(2,1)}, u32[]{:S(2)}, u32[]{:S(2)}) collective-permute-start(bf16[128,896]{1,0:T(8,128)(2,1)} %get-tuple-element.163), channel_id=1, source_target_pairs={{0,12},{4,8},{8,4},{12,0},{16,28},{20,24},{24,20},{28,16},{1,13},{... | collective-permute-start | bytes 688136 | tf_op jit(solution)/shard_map/ppermute | solution.py:44
  165.9 20.0 %collective-permute-start.34 = (bf16[256,896]{1,0:T(8,128)(2,1)}, bf16[256,896]{1,0:T(8,128)(2,1)}, u32[]{:S(2)}, u32[]{:S(2)}) collective-permute-start(bf16[256,896]{1,0:T(8,128)(2,1)} %get-tuple-element.164), channel_id=1, source_target_pairs={{0,16},{4,20},{8,24},{12,28},{16,0},{20,4},{24,8},{28,12},{1,17},{... | collective-permute-start | bytes 1376264 | tf_op jit(solution)/shard_map/ppermute | solution.py:44
  192.8 9.2 %collective-permute-start.39 = (bf16[3072,768]{1,0:T(8,128)(2,1)}, bf16[3072,768]{1,0:T(8,128)(2,1)}, u32[]{:S(2)}, u32[]{:S(2)}) collective-permute-start(bf16[3072,768]{1,0:T(8,128)(2,1)} %get-tuple-element.180), channel_id=1, source_target_pairs={{0,1},{1,0},{2,3},{3,2},{4,5},{5,4},{6,7},{7,6},{8,9},{9,8},{10,11... | collective-permute-start | bytes 14155784 | tf_op jit(solution)/shard_map/ppermute | solution.py:44
  192.9 6.7 %collective-permute-start.37 = (bf16[256,192]{1,0:T(8,128)(2,1)}, bf16[256,192]{1,0:T(8,128)(2,1)}, u32[]{:S(2)}, u32[]{:S(2)}) collective-permute-start(bf16[256,192]{1,0:T(8,128)(2,1)} %get-tuple-element.178), channel_id=1, source_target_pairs={{0,2},{1,3},{2,0},{3,1},{4,6},{5,7},{6,4},{7,5},{8,10},{9,11},{10,... | collective-permute-start | bytes 294920 | tf_op jit(solution)/shard_map/ppermute | solution.py:44
  193.5 8.0 %collective-permute-start.38 = (bf16[256,192]{1,0:T(8,128)(2,1)}, bf16[256,192]{1,0:T(8,128)(2,1)}, u32[]{:S(2)}, u32[]{:S(2)}) collective-permute-start(bf16[256,192]{1,0:T(8,128)(2,1)} %get-tuple-element.179), channel_id=1, source_target_pairs={{0,3},{1,2},{2,1},{3,0},{4,7},{5,6},{6,5},{7,4},{8,11},{9,10},{10,... | collective-permute-start | bytes 294920 | tf_op jit(solution)/shard_map/ppermute | solution.py:44
  194.8 7.2 %collective-permute-start.40 = (bf16[384,768]{1,0:T(8,128)(2,1)}, bf16[384,768]{1,0:T(8,128)(2,1)}, u32[]{:S(2)}, u32[]{:S(2)}) collective-permute-start(bf16[384,768]{1,0:T(8,128)(2,1)} %get-tuple-element.182), channel_id=1, source_target_pairs={{0,1},{1,0},{2,3},{3,2},{4,5},{5,4},{6,7},{7,6},{8,9},{9,8},{10,11... | collective-permute-start | bytes 1769480 | tf_op jit(solution)/shard_map/ppermute | solution.py:44
  207.0 22.6 %collective-permute-start.41 = (bf16[448,768]{1,0:T(8,128)(2,1)}, bf16[448,768]{1,0:T(8,128)(2,1)}, u32[]{:S(2)}, u32[]{:S(2)}) collective-permute-start(bf16[448,768]{1,0:T(8,128)(2,1)} %get-tuple-element.184.refs_11_), channel_id=1, source_target_pairs={{0,2},{1,3},{2,0},{3,1},{4,6},{5,7},{6,4},{7,5},{8,10},{9,11},{10,... | collective-permute-start | bytes 2064392 | tf_op jit(solution)/shard_map/ppermute | solution.py:44
  207.6 22.0 %collective-permute-start.35 = (bf16[256,768]{1,0:T(8,128)(2,1)}, bf16[256,768]{1,0:T(8,128)(2,1)}, u32[]{:S(2)}, u32[]{:S(2)}) collective-permute-start(bf16[256,768]{1,0:T(8,128)(2,1)} %get-tuple-element.175), channel_id=1, source_target_pairs={{0,16},{4,20},{8,24},{12,28},{16,0},{20,4},{24,8},{28,12},{1,17},{... | collective-permute-start | bytes 1179656 | tf_op jit(solution)/shard_map/ppermute | solution.py:44
  210.3 32.1 %collective-permute-start.47 = (bf16[512,768]{1,0:T(8,128)(2,1)}, bf16[512,768]{1,0:T(8,128)(2,1)}, u32[]{:S(2)}, u32[]{:S(2)}) collective-permute-start(bf16[512,768]{1,0:T(8,128)(2,1)} %get-tuple-element.203), channel_id=1, source_target_pairs={{0,2},{1,3},{2,0},{3,1},{4,6},{5,7},{6,4},{7,5},{8,10},{9,11},{10,... | collective-permute-start | bytes 2359304 | tf_op jit(solution)/shard_map/ppermute | solution.py:44
  236.3 17.6 %collective-permute-start.42 = (bf16[512,768]{1,0:T(8,128)(2,1)}, bf16[512,768]{1,0:T(8,128)(2,1)}, u32[]{:S(2)}, u32[]{:S(2)}) collective-permute-start(bf16[512,768]{1,0:T(8,128)(2,1)} %get-tuple-element.196), channel_id=1, source_target_pairs={{0,1},{1,0},{2,3},{3,2},{4,5},{5,4},{6,7},{7,6},{8,9},{9,8},{10,11... | collective-permute-start | bytes 2359304 | tf_op jit(solution)/shard_map/ppermute | solution.py:44
  236.8 35.2 %collective-permute-start.54 = (bf16[768,768]{1,0:T(8,128)(2,1)}, bf16[768,768]{1,0:T(8,128)(2,1)}, u32[]{:S(2)}, u32[]{:S(2)}) collective-permute-start(bf16[768,768]{1,0:T(8,128)(2,1)} %get-tuple-element.211), channel_id=1, source_target_pairs={{0,2},{1,3},{2,0},{3,1},{4,6},{5,7},{6,4},{7,5},{8,10},{9,11},{10,... | collective-permute-start | bytes 3538952 | tf_op jit(solution)/shard_map/ppermute | solution.py:44
  237.4 9.3 %collective-permute-start.44 = (bf16[192,768]{1,0:T(8,128)(2,1)}, bf16[192,768]{1,0:T(8,128)(2,1)}, u32[]{:S(2)}, u32[]{:S(2)}) collective-permute-start(bf16[192,768]{1,0:T(8,128)(2,1)} %get-tuple-element.199), channel_id=1, source_target_pairs={{0,4},{4,0},{8,12},{12,8},{16,20},{20,16},{24,28},{28,24},{1,5},{5... | collective-permute-start | bytes 884744 | tf_op jit(solution)/shard_map/ppermute | solution.py:44
  238.9 10.2 %collective-permute-start.45 = (bf16[192,768]{1,0:T(8,128)(2,1)}, bf16[192,768]{1,0:T(8,128)(2,1)}, u32[]{:S(2)}, u32[]{:S(2)}) collective-permute-start(bf16[192,768]{1,0:T(8,128)(2,1)} %get-tuple-element.200), channel_id=1, source_target_pairs={{0,8},{4,12},{8,0},{12,4},{16,24},{20,28},{24,16},{28,20},{1,9},{5... | collective-permute-start | bytes 884744 | tf_op jit(solution)/shard_map/ppermute | solution.py:44
  242.4 11.5 %collective-permute-start.46 = (bf16[192,768]{1,0:T(8,128)(2,1)}, bf16[192,768]{1,0:T(8,128)(2,1)}, u32[]{:S(2)}, u32[]{:S(2)}) collective-permute-start(bf16[192,768]{1,0:T(8,128)(2,1)} %get-tuple-element.201), channel_id=1, source_target_pairs={{0,12},{4,8},{8,4},{12,0},{16,28},{20,24},{24,20},{28,16},{1,13},{... | collective-permute-start | bytes 884744 | tf_op jit(solution)/shard_map/ppermute | solution.py:44
  281.3 11.2 %collective-permute-start.43 = (bf16[256,768]{1,0:T(8,128)(2,1)S(1)}, bf16[256,768]{1,0:T(8,128)(2,1)S(1)}, u32[]{:S(2)}, u32[]{:S(2)}) collective-permute-start(bf16[256,768]{1,0:T(8,128)(2,1)S(1)} %add_convert_fusion), channel_id=1, source_target_pairs={{0,2},{1,3},{2,0},{3,1},{4,6},{5,7},{6,4},{7,5},{8,10},{9,11},{10,... | collective-permute-start | bytes 1179656 | tf_op jit(solution)/shard_map/ppermute | solution.py:44
  281.8 14.4 %collective-permute-start.53 = (bf16[96,768]{1,0:T(8,128)(2,1)S(1)}, bf16[96,768]{1,0:T(8,128)(2,1)S(1)}, u32[]{:S(2)}, u32[]{:S(2)}) collective-permute-start(bf16[96,768]{1,0:T(8,128)(2,1)S(1)} %copy-done.7), channel_id=1, source_target_pairs={{0,16},{4,20},{8,24},{12,28},{16,0},{20,4},{24,8},{28,12},{1,17},{... | collective-permute-start | bytes 442376 | tf_op jit(solution)/shard_map/ppermute | solution.py:44
  (15 other events, 116.7 us)

commit v7 on v6

--- a/solution.py
+++ b/solution.py
@@ -332,7 +332,7 @@
     return jnp.where(taken, 1.0, 0.0).astype(bf16)
 
 
-def to_slots(name, sets, blocks, size, through=(), cost=None):
+def to_slots(name, sets, blocks, size, after=()):
     width = sets[0][0].shape[1]
 
     def kernel(*refs):
@@ -349,8 +349,7 @@
         name,
         operands,
         [shape((size * len(sets), width), bf16)] * blocks,
-        through=through,
-        cost=cost,
+        after=after,
     )
 
 
@@ -421,56 +420,79 @@
     return jnp.concatenate([ref[...] for ref in refs], axis=0)
 
 
-def experts_forward(
-    name, place, w_in, w_out, w_router, x_blocks, experts, before, cost, through=()
+def run_experts(
+    name, place, w_in, w_out, w_router, x_blocks, g_blocks, at_set, before, cost, after
 ):
     width, units = w_in.shape
     count, size = len(x_blocks), x_blocks[0].shape[0]
-    total, piece, chunk = size * count, 768, 256
-    sets = 1 if before is None else 1 + len(before) // 2
-    blocks = 0 if before is None else count
-    before, through = [] if before is None else list(before), list(through)
+    total, piece, chunk = size * count, 512, 256
+    experts = before[0]
+    held = list(before[1:])
+    sets = g_blocks[0].shape[0] // size
+    last = at_set == sets - 1
 
     def kernel(me_ref, w_in_ref, w_out_ref, router_ref, *refs):
         x_refs, refs = refs[:count], refs[count:]
-        before_refs, refs = refs[: len(before)], refs[len(before) + len(through) :]
-        out_refs, refs = refs[:blocks], refs[blocks:]
-        active_ref, slope_ref, x_all, result_ref, gates_ref = refs[:5]
-        result_sum = refs[-1]
+        g_refs, refs = refs[:count], refs[count:]
+        held_refs, refs = refs[: len(held)], refs[len(held) + len(after) :]
+        back_refs, refs = refs[:count], refs[count:]
+        result_refs, refs = refs[:count] if last else refs[:1], refs[count if last else 1 :]
+        active_ref, pre_grad_ref, x_all, s_all, gates, result_sum, back_sum = refs
 
         @pl.when(pl.program_id(0) == 0)
         def _():
-            x_all[...] = join_rows(x_refs)
+            for b in range(count):
+                rows = slice(b * size, (b + 1) * size)
+                x_all[rows, :] = x_refs[b][...]
             probs = router_softmax(x_all[...], router_ref[...], experts)
             lane = lax.broadcasted_iota(jnp.int32, probs.shape, 1)
             own = jnp.sum(jnp.where(lane == me_ref[0], probs, 0.0), axis=1, keepdims=True)
-            gates_ref[...] = jnp.broadcast_to(own, gates_ref.shape)
+            gates[...] = jnp.broadcast_to(own, gates.shape)
+            for b in range(count):
+                rows = slice(b * size, (b + 1) * size)
+                grad = g_refs[b][at_set * size : (at_set + 1) * size, :].astype(f32)
+                s_all[rows, :] = (gates[rows, 0:1] * grad).astype(bf16)
             result_sum[...] = jnp.zeros_like(result_sum)
+            back_sum[...] = jnp.zeros_like(back_sum)
 
         for c in range(piece // chunk):
             at = slice(c * chunk, (c + 1) * chunk)
             pre_act = dot(x_all[...], w_in_ref[:, at], 1, 0)
+            active_grad = dot(s_all[...], w_out_ref[at, :], 1, 1)
             below = 0.5 + 0.5 * lax.erf(pre_act * math.sqrt(0.5))
             bell = jnp.exp(-0.5 * pre_act * pre_act) * (1.0 / math.sqrt(2.0 * math.pi))
             active_ref[:, at] = (pre_act * below).astype(bf16)
-            slope_ref[:, at] = (below + pre_act * bell).astype(bf16)
+            pre_grad_ref[:, at] = (active_grad * (below + pre_act * bell)).astype(bf16)
         result_sum[...] += dot(active_ref[...], w_out_ref[...], 1, 0)
+        back_sum[...] += dot(pre_grad_ref[...], w_in_ref[...], 1, 1)
 
         @pl.when(pl.program_id(0) == pl.num_programs(0) - 1)
         def _():
-            result = result_sum[...].astype(bf16)
-            result_ref[...] = result
-            if blocks:
-                held = [(before_refs[i], before_refs[i + 1]) for i in range(0, len(before), 2)]
-                held.append((result_ref, gates_ref))
-                for at, (rows_ref, gate_ref) in enumerate(held):
-                    gated = (gate_ref[:, 0:1] * rows_ref[...].astype(f32)).astype(bf16)
-                    for b, ref in enumerate(out_refs):
-                        ref[at * size : (at + 1) * size, :] = gated[b * size : (b + 1) * size, :]
+            lane = lax.broadcasted_iota(jnp.int32, (size, 128), 1)
+            for b, (ref, g_ref) in enumerate(zip(back_refs, g_refs)):
+                rows = slice(b * size, (b + 1) * size)
+                result = result_sum[rows, :].astype(bf16).astype(f32)
+                grad = g_ref[at_set * size : (at_set + 1) * size, :].astype(f32)
+                gate_grad = jnp.sum(grad * result, axis=1, keepdims=True)
+                upper = gate_grad.astype(bf16).astype(f32)
+                ref[:, :width] = back_sum[rows, :].astype(bf16)
+                ref[:, width:] = jnp.where(
+                    lane == me_ref[0],
+                    upper,
+                    jnp.where(lane == me_ref[0] + 64, gate_grad - upper, 0.0),
+                ).astype(bf16)
+                gated = (gates[rows, 0:1] * result).astype(bf16)
+                if last:
+                    for at, other in enumerate(held_refs):
+                        result_refs[b][at * size : (at + 1) * size, :] = other[rows, :]
+                    result_refs[b][at_set * size : (at_set + 1) * size, :] = gated
+                else:
+                    result_refs[0][rows, :] = gated
 
     columns = pl.BlockSpec((total, piece), lambda i: (0, i))
-    outs = [shape((size * sets, width), bf16)] * blocks
-    kept = [shape((total, width), bf16)] * 2 + [shape((total, 128), f32)]
+    outs = [shape((size, width + 128), bf16)] * count
+    results = [shape((size * sets, width), bf16)] * count if last else [shape((total, width), bf16)]
+    rows_out = [shape((total, width), bf16)] * 2
     flat = pl.pallas_call(
         kernel,
         name=name,
@@ -481,99 +503,21 @@
             pl.BlockSpec((piece, width), lambda i: (i, 0)),
             whole(w_router.shape),
         ]
-        + [whole(o.shape) for o in x_blocks]
-        + [whole(o.shape) for o in before]
-        + [pl.BlockSpec(memory_space=pl.ANY)] * len(through),
-        out_specs=[whole(o.shape) for o in outs]
+        + [whole(o.shape) for o in list(x_blocks) + list(g_blocks) + held]
+        + [pl.BlockSpec(memory_space=pl.ANY)] * len(after),
+        out_specs=[whole(o.shape) for o in outs + results]
         + [columns] * 2
-        + [whole(o.shape) for o in kept]
-        + [pl.BlockSpec(memory_space=pl.ANY)] * len(through),
-        out_shape=outs
-        + [shape((total, units), bf16)] * 2
-        + kept
-        + [shape(o.shape, o.dtype) for o in through],
-        input_output_aliases={
-            4 + count + len(before) + i: blocks + 5 + i for i in range(len(through))
-        },
-        scratch_shapes=[pltpu.VMEM((total, width), f32)],
+        + [whole(o.shape) for o in rows_out],
+        out_shape=outs + results + [shape((total, units), bf16)] * 2 + rows_out,
+        scratch_shapes=[
+            pltpu.VMEM((total, 128), f32),
+            pltpu.VMEM((total, width), f32),
+            pltpu.VMEM((total, width), f32),
+        ],
         compiler_params=limit(64),
         cost_estimate=cost,
-    )(place, w_in, w_out, w_router, *x_blocks, *before, *through)
-    return (list(flat[:blocks]), *flat[blocks:])
-
-
-def experts_backward(name, place, w_in, w_out, sets, at_set, slot_grad, g_blocks, count, cost):
-    width, units = w_in.shape
-    slope, result, _ = sets[at_set]
-    total, piece, chunk = slope.shape[0], 768, 256
-    size = total // count
-    number = len(sets)
-    first = slot_grad is None
-    given = [gates for _, _, gates in sets] if first else [slot_grad]
-    made = number if first else 0
-
-    def kernel(me_ref, w_in_ref, w_out_ref, slope_ref, result_ref, *refs):
-        given_refs, refs = refs[: len(given)], refs[len(given) :]
-        g_refs, refs = refs[: len(g_blocks)], refs[len(g_blocks) :]
-        back_refs, refs = refs[:count], refs[count:]
-        s_refs, pre_grad_ref, back_sum = refs[:made], refs[made], refs[made + 1]
-        s_ref = s_refs[at_set] if first else given_refs[0]
-
-        @pl.when(pl.program_id(0) == 0)
-        def _():
-            back_sum[...] = jnp.zeros_like(back_sum)
-            if first:
-                for at in range(number):
-                    for b, ref in enumerate(g_refs):
-                        rows = slice(b * size, (b + 1) * size)
-                        grad = ref[at * size : (at + 1) * size, :].astype(f32)
-                        s_refs[at][rows, :] = (given_refs[at][rows, 0:1] * grad).astype(bf16)
-
-        for c in range(piece // chunk):
-            at = slice(c * chunk, (c + 1) * chunk)
-            active_grad = dot(s_ref[...], w_out_ref[at, :], 1, 1)
-            pre_grad_ref[:, at] = (active_grad * slope_ref[:, at].astype(f32)).astype(bf16)
-        back_sum[...] += dot(pre_grad_ref[...], w_in_ref[...], 1, 1)
-
-        @pl.when(pl.program_id(0) == pl.num_programs(0) - 1)
-        def _():
-            lane = lax.broadcasted_iota(jnp.int32, (size, 128), 1)
-            for b, (ref, g_ref) in enumerate(zip(back_refs, g_refs)):
-                rows = slice(b * size, (b + 1) * size)
-                grad = g_ref[at_set * size : (at_set + 1) * size, :].astype(f32)
-                gate_grad = jnp.sum(
-                    grad * result_ref[rows, :].astype(f32), axis=1, keepdims=True
-                )
-                upper = gate_grad.astype(bf16).astype(f32)
-                ref[:, :width] = back_sum[rows, :].astype(bf16)
-                ref[:, width:] = jnp.where(
-                    lane == me_ref[0],
-                    upper,
-                    jnp.where(lane == me_ref[0] + 64, gate_grad - upper, 0.0),
-                ).astype(bf16)
-
-    by_units = pl.BlockSpec((total, piece), lambda i: (0, i))
-    outs = [shape((size, width + 128), bf16)] * count + [shape((total, width), bf16)] * made
-    flat = pl.pallas_call(
-        kernel,
-        name=name,
-        grid=(units // piece,),
-        in_specs=[
-            pl.BlockSpec(memory_space=pltpu.SMEM),
-            pl.BlockSpec((width, piece), lambda i: (0, i)),
-            pl.BlockSpec((piece, width), lambda i: (i, 0)),
-            by_units,
-            whole(result.shape),
-        ]
-        + [whole(o.shape) for o in given]
-        + [whole(o.shape) for o in g_blocks],
-        out_specs=[whole(o.shape) for o in outs] + [by_units],
-        out_shape=outs + [shape((total, units), bf16)],
-        scratch_shapes=[pltpu.VMEM((total, width), f32)],
-        compiler_params=limit(64),
-        cost_estimate=cost,
-    )(place, w_in, w_out, slope, result, *given, *g_blocks)
-    return list(flat[:count]), list(flat[count : count + made]), flat[-1]
+    )(place, w_in, w_out, w_router, *x_blocks, *g_blocks, *held, *after)
+    return list(flat[:count]), list(flat[count:-4]), flat[-4:]
 
 
 def home(
@@ -847,6 +791,36 @@
     )
 
 
+def add_up(base, near, parts, after):
+    size, width = base.shape[0] // 4, base.shape[1]
+
+    def kernel(in_base, in_near, out_base, out_near, *refs):
+        part_refs, (in_ref, out_ref) = refs[: len(parts)], refs[-2:]
+        first = 0
+        for (array, at), ref in zip(parts[:-1], part_refs[:-1]):
+            rows = slice(first, first + array.shape[0] - at)
+            total = in_base[rows, :] + in_near[rows, :].astype(f32)
+            in_ref[rows, :] = total + ref[at:, :].astype(f32)
+            first = first + array.shape[0] - at
+        total = out_base[...] + out_near[...].astype(f32)
+        out_ref[...] = total + part_refs[-1][...].astype(f32)
+
+    def block(at):
+        return pl.BlockSpec((size, width), lambda *_: (at, 0), pipeline_mode=pl.Buffered(1))
+
+    specs = [block(0), block(0), block(2), block(2)] + [whole(o.shape) for o, _ in parts]
+    return pl.pallas_call(
+        kernel,
+        name="add_up",
+        grid=(1,),
+        in_specs=specs + [pl.BlockSpec(memory_space=pl.ANY)] * len(after),
+        out_specs=[whole((size, width))] * 2,
+        out_shape=[shape((size, width), f32)] * 2,
+        compiler_params=limit(64),
+        cost_estimate=brief,
+    )(base, near, base, near, *[array for array, _ in parts], *after)
+
+
 def fold_weights(base, arrived, after, through):
     part, width = base.shape[0] // 2, base.shape[1]
 
@@ -971,15 +945,6 @@
 
     if few:
         far_cotangent = swap(late_cotangent, "dp", 4)
-        held = to_slots(
-            "grads_to_slots",
-            [(cotangent, slots[0]), (far_cotangent, slots[1])],
-            blocks,
-            size,
-            cost=long,
-        )
-    else:
-        held = to_slots("grads_to_slots", [(cotangent, slots[0])], blocks, size)
 
     line_buckets = jnp.pad(jnp.flip(buckets[: reach + 1]), (0, window - reach - 1))
     bucket_hot = (
@@ -991,7 +956,7 @@
     seg_q = segments.reshape(seq_len, 1)
     seg_k = jnp.pad(segments.reshape(1, seq_len), ((0, 0), (reach, 0)), constant_values=-1)
     mixed_out = attend(
-        place, query, key_rows, value_rows, seg_q, seg_k, line, heads, members, []
+        place, query, key_rows, value_rows, seg_q, seg_k, line, heads, members, [bucket_hot]
     )
     weight_o = gather_mp(w_o)
     mixed_in = [mixed_out[0]] + [swap(mixed_out[r], "mp", r) for r in range(1, members)]
@@ -1010,82 +975,56 @@
         [far_cotangent] if few else [],
     )
     if few:
+        held = to_slots(
+            "grads_to_slots",
+            [(cotangent, slots[0]), (far_cotangent, slots[1])],
+            blocks,
+            size,
+            after=[ffn_input],
+        )
+        g_blocks = [held[0]] + [swap(held[r], "dp", r) for r in (1, 2, 3)]
         far_input = swap(ffn_input, "dp", 4)
         own = [send[0]] + [swap(send[r], "dp", r) for r in (1, 2, 3)]
         far = to_slots(
-            "far_to_slots", [(far_input, slots[1])], blocks, size, through=held[1:]
+            "far_to_slots", [(far_input, slots[1])], blocks, size, after=g_blocks[1:]
         )
-        held = [held[0]] + list(far[blocks:])
         far = [far[0]] + [swap(far[r], "dp", r) for r in (1, 2, 3)]
         x_sets = [own, far]
     else:
+        held = to_slots("grads_to_slots", [(cotangent, slots[0])], blocks, size)
+        g_blocks = [all_to_all_dp(held[0])]
         x_sets = [[all_to_all_dp(send[0])]]
-        g_blocks = [all_to_all_dp(held[0])]
-
-    kept, before, passed = [], [], list(held[1:])
+
+    kept, before, backs = [], [experts], []
     for at, x_blocks in enumerate(x_sets):
-        last = at == len(x_sets) - 1
-        result, *state = experts_forward(
-            "experts_forward" + str(at),
+        back, result, state = run_experts(
+            "run_experts" + str(at),
             place,
             w_in[0],
             w_out[0],
             router_wide,
             x_blocks,
-            experts,
-            before if last else None,
-            brief if last else long,
-            [] if last else passed,
+            g_blocks,
+            at,
+            before,
+            brief if at == len(x_sets) - 1 else long,
+            [] if at == len(x_sets) - 1 else [x_sets[-1][0]],
         )
-        passed = passed if last else state[5:]
-        kept.append(state[:5])
-        before = before + list(state[3:5])
+        kept.append(state)
+        backs.append(back)
+        before = before + result
+    actives, pre_grads, arrived, slot_grads = zip(*kept)
     if few:
-        g_blocks = [held[0]] + [swap(passed[r - 1], "dp", r) for r in (1, 2, 3)]
-    actives, slopes, arrived, plain, slot_gates = zip(*kept)
-    sets = list(zip(slopes, plain, slot_gates))
-    back, slot_grads, pre_grad = experts_backward(
-        "experts_backward" + str(len(sets) - 1),
-        place,
-        w_in[0],
-        w_out[0],
-        sets,
-        len(sets) - 1,
-        None,
-        g_blocks,
-        blocks,
-        brief,
-    )
-    pre_grads = [pre_grad]
-    if few:
-        own_back, _, pre_grad = experts_backward(
-            "experts_backward0",
-            place,
-            w_in[0],
-            w_out[0],
-            sets,
-            0,
-            slot_grads[0],
-            g_blocks,
-            blocks,
-            long,
-        )
-        pre_grads = [pre_grad] + pre_grads
-        far_back = [back[0]] + [swap(back[r], "dp", r) for r in (1, 2, 3)]
-        result_in = [result[0]] + [swap(result[r], "dp", r) for r in (1, 2, 3)]
+        own_back, far_back = backs
+        far_back = [far_back[0]] + [swap(far_back[r], "dp", r) for r in (1, 2, 3)]
         far_total, *passed = from_slots(
-            "back_from_slots",
-            far_back,
-            [slots[1]],
-            size,
-            [bf16],
-            after=result_in[1:],
-            through=own_back[1:],
+            "back_from_slots", far_back, [slots[1]], size, [bf16], through=own_back[1:]
         )
         far_sum = swap(far_total, "dp", 4)
         own_back = [own_back[0]] + [swap(passed[r - 1], "dp", r) for r in (1, 2, 3)]
+        result_in = [result[0]] + [swap(result[r], "dp", r) for r in (1, 2, 3)]
     else:
-        own_back, far_sum = [all_to_all_dp(back[0])], None
+        own_back, far_sum = [all_to_all_dp(backs[0][0])], None
         result_in = [all_to_all_dp(result[0])]
     near_w, base_w = expert_weight_grads(place, arrived, pre_grads, actives, slot_grads, members)
 
@@ -1109,24 +1048,10 @@
     grad_out, homed = homed[:members], homed[members:]
     hidden_grad, ffn_gain_grad, router_grad, near_o, base_o, near_w = homed
     grad_in = [grad_out[0]] + [swap(grad_out[r], "mp", r) for r in range(1, members)]
-    if few:
-        own_result, far_result = from_slots(
-            "result_from_slots",
-            result_in,
-            slots,
-            size,
-            [f32, bf16],
-            after=[hidden_grad],
-            cost=long,
-        )
-        far_result = swap(far_result, "dp", 4)
-    else:
-        (own_result,) = from_slots("result_from_slots", result_in, slots, size, [f32])
-        far_result = own_result
     near_o, near_w = swap(near_o, "mp", 1), swap(near_w, "mp", 1)
     piece = w_in.shape[2] // members
     far_first, far_next, far_last = far_sums(
-        near_w, base_w, near_o, base_o, [rows, piece, 2 * piece], grad_in[2:] + [own_result]
+        near_w, base_w, near_o, base_o, [rows, piece, 2 * piece], grad_in[2:]
     )
 
     *proj_grads, line_grad = attend_back(
@@ -1158,7 +1083,7 @@
         members,
         owners,
         heads,
-        [far_result],
+        result_in[1:],
     )
     near = swap(near, "mp", 1)
     far_normed = swap((base_far + near[rows:].astype(f32)).astype(bf16), "mp", 2)
@@ -1167,10 +1092,10 @@
         own_sum, far_part, small = fold_weights(
             weight_sums[0], arrived_sums, [far_next, near], [small]
         )
-        weight_grads = split_weights([own_sum, swap(far_part, "dp", 4)], span, [far_normed])
+        weight_grads = split_weights([own_sum, swap(far_part, "dp", 4)], span, [])
     else:
         joined_grad = lax.psum_scatter(weight_sums[0], "dp", scatter_dimension=0, tiled=True)
-        weight_grads = split_weights([joined_grad], span, [far_normed])
+        weight_grads = split_weights([joined_grad], span, [])
     normed_grad = base + near[:rows].astype(f32) + far_normed.astype(f32)
     resid = tokens.astype(f32)
     _, inverse_one = normalize(resid, norm_gain)
@@ -1180,14 +1105,18 @@
         hidden_grad + inverse_one * scaled - resid * inverse_one * inverse_one * inverse_one * inner
     ).astype(bf16)
 
-    block_out = hidden + own_result
     if few:
-        block_out = block_out + far_result.astype(f32)
+        own_result, far_result = from_slots(
+            "result_from_slots", result_in, slots, size, [f32, bf16], after=[own_sum]
+        )
+        block_out = hidden + own_result + swap(far_result, "dp", 4).astype(f32)
+    else:
+        (own_result,) = from_slots("result_from_slots", result_in, slots, size, [f32])
+        block_out = hidden + own_result
     block_out = block_out.astype(bf16)
-    far_in = jnp.concatenate([far_first[span:], far_next], axis=0).astype(f32)
-    w_in_grad = base_w[:piece] + near_w[:piece].astype(f32) + far_in
-    own_out = base_w[2 * piece : 3 * piece] + near_w[2 * piece : 3 * piece].astype(f32)
-    w_out_grad = own_out + far_last.astype(f32)
+    w_in_grad, w_out_grad = add_up(
+        base_w, near_w, [(far_first, span), (far_next, 0), (far_last, 0)], [far_normed]
+    )
     small = sum_over(sum_over(small, "dp"), "mp")
     return (
         block_out,

time: 300 us -> 309 us (1.030)
  waiting for transfers between devices: 58.8 us -> 78.6 us
  Pallas kernels: 144 us -> 135 us
  other arithmetic: 19.8 us -> 16.6 us
    ppermute x55, waiting for transfers between devices: 58.8 us -> 78.6 us  [swap(): return lax.ppermute(values, axis, [(i, i ^ step) for i in range(count)])]
    pallas_call x4 -> x3, Pallas kernels: 50.6 us -> 41.4 us  [the longest x2 35.2 us: run_experts(): pl.pallas_call(kernel, name=name, grid=(units // piece,), in_specs=[pl.Bl...]
    broadcast_in_dim x1 -> x0, other arithmetic: 6.42 us -> none  [on_device(): w_out_grad[None]]
  transfers between devices with their start and end apart: 55 -> 55, of which waited for: 18 -> 23; matrix products, arithmetic and copies ran while one was open for 13% -> 9% of each run, Pallas kernels for 41% -> 32%
where the time goes in v7:
time: 309 us; the launch traced here: 307 us
  Pallas kernels  135 us (44%)
  waiting for transfers between devices  78.6 us (25%)
  starting transfers between devices  58.5 us (19%)
  other arithmetic  16.6 us (5%)
  local copies, waits for them, and re-layouts  15.6 us (5%)
    ppermute x55, waiting for transfers between devices, swap(): return lax.ppermute(values, axis, [(i, i ^ step) for i in range(count)])  78.6 us
    pallas_call x14, Pallas kernels, call(): pl.pallas_call(body, name=name, grid=(1,), in_specs=in_specs + [pl.BlockS...  68.6 us
    ppermute x55, starting transfers between devices, swap(): return lax.ppermute(values, axis, [(i, i ^ step) for i in range(count)])  58.5 us
    pallas_call x2, Pallas kernels, run_experts(): pl.pallas_call(kernel, name=name, grid=(units // piece,), in_specs=[pl.Bl...  35.2 us
    pallas_call x1, Pallas kernels, expert_weight_grads(): pl.pallas_call(kernel, name='expert_weight_grads', grid_spec=pltpu.Prefet...  20.1 us
    pallas_call x1, Pallas kernels, add_up(): pl.pallas_call(kernel, name='add_up', grid=(1,), in_specs=specs + [pl.Blo...  6.27 us
  transfers between devices with their start and end apart: 55, of which 23 were waited for; matrix products, arithmetic and copies ran while one was open for 9% of the time, Pallas kernels for 32%

profile of v7, /device:TPU:0, one launch (start us, length us, event | category | flops | bytes accessed | tf_op | source)
XLA Modules:
  0.0 307.4 jit_solution(4277858101949226518)
XLA Ops:
  0.6 3.0 collective-permute-start.1
  3.7 2.6 collective-permute-start.15
  13.8 4.5 %collective-permute-done.3.refs_1_ = bf16[96,768]{1,0:T(8,128)(2,1)} collective-permute-done((bf16[96,768]{1,0:T(8,128)(2,1)}, bf16[96,768]{1,0:T(8,128)(2,1)}, u32[]{:S(2)}, u32[]{:S(2)}) %collective-permute-start.3) | collective-permute-done | bytes 147488 | tf_op jit(solution)/shard_map/ppermute | solution.py:44
  20.0 3.0 collective-permute-start.5
  36.0 5.2 %project.1 = (bf16[1024,768]{1,0:T(8,128)(2,1)}, bf16[1024,192]{1,0:T(8,128)(2,1)}, bf16[1024,192]{1,0:T(8,128)(2,1)}, bf16[1024,192]{1,0:T(8,128)(2,1)}, bf16[7...) custom-call(s32[2]{0:T(128)} %pad_add_fusion.2.refs_0_.me_ref.place_, ...), custom_call_target="tpu_custom_call", output_to_operand_aliasing={{8}: (10, {})} | custom-call | flops 10000000 | bytes 10000 | tf_op jit(solution)/shard_map/project/pallas_call | solution.py:69
  44.4 11.5 %attend.1 = (bf16[256,192]{1,0:T(8,128)(2,1)}, bf16[256,192]{1,0:T(8,128)(2,1)}, bf16[256,192]{1,0:T(8,128)(2,1)}, bf16[256,192]{1,0:T(8,128)(2,1)}) custom-call(s32[2]{0:T(128)} %pad_add_fusion.2.refs_0_.me_ref.place_ref, bf16[1024,192]{1,0:T(8,128)(2,1)} %get-tuple-element.103.refs_1_, bf16[1024,192]{1,0:T(8,128)(2,1)} %get-tuple-element.104.refs_2_, ...), custom_call_target="tpu_custom_call" | custom-call | flops 10000000 | bytes 10000 | tf_op jit(solution)/shard_map/attend/pallas_call | solution.py:69
  59.9 4.1 %collective-permute-done.8.refs_6_.refs_18_ = bf16[256,192]{1,0:T(8,128)(2,1)} collective-permute-done((bf16[256,192]{1,0:T(8,128)(2,1)}, bf16[256,192]{1,0:T(8,128)(2,1)}, u32[]{:S(2)}, u32[]{:S(2)}) %collective-permute-start.8) | collective-permute-done | bytes 98336 | tf_op jit(solution)/shard_map/ppermute | solution.py:44
  63.9 1.9 collective-permute-done.9.refs_7_.refs_19_
  65.8 3.9 %middle.1 = (f32[256,768]{1,0:T(8,128)}, bf16[256,768]{1,0:T(8,128)(2,1)}, f32[256,128]{1,0:T(8,128)}, bf16[128,768]{1,0:T(8,128)(2,1)}, bf16[128,768]{1,0:T(8,1...) custom-call(bf16[256,768]{1,0:T(8,128)(2,1)} %refs_0_.4, f32[1,768]{1,0:T(1,128)} %reshape.191.refs_1_.refs_4_, ...), custom_call_target="tpu_custom_call" | custom-call | flops 10000000 | bytes 10000 | tf_op jit(solution)/shard_map/middle/pallas_call | solution.py:69
  69.7 2.3 collective-permute-start.14
  72.0 2.7 grads_to_slots.1
  76.2 2.0 collective-permute-start.18
  79.7 11.1 %collective-permute-done.14.refs_0_ = bf16[256,768]{1,0:T(8,128)(2,1)} collective-permute-done((bf16[256,768]{1,0:T(8,128)(2,1)}, bf16[256,768]{1,0:T(8,128)(2,1)}, u32[]{:S(2)}, u32[]{:S(2)}) %collective-permute-start.14) | collective-permute-done | bytes 393248 | tf_op jit(solution)/shard_map/ppermute | solution.py:44
  90.8 2.6 collective-permute-start.24
  93.4 2.3 collective-permute-done.17.refs_3_.refs_6_
  95.6 8.1 %collective-permute-done.18.refs_4_.refs_7_ = bf16[256,768]{1,0:T(8,128)(2,1)} collective-permute-done((bf16[256,768]{1,0:T(8,128)(2,1)}, bf16[256,768]{1,0:T(8,128)(2,1)}, u32[]{:S(2)}, u32[]{:S(2)}) %collective-permute-start.18) | collective-permute-done | bytes 393248 | tf_op jit(solution)/shard_map/ppermute | solution.py:44
  103.7 2.1 far_to_slots.1
  105.9 1.8 collective-permute-start.19
  109.4 2.8 collective-permute-done.24.refs_3_
  112.2 17.3 %run_experts0.1 = (bf16[128,896]{1,0:T(8,128)(2,1)}, bf16[128,896]{1,0:T(8,128)(2,1)}, bf16[128,896]{1,0:T(8,128)(2,1)}, bf16[128,896]{1,0:T(8,128)(2,1)}, bf16[...) custom-call(s32[2]{0:T(128)} %pad_add_fusion.2.refs_0_.me_ref.place_, ...), custom_call_target="tpu_custom_call" | custom-call | flops 20000000000 | bytes 10000000 | tf_op jit(solution)/shard_map/run_experts0/pallas_call | solution.py:496
  129.5 17.9 %run_experts1.1 = (bf16[128,896]{1,0:T(8,128)(2,1)}, bf16[128,896]{1,0:T(8,128)(2,1)}, bf16[128,896]{1,0:T(8,128)(2,1)}, bf16[128,896]{1,0:T(8,128)(2,1)}, bf16[...) custom-call(s32[2]{0:T(128)} %pad_add_fusion.2.refs_0_.me_ref.place_, ...), custom_call_target="tpu_custom_call" | custom-call | flops 10000000 | bytes 10000 | tf_op jit(solution)/shard_map/run_experts1/pallas_call | solution.py:496
  147.4 1.9 collective-permute-start.28
  151.0 5.3 %collective-permute-done.28.refs_1_ = bf16[128,896]{1,0:T(8,128)(2,1)} collective-permute-done((bf16[128,896]{1,0:T(8,128)(2,1)}, bf16[128,896]{1,0:T(8,128)(2,1)}, u32[]{:S(2)}, u32[]{:S(2)}) %collective-permute-start.28) | collective-permute-done | bytes 229408 | tf_op jit(solution)/shard_map/ppermute | solution.py:44
  156.9 2.3 collective-permute-done.30.refs_3_
  159.1 2.7 back_from_slots.1
  166.0 20.1 %expert_weight_grads.1 = (bf16[3072,768]{1,0:T(8,128)(2,1)}, f32[3072,768]{1,0:T(8,128)}) custom-call(s32[2]{0:T(128)} %pad_add_fusion.2.refs_0_.me_ref.place_ref, bf16[512,768]{1,0:T(8,128)(2,1)} %get-tuple-element.144.refs_0_, bf16[512,768]{1,0:T(8,128)(2,1)} %get-tuple-element.145.refs_1_, bf16[512,3072]{1,0:T(8,128)(2,1)} %get-tuple-element.146.refs_2_, ...), custom_call_target="tpu_custom_call" | custom-call | flops 20000000000 | bytes 10000000 | tf_op jit(solution)/shard_map/expert_weight_grads/pallas_call | solution.py:647
  186.2 6.9 %home.1 = (bf16[256,192]{1,0:T(8,128)(2,1)}, bf16[256,192]{1,0:T(8,128)(2,1)}, bf16[256,192]{1,0:T(8,128)(2,1)}, bf16[256,192]{1,0:T(8,128)(2,1)}, f32[256,768]{...) custom-call(s32[8,256]{1,0:T(8,128)} %pad.24.refs_3_.refs_1_.refs_0_, ...), custom_call_target="tpu_custom_call", output_to_operand_aliasing={{9}: (20, {})} | custom-call | flops 10000000 | bytes 10000 | tf_op jit(solution)/shard_map/home/pallas_call | solution.py:69
  195.3 5.0 %collective-permute-done.36.refs_0_.refs_9_ = bf16[256,192]{1,0:T(8,128)(2,1)} collective-permute-done((bf16[256,192]{1,0:T(8,128)(2,1)}, bf16[256,192]{1,0:T(8,128)(2,1)}, u32[]{:S(2)}, u32[]{:S(2)}) %collective-permute-start.36) | collective-permute-done | bytes 98336 | tf_op jit(solution)/shard_map/ppermute | solution.py:44
  202.3 4.9 %far_sums.1 = (bf16[448,768]{1,0:T(8,128)(2,1)}, bf16[512,768]{1,0:T(8,128)(2,1)}, bf16[768,768]{1,0:T(8,128)(2,1)}) custom-call(bf16[3072,768]{1,0:T(8,128)(2,1)} %collective-permute-done.38.near_in.near_out.in_near.out_near, bf16[3072,768]{1,0:T(8,128)(2,1)} %collective-permute-done.38.near_in.near_out.in_near.out_near, ...), custom_call_target="tpu_custom_call" | custom-call | flops 10000000 | bytes 10000 | tf_op jit(solution)/shard_map/far_sums/pallas_call | solution.py:693
  214.4 16.1 %attend_back.1 = (bf16[1024,192]{1,0:T(8,128)(2,1)}, bf16[1024,192]{1,0:T(8,128)(2,1)}, bf16[1024,192]{1,0:T(8,128)(2,1)}, f32[8,640]{1,0:T(8,128)}) custom-call(s32[2]{0:T(128)} %pad_add_fusion.2.refs_0_.me_ref.place_ref, bf16[1024,192]{1,0:T(8,128)(2,1)} %get-tuple-element.103.refs_1_, bf16[1024,192]{1,0:T(8,128)(2,1)} %get-tuple-element.104.refs_2_, ...), custom_call_target="tpu_custom_call" | custom-call | flops 10000000 | bytes 10000 | tf_op jit(solution)/shard_map/attend_back/pallas_call | solution.py:69
  230.6 6.7 %input_grads.1 = (bf16[512,768]{1,0:T(8,128)(2,1)}, f32[256,768]{1,0:T(8,128)}, f32[256,768]{1,0:T(8,128)}, f32[24,768]{1,0:T(8,128)}, f32[192,768]{1,0:T(8,128)...) custom-call(s32[2]{0:T(128)} %pad_add_fusion.2.refs_0_.me_ref.place_ref, ...), custom_call_target="tpu_custom_call" | custom-call | flops 10000000 | bytes 10000 | tf_op jit(solution)/shard_map/input_grads/pallas_call | solution.py:69
  243.5 3.7 %collective-permute-done.41.refs_1_ = bf16[192,768]{1,0:T(8,128)(2,1)} collective-permute-done((bf16[192,768]{1,0:T(8,128)(2,1)}, bf16[192,768]{1,0:T(8,128)(2,1)}, u32[]{:S(2)}, u32[]{:S(2)}) %collective-permute-start.41) | collective-permute-done | bytes 294944 | tf_op jit(solution)/shard_map/ppermute | solution.py:44
  247.2 2.1 collective-permute-done.42.refs_2_
  249.3 5.4 %collective-permute-done.43.refs_3_ = bf16[192,768]{1,0:T(8,128)(2,1)} collective-permute-done((bf16[192,768]{1,0:T(8,128)(2,1)}, bf16[192,768]{1,0:T(8,128)(2,1)}, u32[]{:S(2)}, u32[]{:S(2)}) %collective-permute-start.43) | collective-permute-done | bytes 294944 | tf_op jit(solution)/shard_map/ppermute | solution.py:44
  254.7 2.1 fold_weights.1
  258.4 3.0 collective-permute-done.48
  264.0 2.7 collective-permute-done.49
  266.7 2.3 collective-permute-start.50
  269.0 3.0 collective-permute-done.50
  272.1 2.3 collective-permute-start.53
  276.7 2.0 add_convert_fusion
  279.1 3.4 %result_from_slots.1 = (f32[256,768]{1,0:T(8,128)}, bf16[256,768]{1,0:T(8,128)(2,1)}) custom-call(bf16[256,768]{1,0:T(8,128)(2,1)} %get-tuple-element.127.refs_0_, bf16[256,768]{1,0:T(8,128)(2,1)} %collective-permute-done.25.refs_16_.refs_1_, bf16[256,768]{1,0:T(8,128)(2,1)} %collective-permute-done.26.refs_17_.refs_2_, ...), custom_call_target="tpu_custom_call" | custom-call | flops 10000000 | bytes 10000 | tf_op jit(solution)/shard_map/result_from_slots/pallas_call | solution.py:69
  283.7 1.8 split_weights.1
  289.9 6.3 %add_up.1 = (f32[768,768]{1,0:T(8,128)}, f32[768,768]{1,0:T(8,128)}) custom-call(f32[3072,768]{1,0:T(8,128)} %get-tuple-element.158.base_in.base_out.in_base.out_base, bf16[3072,768]{1,0:T(8,128)(2,1)} %collective-permute-done.38.near_in.near_out.in_near.out_near, f32[3072,768]{1,0:T(8,128)} %get-tuple-element.158.base_in.base_out.in_base.out_base, ...), custom_call_target="tpu_custom_call" | custom-call | flops 10000000 | bytes 10000 | tf_op jit(solution)/shard_map/add_up/pallas_call | solution.py:812
  296.2 2.0 fusion
  298.2 4.6 %collective-permute-done.46 = bf16[256,768]{1,0:T(8,128)(2,1)} collective-permute-done((bf16[256,768]{1,0:T(8,128)(2,1)}, bf16[256,768]{1,0:T(8,128)(2,1)}, u32[]{:S(2)}, u32[]{:S(2)}) %collective-permute-start.46) | collective-permute-done | bytes 393248 | tf_op jit(solution)/shard_map/ppermute | solution.py:44
  302.8 2.4 add_convert_fusion.1
  305.1 2.3 fusion.5
  (131 shorter events, 70.7 us)
Async XLA Ops:
  0.6 12.5 %collective-permute-start.1 = (bf16[256,768]{1,0:T(8,128)(2,1)}, bf16[256,768]{1,0:T(8,128)(2,1)}, u32[]{:S(2)}, u32[]{:S(2)}) collective-permute-start(bf16[256,768]{1,0:T(8,128)(2,1)} %refs_0_.4), channel_id=1, source_target_pairs={{0,2},{1,3},{2,0},{3,1},{4,6},{5,7},{6,4},{7,5},{8,10},{9,11},{10,... | collective-permute-start | bytes 1179656 | tf_op jit(solution)/shard_map/ppermute | solution.py:44
  3.7 14.6 %collective-permute-start = (bf16[256,768]{1,0:T(8,128)(2,1)}, bf16[256,768]{1,0:T(8,128)(2,1)}, u32[]{:S(2)}, u32[]{:S(2)}) collective-permute-start(bf16[256,768]{1,0:T(8,128)(2,1)} %refs_0_.4), channel_id=1, source_target_pairs={{0,1},{1,0},{2,3},{3,2},{4,5},{5,4},{6,7},{7,6},{8,9},{9,8},{10,11... | collective-permute-start | bytes 1179656 | tf_op jit(solution)/shard_map/ppermute | solution.py:44
  3.7 38.0 %collective-permute-start.15 = (s32[256,2]{0,1:T(2,128)}, s32[256,2]{0,1:T(2,128)}, u32[]{:S(2)}, u32[]{:S(2)}) collective-permute-start(s32[256,2]{0,1:T(2,128)} %param.28), channel_id=1, source_target_pairs={{0,16},{4,20},{8,24},{12,28},{16,0},{20,4},{24,8},{28,12},{1,17},{... | collective-permute-start | bytes 6152 | tf_op jit(solution)/shard_map/ppermute | solution.py:44
  8.0 10.4 %collective-permute-start.3 = (bf16[96,768]{1,0:T(8,128)(2,1)}, bf16[96,768]{1,0:T(8,128)(2,1)}, u32[]{:S(2)}, u32[]{:S(2)}) collective-permute-start(bf16[96,768]{1,0:T(8,128)(2,1)} %pack_weights.1.refs_0_), channel_id=1, source_target_pairs={{0,16},{4,20},{8,24},{12,28},{16,0},{20,4},{24,8},{28,12},{1,17},{... | collective-permute-start | bytes 442376 | tf_op jit(solution)/shard_map/ppermute | solution.py:44
  13.2 22.8 %collective-permute-start.2 = (bf16[256,768]{1,0:T(8,128)(2,1)}, bf16[256,768]{1,0:T(8,128)(2,1)}, u32[]{:S(2)}, u32[]{:S(2)}) collective-permute-start(bf16[256,768]{1,0:T(8,128)(2,1)} %collective-permute-done.1.refs_3_.refs_4_), channel_id=1, source_target_pairs={{0,1},{1,0},{2,3},{3,2},{4,5},{5,4},{6,7},{7,6},{8,9},{9,8},{10,11... | collective-permute-start | bytes 1179656 | tf_op jit(solution)/shard_map/ppermute | solution.py:44
  20.0 15.9 %collective-permute-start.6 = (bf16[192,768]{1,0:T(8,128)(2,1)}, bf16[192,768]{1,0:T(8,128)(2,1)}, u32[]{:S(2)}, u32[]{:S(2)}) collective-permute-start(bf16[192,768]{1,0:T(8,128)(2,1)} %pair_up.1.refs_6_), channel_id=1, source_target_pairs={{0,12},{4,8},{8,4},{12,0},{16,28},{20,24},{24,20},{28,16},{1,13},{... | collective-permute-start | bytes 884744 | tf_op jit(solution)/shard_map/ppermute | solution.py:44
  20.0 15.9 %collective-permute-start.5 = (bf16[192,768]{1,0:T(8,128)(2,1)}, bf16[192,768]{1,0:T(8,128)(2,1)}, u32[]{:S(2)}, u32[]{:S(2)}) collective-permute-start(bf16[192,768]{1,0:T(8,128)(2,1)} %pair_up.1.refs_6_), channel_id=1, source_target_pairs={{0,8},{4,12},{8,0},{12,4},{16,24},{20,28},{24,16},{28,20},{1,9},{5... | collective-permute-start | bytes 884744 | tf_op jit(solution)/shard_map/ppermute | solution.py:44
  23.0 13.0 %collective-permute-start.4 = (bf16[192,768]{1,0:T(8,128)(2,1)}, bf16[192,768]{1,0:T(8,128)(2,1)}, u32[]{:S(2)}, u32[]{:S(2)}) collective-permute-start(bf16[192,768]{1,0:T(8,128)(2,1)} %pair_up.1.refs_6_), channel_id=1, source_target_pairs={{0,4},{4,0},{8,12},{12,8},{16,20},{20,16},{24,28},{28,24},{1,5},{5... | collective-permute-start | bytes 884744 | tf_op jit(solution)/shard_map/ppermute | solution.py:44
  41.2 15.2 %collective-permute-start.11 = (bf16[192,768]{1,0:T(8,128)(2,1)}, bf16[192,768]{1,0:T(8,128)(2,1)}, u32[]{:S(2)}, u32[]{:S(2)}) collective-permute-start(bf16[192,768]{1,0:T(8,128)(2,1)} %get-tuple-element.110.refs_8_.refs_12_), channel_id=1, source_target_pairs={{0,2},{1,3},{2,0},{3,1},{4,6},{5,7},{6,4},{7,5},{8,10},{9,11},{10,... | collective-permute-start | bytes 884744 | tf_op jit(solution)/shard_map/ppermute | solution.py:44
  42.4 23.4 %collective-permute-start.13 = (bf16[256,768]{1,0:T(8,128)(2,1)}, bf16[256,768]{1,0:T(8,128)(2,1)}, u32[]{:S(2)}, u32[]{:S(2)}) collective-permute-start(bf16[256,768]{1,0:T(8,128)(2,1)} %get-tuple-element.111), channel_id=1, source_target_pairs={{0,16},{4,20},{8,24},{12,28},{16,0},{20,4},{24,8},{28,12},{1,17},{... | collective-permute-start | bytes 1179656 | tf_op jit(solution)/shard_map/ppermute | solution.py:44
  44.4 21.4 %collective-permute-start.10 = (bf16[192,768]{1,0:T(8,128)(2,1)}, bf16[192,768]{1,0:T(8,128)(2,1)}, u32[]{:S(2)}, u32[]{:S(2)}) collective-permute-start(bf16[192,768]{1,0:T(8,128)(2,1)} %get-tuple-element.110.refs_8_.refs_12_), channel_id=1, source_target_pairs={{0,1},{1,0},{2,3},{3,2},{4,5},{5,4},{6,7},{7,6},{8,9},{9,8},{10,11... | collective-permute-start | bytes 884744 | tf_op jit(solution)/shard_map/ppermute | solution.py:44
  56.4 9.4 %collective-permute-start.12 = (bf16[192,768]{1,0:T(8,128)(2,1)}, bf16[192,768]{1,0:T(8,128)(2,1)}, u32[]{:S(2)}, u32[]{:S(2)}) collective-permute-start(bf16[192,768]{1,0:T(8,128)(2,1)} %collective-permute-done.11.refs_10_.refs_14_), channel_id=1, source_target_pairs={{0,1},{1,0},{2,3},{3,2},{4,5},{5,4},{6,7},{7,6},{8,9},{9,8},{10,11... | collective-permute-start | bytes 884744 | tf_op jit(solution)/shard_map/ppermute | solution.py:44
  57.3 6.7 %collective-permute-start.8 = (bf16[256,192]{1,0:T(8,128)(2,1)}, bf16[256,192]{1,0:T(8,128)(2,1)}, u32[]{:S(2)}, u32[]{:S(2)}) collective-permute-start(bf16[256,192]{1,0:T(8,128)(2,1)} %get-tuple-element.108), channel_id=1, source_target_pairs={{0,2},{1,3},{2,0},{3,1},{4,6},{5,7},{6,4},{7,5},{8,10},{9,11},{10,... | collective-permute-start | bytes 294920 | tf_op jit(solution)/shard_map/ppermute | solution.py:44
  58.9 7.0 %collective-permute-start.9 = (bf16[256,192]{1,0:T(8,128)(2,1)}, bf16[256,192]{1,0:T(8,128)(2,1)}, u32[]{:S(2)}, u32[]{:S(2)}) collective-permute-start(bf16[256,192]{1,0:T(8,128)(2,1)} %get-tuple-element.109), channel_id=1, source_target_pairs={{0,3},{1,2},{2,1},{3,0},{4,7},{5,6},{6,5},{7,4},{8,11},{9,10},{10,... | collective-permute-start | bytes 294920 | tf_op jit(solution)/shard_map/ppermute | solution.py:44
  69.7 21.1 %collective-permute-start.14 = (bf16[256,768]{1,0:T(8,128)(2,1)}, bf16[256,768]{1,0:T(8,128)(2,1)}, u32[]{:S(2)}, u32[]{:S(2)}) collective-permute-start(bf16[256,768]{1,0:T(8,128)(2,1)} %get-tuple-element.113.refs_4_.refs_6_), channel_id=1, source_target_pairs={{0,16},{4,20},{8,24},{12,28},{16,0},{20,4},{24,8},{28,12},{1,17},{... | collective-permute-start | bytes 1179656 | tf_op jit(solution)/shard_map/ppermute | solution.py:44
  74.7 16.1 %collective-permute-start.16 = (bf16[256,768]{1,0:T(8,128)(2,1)}, bf16[256,768]{1,0:T(8,128)(2,1)}, u32[]{:S(2)}, u32[]{:S(2)}) collective-permute-start(bf16[256,768]{1,0:T(8,128)(2,1)} %get-tuple-element.114), channel_id=1, source_target_pairs={{0,4},{4,0},{8,12},{12,8},{16,20},{20,16},{24,28},{28,24},{1,5},{5... | collective-permute-start | bytes 1179656 | tf_op jit(solution)/shard_map/ppermute | solution.py:44
  76.2 19.4 %collective-permute-start.17 = (bf16[256,768]{1,0:T(8,128)(2,1)}, bf16[256,768]{1,0:T(8,128)(2,1)}, u32[]{:S(2)}, u32[]{:S(2)}) collective-permute-start(bf16[256,768]{1,0:T(8,128)(2,1)} %get-tuple-element.115), channel_id=1, source_target_pairs={{0,8},{4,12},{8,0},{12,4},{16,24},{20,28},{24,16},{28,20},{1,9},{5... | collective-permute-start | bytes 1179656 | tf_op jit(solution)/shard_map/ppermute | solution.py:44
  76.2 27.5 %collective-permute-start.18 = (bf16[256,768]{1,0:T(8,128)(2,1)}, bf16[256,768]{1,0:T(8,128)(2,1)}, u32[]{:S(2)}, u32[]{:S(2)}) collective-permute-start(bf16[256,768]{1,0:T(8,128)(2,1)} %get-tuple-element.116), channel_id=1, source_target_pairs={{0,12},{4,8},{8,4},{12,0},{16,28},{20,24},{24,20},{28,16},{1,13},{... | collective-permute-start | bytes 1179656 | tf_op jit(solution)/shard_map/ppermute | solution.py:44
  78.2 29.5 %collective-permute-start.22 = (bf16[128,768]{1,0:T(8,128)(2,1)}, bf16[128,768]{1,0:T(8,128)(2,1)}, u32[]{:S(2)}, u32[]{:S(2)}) collective-permute-start(bf16[128,768]{1,0:T(8,128)(2,1)} %get-tuple-element.123), channel_id=1, source_target_pairs={{0,4},{4,0},{8,12},{12,8},{16,20},{20,16},{24,28},{28,24},{1,5},{5... | collective-permute-start | bytes 589832 | tf_op jit(solution)/shard_map/ppermute | solution.py:44
  90.8 18.6 %collective-permute-start.23 = (bf16[128,768]{1,0:T(8,128)(2,1)}, bf16[128,768]{1,0:T(8,128)(2,1)}, u32[]{:S(2)}, u32[]{:S(2)}) collective-permute-start(bf16[128,768]{1,0:T(8,128)(2,1)} %get-tuple-element.124), channel_id=1, source_target_pairs={{0,8},{4,12},{8,0},{12,4},{16,24},{20,28},{24,16},{28,20},{1,9},{5... | collective-permute-start | bytes 589832 | tf_op jit(solution)/shard_map/ppermute | solution.py:44
  90.8 21.4 %collective-permute-start.24 = (bf16[128,768]{1,0:T(8,128)(2,1)}, bf16[128,768]{1,0:T(8,128)(2,1)}, u32[]{:S(2)}, u32[]{:S(2)}) collective-permute-start(bf16[128,768]{1,0:T(8,128)(2,1)} %get-tuple-element.125), channel_id=1, source_target_pairs={{0,12},{4,8},{8,4},{12,0},{16,28},{20,24},{24,20},{28,16},{1,13},{... | collective-permute-start | bytes 589832 | tf_op jit(solution)/shard_map/ppermute | solution.py:44
  105.9 23.6 %collective-permute-start.19 = (bf16[128,768]{1,0:T(8,128)(2,1)}, bf16[128,768]{1,0:T(8,128)(2,1)}, u32[]{:S(2)}, u32[]{:S(2)}) collective-permute-start(bf16[128,768]{1,0:T(8,128)(2,1)} %get-tuple-element.118), channel_id=1, source_target_pairs={{0,4},{4,0},{8,12},{12,8},{16,20},{20,16},{24,28},{28,24},{1,5},{5... | collective-permute-start | bytes 589832 | tf_op jit(solution)/shard_map/ppermute | solution.py:44
  107.7 21.8 %collective-permute-start.20 = (bf16[128,768]{1,0:T(8,128)(2,1)}, bf16[128,768]{1,0:T(8,128)(2,1)}, u32[]{:S(2)}, u32[]{:S(2)}) collective-permute-start(bf16[128,768]{1,0:T(8,128)(2,1)} %get-tuple-element.119), channel_id=1, source_target_pairs={{0,8},{4,12},{8,0},{12,4},{16,24},{20,28},{24,16},{28,20},{1,9},{5... | collective-permute-start | bytes 589832 | tf_op jit(solution)/shard_map/ppermute | solution.py:44
  107.7 21.8 %collective-permute-start.21 = (bf16[128,768]{1,0:T(8,128)(2,1)}, bf16[128,768]{1,0:T(8,128)(2,1)}, u32[]{:S(2)}, u32[]{:S(2)}) collective-permute-start(bf16[128,768]{1,0:T(8,128)(2,1)} %get-tuple-element.120), channel_id=1, source_target_pairs={{0,12},{4,8},{8,4},{12,0},{16,28},{20,24},{24,20},{28,16},{1,13},{... | collective-permute-start | bytes 589832 | tf_op jit(solution)/shard_map/ppermute | solution.py:44
  147.4 8.9 %collective-permute-start.28 = (bf16[128,896]{1,0:T(8,128)(2,1)}, bf16[128,896]{1,0:T(8,128)(2,1)}, u32[]{:S(2)}, u32[]{:S(2)}) collective-permute-start(bf16[128,896]{1,0:T(8,128)(2,1)} %get-tuple-element.134), channel_id=1, source_target_pairs={{0,4},{4,0},{8,12},{12,8},{16,20},{20,16},{24,28},{28,24},{1,5},{5... | collective-permute-start | bytes 688136 | tf_op jit(solution)/shard_map/ppermute | solution.py:44
  149.3 7.6 %collective-permute-start.29 = (bf16[128,896]{1,0:T(8,128)(2,1)}, bf16[128,896]{1,0:T(8,128)(2,1)}, u32[]{:S(2)}, u32[]{:S(2)}) collective-permute-start(bf16[128,896]{1,0:T(8,128)(2,1)} %get-tuple-element.135), channel_id=1, source_target_pairs={{0,8},{4,12},{8,0},{12,4},{16,24},{20,28},{24,16},{28,20},{1,9},{5... | collective-permute-start | bytes 688136 | tf_op jit(solution)/shard_map/ppermute | solution.py:44
  149.3 9.8 %collective-permute-start.30 = (bf16[128,896]{1,0:T(8,128)(2,1)}, bf16[128,896]{1,0:T(8,128)(2,1)}, u32[]{:S(2)}, u32[]{:S(2)}) collective-permute-start(bf16[128,896]{1,0:T(8,128)(2,1)} %get-tuple-element.136), channel_id=1, source_target_pairs={{0,12},{4,8},{8,4},{12,0},{16,28},{20,24},{24,20},{28,16},{1,13},{... | collective-permute-start | bytes 688136 | tf_op jit(solution)/shard_map/ppermute | solution.py:44
  161.8 24.3 %collective-permute-start.31 = (bf16[128,896]{1,0:T(8,128)(2,1)}, bf16[128,896]{1,0:T(8,128)(2,1)}, u32[]{:S(2)}, u32[]{:S(2)}) collective-permute-start(bf16[128,896]{1,0:T(8,128)(2,1)} %get-tuple-element.140), channel_id=1, source_target_pairs={{0,4},{4,0},{8,12},{12,8},{16,20},{20,16},{24,28},{28,24},{1,5},{5... | collective-permute-start | bytes 688136 | tf_op jit(solution)/shard_map/ppermute | solution.py:44
  163.5 22.7 %collective-permute-start.32 = (bf16[128,896]{1,0:T(8,128)(2,1)}, bf16[128,896]{1,0:T(8,128)(2,1)}, u32[]{:S(2)}, u32[]{:S(2)}) collective-permute-start(bf16[128,896]{1,0:T(8,128)(2,1)} %get-tuple-element.141), channel_id=1, source_target_pairs={{0,8},{4,12},{8,0},{12,4},{16,24},{20,28},{24,16},{28,20},{1,9},{5... | collective-permute-start | bytes 688136 | tf_op jit(solution)/shard_map/ppermute | solution.py:44
  163.8 22.4 %collective-permute-start.33 = (bf16[128,896]{1,0:T(8,128)(2,1)}, bf16[128,896]{1,0:T(8,128)(2,1)}, u32[]{:S(2)}, u32[]{:S(2)}) collective-permute-start(bf16[128,896]{1,0:T(8,128)(2,1)} %get-tuple-element.142), channel_id=1, source_target_pairs={{0,12},{4,8},{8,4},{12,0},{16,28},{20,24},{24,20},{28,16},{1,13},{... | collective-permute-start | bytes 688136 | tf_op jit(solution)/shard_map/ppermute | solution.py:44
  165.3 20.9 %collective-permute-start.34 = (bf16[256,896]{1,0:T(8,128)(2,1)}, bf16[256,896]{1,0:T(8,128)(2,1)}, u32[]{:S(2)}, u32[]{:S(2)}) collective-permute-start(bf16[256,896]{1,0:T(8,128)(2,1)} %get-tuple-element.143), channel_id=1, source_target_pairs={{0,16},{4,20},{8,24},{12,28},{16,0},{20,4},{24,8},{28,12},{1,17},{... | collective-permute-start | bytes 1376264 | tf_op jit(solution)/shard_map/ppermute | solution.py:44
  193.1 9.2 %collective-permute-start.38 = (bf16[3072,768]{1,0:T(8,128)(2,1)}, bf16[3072,768]{1,0:T(8,128)(2,1)}, u32[]{:S(2)}, u32[]{:S(2)}) collective-permute-start(bf16[3072,768]{1,0:T(8,128)(2,1)} %get-tuple-element.157), channel_id=1, source_target_pairs={{0,1},{1,0},{2,3},{3,2},{4,5},{5,4},{6,7},{7,6},{8,9},{9,8},{10,11... | collective-permute-start | bytes 14155784 | tf_op jit(solution)/shard_map/ppermute | solution.py:44
  193.2 9.1 %collective-permute-start.39 = (bf16[384,768]{1,0:T(8,128)(2,1)}, bf16[384,768]{1,0:T(8,128)(2,1)}, u32[]{:S(2)}, u32[]{:S(2)}) collective-permute-start(bf16[384,768]{1,0:T(8,128)(2,1)} %get-tuple-element.159), channel_id=1, source_target_pairs={{0,1},{1,0},{2,3},{3,2},{4,5},{5,4},{6,7},{7,6},{8,9},{9,8},{10,11... | collective-permute-start | bytes 1769480 | tf_op jit(solution)/shard_map/ppermute | solution.py:44
  193.7 6.7 %collective-permute-start.36 = (bf16[256,192]{1,0:T(8,128)(2,1)}, bf16[256,192]{1,0:T(8,128)(2,1)}, u32[]{:S(2)}, u32[]{:S(2)}) collective-permute-start(bf16[256,192]{1,0:T(8,128)(2,1)} %get-tuple-element.155), channel_id=1, source_target_pairs={{0,2},{1,3},{2,0},{3,1},{4,6},{5,7},{6,4},{7,5},{8,10},{9,11},{10,... | collective-permute-start | bytes 294920 | tf_op jit(solution)/shard_map/ppermute | solution.py:44
  207.2 23.4 %collective-permute-start.40 = (bf16[448,768]{1,0:T(8,128)(2,1)}, bf16[448,768]{1,0:T(8,128)(2,1)}, u32[]{:S(2)}, u32[]{:S(2)}) collective-permute-start(bf16[448,768]{1,0:T(8,128)(2,1)} %get-tuple-element.161.refs_11_), channel_id=1, source_target_pairs={{0,2},{1,3},{2,0},{3,1},{4,6},{5,7},{6,4},{7,5},{8,10},{9,11},{10,... | collective-permute-start | bytes 2064392 | tf_op jit(solution)/shard_map/ppermute | solution.py:44
  208.9 21.7 %collective-permute-start.25 = (bf16[256,768]{1,0:T(8,128)(2,1)}, bf16[256,768]{1,0:T(8,128)(2,1)}, u32[]{:S(2)}, u32[]{:S(2)}) collective-permute-start(bf16[256,768]{1,0:T(8,128)(2,1)} %get-tuple-element.128), channel_id=1, source_target_pairs={{0,4},{4,0},{8,12},{12,8},{16,20},{20,16},{24,28},{28,24},{1,5},{5... | collective-permute-start | bytes 1179656 | tf_op jit(solution)/shard_map/ppermute | solution.py:44
  210.5 20.1 %collective-permute-start.26 = (bf16[256,768]{1,0:T(8,128)(2,1)}, bf16[256,768]{1,0:T(8,128)(2,1)}, u32[]{:S(2)}, u32[]{:S(2)}) collective-permute-start(bf16[256,768]{1,0:T(8,128)(2,1)} %get-tuple-element.129), channel_id=1, source_target_pairs={{0,8},{4,12},{8,0},{12,4},{16,24},{20,28},{24,16},{28,20},{1,9},{5... | collective-permute-start | bytes 1179656 | tf_op jit(solution)/shard_map/ppermute | solution.py:44
  212.2 18.4 %collective-permute-start.27 = (bf16[256,768]{1,0:T(8,128)(2,1)}, bf16[256,768]{1,0:T(8,128)(2,1)}, u32[]{:S(2)}, u32[]{:S(2)}) collective-permute-start(bf16[256,768]{1,0:T(8,128)(2,1)} %get-tuple-element.130), channel_id=1, source_target_pairs={{0,12},{4,8},{8,4},{12,0},{16,28},{20,24},{24,20},{28,16},{1,13},{... | collective-permute-start | bytes 1179656 | tf_op jit(solution)/shard_map/ppermute | solution.py:44
  214.0 27.8 %collective-permute-start.44 = (bf16[512,768]{1,0:T(8,128)(2,1)}, bf16[512,768]{1,0:T(8,128)(2,1)}, u32[]{:S(2)}, u32[]{:S(2)}) collective-permute-start(bf16[512,768]{1,0:T(8,128)(2,1)} %get-tuple-element.177), channel_id=1, source_target_pairs={{0,2},{1,3},{2,0},{3,1},{4,6},{5,7},{6,4},{7,5},{8,10},{9,11},{10,... | collective-permute-start | bytes 2359304 | tf_op jit(solution)/shard_map/ppermute | solution.py:44
  237.3 17.3 %collective-permute-start.45 = (bf16[512,768]{1,0:T(8,128)(2,1)}, bf16[512,768]{1,0:T(8,128)(2,1)}, u32[]{:S(2)}, u32[]{:S(2)}) collective-permute-start(bf16[512,768]{1,0:T(8,128)(2,1)} %get-tuple-element.178), channel_id=1, source_target_pairs={{0,1},{1,0},{2,3},{3,2},{4,5},{5,4},{6,7},{7,6},{8,9},{9,8},{10,11... | collective-permute-start | bytes 2359304 | tf_op jit(solution)/shard_map/ppermute | solution.py:44
  237.4 9.7 %collective-permute-start.41 = (bf16[192,768]{1,0:T(8,128)(2,1)}, bf16[192,768]{1,0:T(8,128)(2,1)}, u32[]{:S(2)}, u32[]{:S(2)}) collective-permute-start(bf16[192,768]{1,0:T(8,128)(2,1)} %get-tuple-element.173), channel_id=1, source_target_pairs={{0,4},{4,0},{8,12},{12,8},{16,20},{20,16},{24,28},{28,24},{1,5},{5... | collective-permute-start | bytes 884744 | tf_op jit(solution)/shard_map/ppermute | solution.py:44
  239.1 10.2 %collective-permute-start.42 = (bf16[192,768]{1,0:T(8,128)(2,1)}, bf16[192,768]{1,0:T(8,128)(2,1)}, u32[]{:S(2)}, u32[]{:S(2)}) collective-permute-start(bf16[192,768]{1,0:T(8,128)(2,1)} %get-tuple-element.174), channel_id=1, source_target_pairs={{0,8},{4,12},{8,0},{12,4},{16,24},{20,28},{24,16},{28,20},{1,9},{5... | collective-permute-start | bytes 884744 | tf_op jit(solution)/shard_map/ppermute | solution.py:44
  240.8 13.8 %collective-permute-start.43 = (bf16[192,768]{1,0:T(8,128)(2,1)}, bf16[192,768]{1,0:T(8,128)(2,1)}, u32[]{:S(2)}, u32[]{:S(2)}) collective-permute-start(bf16[192,768]{1,0:T(8,128)(2,1)} %get-tuple-element.175), channel_id=1, source_target_pairs={{0,12},{4,8},{8,4},{12,0},{16,28},{20,24},{24,20},{28,16},{1,13},{... | collective-permute-start | bytes 884744 | tf_op jit(solution)/shard_map/ppermute | solution.py:44
  241.9 46.4 %collective-permute-start.54 = (bf16[768,768]{1,0:T(8,128)(2,1)}, bf16[768,768]{1,0:T(8,128)(2,1)}, u32[]{:S(2)}, u32[]{:S(2)}) collective-permute-start(bf16[768,768]{1,0:T(8,128)(2,1)} %get-tuple-element.191), channel_id=1, source_target_pairs={{0,2},{1,3},{2,0},{3,1},{4,6},{5,7},{6,4},{7,5},{8,10},{9,11},{10,... | collective-permute-start | bytes 3538952 | tf_op jit(solution)/shard_map/ppermute | solution.py:44
  272.1 11.6 %collective-permute-start.53 = (bf16[96,768]{1,0:T(8,128)(2,1)}, bf16[96,768]{1,0:T(8,128)(2,1)}, u32[]{:S(2)}, u32[]{:S(2)}) collective-permute-start(bf16[96,768]{1,0:T(8,128)(2,1)} %get-tuple-element.186), channel_id=1, source_target_pairs={{0,16},{4,20},{8,24},{12,28},{16,0},{20,4},{24,8},{28,12},{1,17},{... | collective-permute-start | bytes 442376 | tf_op jit(solution)/shard_map/ppermute | solution.py:44
  275.1 10.5 %collective-permute-start.52 = (f32[24,768]{1,0:T(8,128)}, f32[24,768]{1,0:T(8,128)}, u32[]{:S(2)}, u32[]{:S(2)}) collective-permute-start(f32[24,768]{1,0:T(8,128)} %add.111), channel_id=1, source_target_pairs={{0,2},{1,3},{2,0},{3,1},{4,6},{5,7},{6,4},{7,5},{8,10},{9,11},{10,... | collective-permute-start | bytes 221192 | tf_op jit(solution)/shard_map/ppermute | solution.py:44
  278.7 11.2 %collective-permute-start.47 = (bf16[256,768]{1,0:T(8,128)(2,1)}, bf16[256,768]{1,0:T(8,128)(2,1)}, u32[]{:S(2)}, u32[]{:S(2)}) collective-permute-start(bf16[256,768]{1,0:T(8,128)(2,1)} %add_convert_fusion), channel_id=1, source_target_pairs={{0,2},{1,3},{2,0},{3,1},{4,6},{5,7},{6,4},{7,5},{8,10},{9,11},{10,... | collective-permute-start | bytes 1179656 | tf_op jit(solution)/shard_map/ppermute | solution.py:44
  282.5 20.3 %collective-permute-start.46 = (bf16[256,768]{1,0:T(8,128)(2,1)}, bf16[256,768]{1,0:T(8,128)(2,1)}, u32[]{:S(2)}, u32[]{:S(2)}) collective-permute-start(bf16[256,768]{1,0:T(8,128)(2,1)} %get-tuple-element.181), channel_id=1, source_target_pairs={{0,16},{4,20},{8,24},{12,28},{16,0},{20,4},{24,8},{28,12},{1,17},{... | collective-permute-start | bytes 1179656 | tf_op jit(solution)/shard_map/ppermute | solution.py:44
  (12 other events, 63.7 us)

commit v8 on v7

--- a/solution.py
+++ b/solution.py
@@ -282,7 +282,7 @@
     return both
 
 
-def project(place, token_blocks, pack_blocks, gain, cotangent, span):
+def project(place, token_blocks, pack_blocks, gain, cotangent, span, after):
     rows, width = token_blocks[0].shape
     members = len(token_blocks)
     seq_len = rows * members
@@ -322,6 +322,7 @@
         scratch=[pltpu.VMEM((width, width), bf16)],
         scalars=place,
         through=[cotangent],
+        after=after,
     )
 
 
@@ -418,6 +419,123 @@
 
 def join_rows(refs):
     return jnp.concatenate([ref[...] for ref in refs], axis=0)
+
+
+def experts_forward(place, w_in, w_out, w_router, x_blocks, experts, after):
+    width, units = w_in.shape
+    count, size = len(x_blocks), x_blocks[0].shape[0]
+    total, piece, chunk = size * count, 768, 256
+
+    def kernel(me_ref, w_in_ref, w_out_ref, router_ref, *refs):
+        x_refs, refs = refs[:count], refs[count + len(after) :]
+        active_ref, slope_ref, x_all, result_ref, gates_ref, gated_ref, result_sum = refs
+
+        @pl.when(pl.program_id(0) == 0)
+        def _():
+            x_all[...] = jnp.concatenate([ref[...] for ref in x_refs], axis=0)
+            probs = router_softmax(x_all[...], router_ref[...], experts)
+            lane = lax.broadcasted_iota(jnp.int32, probs.shape, 1)
+            own = jnp.sum(jnp.where(lane == me_ref[0], probs, 0.0), axis=1, keepdims=True)
+            gates_ref[...] = jnp.broadcast_to(own, gates_ref.shape)
+            result_sum[...] = jnp.zeros_like(result_sum)
+
+        for c in range(piece // chunk):
+            at = slice(c * chunk, (c + 1) * chunk)
+            pre_act = dot(x_all[...], w_in_ref[:, at], 1, 0)
+            below = 0.5 + 0.5 * lax.erf(pre_act * math.sqrt(0.5))
+            bell = jnp.exp(-0.5 * pre_act * pre_act) * (1.0 / math.sqrt(2.0 * math.pi))
+            active_ref[:, at] = (pre_act * below).astype(bf16)
+            slope_ref[:, at] = (below + pre_act * bell).astype(bf16)
+        result_sum[...] += dot(active_ref[...], w_out_ref[...], 1, 0)
+
+        @pl.when(pl.program_id(0) == pl.num_programs(0) - 1)
+        def _():
+            result = result_sum[...].astype(bf16)
+            result_ref[...] = result
+            gated_ref[...] = (gates_ref[:, 0:1] * result.astype(f32)).astype(bf16)
+
+    columns = pl.BlockSpec((total, piece), lambda i: (0, i))
+    rows = shape((total, width), bf16)
+    kept = [rows, rows, shape((total, 128), f32), rows]
+    return pl.pallas_call(
+        kernel,
+        name="experts_forward",
+        grid=(units // piece,),
+        in_specs=[
+            pl.BlockSpec(memory_space=pltpu.SMEM),
+            pl.BlockSpec((width, piece), lambda i: (0, i)),
+            pl.BlockSpec((piece, width), lambda i: (i, 0)),
+            whole(w_router.shape),
+        ]
+        + [whole(o.shape) for o in x_blocks]
+        + [pl.BlockSpec(memory_space=pl.ANY)] * len(after),
+        out_specs=[columns] * 2 + [whole(o.shape) for o in kept],
+        out_shape=[shape((total, units), bf16)] * 2 + kept,
+        scratch_shapes=[pltpu.VMEM((total, width), f32)],
+        compiler_params=limit(64),
+        cost_estimate=long,
+    )(place, w_in, w_out, w_router, *x_blocks, *after)
+
+
+def experts_backward(place, w_in, w_out, slope, result, gates, g_blocks, size):
+    width, units = w_in.shape
+    total, piece, chunk = slope.shape[0], 768, 256
+    count = len(g_blocks)
+
+    def kernel(me_ref, w_in_ref, w_out_ref, slope_ref, result_ref, gates_ref, *refs):
+        g_refs, back_refs = refs[:count], refs[count : 2 * count]
+        pre_grad_ref, s_all, back_sum = refs[2 * count :]
+
+        @pl.when(pl.program_id(0) == 0)
+        def _():
+            back_sum[...] = jnp.zeros_like(back_sum)
+            for b, ref in enumerate(g_refs):
+                rows = slice(b * size, (b + 1) * size)
+                s_all[rows, :] = (gates_ref[rows, 0:1] * ref[...].astype(f32)).astype(bf16)
+
+        for c in range(piece // chunk):
+            at = slice(c * chunk, (c + 1) * chunk)
+            active_grad = dot(s_all[...], w_out_ref[at, :], 1, 1)
+            pre_grad_ref[:, at] = (active_grad * slope_ref[:, at].astype(f32)).astype(bf16)
+        back_sum[...] += dot(pre_grad_ref[...], w_in_ref[...], 1, 1)
+
+        @pl.when(pl.program_id(0) == pl.num_programs(0) - 1)
+        def _():
+            lane = lax.broadcasted_iota(jnp.int32, (size, 128), 1)
+            for b, (ref, g_ref) in enumerate(zip(back_refs, g_refs)):
+                rows = slice(b * size, (b + 1) * size)
+                products = g_ref[...].astype(f32) * result_ref[rows, :].astype(f32)
+                gate_grad = jnp.sum(products, axis=1, keepdims=True)
+                upper = gate_grad.astype(bf16).astype(f32)
+                ref[:, :width] = back_sum[rows, :].astype(bf16)
+                ref[:, width:] = jnp.where(
+                    lane == me_ref[0],
+                    upper,
+                    jnp.where(lane == me_ref[0] + 64, gate_grad - upper, 0.0),
+                ).astype(bf16)
+
+    by_units = pl.BlockSpec((total, piece), lambda i: (0, i))
+    outs = [shape((size, width + 128), bf16)] * count
+    flat = pl.pallas_call(
+        kernel,
+        name="experts_backward",
+        grid=(units // piece,),
+        in_specs=[
+            pl.BlockSpec(memory_space=pltpu.SMEM),
+            pl.BlockSpec((width, piece), lambda i: (0, i)),
+            pl.BlockSpec((piece, width), lambda i: (i, 0)),
+            by_units,
+            whole(result.shape),
+            whole(gates.shape),
+        ]
+        + [whole((size, width))] * count,
+        out_specs=[whole(o.shape) for o in outs] + [by_units, whole((total, width))],
+        out_shape=outs + [shape((total, units), bf16), shape((total, width), bf16)],
+        scratch_shapes=[pltpu.VMEM((total, width), f32)],
+        compiler_params=limit(64),
+        cost_estimate=long,
+    )(place, w_in, w_out, slope, result, gates, *g_blocks)
+    return list(flat[:count]), flat[count], flat[count + 1]
 
 
 def run_experts(
@@ -718,6 +836,7 @@
     members,
     owners,
     heads,
+    buckets_all,
     after,
 ):
     seq_len, width = normed.shape
@@ -726,6 +845,7 @@
     part = width // owners
     few = owners == 8
     experts = router_grad.shape[0]
+    extra = -(-(3 + experts) // 16) * 16
 
     def kernel(place_ref, *refs):
         dq_ref, dk_ref, dv_ref, normed_ref, wq_ref, wk_ref, wv_ref, gain_ref = refs[:8]
@@ -757,17 +877,29 @@
                 grad * normed_ref[at, :].astype(f32), axis=0, keepdims=True
             )
             ref[first : first + rows, :] = grad.astype(ref.dtype)
+        table = dot(line_ref[...], hot_ref[...], 1, 0, highest)
+        bucket = lax.broadcasted_iota(jnp.int32, (128, width), 0)
+        lane = lax.broadcasted_iota(jnp.int32, (128, width), 1)
+        flat = jnp.zeros((1, width), f32)
+        for head in range(heads):
+            first = (place_ref[1] * heads + head) * buckets_all
+            spread = jnp.where((bucket < buckets_all) & (lane == bucket + first), 1.0, 0.0)
+            flat = flat + dot(table[head : head + 1, :], spread, 1, 0, highest)
         small_ref[...] = jnp.zeros_like(small_ref)
         small_ref[0:1, :] = gain_grad / gain_ref[...]
         small_ref[1:2, :] = ffn_gain_ref[...]
-        table = dot(line_ref[...], hot_ref[...], 1, 0, highest)
-        for m in range(members):
-            own = jnp.where(place_ref[1] == m, table[:heads, :], 0.0)
-            small_ref[2 + m * heads : 2 + (m + 1) * heads, :128] = own
-        small_ref[16:, :] = router_ref[...]
+        small_ref[2:3, :] = flat
+        small_ref[3 : 3 + experts, :] = router_ref[...]
+        if few:
+            upper, lower = two_halves(small_ref[...])
+            small_ref[...] = upper.astype(f32) + lower.astype(f32)
+            for ref in weight_refs[1:]:
+                ref[2 * part : 2 * part + extra, :] = upper
+                ref[2 * part + extra :, :] = lower
 
     if few:
-        weight_outs = [shape((2 * part, 4 * span), f32)] + [shape((2 * part, 4 * span), bf16)] * 3
+        weight_outs = [shape((2 * part, 4 * span), f32)]
+        weight_outs += [shape((2 * part + 2 * extra, 4 * span), bf16)] * 3
     else:
         weight_outs = [shape((width, 4 * span), f32)]
     return call(
@@ -782,7 +914,7 @@
             shape((2 * rows, width), bf16),
             shape((rows, width), f32),
             shape((rows, width), f32),
-            shape((16 + experts, width), f32),
+            shape((extra, width), f32),
         ]
         + weight_outs,
         scratch=[pltpu.VMEM((width, 4 * span), f32)],
@@ -791,7 +923,7 @@
     )
 
 
-def add_up(base, near, parts, after):
+def add_up(base, near, parts):
     size, width = base.shape[0] // 4, base.shape[1]
 
     def kernel(in_base, in_near, out_base, out_near, *refs):
@@ -813,52 +945,75 @@
         kernel,
         name="add_up",
         grid=(1,),
-        in_specs=specs + [pl.BlockSpec(memory_space=pl.ANY)] * len(after),
+        in_specs=specs,
         out_specs=[whole((size, width))] * 2,
         out_shape=[shape((size, width), f32)] * 2,
         compiler_params=limit(64),
-        cost_estimate=brief,
-    )(base, near, base, near, *[array for array, _ in parts], *after)
-
-
-def fold_weights(base, arrived, after, through):
-    part, width = base.shape[0] // 2, base.shape[1]
-
-    def kernel(base_ref, *refs):
-        own_ref, far_ref = refs[-2:]
+        cost_estimate=long,
+    )(base, near, base, near, *[array for array, _ in parts])
+
+
+def two_halves(values):
+    upper = values.astype(bf16)
+    return upper, (values - upper.astype(f32)).astype(bf16)
+
+
+def fold_weights(base, arrived, small, after):
+    part, width, extra = base.shape[0] // 2, base.shape[1], small.shape[0]
+
+    def kernel(base_ref, one_ref, two_ref, three_ref, small_ref, own_ref, far_ref, half_ref):
+        refs = (one_ref, two_ref, three_ref)
         total = base_ref[...]
-        for ref in refs[:-2]:
-            total = total + ref[...].astype(f32)
+        for ref in refs:
+            total = total + ref[: 2 * part, :].astype(f32)
         own_ref[...] = total[:part, :]
-        far_ref[...] = total[part:, :].astype(bf16)
+        far_ref[:part, :] = total[part:, :].astype(bf16)
+        one, two, three = [
+            ref[2 * part : 2 * part + extra, :].astype(f32)
+            + ref[2 * part + extra :, :].astype(f32)
+            for ref in refs
+        ]
+        upper, lower = two_halves((small_ref[...] + one) + (two + three))
+        far_ref[part : part + extra, :] = upper
+        far_ref[part + extra :, :] = lower
+        half_ref[...] = upper.astype(f32) + lower.astype(f32)
 
     return call(
         kernel,
         "fold_weights",
-        [base] + arrived,
-        [shape((part, width), f32), shape((part, width), bf16)],
+        [base] + arrived + [small],
+        [
+            shape((part, width), f32),
+            shape((part + 2 * extra, width), bf16),
+            shape((extra, width), f32),
+        ],
         after=after,
-        through=through,
-    )
-
-
-def split_weights(parts, span, after):
-    part = parts[0].shape[0]
+    )
+
+
+def split_weights(own, far, small, span, after):
+    part, extra = own.shape[0], small.shape[0]
 
     def kernel(*refs):
-        q_ref, k_ref, v_ref, o_ref = refs[-4:]
-        total = refs[0][...]
-        for ref in refs[1:-4]:
-            total = total + ref[...].astype(f32)
+        own_ref, small_ref, *far_refs = refs[:-5]
+        q_ref, k_ref, v_ref, o_ref, sum_ref = refs[-5:]
+        total, sums = own_ref[...], small_ref[...]
+        for ref in far_refs:
+            total = total + ref[:part, :].astype(f32)
+            sums = sums + (
+                ref[part : part + extra, :].astype(f32) + ref[part + extra :, :].astype(f32)
+            )
         for at, ref in enumerate((q_ref, k_ref, v_ref)):
             ref[...] = total[:, at * span : (at + 1) * span]
         o_ref[...] = total[:, 3 * span :].T
+        sum_ref[...] = sums
 
     return call(
         kernel,
         "split_weights",
-        parts,
-        [shape((part, span), f32)] * 3 + [shape((span, part), f32)],
+        [own, small] + ([] if far is None else [far]),
+        [shape((part, span), f32)] * 3
+        + [shape((span, part), f32), shape((extra, own.shape[1]), f32)],
         after=after,
     )
 
@@ -931,10 +1086,6 @@
     else:
         pack_blocks = [(lax.all_gather(pack, "dp", axis=0, tiled=True), (0,))]
     gain_one, gain_two = norm_gain.reshape(1, width), ffn_gain.reshape(1, width)
-    normed, query, key_rows, value_rows, weight_q, weight_k, weight_v, w_o, late_cotangent = (
-        project(place, token_blocks, pack_blocks, gain_one, cotangent, span)
-    )
-
     if few:
         blocks, size = 4, capacity
         slots = [slots_of(routes, me, capacity, experts, 4)]
@@ -942,9 +1093,6 @@
     else:
         blocks, size = 1, experts * capacity
         slots = [slots_of(routes, 0, capacity, experts, experts)]
-
-    if few:
-        far_cotangent = swap(late_cotangent, "dp", 4)
 
     line_buckets = jnp.pad(jnp.flip(buckets[: reach + 1]), (0, window - reach - 1))
     bucket_hot = (
@@ -955,13 +1103,22 @@
     line = jnp.dot(table, bucket_hot.T, precision=highest)
     seg_q = segments.reshape(seq_len, 1)
     seg_k = jnp.pad(segments.reshape(1, seq_len), ((0, 0), (reach, 0)), constant_values=-1)
+    router_wide = jnp.pad(w_router, ((0, 0), (0, 128 - experts)))
+    ready = [line, bucket_hot, seg_q, seg_k, router_wide, gain_two] + slots
+    normed, query, key_rows, value_rows, weight_q, weight_k, weight_v, w_o, late_cotangent = (
+        project(place, token_blocks, pack_blocks, gain_one, cotangent, span, ready)
+    )
+
+
+    if few:
+        far_cotangent = swap(late_cotangent, "dp", 4)
+
     mixed_out = attend(
         place, query, key_rows, value_rows, seg_q, seg_k, line, heads, members, [bucket_hot]
     )
     weight_o = gather_mp(w_o)
     mixed_in = [mixed_out[0]] + [swap(mixed_out[r], "mp", r) for r in range(1, members)]
 
-    router_wide = jnp.pad(w_router, ((0, 0), (0, 128 - experts)))
     hidden, ffn_input, router_probs, *send = middle(
         tokens,
         mixed_in,
@@ -986,7 +1143,7 @@
         far_input = swap(ffn_input, "dp", 4)
         own = [send[0]] + [swap(send[r], "dp", r) for r in (1, 2, 3)]
         far = to_slots(
-            "far_to_slots", [(far_input, slots[1])], blocks, size, after=g_blocks[1:]
+            "far_to_slots", [(far_input, slots[1])], blocks, size, after=g_blocks[1:3]
         )
         far = [far[0]] + [swap(far[r], "dp", r) for r in (1, 2, 3)]
         x_sets = [own, far]
@@ -995,24 +1152,32 @@
         g_blocks = [all_to_all_dp(held[0])]
         x_sets = [[all_to_all_dp(send[0])]]
 
-    kept, before, backs = [], [experts], []
-    for at, x_blocks in enumerate(x_sets):
-        back, result, state = run_experts(
-            "run_experts" + str(at),
-            place,
-            w_in[0],
-            w_out[0],
-            router_wide,
-            x_blocks,
-            g_blocks,
-            at,
-            before,
-            brief if at == len(x_sets) - 1 else long,
-            [] if at == len(x_sets) - 1 else [x_sets[-1][0]],
+    before = [experts]
+    if few:
+        active, slope, rows_in, plain, slot_gates, gated = experts_forward(
+            place, w_in[0], w_out[0], router_wide, x_sets[0], experts, far[:1]
         )
-        kept.append(state)
-        backs.append(back)
-        before = before + result
+        before = before + [gated]
+    back, result, state = run_experts(
+        "run_experts",
+        place,
+        w_in[0],
+        w_out[0],
+        router_wide,
+        x_sets[-1],
+        g_blocks,
+        len(x_sets) - 1,
+        before,
+        brief,
+        [],
+    )
+    kept, backs = [state], [back]
+    if few:
+        back, pre_grad, slot_grad = experts_backward(
+            place, w_in[0], w_out[0], slope, plain, slot_gates, g_blocks, size
+        )
+        kept = [(active, pre_grad, rows_in, slot_grad)] + kept
+        backs = [back] + backs
     actives, pre_grads, arrived, slot_grads = zip(*kept)
     if few:
         own_back, far_back = backs
@@ -1083,19 +1248,33 @@
         members,
         owners,
         heads,
+        buckets_all,
         result_in[1:],
+    )
+    w_in_grad, w_out_grad = add_up(
+        base_w, near_w, [(far_first, span), (far_next, 0), (far_last, 0)]
     )
     near = swap(near, "mp", 1)
     far_normed = swap((base_far + near[rows:].astype(f32)).astype(bf16), "mp", 2)
     if few:
         arrived_sums = [swap(weight_sums[r], "dp", r) for r in (1, 2, 3)]
         own_sum, far_part, small = fold_weights(
-            weight_sums[0], arrived_sums, [far_next, near], [small]
+            weight_sums[0], arrived_sums, small, [far_next, near]
         )
-        weight_grads = split_weights([own_sum, swap(far_part, "dp", 4)], span, [])
+        own_result, far_result = from_slots(
+            "result_from_slots", result_in, slots, size, [f32, bf16], after=[own_sum]
+        )
+        far_result = swap(far_result, "dp", 4)
+        *weight_grads, small = split_weights(
+            own_sum, swap(far_part, "dp", 4), small, span, [w_in_grad, far_normed]
+        )
     else:
         joined_grad = lax.psum_scatter(weight_sums[0], "dp", scatter_dimension=0, tiled=True)
-        weight_grads = split_weights([joined_grad], span, [])
+        *weight_grads, small = split_weights(
+            joined_grad, None, sum_over(small, "dp"), span, []
+        )
+        (own_result,) = from_slots("result_from_slots", result_in, slots, size, [f32])
+    small = sum_over(small, "mp")
     normed_grad = base + near[:rows].astype(f32) + far_normed.astype(f32)
     resid = tokens.astype(f32)
     _, inverse_one = normalize(resid, norm_gain)
@@ -1105,27 +1284,18 @@
         hidden_grad + inverse_one * scaled - resid * inverse_one * inverse_one * inverse_one * inner
     ).astype(bf16)
 
+    block_out = hidden + own_result
     if few:
-        own_result, far_result = from_slots(
-            "result_from_slots", result_in, slots, size, [f32, bf16], after=[own_sum]
-        )
-        block_out = hidden + own_result + swap(far_result, "dp", 4).astype(f32)
-    else:
-        (own_result,) = from_slots("result_from_slots", result_in, slots, size, [f32])
-        block_out = hidden + own_result
+        block_out = block_out + far_result.astype(f32)
     block_out = block_out.astype(bf16)
-    w_in_grad, w_out_grad = add_up(
-        base_w, near_w, [(far_first, span), (far_next, 0), (far_last, 0)], [far_normed]
-    )
-    small = sum_over(sum_over(small, "dp"), "mp")
     return (
         block_out,
         tokens_grad,
         small[0],
         *weight_grads,
-        small[2 : 2 + heads * members, :buckets_all].T,
+        small[2, : heads * members * buckets_all].reshape(heads * members, buckets_all).T,
         small[1],
-        small[16:].T,
+        small[3 : 3 + experts].T,
         w_in_grad[None],
         w_out_grad[None],
     )

time: 309 us -> 313 us (1.013)
  waiting for transfers between devices: 78.6 us -> 88 us
  Pallas kernels: 135 us -> 143 us
  starting transfers between devices: 58.5 us -> 51.1 us
  other arithmetic: 16.6 us -> 12.7 us
    pallas_call x1 -> x3, Pallas kernels: 6.27 us -> 31 us  [the longest x1 12.8 us: experts_forward(): pl.pallas_call(kernel, name='experts_forward', grid=(units // piece,), in...]
    pallas_call x2 -> x1, Pallas kernels: 35.2 us -> 17.9 us  [run_experts(): pl.pallas_call(kernel, name=name, grid=(units // piece,), in_specs=[pl.Bl...]
    ppermute x55 -> x52, waiting for transfers between devices: 78.6 us -> 88 us  [swap(): return lax.ppermute(values, axis, [(i, i ^ step) for i in range(count)])]
    ppermute x55 -> x52, starting transfers between devices: 58.5 us -> 51.1 us  [swap(): return lax.ppermute(values, axis, [(i, i ^ step) for i in range(count)])]
  transfers between devices with their start and end apart: 55 -> 52, of which waited for: 23 -> 18; matrix products, arithmetic and copies ran while one was open for 9% -> 9% of each run, Pallas kernels for 32% -> 33%
where the time goes in v8:
time: 313 us; the launch traced here: 312 us
  Pallas kernels  143 us (46%)
  waiting for transfers between devices  88 us (28%)
  starting transfers between devices  51.1 us (16%)
  local copies, waits for them, and re-layouts  14.4 us (5%)
  other arithmetic  12.7 us (4%)
    ppermute x52, waiting for transfers between devices, swap(): return lax.ppermute(values, axis, [(i, i ^ step) for i in range(count)])  88 us
    pallas_call x14, Pallas kernels, call(): pl.pallas_call(body, name=name, grid=(1,), in_specs=in_specs + [pl.BlockS...  69.3 us
    ppermute x52, starting transfers between devices, swap(): return lax.ppermute(values, axis, [(i, i ^ step) for i in range(count)])  51.1 us
    pallas_call x1, Pallas kernels, expert_weight_grads(): pl.pallas_call(kernel, name='expert_weight_grads', grid_spec=pltpu.Prefet...  19.9 us
    pallas_call x1, Pallas kernels, run_experts(): pl.pallas_call(kernel, name=name, grid=(units // piece,), in_specs=[pl.Bl...  17.9 us
    pallas_call x1, Pallas kernels, experts_forward(): pl.pallas_call(kernel, name='experts_forward', grid=(units // piece,), in...  12.8 us
    pallas_call x1, Pallas kernels, experts_backward(): pl.pallas_call(kernel, name='experts_backward', grid=(units // piece,), i...  11.8 us
    pallas_call x1, Pallas kernels, add_up(): pl.pallas_call(kernel, name='add_up', grid=(1,), in_specs=specs, out_spec...  6.31 us
  transfers between devices with their start and end apart: 52, of which 18 were waited for; matrix products, arithmetic and copies ran while one was open for 9% of the time, Pallas kernels for 33%

profile of v8, /device:TPU:0, one launch (start us, length us, event | category | flops | bytes accessed | tf_op | source)
XLA Modules:
  0.0 312.1 jit_solution(18125533461091676737)
XLA Ops:
  0.6 3.0 collective-permute-start.1
  3.7 2.6 collective-permute-start.7
  6.3 1.7 pack_weights.1.refs_0_
  11.0 1.7 fusion.8.refs_11_.refs_6_
  19.3 1.8 copy.37.refs_10_
  21.1 1.7 copy.34.refs_13_.refs_4_
  25.7 1.7 pair_up.1.refs_6_
  27.4 2.5 collective-permute-start.6
  32.2 6.2 %collective-permute-done.6.refs_9_ = bf16[192,768]{1,0:T(8,128)(2,1)} collective-permute-done((bf16[192,768]{1,0:T(8,128)(2,1)}, bf16[192,768]{1,0:T(8,128)(2,1)}, u32[]{:S(2)}, u32[]{:S(2)}) %collective-permute-start.6) | collective-permute-done | bytes 294944 | tf_op jit(solution)/shard_map/ppermute | solution.py:44
  38.4 6.0 %collective-permute-done.5.refs_8_ = bf16[192,768]{1,0:T(8,128)(2,1)} collective-permute-done((bf16[192,768]{1,0:T(8,128)(2,1)}, bf16[192,768]{1,0:T(8,128)(2,1)}, u32[]{:S(2)}, u32[]{:S(2)}) %collective-permute-start.5) | collective-permute-done | bytes 294944 | tf_op jit(solution)/shard_map/ppermute | solution.py:44
  44.4 5.2 %project.1 = (bf16[1024,768]{1,0:T(8,128)(2,1)}, bf16[1024,192]{1,0:T(8,128)(2,1)}, bf16[1024,192]{1,0:T(8,128)(2,1)}, bf16[1024,192]{1,0:T(8,128)(2,1)}, bf16[7...) custom-call(s32[2]{0:T(128)} %pad_add_fusion.2.refs_0_.me_ref.place_, ...), custom_call_target="tpu_custom_call", output_to_operand_aliasing={{8}: (10, {})} | custom-call | flops 10000000 | bytes 10000 | tf_op jit(solution)/shard_map/project/pallas_call | solution.py:69
  50.1 2.6 collective-permute-start.14
  52.7 6.1 %collective-permute-done.12.refs_10_.refs_14_ = bf16[192,768]{1,0:T(8,128)(2,1)} collective-permute-done((bf16[192,768]{1,0:T(8,128)(2,1)}, bf16[192,768]{1,0:T(8,128)(2,1)}, u32[]{:S(2)}, u32[]{:S(2)}) %collective-permute-start.12) | collective-permute-done | bytes 294944 | tf_op jit(solution)/shard_map/ppermute | solution.py:44
  58.8 11.5 %attend.1 = (bf16[256,192]{1,0:T(8,128)(2,1)}, bf16[256,192]{1,0:T(8,128)(2,1)}, bf16[256,192]{1,0:T(8,128)(2,1)}, bf16[256,192]{1,0:T(8,128)(2,1)}) custom-call(s32[2]{0:T(128)} %pad_add_fusion.2.refs_0_.me_ref.place_ref, bf16[1024,192]{1,0:T(8,128)(2,1)} %get-tuple-element.107.refs_1_, bf16[1024,192]{1,0:T(8,128)(2,1)} %get-tuple-element.108.refs_2_, ...), custom_call_target="tpu_custom_call" | custom-call | flops 10000000 | bytes 10000 | tf_op jit(solution)/shard_map/attend/pallas_call | solution.py:69
  72.4 5.0 %collective-permute-done.9.refs_6_.refs_18_ = bf16[256,192]{1,0:T(8,128)(2,1)} collective-permute-done((bf16[256,192]{1,0:T(8,128)(2,1)}, bf16[256,192]{1,0:T(8,128)(2,1)}, u32[]{:S(2)}, u32[]{:S(2)}) %collective-permute-start.9) | collective-permute-done | bytes 98336 | tf_op jit(solution)/shard_map/ppermute | solution.py:44
  78.4 3.9 %middle.1 = (f32[256,768]{1,0:T(8,128)}, bf16[256,768]{1,0:T(8,128)(2,1)}, f32[256,128]{1,0:T(8,128)}, bf16[128,768]{1,0:T(8,128)(2,1)}, bf16[128,768]{1,0:T(8,1...) custom-call(bf16[256,768]{1,0:T(8,128)(2,1)} %refs_0_.4, f32[1,768]{1,0:T(1,128)} %reshape.191.refs_16_.refs_1_.refs_4_, ...), custom_call_target="tpu_custom_call" | custom-call | flops 10000000 | bytes 10000 | tf_op jit(solution)/shard_map/middle/pallas_call | solution.py:69
  82.3 2.6 collective-permute-start.15
  84.9 2.7 grads_to_slots.1
  91.7 12.1 %collective-permute-done.15.refs_0_ = bf16[256,768]{1,0:T(8,128)(2,1)} collective-permute-done((bf16[256,768]{1,0:T(8,128)(2,1)}, bf16[256,768]{1,0:T(8,128)(2,1)}, u32[]{:S(2)}, u32[]{:S(2)}) %collective-permute-start.15) | collective-permute-done | bytes 393248 | tf_op jit(solution)/shard_map/ppermute | solution.py:44
  106.8 2.0 collective-permute-done.17.refs_3_.refs_6_.refs_2_
  108.7 2.2 far_to_slots.1
  114.4 2.9 collective-permute-done.24.refs_3_
  117.2 12.8 %experts_forward.1 = (bf16[512,3072]{1,0:T(8,128)(2,1)}, bf16[512,3072]{1,0:T(8,128)(2,1)}, bf16[512,768]{1,0:T(8,128)(2,1)}, bf16[512,768]{1,0:T(8,128)(2,1)}, ...) custom-call(s32[2]{0:T(128)} %pad_add_fusion.2.refs_0_.me_ref.place_ref, bf16[768,3072]{1,0:T(8,128)(2,1)} %bitcast.45, ...), custom_call_target="tpu_custom_call" | custom-call | flops 20000000000 | bytes 10000000 | tf_op jit(solution)/shard_map/experts_forward/pallas_call | solution.py:460
  130.1 3.2 %collective-permute-done.20.refs_3_ = bf16[128,768]{1,0:T(8,128)(2,1)} collective-permute-done((bf16[128,768]{1,0:T(8,128)(2,1)}, bf16[128,768]{1,0:T(8,128)(2,1)}, u32[]{:S(2)}, u32[]{:S(2)}) %collective-permute-start.20) | collective-permute-done | bytes 196640 | tf_op jit(solution)/shard_map/ppermute | solution.py:44
  133.3 17.9 %run_experts.1 = (bf16[128,896]{1,0:T(8,128)(2,1)}, bf16[128,896]{1,0:T(8,128)(2,1)}, bf16[128,896]{1,0:T(8,128)(2,1)}, bf16[128,896]{1,0:T(8,128)(2,1)}, bf16[2...) custom-call(s32[2]{0:T(128)} %pad_add_fusion.2.refs_0_.me_ref.place_, ...), custom_call_target="tpu_custom_call" | custom-call | flops 10000000 | bytes 10000 | tf_op jit(solution)/shard_map/run_experts/pallas_call | solution.py:614
  152.7 2.0 collective-permute-start.30
  154.7 11.8 %experts_backward.1 = (bf16[128,896]{1,0:T(8,128)(2,1)}, bf16[128,896]{1,0:T(8,128)(2,1)}, bf16[128,896]{1,0:T(8,128)(2,1)}, bf16[128,896]{1,0:T(8,128)(2,1)}, b...) custom-call(s32[2]{0:T(128)} %pad_add_fusion.2.refs_0_.me_ref.place_ref, bf16[768,3072]{1,0:T(8,128)(2,1)} %bitcast.47, ...), custom_call_target="tpu_custom_call" | custom-call | flops 20000000000 | bytes 10000000 | tf_op jit(solution)/shard_map/experts_backward/pallas_call | solution.py:519
  166.6 2.7 back_from_slots.1
  170.8 2.0 collective-permute-start.33
  173.7 19.9 %expert_weight_grads.1 = (bf16[3072,768]{1,0:T(8,128)(2,1)}, f32[3072,768]{1,0:T(8,128)}) custom-call(s32[2]{0:T(128)} %pad_add_fusion.2.refs_0_.me_ref.place_ref, bf16[512,768]{1,0:T(8,128)(2,1)} %get-tuple-element.151.refs_0_, bf16[512,768]{1,0:T(8,128)(2,1)} %get-tuple-element.152.refs_1_, bf16[512,3072]{1,0:T(8,128)(2,1)} %get-tuple-element.153.refs_2_, ...), custom_call_target="tpu_custom_call" | custom-call | flops 20000000000 | bytes 10000000 | tf_op jit(solution)/shard_map/expert_weight_grads/pallas_call | solution.py:765
  194.0 6.9 %home.1 = (bf16[256,192]{1,0:T(8,128)(2,1)}, bf16[256,192]{1,0:T(8,128)(2,1)}, bf16[256,192]{1,0:T(8,128)(2,1)}, bf16[256,192]{1,0:T(8,128)(2,1)}, f32[256,768]{...) custom-call(s32[8,256]{1,0:T(8,128)} %pad.24.refs_17_.refs_3_.refs_1, ...), custom_call_target="tpu_custom_call", output_to_operand_aliasing={{9}: (20, {})} | custom-call | flops 10000000 | bytes 10000 | tf_op jit(solution)/shard_map/home/pallas_call | solution.py:69
  202.9 5.2 %collective-permute-done.36.refs_0_.refs_9_ = bf16[256,192]{1,0:T(8,128)(2,1)} collective-permute-done((bf16[256,192]{1,0:T(8,128)(2,1)}, bf16[256,192]{1,0:T(8,128)(2,1)}, u32[]{:S(2)}, u32[]{:S(2)}) %collective-permute-start.36) | collective-permute-done | bytes 98336 | tf_op jit(solution)/shard_map/ppermute | solution.py:44
  210.0 4.9 %far_sums.1 = (bf16[448,768]{1,0:T(8,128)(2,1)}, bf16[512,768]{1,0:T(8,128)(2,1)}, bf16[768,768]{1,0:T(8,128)(2,1)}) custom-call(bf16[3072,768]{1,0:T(8,128)(2,1)} %collective-permute-done.38.near_in.near_out.in_near.out_near, bf16[3072,768]{1,0:T(8,128)(2,1)} %collective-permute-done.38.near_in.near_out.in_near.out_near, ...), custom_call_target="tpu_custom_call" | custom-call | flops 10000000 | bytes 10000 | tf_op jit(solution)/shard_map/far_sums/pallas_call | solution.py:811
  216.8 1.7 collective-permute-start.26
  218.9 1.7 collective-permute-done.35.refs_8_
  222.1 16.1 %attend_back.1 = (bf16[1024,192]{1,0:T(8,128)(2,1)}, bf16[1024,192]{1,0:T(8,128)(2,1)}, bf16[1024,192]{1,0:T(8,128)(2,1)}, f32[8,640]{1,0:T(8,128)}) custom-call(s32[2]{0:T(128)} %pad_add_fusion.2.refs_0_.me_ref.place_ref, bf16[1024,192]{1,0:T(8,128)(2,1)} %get-tuple-element.107.refs_1_, bf16[1024,192]{1,0:T(8,128)(2,1)} %get-tuple-element.108.refs_2_, ...), custom_call_target="tpu_custom_call" | custom-call | flops 10000000 | bytes 10000 | tf_op jit(solution)/shard_map/attend_back/pallas_call | solution.py:69
  238.2 7.2 %input_grads.1 = (bf16[512,768]{1,0:T(8,128)(2,1)}, f32[256,768]{1,0:T(8,128)}, f32[256,768]{1,0:T(8,128)}, f32[16,768]{1,0:T(8,128)}, f32[192,768]{1,0:T(8,128)...) custom-call(s32[2]{0:T(128)} %pad_add_fusion.2.refs_0_.me_ref.place_ref, ...), custom_call_target="tpu_custom_call" | custom-call | flops 10000000 | bytes 10000 | tf_op jit(solution)/shard_map/input_grads/pallas_call | solution.py:69
  247.5 1.7 collective-permute-start.42
  250.6 1.9 add_convert_fusion
  252.6 22.2 %collective-permute-done.44.refs_5_.refs_1_ = bf16[512,768]{1,0:T(8,128)(2,1)} collective-permute-done((bf16[512,768]{1,0:T(8,128)(2,1)}, bf16[512,768]{1,0:T(8,128)(2,1)}, u32[]{:S(2)}, u32[]{:S(2)}) %collective-permute-start.44) | collective-permute-done | bytes 786464 | tf_op jit(solution)/shard_map/ppermute | solution.py:44
  275.3 2.2 fold_weights.1
  279.2 6.3 %add_up.1 = (f32[768,768]{1,0:T(8,128)}, f32[768,768]{1,0:T(8,128)}) custom-call(f32[3072,768]{1,0:T(8,128)} %get-tuple-element.165.base_in.base_out.in_base.out_base, bf16[3072,768]{1,0:T(8,128)(2,1)} %collective-permute-done.38.near_in.near_out.in_near.out_near, f32[3072,768]{1,0:T(8,128)} %get-tuple-element.165.base_in.base_out.in_base.out_base, ...), custom_call_target="tpu_custom_call" | custom-call | flops 20000000000 | bytes 10000000 | tf_op jit(solution)/shard_map/add_up/pallas_call | solution.py:944
  285.5 3.4 %result_from_slots.1 = (f32[256,768]{1,0:T(8,128)}, bf16[256,768]{1,0:T(8,128)(2,1)}) custom-call(bf16[256,768]{1,0:T(8,128)(2,1)} %get-tuple-element.131.refs_0_, bf16[256,768]{1,0:T(8,128)(2,1)} %collective-permute-done.25.refs_16_.refs_1_, bf16[256,768]{1,0:T(8,128)(2,1)} %collective-permute-done.26.refs_17_.refs_2_, ...), custom_call_target="tpu_custom_call" | custom-call | flops 10000000 | bytes 10000 | tf_op jit(solution)/shard_map/result_from_slots/pallas_call | solution.py:69
  290.2 1.9 split_weights.1
  292.1 1.9 fusion
  294.1 2.8 fusion.5
  298.5 9.7 %collective-permute-done.46 = bf16[256,768]{1,0:T(8,128)(2,1)} collective-permute-done((bf16[256,768]{1,0:T(8,128)(2,1)}, bf16[256,768]{1,0:T(8,128)(2,1)}, u32[]{:S(2)}, u32[]{:S(2)}) %collective-permute-start.46) | collective-permute-done | bytes 393248 | tf_op jit(solution)/shard_map/ppermute | solution.py:44
  308.3 1.9 add_convert_fusion.1
  (122 shorter events, 51.6 us)
Async XLA Ops:
  0.6 23.6 %collective-permute-start.1 = (bf16[256,768]{1,0:T(8,128)(2,1)}, bf16[256,768]{1,0:T(8,128)(2,1)}, u32[]{:S(2)}, u32[]{:S(2)}) collective-permute-start(bf16[256,768]{1,0:T(8,128)(2,1)} %refs_0_.4), channel_id=1, source_target_pairs={{0,2},{1,3},{2,0},{3,1},{4,6},{5,7},{6,4},{7,5},{8,10},{9,11},{10,... | collective-permute-start | bytes 1179656 | tf_op jit(solution)/shard_map/ppermute | solution.py:44
  3.7 22.0 %collective-permute-start = (bf16[256,768]{1,0:T(8,128)(2,1)}, bf16[256,768]{1,0:T(8,128)(2,1)}, u32[]{:S(2)}, u32[]{:S(2)}) collective-permute-start(bf16[256,768]{1,0:T(8,128)(2,1)} %refs_0_.4), channel_id=1, source_target_pairs={{0,1},{1,0},{2,3},{3,2},{4,5},{5,4},{6,7},{7,6},{8,9},{9,8},{10,11... | collective-permute-start | bytes 1179656 | tf_op jit(solution)/shard_map/ppermute | solution.py:44
  3.7 19.9 %collective-permute-start.7 = (s32[256,2]{0,1:T(2,128)}, s32[256,2]{0,1:T(2,128)}, u32[]{:S(2)}, u32[]{:S(2)}) collective-permute-start(s32[256,2]{0,1:T(2,128)} %param.28), channel_id=1, source_target_pairs={{0,16},{4,20},{8,24},{12,28},{16,0},{20,4},{24,8},{28,12},{1,17},{... | collective-permute-start | bytes 6152 | tf_op jit(solution)/shard_map/ppermute | solution.py:44
  8.0 17.7 %collective-permute-start.3 = (bf16[96,768]{1,0:T(8,128)(2,1)}, bf16[96,768]{1,0:T(8,128)(2,1)}, u32[]{:S(2)}, u32[]{:S(2)}) collective-permute-start(bf16[96,768]{1,0:T(8,128)(2,1)} %pack_weights.1.refs_0_), channel_id=1, source_target_pairs={{0,16},{4,20},{8,24},{12,28},{16,0},{20,4},{24,8},{28,12},{1,17},{... | collective-permute-start | bytes 442376 | tf_op jit(solution)/shard_map/ppermute | solution.py:44
  24.3 20.1 %collective-permute-start.2 = (bf16[256,768]{1,0:T(8,128)(2,1)}, bf16[256,768]{1,0:T(8,128)(2,1)}, u32[]{:S(2)}, u32[]{:S(2)}) collective-permute-start(bf16[256,768]{1,0:T(8,128)(2,1)} %collective-permute-done.1.refs_3_.refs_4_), channel_id=1, source_target_pairs={{0,1},{1,0},{2,3},{3,2},{4,5},{5,4},{6,7},{7,6},{8,9},{9,8},{10,11... | collective-permute-start | bytes 1179656 | tf_op jit(solution)/shard_map/ppermute | solution.py:44
  27.4 11.1 %collective-permute-start.6 = (bf16[192,768]{1,0:T(8,128)(2,1)}, bf16[192,768]{1,0:T(8,128)(2,1)}, u32[]{:S(2)}, u32[]{:S(2)}) collective-permute-start(bf16[192,768]{1,0:T(8,128)(2,1)} %pair_up.1.refs_6_), channel_id=1, source_target_pairs={{0,12},{4,8},{8,4},{12,0},{16,28},{20,24},{24,20},{28,16},{1,13},{... | collective-permute-start | bytes 884744 | tf_op jit(solution)/shard_map/ppermute | solution.py:44
  29.9 14.5 %collective-permute-start.5 = (bf16[192,768]{1,0:T(8,128)(2,1)}, bf16[192,768]{1,0:T(8,128)(2,1)}, u32[]{:S(2)}, u32[]{:S(2)}) collective-permute-start(bf16[192,768]{1,0:T(8,128)(2,1)} %pair_up.1.refs_6_), channel_id=1, source_target_pairs={{0,8},{4,12},{8,0},{12,4},{16,24},{20,28},{24,16},{28,20},{1,9},{5... | collective-permute-start | bytes 884744 | tf_op jit(solution)/shard_map/ppermute | solution.py:44
  30.3 14.1 %collective-permute-start.4 = (bf16[192,768]{1,0:T(8,128)(2,1)}, bf16[192,768]{1,0:T(8,128)(2,1)}, u32[]{:S(2)}, u32[]{:S(2)}) collective-permute-start(bf16[192,768]{1,0:T(8,128)(2,1)} %pair_up.1.refs_6_), channel_id=1, source_target_pairs={{0,4},{4,0},{8,12},{12,8},{16,20},{20,16},{24,28},{28,24},{1,5},{5... | collective-permute-start | bytes 884744 | tf_op jit(solution)/shard_map/ppermute | solution.py:44
  49.6 9.2 %collective-permute-start.12 = (bf16[192,768]{1,0:T(8,128)(2,1)}, bf16[192,768]{1,0:T(8,128)(2,1)}, u32[]{:S(2)}, u32[]{:S(2)}) collective-permute-start(bf16[192,768]{1,0:T(8,128)(2,1)} %get-tuple-element.114.refs_8_.refs_12_), channel_id=1, source_target_pairs={{0,2},{1,3},{2,0},{3,1},{4,6},{5,7},{6,4},{7,5},{8,10},{9,11},{10,... | collective-permute-start | bytes 884744 | tf_op jit(solution)/shard_map/ppermute | solution.py:44
  50.1 28.3 %collective-permute-start.14 = (bf16[256,768]{1,0:T(8,128)(2,1)}, bf16[256,768]{1,0:T(8,128)(2,1)}, u32[]{:S(2)}, u32[]{:S(2)}) collective-permute-start(bf16[256,768]{1,0:T(8,128)(2,1)} %get-tuple-element.115), channel_id=1, source_target_pairs={{0,16},{4,20},{8,24},{12,28},{16,0},{20,4},{24,8},{28,12},{1,17},{... | collective-permute-start | bytes 1179656 | tf_op jit(solution)/shard_map/ppermute | solution.py:44
  52.7 25.7 %collective-permute-start.11 = (bf16[192,768]{1,0:T(8,128)(2,1)}, bf16[192,768]{1,0:T(8,128)(2,1)}, u32[]{:S(2)}, u32[]{:S(2)}) collective-permute-start(bf16[192,768]{1,0:T(8,128)(2,1)} %get-tuple-element.114.refs_8_.refs_12_), channel_id=1, source_target_pairs={{0,1},{1,0},{2,3},{3,2},{4,5},{5,4},{6,7},{7,6},{8,9},{9,8},{10,11... | collective-permute-start | bytes 884744 | tf_op jit(solution)/shard_map/ppermute | solution.py:44
  58.8 19.7 %collective-permute-start.13 = (bf16[192,768]{1,0:T(8,128)(2,1)}, bf16[192,768]{1,0:T(8,128)(2,1)}, u32[]{:S(2)}, u32[]{:S(2)}) collective-permute-start(bf16[192,768]{1,0:T(8,128)(2,1)} %collective-permute-done.12.refs_10_.refs_14_), channel_id=1, source_target_pairs={{0,1},{1,0},{2,3},{3,2},{4,5},{5,4},{6,7},{7,6},{8,9},{9,8},{10,11... | collective-permute-start | bytes 884744 | tf_op jit(solution)/shard_map/ppermute | solution.py:44
  70.8 6.7 %collective-permute-start.9 = (bf16[256,192]{1,0:T(8,128)(2,1)}, bf16[256,192]{1,0:T(8,128)(2,1)}, u32[]{:S(2)}, u32[]{:S(2)}) collective-permute-start(bf16[256,192]{1,0:T(8,128)(2,1)} %get-tuple-element.112), channel_id=1, source_target_pairs={{0,2},{1,3},{2,0},{3,1},{4,6},{5,7},{6,4},{7,5},{8,10},{9,11},{10,... | collective-permute-start | bytes 294920 | tf_op jit(solution)/shard_map/ppermute | solution.py:44
  72.1 6.3 %collective-permute-start.10 = (bf16[256,192]{1,0:T(8,128)(2,1)}, bf16[256,192]{1,0:T(8,128)(2,1)}, u32[]{:S(2)}, u32[]{:S(2)}) collective-permute-start(bf16[256,192]{1,0:T(8,128)(2,1)} %get-tuple-element.113), channel_id=1, source_target_pairs={{0,3},{1,2},{2,1},{3,0},{4,7},{5,6},{6,5},{7,4},{8,11},{9,10},{10,... | collective-permute-start | bytes 294920 | tf_op jit(solution)/shard_map/ppermute | solution.py:44
  82.3 21.5 %collective-permute-start.15 = (bf16[256,768]{1,0:T(8,128)(2,1)}, bf16[256,768]{1,0:T(8,128)(2,1)}, u32[]{:S(2)}, u32[]{:S(2)}) collective-permute-start(bf16[256,768]{1,0:T(8,128)(2,1)} %get-tuple-element.117.refs_4_.refs_6_), channel_id=1, source_target_pairs={{0,16},{4,20},{8,24},{12,28},{16,0},{20,4},{24,8},{28,12},{1,17},{... | collective-permute-start | bytes 1179656 | tf_op jit(solution)/shard_map/ppermute | solution.py:44
  87.6 17.7 %collective-permute-start.16 = (bf16[256,768]{1,0:T(8,128)(2,1)}, bf16[256,768]{1,0:T(8,128)(2,1)}, u32[]{:S(2)}, u32[]{:S(2)}) collective-permute-start(bf16[256,768]{1,0:T(8,128)(2,1)} %get-tuple-element.118), channel_id=1, source_target_pairs={{0,4},{4,0},{8,12},{12,8},{16,20},{20,16},{24,28},{28,24},{1,5},{5... | collective-permute-start | bytes 1179656 | tf_op jit(solution)/shard_map/ppermute | solution.py:44
  89.1 19.6 %collective-permute-start.17 = (bf16[256,768]{1,0:T(8,128)(2,1)}, bf16[256,768]{1,0:T(8,128)(2,1)}, u32[]{:S(2)}, u32[]{:S(2)}) collective-permute-start(bf16[256,768]{1,0:T(8,128)(2,1)} %get-tuple-element.119), channel_id=1, source_target_pairs={{0,8},{4,12},{8,0},{12,4},{16,24},{20,28},{24,16},{28,20},{1,9},{5... | collective-permute-start | bytes 1179656 | tf_op jit(solution)/shard_map/ppermute | solution.py:44
  90.7 20.7 %collective-permute-start.22 = (bf16[128,768]{1,0:T(8,128)(2,1)}, bf16[128,768]{1,0:T(8,128)(2,1)}, u32[]{:S(2)}, u32[]{:S(2)}) collective-permute-start(bf16[128,768]{1,0:T(8,128)(2,1)} %get-tuple-element.127), channel_id=1, source_target_pairs={{0,4},{4,0},{8,12},{12,8},{16,20},{20,16},{24,28},{28,24},{1,5},{5... | collective-permute-start | bytes 589832 | tf_op jit(solution)/shard_map/ppermute | solution.py:44
  91.3 21.7 %collective-permute-start.23 = (bf16[128,768]{1,0:T(8,128)(2,1)}, bf16[128,768]{1,0:T(8,128)(2,1)}, u32[]{:S(2)}, u32[]{:S(2)}) collective-permute-start(bf16[128,768]{1,0:T(8,128)(2,1)} %get-tuple-element.128), channel_id=1, source_target_pairs={{0,8},{4,12},{8,0},{12,4},{16,24},{20,28},{24,16},{28,20},{1,9},{5... | collective-permute-start | bytes 589832 | tf_op jit(solution)/shard_map/ppermute | solution.py:44
  103.8 13.4 %collective-permute-start.24 = (bf16[128,768]{1,0:T(8,128)(2,1)}, bf16[128,768]{1,0:T(8,128)(2,1)}, u32[]{:S(2)}, u32[]{:S(2)}) collective-permute-start(bf16[128,768]{1,0:T(8,128)(2,1)} %get-tuple-element.129), channel_id=1, source_target_pairs={{0,12},{4,8},{8,4},{12,0},{16,28},{20,24},{24,20},{28,16},{1,13},{... | collective-permute-start | bytes 589832 | tf_op jit(solution)/shard_map/ppermute | solution.py:44
  105.4 24.7 %collective-permute-start.21 = (bf16[256,768]{1,0:T(8,128)(2,1)}, bf16[256,768]{1,0:T(8,128)(2,1)}, u32[]{:S(2)}, u32[]{:S(2)}) collective-permute-start(bf16[256,768]{1,0:T(8,128)(2,1)} %get-tuple-element.125), channel_id=1, source_target_pairs={{0,12},{4,8},{8,4},{12,0},{16,28},{20,24},{24,20},{28,16},{1,13},{... | collective-permute-start | bytes 1179656 | tf_op jit(solution)/shard_map/ppermute | solution.py:44
  110.9 19.2 %collective-permute-start.18 = (bf16[128,768]{1,0:T(8,128)(2,1)}, bf16[128,768]{1,0:T(8,128)(2,1)}, u32[]{:S(2)}, u32[]{:S(2)}) collective-permute-start(bf16[128,768]{1,0:T(8,128)(2,1)} %get-tuple-element.121), channel_id=1, source_target_pairs={{0,4},{4,0},{8,12},{12,8},{16,20},{20,16},{24,28},{28,24},{1,5},{5... | collective-permute-start | bytes 589832 | tf_op jit(solution)/shard_map/ppermute | solution.py:44
  111.4 18.7 %collective-permute-start.19 = (bf16[128,768]{1,0:T(8,128)(2,1)}, bf16[128,768]{1,0:T(8,128)(2,1)}, u32[]{:S(2)}, u32[]{:S(2)}) collective-permute-start(bf16[128,768]{1,0:T(8,128)(2,1)} %get-tuple-element.122), channel_id=1, source_target_pairs={{0,8},{4,12},{8,0},{12,4},{16,24},{20,28},{24,16},{28,20},{1,9},{5... | collective-permute-start | bytes 589832 | tf_op jit(solution)/shard_map/ppermute | solution.py:44
  112.9 20.3 %collective-permute-start.20 = (bf16[128,768]{1,0:T(8,128)(2,1)}, bf16[128,768]{1,0:T(8,128)(2,1)}, u32[]{:S(2)}, u32[]{:S(2)}) collective-permute-start(bf16[128,768]{1,0:T(8,128)(2,1)} %get-tuple-element.123), channel_id=1, source_target_pairs={{0,12},{4,8},{8,4},{12,0},{16,28},{20,24},{24,20},{28,16},{1,13},{... | collective-permute-start | bytes 589832 | tf_op jit(solution)/shard_map/ppermute | solution.py:44
  151.1 15.4 %collective-permute-start.28 = (bf16[128,896]{1,0:T(8,128)(2,1)}, bf16[128,896]{1,0:T(8,128)(2,1)}, u32[]{:S(2)}, u32[]{:S(2)}) collective-permute-start(bf16[128,896]{1,0:T(8,128)(2,1)} %get-tuple-element.141), channel_id=1, source_target_pairs={{0,4},{4,0},{8,12},{12,8},{16,20},{20,16},{24,28},{28,24},{1,5},{5... | collective-permute-start | bytes 688136 | tf_op jit(solution)/shard_map/ppermute | solution.py:44
  152.7 13.9 %collective-permute-start.29 = (bf16[128,896]{1,0:T(8,128)(2,1)}, bf16[128,896]{1,0:T(8,128)(2,1)}, u32[]{:S(2)}, u32[]{:S(2)}) collective-permute-start(bf16[128,896]{1,0:T(8,128)(2,1)} %get-tuple-element.142), channel_id=1, source_target_pairs={{0,8},{4,12},{8,0},{12,4},{16,24},{20,28},{24,16},{28,20},{1,9},{5... | collective-permute-start | bytes 688136 | tf_op jit(solution)/shard_map/ppermute | solution.py:44
  152.7 13.9 %collective-permute-start.30 = (bf16[128,896]{1,0:T(8,128)(2,1)}, bf16[128,896]{1,0:T(8,128)(2,1)}, u32[]{:S(2)}, u32[]{:S(2)}) collective-permute-start(bf16[128,896]{1,0:T(8,128)(2,1)} %get-tuple-element.143), channel_id=1, source_target_pairs={{0,12},{4,8},{8,4},{12,0},{16,28},{20,24},{24,20},{28,16},{1,13},{... | collective-permute-start | bytes 688136 | tf_op jit(solution)/shard_map/ppermute | solution.py:44
  169.3 24.3 %collective-permute-start.31 = (bf16[128,896]{1,0:T(8,128)(2,1)}, bf16[128,896]{1,0:T(8,128)(2,1)}, u32[]{:S(2)}, u32[]{:S(2)}) collective-permute-start(bf16[128,896]{1,0:T(8,128)(2,1)} %get-tuple-element.147), channel_id=1, source_target_pairs={{0,4},{4,0},{8,12},{12,8},{16,20},{20,16},{24,28},{28,24},{1,5},{5... | collective-permute-start | bytes 688136 | tf_op jit(solution)/shard_map/ppermute | solution.py:44
  170.8 22.9 %collective-permute-start.32 = (bf16[128,896]{1,0:T(8,128)(2,1)}, bf16[128,896]{1,0:T(8,128)(2,1)}, u32[]{:S(2)}, u32[]{:S(2)}) collective-permute-start(bf16[128,896]{1,0:T(8,128)(2,1)} %get-tuple-element.148), channel_id=1, source_target_pairs={{0,8},{4,12},{8,0},{12,4},{16,24},{20,28},{24,16},{28,20},{1,9},{5... | collective-permute-start | bytes 688136 | tf_op jit(solution)/shard_map/ppermute | solution.py:44
  170.8 22.9 %collective-permute-start.33 = (bf16[128,896]{1,0:T(8,128)(2,1)}, bf16[128,896]{1,0:T(8,128)(2,1)}, u32[]{:S(2)}, u32[]{:S(2)}) collective-permute-start(bf16[128,896]{1,0:T(8,128)(2,1)} %get-tuple-element.149), channel_id=1, source_target_pairs={{0,12},{4,8},{8,4},{12,0},{16,28},{20,24},{24,20},{28,16},{1,13},{... | collective-permute-start | bytes 688136 | tf_op jit(solution)/shard_map/ppermute | solution.py:44
  172.8 21.2 %collective-permute-start.34 = (bf16[256,896]{1,0:T(8,128)(2,1)}, bf16[256,896]{1,0:T(8,128)(2,1)}, u32[]{:S(2)}, u32[]{:S(2)}) collective-permute-start(bf16[256,896]{1,0:T(8,128)(2,1)} %get-tuple-element.150), channel_id=1, source_target_pairs={{0,16},{4,20},{8,24},{12,28},{16,0},{20,4},{24,8},{28,12},{1,17},{... | collective-permute-start | bytes 1376264 | tf_op jit(solution)/shard_map/ppermute | solution.py:44
  200.9 9.2 %collective-permute-start.38 = (bf16[3072,768]{1,0:T(8,128)(2,1)}, bf16[3072,768]{1,0:T(8,128)(2,1)}, u32[]{:S(2)}, u32[]{:S(2)}) collective-permute-start(bf16[3072,768]{1,0:T(8,128)(2,1)} %get-tuple-element.164), channel_id=1, source_target_pairs={{0,1},{1,0},{2,3},{3,2},{4,5},{5,4},{6,7},{7,6},{8,9},{9,8},{10,11... | collective-permute-start | bytes 14155784 | tf_op jit(solution)/shard_map/ppermute | solution.py:44
  200.9 9.1 %collective-permute-start.39 = (bf16[384,768]{1,0:T(8,128)(2,1)}, bf16[384,768]{1,0:T(8,128)(2,1)}, u32[]{:S(2)}, u32[]{:S(2)}) collective-permute-start(bf16[384,768]{1,0:T(8,128)(2,1)} %get-tuple-element.166), channel_id=1, source_target_pairs={{0,1},{1,0},{2,3},{3,2},{4,5},{5,4},{6,7},{7,6},{8,9},{9,8},{10,11... | collective-permute-start | bytes 1769480 | tf_op jit(solution)/shard_map/ppermute | solution.py:44
  201.4 6.7 %collective-permute-start.36 = (bf16[256,192]{1,0:T(8,128)(2,1)}, bf16[256,192]{1,0:T(8,128)(2,1)}, u32[]{:S(2)}, u32[]{:S(2)}) collective-permute-start(bf16[256,192]{1,0:T(8,128)(2,1)} %get-tuple-element.162), channel_id=1, source_target_pairs={{0,2},{1,3},{2,0},{3,1},{4,6},{5,7},{6,4},{7,5},{8,10},{9,11},{10,... | collective-permute-start | bytes 294920 | tf_op jit(solution)/shard_map/ppermute | solution.py:44
  201.9 7.2 %collective-permute-start.37 = (bf16[256,192]{1,0:T(8,128)(2,1)}, bf16[256,192]{1,0:T(8,128)(2,1)}, u32[]{:S(2)}, u32[]{:S(2)}) collective-permute-start(bf16[256,192]{1,0:T(8,128)(2,1)} %get-tuple-element.163), channel_id=1, source_target_pairs={{0,3},{1,2},{2,1},{3,0},{4,7},{5,6},{6,5},{7,4},{8,11},{9,10},{10,... | collective-permute-start | bytes 294920 | tf_op jit(solution)/shard_map/ppermute | solution.py:44
  214.9 23.3 %collective-permute-start.40 = (bf16[448,768]{1,0:T(8,128)(2,1)}, bf16[448,768]{1,0:T(8,128)(2,1)}, u32[]{:S(2)}, u32[]{:S(2)}) collective-permute-start(bf16[448,768]{1,0:T(8,128)(2,1)} %get-tuple-element.168.refs_11_), channel_id=1, source_target_pairs={{0,2},{1,3},{2,0},{3,1},{4,6},{5,7},{6,4},{7,5},{8,10},{9,11},{10,... | collective-permute-start | bytes 2064392 | tf_op jit(solution)/shard_map/ppermute | solution.py:44
  215.4 22.8 %collective-permute-start.25 = (bf16[256,768]{1,0:T(8,128)(2,1)}, bf16[256,768]{1,0:T(8,128)(2,1)}, u32[]{:S(2)}, u32[]{:S(2)}) collective-permute-start(bf16[256,768]{1,0:T(8,128)(2,1)} %get-tuple-element.132), channel_id=1, source_target_pairs={{0,4},{4,0},{8,12},{12,8},{16,20},{20,16},{24,28},{28,24},{1,5},{5... | collective-permute-start | bytes 1179656 | tf_op jit(solution)/shard_map/ppermute | solution.py:44
  216.8 21.3 %collective-permute-start.26 = (bf16[256,768]{1,0:T(8,128)(2,1)}, bf16[256,768]{1,0:T(8,128)(2,1)}, u32[]{:S(2)}, u32[]{:S(2)}) collective-permute-start(bf16[256,768]{1,0:T(8,128)(2,1)} %get-tuple-element.133), channel_id=1, source_target_pairs={{0,8},{4,12},{8,0},{12,4},{16,24},{20,28},{24,16},{28,20},{1,9},{5... | collective-permute-start | bytes 1179656 | tf_op jit(solution)/shard_map/ppermute | solution.py:44
  218.5 19.6 %collective-permute-start.27 = (bf16[256,768]{1,0:T(8,128)(2,1)}, bf16[256,768]{1,0:T(8,128)(2,1)}, u32[]{:S(2)}, u32[]{:S(2)}) collective-permute-start(bf16[256,768]{1,0:T(8,128)(2,1)} %get-tuple-element.134), channel_id=1, source_target_pairs={{0,12},{4,8},{8,4},{12,0},{16,28},{20,24},{24,20},{28,16},{1,13},{... | collective-permute-start | bytes 1179656 | tf_op jit(solution)/shard_map/ppermute | solution.py:44
  220.5 58.7 %collective-permute-start.49 = (bf16[768,768]{1,0:T(8,128)(2,1)}, bf16[768,768]{1,0:T(8,128)(2,1)}, u32[]{:S(2)}, u32[]{:S(2)}) collective-permute-start(bf16[768,768]{1,0:T(8,128)(2,1)} %get-tuple-element.194), channel_id=1, source_target_pairs={{0,2},{1,3},{2,0},{3,1},{4,6},{5,7},{6,4},{7,5},{8,10},{9,11},{10,... | collective-permute-start | bytes 3538952 | tf_op jit(solution)/shard_map/ppermute | solution.py:44
  245.5 29.3 %collective-permute-start.44 = (bf16[512,768]{1,0:T(8,128)(2,1)}, bf16[512,768]{1,0:T(8,128)(2,1)}, u32[]{:S(2)}, u32[]{:S(2)}) collective-permute-start(bf16[512,768]{1,0:T(8,128)(2,1)} %get-tuple-element.184), channel_id=1, source_target_pairs={{0,2},{1,3},{2,0},{3,1},{4,6},{5,7},{6,4},{7,5},{8,10},{9,11},{10,... | collective-permute-start | bytes 2359304 | tf_op jit(solution)/shard_map/ppermute | solution.py:44
  246.0 29.3 %collective-permute-start.41 = (bf16[224,768]{1,0:T(8,128)(2,1)}, bf16[224,768]{1,0:T(8,128)(2,1)}, u32[]{:S(2)}, u32[]{:S(2)}) collective-permute-start(bf16[224,768]{1,0:T(8,128)(2,1)} %get-tuple-element.180), channel_id=1, source_target_pairs={{0,4},{4,0},{8,12},{12,8},{16,20},{20,16},{24,28},{28,24},{1,5},{5... | collective-permute-start | bytes 1032200 | tf_op jit(solution)/shard_map/ppermute | solution.py:44
  247.5 27.8 %collective-permute-start.42 = (bf16[224,768]{1,0:T(8,128)(2,1)}, bf16[224,768]{1,0:T(8,128)(2,1)}, u32[]{:S(2)}, u32[]{:S(2)}) collective-permute-start(bf16[224,768]{1,0:T(8,128)(2,1)} %get-tuple-element.181), channel_id=1, source_target_pairs={{0,8},{4,12},{8,0},{12,4},{16,24},{20,28},{24,16},{28,20},{1,9},{5... | collective-permute-start | bytes 1032200 | tf_op jit(solution)/shard_map/ppermute | solution.py:44
  249.2 26.1 %collective-permute-start.43 = (bf16[224,768]{1,0:T(8,128)(2,1)}, bf16[224,768]{1,0:T(8,128)(2,1)}, u32[]{:S(2)}, u32[]{:S(2)}) collective-permute-start(bf16[224,768]{1,0:T(8,128)(2,1)} %get-tuple-element.182), channel_id=1, source_target_pairs={{0,12},{4,8},{8,4},{12,0},{16,28},{20,24},{24,20},{28,16},{1,13},{... | collective-permute-start | bytes 1032200 | tf_op jit(solution)/shard_map/ppermute | solution.py:44
  274.8 15.3 %collective-permute-start.47 = (bf16[256,768]{1,0:T(8,128)(2,1)}, bf16[256,768]{1,0:T(8,128)(2,1)}, u32[]{:S(2)}, u32[]{:S(2)}) collective-permute-start(bf16[256,768]{1,0:T(8,128)(2,1)} %add_convert_fusion), channel_id=1, source_target_pairs={{0,2},{1,3},{2,0},{3,1},{4,6},{5,7},{6,4},{7,5},{8,10},{9,11},{10,... | collective-permute-start | bytes 1179656 | tf_op jit(solution)/shard_map/ppermute | solution.py:44
  277.5 12.6 %collective-permute-start.48 = (bf16[128,768]{1,0:T(8,128)(2,1)}, bf16[128,768]{1,0:T(8,128)(2,1)}, u32[]{:S(2)}, u32[]{:S(2)}) collective-permute-start(bf16[128,768]{1,0:T(8,128)(2,1)} %get-tuple-element.193), channel_id=1, source_target_pairs={{0,16},{4,20},{8,24},{12,28},{16,0},{20,4},{24,8},{28,12},{1,17},{... | collective-permute-start | bytes 589832 | tf_op jit(solution)/shard_map/ppermute | solution.py:44
  288.9 19.4 %collective-permute-start.46 = (bf16[256,768]{1,0:T(8,128)(2,1)}, bf16[256,768]{1,0:T(8,128)(2,1)}, u32[]{:S(2)}, u32[]{:S(2)}) collective-permute-start(bf16[256,768]{1,0:T(8,128)(2,1)} %get-tuple-element.188), channel_id=1, source_target_pairs={{0,16},{4,20},{8,24},{12,28},{16,0},{20,4},{24,8},{28,12},{1,17},{... | collective-permute-start | bytes 1179656 | tf_op jit(solution)/shard_map/ppermute | solution.py:44
  296.9 13.3 %collective-permute-start.51 = (f32[16,768]{1,0:T(8,128)S(1)}, f32[16,768]{1,0:T(8,128)S(1)}, u32[]{:S(2)}, u32[]{:S(2)}) collective-permute-start(f32[16,768]{1,0:T(8,128)S(1)} %add.99), channel_id=1, source_target_pairs={{0,2},{1,3},{2,0},{3,1},{4,6},{5,7},{6,4},{7,5},{8,10},{9,11},{10,... | collective-permute-start | bytes 147464 | tf_op jit(solution)/shard_map/ppermute | solution.py:44
  (8 other events, 51.0 us)

commit v9 on v8

--- a/solution.py
+++ b/solution.py
@@ -923,7 +923,7 @@
     )
 
 
-def add_up(base, near, parts):
+def add_up(base, near, parts, after):
     size, width = base.shape[0] // 4, base.shape[1]
 
     def kernel(in_base, in_near, out_base, out_near, *refs):
@@ -945,12 +945,12 @@
         kernel,
         name="add_up",
         grid=(1,),
-        in_specs=specs,
+        in_specs=specs + [pl.BlockSpec(memory_space=pl.ANY)] * len(after),
         out_specs=[whole((size, width))] * 2,
         out_shape=[shape((size, width), f32)] * 2,
         compiler_params=limit(64),
         cost_estimate=long,
-    )(base, near, base, near, *[array for array, _ in parts])
+    )(base, near, base, near, *[array for array, _ in parts], *after)
 
 
 def two_halves(values):
@@ -1104,7 +1104,7 @@
     seg_q = segments.reshape(seq_len, 1)
     seg_k = jnp.pad(segments.reshape(1, seq_len), ((0, 0), (reach, 0)), constant_values=-1)
     router_wide = jnp.pad(w_router, ((0, 0), (0, 128 - experts)))
-    ready = [line, bucket_hot, seg_q, seg_k, router_wide, gain_two] + slots
+    ready = slots[:1] + [seg_q, seg_k, router_wide, gain_two]
     normed, query, key_rows, value_rows, weight_q, weight_k, weight_v, w_o, late_cotangent = (
         project(place, token_blocks, pack_blocks, gain_one, cotangent, span, ready)
     )
@@ -1251,20 +1251,19 @@
         buckets_all,
         result_in[1:],
     )
-    w_in_grad, w_out_grad = add_up(
-        base_w, near_w, [(far_first, span), (far_next, 0), (far_last, 0)]
-    )
+    far_parts = [(far_first, span), (far_next, 0), (far_last, 0)]
     near = swap(near, "mp", 1)
     far_normed = swap((base_far + near[rows:].astype(f32)).astype(bf16), "mp", 2)
     if few:
         arrived_sums = [swap(weight_sums[r], "dp", r) for r in (1, 2, 3)]
         own_sum, far_part, small = fold_weights(
-            weight_sums[0], arrived_sums, small, [far_next, near]
+            weight_sums[0], arrived_sums, small, [near]
         )
         own_result, far_result = from_slots(
             "result_from_slots", result_in, slots, size, [f32, bf16], after=[own_sum]
         )
         far_result = swap(far_result, "dp", 4)
+        w_in_grad, w_out_grad = add_up(base_w, near_w, far_parts, [own_result])
         *weight_grads, small = split_weights(
             own_sum, swap(far_part, "dp", 4), small, span, [w_in_grad, far_normed]
         )
@@ -1274,6 +1273,7 @@
             joined_grad, None, sum_over(small, "dp"), span, []
         )
         (own_result,) = from_slots("result_from_slots", result_in, slots, size, [f32])
+        w_in_grad, w_out_grad = add_up(base_w, near_w, far_parts, [])
     small = sum_over(small, "mp")
     normed_grad = base + near[:rows].astype(f32) + far_normed.astype(f32)
     resid = tokens.astype(f32)

time: 313 us -> 292 us (0.933)
  waiting for transfers between devices: 88 us -> 62.5 us
    ppermute x52, waiting for transfers between devices: 88 us -> 62.5 us  [swap(): return lax.ppermute(values, axis, [(i, i ^ step) for i in range(count)])]
  transfers between devices with their start and end apart: 52 -> 52, of which waited for: 18 -> 17; matrix products, arithmetic and copies ran while one was open for 9% -> 10% of each run, Pallas kernels for 33% -> 37%
where the time goes in v9:
time: 292 us; the launch traced here: 291 us
  Pallas kernels  143 us (49%)
  waiting for transfers between devices  62.5 us (21%)
  starting transfers between devices  53.1 us (18%)
  local copies, waits for them, and re-layouts  15 us (5%)
  other arithmetic  14.7 us (5%)
    pallas_call x14, Pallas kernels, call(): pl.pallas_call(body, name=name, grid=(1,), in_specs=in_specs + [pl.BlockS...  69.3 us
    ppermute x52, waiting for transfers between devices, swap(): return lax.ppermute(values, axis, [(i, i ^ step) for i in range(count)])  62.5 us
    ppermute x52, starting transfers between devices, swap(): return lax.ppermute(values, axis, [(i, i ^ step) for i in range(count)])  53.1 us
    pallas_call x1, Pallas kernels, expert_weight_grads(): pl.pallas_call(kernel, name='expert_weight_grads', grid_spec=pltpu.Prefet...  19.8 us
    pallas_call x1, Pallas kernels, run_experts(): pl.pallas_call(kernel, name=name, grid=(units // piece,), in_specs=[pl.Bl...  17.9 us
    pallas_call x1, Pallas kernels, experts_forward(): pl.pallas_call(kernel, name='experts_forward', grid=(units // piece,), in...  12.8 us
    pallas_call x1, Pallas kernels, experts_backward(): pl.pallas_call(kernel, name='experts_backward', grid=(units // piece,), i...  12 us
    pallas_call x1, Pallas kernels, add_up(): pl.pallas_call(kernel, name='add_up', grid=(1,), in_specs=specs + [pl.Blo...  6.27 us
  transfers between devices with their start and end apart: 52, of which 17 were waited for; matrix products, arithmetic and copies ran while one was open for 10% of the time, Pallas kernels for 37%

profile of v9, /device:TPU:0, one launch (start us, length us, event | category | flops | bytes accessed | tf_op | source)
XLA Modules:
  0.0 291.2 jit_solution(6071799009514898059)
XLA Ops:
  0.6 3.0 %collective-permute-start.1 = (bf16[256,768]{1,0:T(8,128)(2,1)}, bf16[256,768]{1,0:T(8,128)(2,1)}, u32[]{:S(2)}, u32[]{:S(2)}) collective-permute-start(bf16[256,768]{1,0:T(8,128)(2,1)} %refs_0_.4), channel_id=1, source_target_pairs={{0,2},{1,3},{2,0},{3,1},{4,6},{5,7},{6,4},{7,5},{8,10},{9,11},{10,... | collective-permute-start | bytes 1179656 | tf_op jit(solution)/shard_map/ppermute | solution.py:44
  3.7 2.6 collective-permute-start.15
  10.4 7.9 %collective-permute-done.3.refs_1_ = bf16[96,768]{1,0:T(8,128)(2,1)} collective-permute-done((bf16[96,768]{1,0:T(8,128)(2,1)}, bf16[96,768]{1,0:T(8,128)(2,1)}, u32[]{:S(2)}, u32[]{:S(2)}) %collective-permute-start.3) | collective-permute-done | bytes 147488 | tf_op jit(solution)/shard_map/ppermute | solution.py:44
  20.0 3.0 %collective-permute-start.5 = (bf16[192,768]{1,0:T(8,128)(2,1)}, bf16[192,768]{1,0:T(8,128)(2,1)}, u32[]{:S(2)}, u32[]{:S(2)}) collective-permute-start(bf16[192,768]{1,0:T(8,128)(2,1)} %pair_up.1.refs_6_), channel_id=1, source_target_pairs={{0,8},{4,12},{8,0},{12,4},{16,24},{20,28},{24,16},{28,20},{1,9},{5... | collective-permute-start | bytes 884744 | tf_op jit(solution)/shard_map/ppermute | solution.py:44
  30.5 1.8 copy.37.refs_10_
  36.0 5.2 %project.1 = (bf16[1024,768]{1,0:T(8,128)(2,1)}, bf16[1024,192]{1,0:T(8,128)(2,1)}, bf16[1024,192]{1,0:T(8,128)(2,1)}, bf16[1024,192]{1,0:T(8,128)(2,1)}, bf16[7...) custom-call(s32[2]{0:T(128)} %pad_add_fusion.2.refs_0_.me_ref.place_, ...), custom_call_target="tpu_custom_call", output_to_operand_aliasing={{8}: (10, {})} | custom-call | flops 10000000 | bytes 10000 | tf_op jit(solution)/shard_map/project/pallas_call | solution.py:69
  45.6 11.5 %attend.1 = (bf16[256,192]{1,0:T(8,128)(2,1)}, bf16[256,192]{1,0:T(8,128)(2,1)}, bf16[256,192]{1,0:T(8,128)(2,1)}, bf16[256,192]{1,0:T(8,128)(2,1)}) custom-call(s32[2]{0:T(128)} %pad_add_fusion.2.refs_0_.me_ref.place_ref, bf16[1024,192]{1,0:T(8,128)(2,1)} %get-tuple-element.107.refs_1_, bf16[1024,192]{1,0:T(8,128)(2,1)} %get-tuple-element.108.refs_2_, ...), custom_call_target="tpu_custom_call" | custom-call | flops 10000000 | bytes 10000 | tf_op jit(solution)/shard_map/attend/pallas_call | solution.py:69
  61.7 3.3 %collective-permute-done.8.refs_6_.refs_18_ = bf16[256,192]{1,0:T(8,128)(2,1)} collective-permute-done((bf16[256,192]{1,0:T(8,128)(2,1)}, bf16[256,192]{1,0:T(8,128)(2,1)}, u32[]{:S(2)}, u32[]{:S(2)}) %collective-permute-start.8) | collective-permute-done | bytes 98336 | tf_op jit(solution)/shard_map/ppermute | solution.py:44
  65.0 1.9 collective-permute-done.9.refs_7_.refs_19_
  66.9 3.9 %middle.1 = (f32[256,768]{1,0:T(8,128)}, bf16[256,768]{1,0:T(8,128)(2,1)}, f32[256,128]{1,0:T(8,128)}, bf16[128,768]{1,0:T(8,128)(2,1)}, bf16[128,768]{1,0:T(8,1...) custom-call(bf16[256,768]{1,0:T(8,128)(2,1)} %refs_0_.4, f32[1,768]{1,0:T(1,128)} %reshape.191.refs_15_.refs_1_.refs_4_, ...), custom_call_target="tpu_custom_call" | custom-call | flops 10000000 | bytes 10000 | tf_op jit(solution)/shard_map/middle/pallas_call | solution.py:69
  70.7 2.3 collective-permute-start.14
  74.4 2.8 grads_to_slots.1
  79.4 1.8 collective-permute-start.23
  81.2 10.6 %collective-permute-done.14.refs_0_ = bf16[256,768]{1,0:T(8,128)(2,1)} collective-permute-done((bf16[256,768]{1,0:T(8,128)(2,1)}, bf16[256,768]{1,0:T(8,128)(2,1)}, u32[]{:S(2)}, u32[]{:S(2)}) %collective-permute-start.14) | collective-permute-done | bytes 393248 | tf_op jit(solution)/shard_map/ppermute | solution.py:44
  91.8 2.9 %collective-permute-start.21 = (bf16[256,768]{1,0:T(8,128)(2,1)}, bf16[256,768]{1,0:T(8,128)(2,1)}, u32[]{:S(2)}, u32[]{:S(2)}) collective-permute-start(bf16[256,768]{1,0:T(8,128)(2,1)} %get-tuple-element.125), channel_id=1, source_target_pairs={{0,12},{4,8},{8,4},{12,0},{16,28},{20,24},{24,20},{28,16},{1,13},{... | collective-permute-start | bytes 1179656 | tf_op jit(solution)/shard_map/ppermute | solution.py:44
  94.7 3.4 %collective-permute-done.17.refs_3_.refs_6_.refs_2_ = bf16[256,768]{1,0:T(8,128)(2,1)} collective-permute-done((bf16[256,768]{1,0:T(8,128)(2,1)}, bf16[256,768]{1,0:T(8,128)(2,1)}, u32[]{:S(2)}, u32[]{:S(2)}) %collective-permute-start.17) | collective-permute-done | bytes 393248 | tf_op jit(solution)/shard_map/ppermute | solution.py:44
  98.1 2.1 far_to_slots.1
  100.5 1.8 collective-permute-done.23.refs_2_
  103.7 2.6 collective-permute-done.24.refs_3_
  106.3 12.8 %experts_forward.1 = (bf16[512,3072]{1,0:T(8,128)(2,1)}, bf16[512,3072]{1,0:T(8,128)(2,1)}, bf16[512,768]{1,0:T(8,128)(2,1)}, bf16[512,768]{1,0:T(8,128)(2,1)}, ...) custom-call(s32[2]{0:T(128)} %pad_add_fusion.2.refs_0_.me_ref.place_ref, bf16[768,3072]{1,0:T(8,128)(2,1)} %bitcast.45, ...), custom_call_target="tpu_custom_call" | custom-call | flops 20000000000 | bytes 10000000 | tf_op jit(solution)/shard_map/experts_forward/pallas_call | solution.py:460
  119.2 2.6 collective-permute-done.20.refs_3_
  121.8 17.9 %run_experts.1 = (bf16[128,896]{1,0:T(8,128)(2,1)}, bf16[128,896]{1,0:T(8,128)(2,1)}, bf16[128,896]{1,0:T(8,128)(2,1)}, bf16[128,896]{1,0:T(8,128)(2,1)}, bf16[2...) custom-call(s32[2]{0:T(128)} %pad_add_fusion.2.refs_0_.me_ref.place_, ...), custom_call_target="tpu_custom_call" | custom-call | flops 10000000 | bytes 10000 | tf_op jit(solution)/shard_map/run_experts/pallas_call | solution.py:614
  139.7 1.8 collective-permute-start.28
  141.6 1.7 collective-permute-start.30
  143.3 12.0 %experts_backward.1 = (bf16[128,896]{1,0:T(8,128)(2,1)}, bf16[128,896]{1,0:T(8,128)(2,1)}, bf16[128,896]{1,0:T(8,128)(2,1)}, bf16[128,896]{1,0:T(8,128)(2,1)}, b...) custom-call(s32[2]{0:T(128)} %pad_add_fusion.2.refs_0_.me_ref.place_ref, bf16[768,3072]{1,0:T(8,128)(2,1)} %bitcast.47, ...), custom_call_target="tpu_custom_call" | custom-call | flops 20000000000 | bytes 10000000 | tf_op jit(solution)/shard_map/experts_backward/pallas_call | solution.py:519
  155.3 2.7 back_from_slots.1
  158.0 1.8 collective-permute-start.31
  159.8 1.7 collective-permute-start.33
  162.1 19.8 %expert_weight_grads.1 = (bf16[3072,768]{1,0:T(8,128)(2,1)}, f32[3072,768]{1,0:T(8,128)}) custom-call(s32[2]{0:T(128)} %pad_add_fusion.2.refs_0_.me_ref.place_ref, bf16[512,768]{1,0:T(8,128)(2,1)} %get-tuple-element.151.refs_0_, bf16[512,768]{1,0:T(8,128)(2,1)} %get-tuple-element.152.refs_1_, bf16[512,3072]{1,0:T(8,128)(2,1)} %get-tuple-element.153.refs_2_, ...), custom_call_target="tpu_custom_call" | custom-call | flops 20000000000 | bytes 10000000 | tf_op jit(solution)/shard_map/expert_weight_grads/pallas_call | solution.py:765
  182.3 6.9 %home.1 = (bf16[256,192]{1,0:T(8,128)(2,1)}, bf16[256,192]{1,0:T(8,128)(2,1)}, bf16[256,192]{1,0:T(8,128)(2,1)}, bf16[256,192]{1,0:T(8,128)(2,1)}, f32[256,768]{...) custom-call(s32[8,256]{1,0:T(8,128)} %pad.24.refs_11_.refs_3_.refs_1, ...), custom_call_target="tpu_custom_call", output_to_operand_aliasing={{9}: (20, {})} | custom-call | flops 10000000 | bytes 10000 | tf_op jit(solution)/shard_map/home/pallas_call | solution.py:69
  191.2 5.2 %collective-permute-done.36.refs_0_.refs_9_ = bf16[256,192]{1,0:T(8,128)(2,1)} collective-permute-done((bf16[256,192]{1,0:T(8,128)(2,1)}, bf16[256,192]{1,0:T(8,128)(2,1)}, u32[]{:S(2)}, u32[]{:S(2)}) %collective-permute-start.36) | collective-permute-done | bytes 98336 | tf_op jit(solution)/shard_map/ppermute | solution.py:44
  198.3 4.9 %far_sums.1 = (bf16[448,768]{1,0:T(8,128)(2,1)}, bf16[512,768]{1,0:T(8,128)(2,1)}, bf16[768,768]{1,0:T(8,128)(2,1)}) custom-call(bf16[3072,768]{1,0:T(8,128)(2,1)} %collective-permute-done.38.near_in.near_out.in_near.out_near, bf16[3072,768]{1,0:T(8,128)(2,1)} %collective-permute-done.38.near_in.near_out.in_near.out_near, ...), custom_call_target="tpu_custom_call" | custom-call | flops 10000000 | bytes 10000 | tf_op jit(solution)/shard_map/far_sums/pallas_call | solution.py:811
  210.4 16.1 %attend_back.1 = (bf16[1024,192]{1,0:T(8,128)(2,1)}, bf16[1024,192]{1,0:T(8,128)(2,1)}, bf16[1024,192]{1,0:T(8,128)(2,1)}, f32[8,640]{1,0:T(8,128)}) custom-call(s32[2]{0:T(128)} %pad_add_fusion.2.refs_0_.me_ref.place_ref, bf16[1024,192]{1,0:T(8,128)(2,1)} %get-tuple-element.107.refs_1_, bf16[1024,192]{1,0:T(8,128)(2,1)} %get-tuple-element.108.refs_2_, ...), custom_call_target="tpu_custom_call" | custom-call | flops 10000000 | bytes 10000 | tf_op jit(solution)/shard_map/attend_back/pallas_call | solution.py:69
  226.5 7.2 %input_grads.1 = (bf16[512,768]{1,0:T(8,128)(2,1)}, f32[256,768]{1,0:T(8,128)}, f32[256,768]{1,0:T(8,128)}, f32[16,768]{1,0:T(8,128)}, f32[192,768]{1,0:T(8,128)...) custom-call(s32[2]{0:T(128)} %pad_add_fusion.2.refs_0_.me_ref.place_ref, ...), custom_call_target="tpu_custom_call" | custom-call | flops 10000000 | bytes 10000 | tf_op jit(solution)/shard_map/input_grads/pallas_call | solution.py:69
  233.8 1.7 collective-permute-start.41
  238.7 5.9 %collective-permute-done.41.refs_1_ = bf16[224,768]{1,0:T(8,128)(2,1)} collective-permute-done((bf16[224,768]{1,0:T(8,128)(2,1)}, bf16[224,768]{1,0:T(8,128)(2,1)}, u32[]{:S(2)}, u32[]{:S(2)}) %collective-permute-start.41) | collective-permute-done | bytes 344096 | tf_op jit(solution)/shard_map/ppermute | solution.py:44
  244.6 2.7 collective-permute-start.43
  247.3 8.2 %collective-permute-done.43.refs_3_ = bf16[224,768]{1,0:T(8,128)(2,1)} collective-permute-done((bf16[224,768]{1,0:T(8,128)(2,1)}, bf16[224,768]{1,0:T(8,128)(2,1)}, u32[]{:S(2)}, u32[]{:S(2)}) %collective-permute-start.43) | collective-permute-done | bytes 344096 | tf_op jit(solution)/shard_map/ppermute | solution.py:44
  255.5 2.2 fold_weights.1
  257.8 2.1 collective-permute-start.47
  259.8 3.4 %result_from_slots.1 = (f32[256,768]{1,0:T(8,128)}, bf16[256,768]{1,0:T(8,128)(2,1)}) custom-call(bf16[256,768]{1,0:T(8,128)(2,1)} %get-tuple-element.131.refs_0_, bf16[256,768]{1,0:T(8,128)(2,1)} %collective-permute-done.25.refs_16_.refs_1_, bf16[256,768]{1,0:T(8,128)(2,1)} %collective-permute-done.26.refs_17_.refs_2_, ...), custom_call_target="tpu_custom_call" | custom-call | flops 10000000 | bytes 10000 | tf_op jit(solution)/shard_map/result_from_slots/pallas_call | solution.py:69
  264.1 2.0 add_convert_fusion
  267.6 6.3 %add_up.1 = (f32[768,768]{1,0:T(8,128)}, f32[768,768]{1,0:T(8,128)}) custom-call(f32[3072,768]{1,0:T(8,128)} %get-tuple-element.165.base_in.base_out.in_base.out_base, bf16[3072,768]{1,0:T(8,128)(2,1)} %collective-permute-done.38.near_in.near_out.in_near.out_near, f32[3072,768]{1,0:T(8,128)} %get-tuple-element.165.base_in.base_out.in_base.out_base, ...), custom_call_target="tpu_custom_call" | custom-call | flops 20000000000 | bytes 10000000 | tf_op jit(solution)/shard_map/add_up/pallas_call | solution.py:944
  273.9 4.5 %collective-permute-done.47.refs_2_ = bf16[128,768]{1,0:T(8,128)(2,1)} collective-permute-done((bf16[128,768]{1,0:T(8,128)(2,1)}, bf16[128,768]{1,0:T(8,128)(2,1)}, u32[]{:S(2)}, u32[]{:S(2)}) %collective-permute-start.47) | collective-permute-done | bytes 196640 | tf_op jit(solution)/shard_map/ppermute | solution.py:44
  278.4 1.9 split_weights.1
  280.3 1.9 fusion
  282.3 2.8 fusion.5
  286.7 1.9 add_convert_fusion.1
  (120 shorter events, 53.4 us)
Async XLA Ops:
  0.6 17.7 %collective-permute-start.1 = (bf16[256,768]{1,0:T(8,128)(2,1)}, bf16[256,768]{1,0:T(8,128)(2,1)}, u32[]{:S(2)}, u32[]{:S(2)}) collective-permute-start(bf16[256,768]{1,0:T(8,128)(2,1)} %refs_0_.4), channel_id=1, source_target_pairs={{0,2},{1,3},{2,0},{3,1},{4,6},{5,7},{6,4},{7,5},{8,10},{9,11},{10,... | collective-permute-start | bytes 1179656 | tf_op jit(solution)/shard_map/ppermute | solution.py:44
  3.7 14.6 %collective-permute-start = (bf16[256,768]{1,0:T(8,128)(2,1)}, bf16[256,768]{1,0:T(8,128)(2,1)}, u32[]{:S(2)}, u32[]{:S(2)}) collective-permute-start(bf16[256,768]{1,0:T(8,128)(2,1)} %refs_0_.4), channel_id=1, source_target_pairs={{0,1},{1,0},{2,3},{3,2},{4,5},{5,4},{6,7},{7,6},{8,9},{9,8},{10,11... | collective-permute-start | bytes 1179656 | tf_op jit(solution)/shard_map/ppermute | solution.py:44
  3.7 54.0 %collective-permute-start.15 = (s32[256,2]{0,1:T(2,128)}, s32[256,2]{0,1:T(2,128)}, u32[]{:S(2)}, u32[]{:S(2)}) collective-permute-start(s32[256,2]{0,1:T(2,128)} %param.28), channel_id=1, source_target_pairs={{0,16},{4,20},{8,24},{12,28},{16,0},{20,4},{24,8},{28,12},{1,17},{... | collective-permute-start | bytes 6152 | tf_op jit(solution)/shard_map/ppermute | solution.py:44
  8.0 10.4 %collective-permute-start.3 = (bf16[96,768]{1,0:T(8,128)(2,1)}, bf16[96,768]{1,0:T(8,128)(2,1)}, u32[]{:S(2)}, u32[]{:S(2)}) collective-permute-start(bf16[96,768]{1,0:T(8,128)(2,1)} %pack_weights.1.refs_0_), channel_id=1, source_target_pairs={{0,16},{4,20},{8,24},{12,28},{16,0},{20,4},{24,8},{28,12},{1,17},{... | collective-permute-start | bytes 442376 | tf_op jit(solution)/shard_map/ppermute | solution.py:44
  20.0 15.9 %collective-permute-start.6 = (bf16[192,768]{1,0:T(8,128)(2,1)}, bf16[192,768]{1,0:T(8,128)(2,1)}, u32[]{:S(2)}, u32[]{:S(2)}) collective-permute-start(bf16[192,768]{1,0:T(8,128)(2,1)} %pair_up.1.refs_6_), channel_id=1, source_target_pairs={{0,12},{4,8},{8,4},{12,0},{16,28},{20,24},{24,20},{28,16},{1,13},{... | collective-permute-start | bytes 884744 | tf_op jit(solution)/shard_map/ppermute | solution.py:44
  20.0 15.9 %collective-permute-start.5 = (bf16[192,768]{1,0:T(8,128)(2,1)}, bf16[192,768]{1,0:T(8,128)(2,1)}, u32[]{:S(2)}, u32[]{:S(2)}) collective-permute-start(bf16[192,768]{1,0:T(8,128)(2,1)} %pair_up.1.refs_6_), channel_id=1, source_target_pairs={{0,8},{4,12},{8,0},{12,4},{16,24},{20,28},{24,16},{28,20},{1,9},{5... | collective-permute-start | bytes 884744 | tf_op jit(solution)/shard_map/ppermute | solution.py:44
  23.0 13.0 %collective-permute-start.4 = (bf16[192,768]{1,0:T(8,128)(2,1)}, bf16[192,768]{1,0:T(8,128)(2,1)}, u32[]{:S(2)}, u32[]{:S(2)}) collective-permute-start(bf16[192,768]{1,0:T(8,128)(2,1)} %pair_up.1.refs_6_), channel_id=1, source_target_pairs={{0,4},{4,0},{8,12},{12,8},{16,20},{20,16},{24,28},{28,24},{1,5},{5... | collective-permute-start | bytes 884744 | tf_op jit(solution)/shard_map/ppermute | solution.py:44
  23.5 12.4 %collective-permute-start.2 = (bf16[256,768]{1,0:T(8,128)(2,1)}, bf16[256,768]{1,0:T(8,128)(2,1)}, u32[]{:S(2)}, u32[]{:S(2)}) collective-permute-start(bf16[256,768]{1,0:T(8,128)(2,1)} %collective-permute-done.1.refs_3_.refs_4_), channel_id=1, source_target_pairs={{0,1},{1,0},{2,3},{3,2},{4,5},{5,4},{6,7},{7,6},{8,9},{9,8},{10,11... | collective-permute-start | bytes 1179656 | tf_op jit(solution)/shard_map/ppermute | solution.py:44
  41.2 16.4 %collective-permute-start.11 = (bf16[192,768]{1,0:T(8,128)(2,1)}, bf16[192,768]{1,0:T(8,128)(2,1)}, u32[]{:S(2)}, u32[]{:S(2)}) collective-permute-start(bf16[192,768]{1,0:T(8,128)(2,1)} %get-tuple-element.114.refs_8_.refs_12_), channel_id=1, source_target_pairs={{0,2},{1,3},{2,0},{3,1},{4,6},{5,7},{6,4},{7,5},{8,10},{9,11},{10,... | collective-permute-start | bytes 884744 | tf_op jit(solution)/shard_map/ppermute | solution.py:44
  43.2 23.6 %collective-permute-start.13 = (bf16[256,768]{1,0:T(8,128)(2,1)}, bf16[256,768]{1,0:T(8,128)(2,1)}, u32[]{:S(2)}, u32[]{:S(2)}) collective-permute-start(bf16[256,768]{1,0:T(8,128)(2,1)} %get-tuple-element.115), channel_id=1, source_target_pairs={{0,16},{4,20},{8,24},{12,28},{16,0},{20,4},{24,8},{28,12},{1,17},{... | collective-permute-start | bytes 1179656 | tf_op jit(solution)/shard_map/ppermute | solution.py:44
  45.6 21.3 %collective-permute-start.10 = (bf16[192,768]{1,0:T(8,128)(2,1)}, bf16[192,768]{1,0:T(8,128)(2,1)}, u32[]{:S(2)}, u32[]{:S(2)}) collective-permute-start(bf16[192,768]{1,0:T(8,128)(2,1)} %get-tuple-element.114.refs_8_.refs_12_), channel_id=1, source_target_pairs={{0,1},{1,0},{2,3},{3,2},{4,5},{5,4},{6,7},{7,6},{8,9},{9,8},{10,11... | collective-permute-start | bytes 884744 | tf_op jit(solution)/shard_map/ppermute | solution.py:44
  57.6 9.3 %collective-permute-start.12 = (bf16[192,768]{1,0:T(8,128)(2,1)}, bf16[192,768]{1,0:T(8,128)(2,1)}, u32[]{:S(2)}, u32[]{:S(2)}) collective-permute-start(bf16[192,768]{1,0:T(8,128)(2,1)} %collective-permute-done.11.refs_10_.refs_14_), channel_id=1, source_target_pairs={{0,1},{1,0},{2,3},{3,2},{4,5},{5,4},{6,7},{7,6},{8,9},{9,8},{10,11... | collective-permute-start | bytes 884744 | tf_op jit(solution)/shard_map/ppermute | solution.py:44
  58.4 6.6 %collective-permute-start.8 = (bf16[256,192]{1,0:T(8,128)(2,1)}, bf16[256,192]{1,0:T(8,128)(2,1)}, u32[]{:S(2)}, u32[]{:S(2)}) collective-permute-start(bf16[256,192]{1,0:T(8,128)(2,1)} %get-tuple-element.112), channel_id=1, source_target_pairs={{0,2},{1,3},{2,0},{3,1},{4,6},{5,7},{6,4},{7,5},{8,10},{9,11},{10,... | collective-permute-start | bytes 294920 | tf_op jit(solution)/shard_map/ppermute | solution.py:44
  59.9 7.0 %collective-permute-start.9 = (bf16[256,192]{1,0:T(8,128)(2,1)}, bf16[256,192]{1,0:T(8,128)(2,1)}, u32[]{:S(2)}, u32[]{:S(2)}) collective-permute-start(bf16[256,192]{1,0:T(8,128)(2,1)} %get-tuple-element.113), channel_id=1, source_target_pairs={{0,3},{1,2},{2,1},{3,0},{4,7},{5,6},{6,5},{7,4},{8,11},{9,10},{10,... | collective-permute-start | bytes 294920 | tf_op jit(solution)/shard_map/ppermute | solution.py:44
  70.7 21.1 %collective-permute-start.14 = (bf16[256,768]{1,0:T(8,128)(2,1)}, bf16[256,768]{1,0:T(8,128)(2,1)}, u32[]{:S(2)}, u32[]{:S(2)}) collective-permute-start(bf16[256,768]{1,0:T(8,128)(2,1)} %get-tuple-element.117.refs_4_.refs_6_), channel_id=1, source_target_pairs={{0,16},{4,20},{8,24},{12,28},{16,0},{20,4},{24,8},{28,12},{1,17},{... | collective-permute-start | bytes 1179656 | tf_op jit(solution)/shard_map/ppermute | solution.py:44
  77.2 14.6 %collective-permute-start.16 = (bf16[256,768]{1,0:T(8,128)(2,1)}, bf16[256,768]{1,0:T(8,128)(2,1)}, u32[]{:S(2)}, u32[]{:S(2)}) collective-permute-start(bf16[256,768]{1,0:T(8,128)(2,1)} %get-tuple-element.118), channel_id=1, source_target_pairs={{0,4},{4,0},{8,12},{12,8},{16,20},{20,16},{24,28},{28,24},{1,5},{5... | collective-permute-start | bytes 1179656 | tf_op jit(solution)/shard_map/ppermute | solution.py:44
  78.7 19.4 %collective-permute-start.17 = (bf16[256,768]{1,0:T(8,128)(2,1)}, bf16[256,768]{1,0:T(8,128)(2,1)}, u32[]{:S(2)}, u32[]{:S(2)}) collective-permute-start(bf16[256,768]{1,0:T(8,128)(2,1)} %get-tuple-element.119), channel_id=1, source_target_pairs={{0,8},{4,12},{8,0},{12,4},{16,24},{20,28},{24,16},{28,20},{1,9},{5... | collective-permute-start | bytes 1179656 | tf_op jit(solution)/shard_map/ppermute | solution.py:44
  78.7 21.8 %collective-permute-start.22 = (bf16[128,768]{1,0:T(8,128)(2,1)}, bf16[128,768]{1,0:T(8,128)(2,1)}, u32[]{:S(2)}, u32[]{:S(2)}) collective-permute-start(bf16[128,768]{1,0:T(8,128)(2,1)} %get-tuple-element.127), channel_id=1, source_target_pairs={{0,4},{4,0},{8,12},{12,8},{16,20},{20,16},{24,28},{28,24},{1,5},{5... | collective-permute-start | bytes 589832 | tf_op jit(solution)/shard_map/ppermute | solution.py:44
  79.4 22.9 %collective-permute-start.23 = (bf16[128,768]{1,0:T(8,128)(2,1)}, bf16[128,768]{1,0:T(8,128)(2,1)}, u32[]{:S(2)}, u32[]{:S(2)}) collective-permute-start(bf16[128,768]{1,0:T(8,128)(2,1)} %get-tuple-element.128), channel_id=1, source_target_pairs={{0,8},{4,12},{8,0},{12,4},{16,24},{20,28},{24,16},{28,20},{1,9},{5... | collective-permute-start | bytes 589832 | tf_op jit(solution)/shard_map/ppermute | solution.py:44
  91.8 14.5 %collective-permute-start.24 = (bf16[128,768]{1,0:T(8,128)(2,1)}, bf16[128,768]{1,0:T(8,128)(2,1)}, u32[]{:S(2)}, u32[]{:S(2)}) collective-permute-start(bf16[128,768]{1,0:T(8,128)(2,1)} %get-tuple-element.129), channel_id=1, source_target_pairs={{0,12},{4,8},{8,4},{12,0},{16,28},{20,24},{24,20},{28,16},{1,13},{... | collective-permute-start | bytes 589832 | tf_op jit(solution)/shard_map/ppermute | solution.py:44
  91.8 27.3 %collective-permute-start.21 = (bf16[256,768]{1,0:T(8,128)(2,1)}, bf16[256,768]{1,0:T(8,128)(2,1)}, u32[]{:S(2)}, u32[]{:S(2)}) collective-permute-start(bf16[256,768]{1,0:T(8,128)(2,1)} %get-tuple-element.125), channel_id=1, source_target_pairs={{0,12},{4,8},{8,4},{12,0},{16,28},{20,24},{24,20},{28,16},{1,13},{... | collective-permute-start | bytes 1179656 | tf_op jit(solution)/shard_map/ppermute | solution.py:44
  100.2 18.9 %collective-permute-start.18 = (bf16[128,768]{1,0:T(8,128)(2,1)}, bf16[128,768]{1,0:T(8,128)(2,1)}, u32[]{:S(2)}, u32[]{:S(2)}) collective-permute-start(bf16[128,768]{1,0:T(8,128)(2,1)} %get-tuple-element.121), channel_id=1, source_target_pairs={{0,4},{4,0},{8,12},{12,8},{16,20},{20,16},{24,28},{28,24},{1,5},{5... | collective-permute-start | bytes 589832 | tf_op jit(solution)/shard_map/ppermute | solution.py:44
  100.5 18.7 %collective-permute-start.19 = (bf16[128,768]{1,0:T(8,128)(2,1)}, bf16[128,768]{1,0:T(8,128)(2,1)}, u32[]{:S(2)}, u32[]{:S(2)}) collective-permute-start(bf16[128,768]{1,0:T(8,128)(2,1)} %get-tuple-element.122), channel_id=1, source_target_pairs={{0,8},{4,12},{8,0},{12,4},{16,24},{20,28},{24,16},{28,20},{1,9},{5... | collective-permute-start | bytes 589832 | tf_op jit(solution)/shard_map/ppermute | solution.py:44
  102.3 19.5 %collective-permute-start.20 = (bf16[128,768]{1,0:T(8,128)(2,1)}, bf16[128,768]{1,0:T(8,128)(2,1)}, u32[]{:S(2)}, u32[]{:S(2)}) collective-permute-start(bf16[128,768]{1,0:T(8,128)(2,1)} %get-tuple-element.123), channel_id=1, source_target_pairs={{0,12},{4,8},{8,4},{12,0},{16,28},{20,24},{24,20},{28,16},{1,13},{... | collective-permute-start | bytes 589832 | tf_op jit(solution)/shard_map/ppermute | solution.py:44
  139.7 15.5 %collective-permute-start.28 = (bf16[128,896]{1,0:T(8,128)(2,1)}, bf16[128,896]{1,0:T(8,128)(2,1)}, u32[]{:S(2)}, u32[]{:S(2)}) collective-permute-start(bf16[128,896]{1,0:T(8,128)(2,1)} %get-tuple-element.141), channel_id=1, source_target_pairs={{0,4},{4,0},{8,12},{12,8},{16,20},{20,16},{24,28},{28,24},{1,5},{5... | collective-permute-start | bytes 688136 | tf_op jit(solution)/shard_map/ppermute | solution.py:44
  141.5 13.7 %collective-permute-start.29 = (bf16[128,896]{1,0:T(8,128)(2,1)}, bf16[128,896]{1,0:T(8,128)(2,1)}, u32[]{:S(2)}, u32[]{:S(2)}) collective-permute-start(bf16[128,896]{1,0:T(8,128)(2,1)} %get-tuple-element.142), channel_id=1, source_target_pairs={{0,8},{4,12},{8,0},{12,4},{16,24},{20,28},{24,16},{28,20},{1,9},{5... | collective-permute-start | bytes 688136 | tf_op jit(solution)/shard_map/ppermute | solution.py:44
  141.6 13.7 %collective-permute-start.30 = (bf16[128,896]{1,0:T(8,128)(2,1)}, bf16[128,896]{1,0:T(8,128)(2,1)}, u32[]{:S(2)}, u32[]{:S(2)}) collective-permute-start(bf16[128,896]{1,0:T(8,128)(2,1)} %get-tuple-element.143), channel_id=1, source_target_pairs={{0,12},{4,8},{8,4},{12,0},{16,28},{20,24},{24,20},{28,16},{1,13},{... | collective-permute-start | bytes 688136 | tf_op jit(solution)/shard_map/ppermute | solution.py:44
  158.0 24.0 %collective-permute-start.31 = (bf16[128,896]{1,0:T(8,128)(2,1)}, bf16[128,896]{1,0:T(8,128)(2,1)}, u32[]{:S(2)}, u32[]{:S(2)}) collective-permute-start(bf16[128,896]{1,0:T(8,128)(2,1)} %get-tuple-element.147), channel_id=1, source_target_pairs={{0,4},{4,0},{8,12},{12,8},{16,20},{20,16},{24,28},{28,24},{1,5},{5... | collective-permute-start | bytes 688136 | tf_op jit(solution)/shard_map/ppermute | solution.py:44
  159.8 22.2 %collective-permute-start.32 = (bf16[128,896]{1,0:T(8,128)(2,1)}, bf16[128,896]{1,0:T(8,128)(2,1)}, u32[]{:S(2)}, u32[]{:S(2)}) collective-permute-start(bf16[128,896]{1,0:T(8,128)(2,1)} %get-tuple-element.148), channel_id=1, source_target_pairs={{0,8},{4,12},{8,0},{12,4},{16,24},{20,28},{24,16},{28,20},{1,9},{5... | collective-permute-start | bytes 688136 | tf_op jit(solution)/shard_map/ppermute | solution.py:44
  159.8 22.2 %collective-permute-start.33 = (bf16[128,896]{1,0:T(8,128)(2,1)}, bf16[128,896]{1,0:T(8,128)(2,1)}, u32[]{:S(2)}, u32[]{:S(2)}) collective-permute-start(bf16[128,896]{1,0:T(8,128)(2,1)} %get-tuple-element.149), channel_id=1, source_target_pairs={{0,12},{4,8},{8,4},{12,0},{16,28},{20,24},{24,20},{28,16},{1,13},{... | collective-permute-start | bytes 688136 | tf_op jit(solution)/shard_map/ppermute | solution.py:44
  161.5 20.8 %collective-permute-start.34 = (bf16[256,896]{1,0:T(8,128)(2,1)}, bf16[256,896]{1,0:T(8,128)(2,1)}, u32[]{:S(2)}, u32[]{:S(2)}) collective-permute-start(bf16[256,896]{1,0:T(8,128)(2,1)} %get-tuple-element.150), channel_id=1, source_target_pairs={{0,16},{4,20},{8,24},{12,28},{16,0},{20,4},{24,8},{28,12},{1,17},{... | collective-permute-start | bytes 1376264 | tf_op jit(solution)/shard_map/ppermute | solution.py:44
  189.2 9.2 %collective-permute-start.38 = (bf16[3072,768]{1,0:T(8,128)(2,1)}, bf16[3072,768]{1,0:T(8,128)(2,1)}, u32[]{:S(2)}, u32[]{:S(2)}) collective-permute-start(bf16[3072,768]{1,0:T(8,128)(2,1)} %get-tuple-element.164), channel_id=1, source_target_pairs={{0,1},{1,0},{2,3},{3,2},{4,5},{5,4},{6,7},{7,6},{8,9},{9,8},{10,11... | collective-permute-start | bytes 14155784 | tf_op jit(solution)/shard_map/ppermute | solution.py:44
  189.2 9.1 %collective-permute-start.39 = (bf16[384,768]{1,0:T(8,128)(2,1)}, bf16[384,768]{1,0:T(8,128)(2,1)}, u32[]{:S(2)}, u32[]{:S(2)}) collective-permute-start(bf16[384,768]{1,0:T(8,128)(2,1)} %get-tuple-element.166), channel_id=1, source_target_pairs={{0,1},{1,0},{2,3},{3,2},{4,5},{5,4},{6,7},{7,6},{8,9},{9,8},{10,11... | collective-permute-start | bytes 1769480 | tf_op jit(solution)/shard_map/ppermute | solution.py:44
  189.7 6.7 %collective-permute-start.36 = (bf16[256,192]{1,0:T(8,128)(2,1)}, bf16[256,192]{1,0:T(8,128)(2,1)}, u32[]{:S(2)}, u32[]{:S(2)}) collective-permute-start(bf16[256,192]{1,0:T(8,128)(2,1)} %get-tuple-element.162), channel_id=1, source_target_pairs={{0,2},{1,3},{2,0},{3,1},{4,6},{5,7},{6,4},{7,5},{8,10},{9,11},{10,... | collective-permute-start | bytes 294920 | tf_op jit(solution)/shard_map/ppermute | solution.py:44
  191.2 6.2 %collective-permute-start.37 = (bf16[256,192]{1,0:T(8,128)(2,1)}, bf16[256,192]{1,0:T(8,128)(2,1)}, u32[]{:S(2)}, u32[]{:S(2)}) collective-permute-start(bf16[256,192]{1,0:T(8,128)(2,1)} %get-tuple-element.163), channel_id=1, source_target_pairs={{0,3},{1,2},{2,1},{3,0},{4,7},{5,6},{6,5},{7,4},{8,11},{9,10},{10,... | collective-permute-start | bytes 294920 | tf_op jit(solution)/shard_map/ppermute | solution.py:44
  203.2 23.3 %collective-permute-start.40 = (bf16[448,768]{1,0:T(8,128)(2,1)}, bf16[448,768]{1,0:T(8,128)(2,1)}, u32[]{:S(2)}, u32[]{:S(2)}) collective-permute-start(bf16[448,768]{1,0:T(8,128)(2,1)} %get-tuple-element.168.refs_11_), channel_id=1, source_target_pairs={{0,2},{1,3},{2,0},{3,1},{4,6},{5,7},{6,4},{7,5},{8,10},{9,11},{10,... | collective-permute-start | bytes 2064392 | tf_op jit(solution)/shard_map/ppermute | solution.py:44
  204.7 21.8 %collective-permute-start.25 = (bf16[256,768]{1,0:T(8,128)(2,1)}, bf16[256,768]{1,0:T(8,128)(2,1)}, u32[]{:S(2)}, u32[]{:S(2)}) collective-permute-start(bf16[256,768]{1,0:T(8,128)(2,1)} %get-tuple-element.132), channel_id=1, source_target_pairs={{0,4},{4,0},{8,12},{12,8},{16,20},{20,16},{24,28},{28,24},{1,5},{5... | collective-permute-start | bytes 1179656 | tf_op jit(solution)/shard_map/ppermute | solution.py:44
  206.4 20.1 %collective-permute-start.26 = (bf16[256,768]{1,0:T(8,128)(2,1)}, bf16[256,768]{1,0:T(8,128)(2,1)}, u32[]{:S(2)}, u32[]{:S(2)}) collective-permute-start(bf16[256,768]{1,0:T(8,128)(2,1)} %get-tuple-element.133), channel_id=1, source_target_pairs={{0,8},{4,12},{8,0},{12,4},{16,24},{20,28},{24,16},{28,20},{1,9},{5... | collective-permute-start | bytes 1179656 | tf_op jit(solution)/shard_map/ppermute | solution.py:44
  208.0 18.5 %collective-permute-start.27 = (bf16[256,768]{1,0:T(8,128)(2,1)}, bf16[256,768]{1,0:T(8,128)(2,1)}, u32[]{:S(2)}, u32[]{:S(2)}) collective-permute-start(bf16[256,768]{1,0:T(8,128)(2,1)} %get-tuple-element.134), channel_id=1, source_target_pairs={{0,12},{4,8},{8,4},{12,0},{16,28},{20,24},{24,20},{28,16},{1,13},{... | collective-permute-start | bytes 1179656 | tf_op jit(solution)/shard_map/ppermute | solution.py:44
  209.9 57.7 %collective-permute-start.49 = (bf16[768,768]{1,0:T(8,128)(2,1)}, bf16[768,768]{1,0:T(8,128)(2,1)}, u32[]{:S(2)}, u32[]{:S(2)}) collective-permute-start(bf16[768,768]{1,0:T(8,128)(2,1)} %get-tuple-element.194), channel_id=1, source_target_pairs={{0,2},{1,3},{2,0},{3,1},{4,6},{5,7},{6,4},{7,5},{8,10},{9,11},{10,... | collective-permute-start | bytes 3538952 | tf_op jit(solution)/shard_map/ppermute | solution.py:44
  233.7 21.8 %collective-permute-start.44 = (bf16[512,768]{1,0:T(8,128)(2,1)}, bf16[512,768]{1,0:T(8,128)(2,1)}, u32[]{:S(2)}, u32[]{:S(2)}) collective-permute-start(bf16[512,768]{1,0:T(8,128)(2,1)} %get-tuple-element.184), channel_id=1, source_target_pairs={{0,1},{1,0},{2,3},{3,2},{4,5},{5,4},{6,7},{7,6},{8,9},{9,8},{10,11... | collective-permute-start | bytes 2359304 | tf_op jit(solution)/shard_map/ppermute | solution.py:44
  233.8 10.8 %collective-permute-start.41 = (bf16[224,768]{1,0:T(8,128)(2,1)}, bf16[224,768]{1,0:T(8,128)(2,1)}, u32[]{:S(2)}, u32[]{:S(2)}) collective-permute-start(bf16[224,768]{1,0:T(8,128)(2,1)} %get-tuple-element.180), channel_id=1, source_target_pairs={{0,4},{4,0},{8,12},{12,8},{16,20},{20,16},{24,28},{28,24},{1,5},{5... | collective-permute-start | bytes 1032200 | tf_op jit(solution)/shard_map/ppermute | solution.py:44
  235.5 32.1 %collective-permute-start.48 = (bf16[512,768]{1,0:T(8,128)(2,1)}, bf16[512,768]{1,0:T(8,128)(2,1)}, u32[]{:S(2)}, u32[]{:S(2)}) collective-permute-start(bf16[512,768]{1,0:T(8,128)(2,1)} %get-tuple-element.193), channel_id=1, source_target_pairs={{0,2},{1,3},{2,0},{3,1},{4,6},{5,7},{6,4},{7,5},{8,10},{9,11},{10,... | collective-permute-start | bytes 2359304 | tf_op jit(solution)/shard_map/ppermute | solution.py:44
  237.0 10.3 %collective-permute-start.42 = (bf16[224,768]{1,0:T(8,128)(2,1)}, bf16[224,768]{1,0:T(8,128)(2,1)}, u32[]{:S(2)}, u32[]{:S(2)}) collective-permute-start(bf16[224,768]{1,0:T(8,128)(2,1)} %get-tuple-element.181), channel_id=1, source_target_pairs={{0,8},{4,12},{8,0},{12,4},{16,24},{20,28},{24,16},{28,20},{1,9},{5... | collective-permute-start | bytes 1032200 | tf_op jit(solution)/shard_map/ppermute | solution.py:44
  244.6 10.9 %collective-permute-start.43 = (bf16[224,768]{1,0:T(8,128)(2,1)}, bf16[224,768]{1,0:T(8,128)(2,1)}, u32[]{:S(2)}, u32[]{:S(2)}) collective-permute-start(bf16[224,768]{1,0:T(8,128)(2,1)} %get-tuple-element.182), channel_id=1, source_target_pairs={{0,12},{4,8},{8,4},{12,0},{16,28},{20,24},{24,20},{28,16},{1,13},{... | collective-permute-start | bytes 1032200 | tf_op jit(solution)/shard_map/ppermute | solution.py:44
  257.8 20.6 %collective-permute-start.47 = (bf16[128,768]{1,0:T(8,128)(2,1)}, bf16[128,768]{1,0:T(8,128)(2,1)}, u32[]{:S(2)}, u32[]{:S(2)}) collective-permute-start(bf16[128,768]{1,0:T(8,128)(2,1)} %get-tuple-element.192), channel_id=1, source_target_pairs={{0,16},{4,20},{8,24},{12,28},{16,0},{20,4},{24,8},{28,12},{1,17},{... | collective-permute-start | bytes 589832 | tf_op jit(solution)/shard_map/ppermute | solution.py:44
  263.2 23.5 %collective-permute-start.45 = (bf16[256,768]{1,0:T(8,128)(2,1)}, bf16[256,768]{1,0:T(8,128)(2,1)}, u32[]{:S(2)}, u32[]{:S(2)}) collective-permute-start(bf16[256,768]{1,0:T(8,128)(2,1)} %get-tuple-element.187), channel_id=1, source_target_pairs={{0,16},{4,20},{8,24},{12,28},{16,0},{20,4},{24,8},{28,12},{1,17},{... | collective-permute-start | bytes 1179656 | tf_op jit(solution)/shard_map/ppermute | solution.py:44
  266.1 12.3 %collective-permute-start.46 = (bf16[256,768]{1,0:T(8,128)(2,1)}, bf16[256,768]{1,0:T(8,128)(2,1)}, u32[]{:S(2)}, u32[]{:S(2)}) collective-permute-start(bf16[256,768]{1,0:T(8,128)(2,1)} %add_convert_fusion), channel_id=1, source_target_pairs={{0,2},{1,3},{2,0},{3,1},{4,6},{5,7},{6,4},{7,5},{8,10},{9,11},{10,... | collective-permute-start | bytes 1179656 | tf_op jit(solution)/shard_map/ppermute | solution.py:44
  (7 other events, 31.4 us)

commit v10 on v9

--- a/solution.py
+++ b/solution.py
@@ -731,7 +731,7 @@
 
     def kernel(place_ref, *refs):
         x_refs, p_refs, a_refs, s_refs = [refs[i * sets : (i + 1) * sets] for i in range(4)]
-        near_ref, base_ref, out = refs[4 * sets :]
+        near_ref, base_ref = refs[4 * sets :]
         step = pl.program_id(0)
 
         def total_of(lefts, rights):
@@ -740,21 +740,21 @@
                 held = held + dot(left[...], right[...], 0, 0)
             return held
 
-        @pl.when(step < 4)
+        @pl.when(step < 2)
         def _():
-            out[...] = total_of(x_refs, p_refs)
-
-        @pl.when(step >= 4)
+            near_ref[...] = total_of(x_refs, p_refs).astype(bf16)
+
+        @pl.when((step >= 2) & (step < 4))
         def _():
-            out[...] = total_of(a_refs, s_refs)
-
-        @pl.when(step % 4 < 2)
+            base_ref[...] = total_of(x_refs, p_refs)
+
+        @pl.when((step >= 4) & (step < 6))
         def _():
-            near_ref[...] = out[...].astype(bf16)
-
-        @pl.when(step % 4 >= 2)
+            near_ref[...] = total_of(a_refs, s_refs).astype(bf16)
+
+        @pl.when(step >= 6)
         def _():
-            base_ref[...] = out[...]
+            base_ref[...] = total_of(a_refs, s_refs)
 
     def partner(i):
         return jnp.where(i < 2, 2 * i + 1, 2 * i - 4)
@@ -777,7 +777,6 @@
                     (piece, width), lambda i, p: (2 * (i // 4) + jnp.maximum(i % 4 - 2, 0), 0)
                 ),
             ],
-            scratch_shapes=[pltpu.VMEM((piece, width), f32)],
         ),
         out_shape=[shape((4 * piece, width), bf16), shape((4 * piece, width), f32)],
         compiler_params=limit(64),

time: 292 us -> 292 us (level)
  transfers between devices with their start and end apart: 52 -> 52, of which waited for: 17 -> 18; matrix products, arithmetic and copies ran while one was open for 10% -> 10% of each run, Pallas kernels for 37% -> 36%
where the time goes in v10:
time: 292 us; the launch traced here: 290 us
  Pallas kernels  142 us (49%)
  waiting for transfers between devices  64.2 us (22%)
  starting transfers between devices  51.4 us (18%)
  local copies, waits for them, and re-layouts  15 us (5%)
  other arithmetic  14.7 us (5%)
    pallas_call x14, Pallas kernels, call(): pl.pallas_call(body, name=name, grid=(1,), in_specs=in_specs + [pl.BlockS...  69.3 us
    ppermute x52, waiting for transfers between devices, swap(): return lax.ppermute(values, axis, [(i, i ^ step) for i in range(count)])  64.2 us
    ppermute x52, starting transfers between devices, swap(): return lax.ppermute(values, axis, [(i, i ^ step) for i in range(count)])  51.4 us
    pallas_call x1, Pallas kernels, expert_weight_grads(): pl.pallas_call(kernel, name='expert_weight_grads', grid_spec=pltpu.Prefet...  19 us
    pallas_call x1, Pallas kernels, run_experts(): pl.pallas_call(kernel, name=name, grid=(units // piece,), in_specs=[pl.Bl...  17.9 us
    pallas_call x1, Pallas kernels, experts_forward(): pl.pallas_call(kernel, name='experts_forward', grid=(units // piece,), in...  12.8 us
    pallas_call x1, Pallas kernels, experts_backward(): pl.pallas_call(kernel, name='experts_backward', grid=(units // piece,), i...  12 us
    pallas_call x1, Pallas kernels, add_up(): pl.pallas_call(kernel, name='add_up', grid=(1,), in_specs=specs + [pl.Blo...  6.27 us
  transfers between devices with their start and end apart: 52, of which 18 were waited for; matrix products, arithmetic and copies ran while one was open for 10% of the time, Pallas kernels for 36%

profile of v10, /device:TPU:0, one launch (start us, length us, event | category | flops | bytes accessed | tf_op | source)
XLA Modules:
  0.0 290.3 jit_solution(16830542409754969756)
XLA Ops:
  0.6 3.0 %collective-permute-start.1 = (bf16[256,768]{1,0:T(8,128)(2,1)}, bf16[256,768]{1,0:T(8,128)(2,1)}, u32[]{:S(2)}, u32[]{:S(2)}) collective-permute-start(bf16[256,768]{1,0:T(8,128)(2,1)} %refs_0_.4), channel_id=1, source_target_pairs={{0,2},{1,3},{2,0},{3,1},{4,6},{5,7},{6,4},{7,5},{8,10},{9,11},{10,... | collective-permute-start | bytes 1179656 | tf_op jit(solution)/shard_map/ppermute | solution.py:44
  3.7 2.6 collective-permute-start.15
  10.4 7.9 %collective-permute-done.3.refs_1_ = bf16[96,768]{1,0:T(8,128)(2,1)} collective-permute-done((bf16[96,768]{1,0:T(8,128)(2,1)}, bf16[96,768]{1,0:T(8,128)(2,1)}, u32[]{:S(2)}, u32[]{:S(2)}) %collective-permute-start.3) | collective-permute-done | bytes 147488 | tf_op jit(solution)/shard_map/ppermute | solution.py:44
  20.0 3.0 %collective-permute-start.5 = (bf16[192,768]{1,0:T(8,128)(2,1)}, bf16[192,768]{1,0:T(8,128)(2,1)}, u32[]{:S(2)}, u32[]{:S(2)}) collective-permute-start(bf16[192,768]{1,0:T(8,128)(2,1)} %pair_up.1.refs_6_), channel_id=1, source_target_pairs={{0,8},{4,12},{8,0},{12,4},{16,24},{20,28},{24,16},{28,20},{1,9},{5... | collective-permute-start | bytes 884744 | tf_op jit(solution)/shard_map/ppermute | solution.py:44
  30.5 1.8 copy.37.refs_10_
  32.3 1.7 copy.34.refs_12_.refs_4_
  36.0 5.2 %project.1 = (bf16[1024,768]{1,0:T(8,128)(2,1)}, bf16[1024,192]{1,0:T(8,128)(2,1)}, bf16[1024,192]{1,0:T(8,128)(2,1)}, bf16[1024,192]{1,0:T(8,128)(2,1)}, bf16[7...) custom-call(s32[2]{0:T(128)} %pad_add_fusion.2.refs_0_.me_ref.place_, ...), custom_call_target="tpu_custom_call", output_to_operand_aliasing={{8}: (10, {})} | custom-call | flops 10000000 | bytes 10000 | tf_op jit(solution)/shard_map/project/pallas_call | solution.py:69
  45.6 11.5 %attend.1 = (bf16[256,192]{1,0:T(8,128)(2,1)}, bf16[256,192]{1,0:T(8,128)(2,1)}, bf16[256,192]{1,0:T(8,128)(2,1)}, bf16[256,192]{1,0:T(8,128)(2,1)}) custom-call(s32[2]{0:T(128)} %pad_add_fusion.2.refs_0_.me_ref.place_ref, bf16[1024,192]{1,0:T(8,128)(2,1)} %get-tuple-element.107.refs_1_, bf16[1024,192]{1,0:T(8,128)(2,1)} %get-tuple-element.108.refs_2_, ...), custom_call_target="tpu_custom_call" | custom-call | flops 10000000 | bytes 10000 | tf_op jit(solution)/shard_map/attend/pallas_call | solution.py:69
  61.7 3.3 %collective-permute-done.8.refs_6_.refs_18_ = bf16[256,192]{1,0:T(8,128)(2,1)} collective-permute-done((bf16[256,192]{1,0:T(8,128)(2,1)}, bf16[256,192]{1,0:T(8,128)(2,1)}, u32[]{:S(2)}, u32[]{:S(2)}) %collective-permute-start.8) | collective-permute-done | bytes 98336 | tf_op jit(solution)/shard_map/ppermute | solution.py:44
  65.0 1.9 collective-permute-done.9.refs_7_.refs_19_
  66.9 3.9 %middle.1 = (f32[256,768]{1,0:T(8,128)}, bf16[256,768]{1,0:T(8,128)(2,1)}, f32[256,128]{1,0:T(8,128)}, bf16[128,768]{1,0:T(8,128)(2,1)}, bf16[128,768]{1,0:T(8,1...) custom-call(bf16[256,768]{1,0:T(8,128)(2,1)} %refs_0_.4, f32[1,768]{1,0:T(1,128)} %reshape.191.refs_15_.refs_1_.refs_4_, ...), custom_call_target="tpu_custom_call" | custom-call | flops 10000000 | bytes 10000 | tf_op jit(solution)/shard_map/middle/pallas_call | solution.py:69
  70.7 2.3 collective-permute-start.14
  74.4 2.8 grads_to_slots.1
  79.4 1.8 collective-permute-start.23
  81.2 10.6 %collective-permute-done.14.refs_0_ = bf16[256,768]{1,0:T(8,128)(2,1)} collective-permute-done((bf16[256,768]{1,0:T(8,128)(2,1)}, bf16[256,768]{1,0:T(8,128)(2,1)}, u32[]{:S(2)}, u32[]{:S(2)}) %collective-permute-start.14) | collective-permute-done | bytes 393248 | tf_op jit(solution)/shard_map/ppermute | solution.py:44
  91.8 2.9 %collective-permute-start.21 = (bf16[256,768]{1,0:T(8,128)(2,1)}, bf16[256,768]{1,0:T(8,128)(2,1)}, u32[]{:S(2)}, u32[]{:S(2)}) collective-permute-start(bf16[256,768]{1,0:T(8,128)(2,1)} %get-tuple-element.125), channel_id=1, source_target_pairs={{0,12},{4,8},{8,4},{12,0},{16,28},{20,24},{24,20},{28,16},{1,13},{... | collective-permute-start | bytes 1179656 | tf_op jit(solution)/shard_map/ppermute | solution.py:44
  94.7 3.4 %collective-permute-done.17.refs_3_.refs_6_.refs_2_ = bf16[256,768]{1,0:T(8,128)(2,1)} collective-permute-done((bf16[256,768]{1,0:T(8,128)(2,1)}, bf16[256,768]{1,0:T(8,128)(2,1)}, u32[]{:S(2)}, u32[]{:S(2)}) %collective-permute-start.17) | collective-permute-done | bytes 393248 | tf_op jit(solution)/shard_map/ppermute | solution.py:44
  98.1 2.1 far_to_slots.1
  100.5 1.8 collective-permute-done.23.refs_2_
  103.7 2.6 collective-permute-done.24.refs_3_
  106.3 12.8 %experts_forward.1 = (bf16[512,3072]{1,0:T(8,128)(2,1)}, bf16[512,3072]{1,0:T(8,128)(2,1)}, bf16[512,768]{1,0:T(8,128)(2,1)}, bf16[512,768]{1,0:T(8,128)(2,1)}, ...) custom-call(s32[2]{0:T(128)} %pad_add_fusion.2.refs_0_.me_ref.place_ref, bf16[768,3072]{1,0:T(8,128)(2,1)} %bitcast.45, ...), custom_call_target="tpu_custom_call" | custom-call | flops 20000000000 | bytes 10000000 | tf_op jit(solution)/shard_map/experts_forward/pallas_call | solution.py:460
  119.2 2.6 collective-permute-done.20.refs_3_
  121.8 17.9 %run_experts.1 = (bf16[128,896]{1,0:T(8,128)(2,1)}, bf16[128,896]{1,0:T(8,128)(2,1)}, bf16[128,896]{1,0:T(8,128)(2,1)}, bf16[128,896]{1,0:T(8,128)(2,1)}, bf16[2...) custom-call(s32[2]{0:T(128)} %pad_add_fusion.2.refs_0_.me_ref.place_, ...), custom_call_target="tpu_custom_call" | custom-call | flops 10000000 | bytes 10000 | tf_op jit(solution)/shard_map/run_experts/pallas_call | solution.py:614
  139.7 1.8 collective-permute-start.28
  141.6 1.7 collective-permute-start.30
  143.3 12.0 %experts_backward.1 = (bf16[128,896]{1,0:T(8,128)(2,1)}, bf16[128,896]{1,0:T(8,128)(2,1)}, bf16[128,896]{1,0:T(8,128)(2,1)}, bf16[128,896]{1,0:T(8,128)(2,1)}, b...) custom-call(s32[2]{0:T(128)} %pad_add_fusion.2.refs_0_.me_ref.place_ref, bf16[768,3072]{1,0:T(8,128)(2,1)} %bitcast.47, ...), custom_call_target="tpu_custom_call" | custom-call | flops 20000000000 | bytes 10000000 | tf_op jit(solution)/shard_map/experts_backward/pallas_call | solution.py:519
  155.3 2.7 back_from_slots.1
  158.0 1.8 collective-permute-start.31
  159.8 1.7 collective-permute-start.33
  162.1 19.0 %expert_weight_grads.1 = (bf16[3072,768]{1,0:T(8,128)(2,1)}, f32[3072,768]{1,0:T(8,128)}) custom-call(s32[2]{0:T(128)} %pad_add_fusion.2.refs_0_.me_ref.place_ref, bf16[512,768]{1,0:T(8,128)(2,1)} %get-tuple-element.151.refs_0_, bf16[512,768]{1,0:T(8,128)(2,1)} %get-tuple-element.152.refs_1_, bf16[512,3072]{1,0:T(8,128)(2,1)} %get-tuple-element.153.refs_2_, ...), custom_call_target="tpu_custom_call" | custom-call | flops 20000000000 | bytes 10000000 | tf_op jit(solution)/shard_map/expert_weight_grads/pallas_call | solution.py:765
  182.3 6.9 %home.1 = (bf16[256,192]{1,0:T(8,128)(2,1)}, bf16[256,192]{1,0:T(8,128)(2,1)}, bf16[256,192]{1,0:T(8,128)(2,1)}, bf16[256,192]{1,0:T(8,128)(2,1)}, f32[256,768]{...) custom-call(s32[8,256]{1,0:T(8,128)} %pad.24.refs_11_.refs_3_.refs_1, ...), custom_call_target="tpu_custom_call", output_to_operand_aliasing={{9}: (20, {})} | custom-call | flops 10000000 | bytes 10000 | tf_op jit(solution)/shard_map/home/pallas_call | solution.py:69
  191.2 5.2 %collective-permute-done.36.refs_0_.refs_9_ = bf16[256,192]{1,0:T(8,128)(2,1)} collective-permute-done((bf16[256,192]{1,0:T(8,128)(2,1)}, bf16[256,192]{1,0:T(8,128)(2,1)}, u32[]{:S(2)}, u32[]{:S(2)}) %collective-permute-start.36) | collective-permute-done | bytes 98336 | tf_op jit(solution)/shard_map/ppermute | solution.py:44
  198.3 4.9 %far_sums.1 = (bf16[448,768]{1,0:T(8,128)(2,1)}, bf16[512,768]{1,0:T(8,128)(2,1)}, bf16[768,768]{1,0:T(8,128)(2,1)}) custom-call(bf16[3072,768]{1,0:T(8,128)(2,1)} %collective-permute-done.38.near_in.near_out.in_near.out_near, bf16[3072,768]{1,0:T(8,128)(2,1)} %collective-permute-done.38.near_in.near_out.in_near.out_near, ...), custom_call_target="tpu_custom_call" | custom-call | flops 10000000 | bytes 10000 | tf_op jit(solution)/shard_map/far_sums/pallas_call | solution.py:810
  210.4 16.1 %attend_back.1 = (bf16[1024,192]{1,0:T(8,128)(2,1)}, bf16[1024,192]{1,0:T(8,128)(2,1)}, bf16[1024,192]{1,0:T(8,128)(2,1)}, f32[8,640]{1,0:T(8,128)}) custom-call(s32[2]{0:T(128)} %pad_add_fusion.2.refs_0_.me_ref.place_ref, bf16[1024,192]{1,0:T(8,128)(2,1)} %get-tuple-element.107.refs_1_, bf16[1024,192]{1,0:T(8,128)(2,1)} %get-tuple-element.108.refs_2_, ...), custom_call_target="tpu_custom_call" | custom-call | flops 10000000 | bytes 10000 | tf_op jit(solution)/shard_map/attend_back/pallas_call | solution.py:69
  226.5 7.2 %input_grads.1 = (bf16[512,768]{1,0:T(8,128)(2,1)}, f32[256,768]{1,0:T(8,128)}, f32[256,768]{1,0:T(8,128)}, f32[16,768]{1,0:T(8,128)}, f32[192,768]{1,0:T(8,128)...) custom-call(s32[2]{0:T(128)} %pad_add_fusion.2.refs_0_.me_ref.place_ref, ...), custom_call_target="tpu_custom_call" | custom-call | flops 10000000 | bytes 10000 | tf_op jit(solution)/shard_map/input_grads/pallas_call | solution.py:69
  233.8 1.7 collective-permute-start.41
  237.8 6.8 %collective-permute-done.41.refs_1_ = bf16[224,768]{1,0:T(8,128)(2,1)} collective-permute-done((bf16[224,768]{1,0:T(8,128)(2,1)}, bf16[224,768]{1,0:T(8,128)(2,1)}, u32[]{:S(2)}, u32[]{:S(2)}) %collective-permute-start.41) | collective-permute-done | bytes 344096 | tf_op jit(solution)/shard_map/ppermute | solution.py:44
  244.6 1.8 collective-permute-start.43
  247.2 8.2 %collective-permute-done.43.refs_3_ = bf16[224,768]{1,0:T(8,128)(2,1)} collective-permute-done((bf16[224,768]{1,0:T(8,128)(2,1)}, bf16[224,768]{1,0:T(8,128)(2,1)}, u32[]{:S(2)}, u32[]{:S(2)}) %collective-permute-start.43) | collective-permute-done | bytes 344096 | tf_op jit(solution)/shard_map/ppermute | solution.py:44
  255.5 2.2 fold_weights.1
  259.0 3.4 %result_from_slots.1 = (f32[256,768]{1,0:T(8,128)}, bf16[256,768]{1,0:T(8,128)(2,1)}) custom-call(bf16[256,768]{1,0:T(8,128)(2,1)} %get-tuple-element.131.refs_0_, bf16[256,768]{1,0:T(8,128)(2,1)} %collective-permute-done.25.refs_16_.refs_1_, bf16[256,768]{1,0:T(8,128)(2,1)} %collective-permute-done.26.refs_17_.refs_2_, ...), custom_call_target="tpu_custom_call" | custom-call | flops 10000000 | bytes 10000 | tf_op jit(solution)/shard_map/result_from_slots/pallas_call | solution.py:69
  264.0 2.0 add_convert_fusion
  267.5 6.3 %add_up.1 = (f32[768,768]{1,0:T(8,128)}, f32[768,768]{1,0:T(8,128)}) custom-call(f32[3072,768]{1,0:T(8,128)} %get-tuple-element.165.base_in.base_out.in_base.out_base, bf16[3072,768]{1,0:T(8,128)(2,1)} %collective-permute-done.38.near_in.near_out.in_near.out_near, f32[3072,768]{1,0:T(8,128)} %get-tuple-element.165.base_in.base_out.in_base.out_base, ...), custom_call_target="tpu_custom_call" | custom-call | flops 20000000000 | bytes 10000000 | tf_op jit(solution)/shard_map/add_up/pallas_call | solution.py:943
  273.8 3.6 %collective-permute-done.47.refs_2_ = bf16[128,768]{1,0:T(8,128)(2,1)} collective-permute-done((bf16[128,768]{1,0:T(8,128)(2,1)}, bf16[128,768]{1,0:T(8,128)(2,1)}, u32[]{:S(2)}, u32[]{:S(2)}) %collective-permute-start.47) | collective-permute-done | bytes 196640 | tf_op jit(solution)/shard_map/ppermute | solution.py:44
  277.4 1.9 split_weights.1
  279.4 1.9 fusion
  281.4 2.8 fusion.5
  285.8 1.9 add_convert_fusion.1
  (120 shorter events, 54.4 us)
Async XLA Ops:
  0.6 17.7 %collective-permute-start.1 = (bf16[256,768]{1,0:T(8,128)(2,1)}, bf16[256,768]{1,0:T(8,128)(2,1)}, u32[]{:S(2)}, u32[]{:S(2)}) collective-permute-start(bf16[256,768]{1,0:T(8,128)(2,1)} %refs_0_.4), channel_id=1, source_target_pairs={{0,2},{1,3},{2,0},{3,1},{4,6},{5,7},{6,4},{7,5},{8,10},{9,11},{10,... | collective-permute-start | bytes 1179656 | tf_op jit(solution)/shard_map/ppermute | solution.py:44
  3.7 14.6 %collective-permute-start = (bf16[256,768]{1,0:T(8,128)(2,1)}, bf16[256,768]{1,0:T(8,128)(2,1)}, u32[]{:S(2)}, u32[]{:S(2)}) collective-permute-start(bf16[256,768]{1,0:T(8,128)(2,1)} %refs_0_.4), channel_id=1, source_target_pairs={{0,1},{1,0},{2,3},{3,2},{4,5},{5,4},{6,7},{7,6},{8,9},{9,8},{10,11... | collective-permute-start | bytes 1179656 | tf_op jit(solution)/shard_map/ppermute | solution.py:44
  3.7 54.0 %collective-permute-start.15 = (s32[256,2]{0,1:T(2,128)}, s32[256,2]{0,1:T(2,128)}, u32[]{:S(2)}, u32[]{:S(2)}) collective-permute-start(s32[256,2]{0,1:T(2,128)} %param.28), channel_id=1, source_target_pairs={{0,16},{4,20},{8,24},{12,28},{16,0},{20,4},{24,8},{28,12},{1,17},{... | collective-permute-start | bytes 6152 | tf_op jit(solution)/shard_map/ppermute | solution.py:44
  8.0 10.4 %collective-permute-start.3 = (bf16[96,768]{1,0:T(8,128)(2,1)}, bf16[96,768]{1,0:T(8,128)(2,1)}, u32[]{:S(2)}, u32[]{:S(2)}) collective-permute-start(bf16[96,768]{1,0:T(8,128)(2,1)} %pack_weights.1.refs_0_), channel_id=1, source_target_pairs={{0,16},{4,20},{8,24},{12,28},{16,0},{20,4},{24,8},{28,12},{1,17},{... | collective-permute-start | bytes 442376 | tf_op jit(solution)/shard_map/ppermute | solution.py:44
  20.0 15.9 %collective-permute-start.6 = (bf16[192,768]{1,0:T(8,128)(2,1)}, bf16[192,768]{1,0:T(8,128)(2,1)}, u32[]{:S(2)}, u32[]{:S(2)}) collective-permute-start(bf16[192,768]{1,0:T(8,128)(2,1)} %pair_up.1.refs_6_), channel_id=1, source_target_pairs={{0,12},{4,8},{8,4},{12,0},{16,28},{20,24},{24,20},{28,16},{1,13},{... | collective-permute-start | bytes 884744 | tf_op jit(solution)/shard_map/ppermute | solution.py:44
  20.0 15.9 %collective-permute-start.5 = (bf16[192,768]{1,0:T(8,128)(2,1)}, bf16[192,768]{1,0:T(8,128)(2,1)}, u32[]{:S(2)}, u32[]{:S(2)}) collective-permute-start(bf16[192,768]{1,0:T(8,128)(2,1)} %pair_up.1.refs_6_), channel_id=1, source_target_pairs={{0,8},{4,12},{8,0},{12,4},{16,24},{20,28},{24,16},{28,20},{1,9},{5... | collective-permute-start | bytes 884744 | tf_op jit(solution)/shard_map/ppermute | solution.py:44
  23.0 13.0 %collective-permute-start.4 = (bf16[192,768]{1,0:T(8,128)(2,1)}, bf16[192,768]{1,0:T(8,128)(2,1)}, u32[]{:S(2)}, u32[]{:S(2)}) collective-permute-start(bf16[192,768]{1,0:T(8,128)(2,1)} %pair_up.1.refs_6_), channel_id=1, source_target_pairs={{0,4},{4,0},{8,12},{12,8},{16,20},{20,16},{24,28},{28,24},{1,5},{5... | collective-permute-start | bytes 884744 | tf_op jit(solution)/shard_map/ppermute | solution.py:44
  23.5 12.4 %collective-permute-start.2 = (bf16[256,768]{1,0:T(8,128)(2,1)}, bf16[256,768]{1,0:T(8,128)(2,1)}, u32[]{:S(2)}, u32[]{:S(2)}) collective-permute-start(bf16[256,768]{1,0:T(8,128)(2,1)} %collective-permute-done.1.refs_3_.refs_4_), channel_id=1, source_target_pairs={{0,1},{1,0},{2,3},{3,2},{4,5},{5,4},{6,7},{7,6},{8,9},{9,8},{10,11... | collective-permute-start | bytes 1179656 | tf_op jit(solution)/shard_map/ppermute | solution.py:44
  41.2 16.4 %collective-permute-start.11 = (bf16[192,768]{1,0:T(8,128)(2,1)}, bf16[192,768]{1,0:T(8,128)(2,1)}, u32[]{:S(2)}, u32[]{:S(2)}) collective-permute-start(bf16[192,768]{1,0:T(8,128)(2,1)} %get-tuple-element.114.refs_8_.refs_12_), channel_id=1, source_target_pairs={{0,2},{1,3},{2,0},{3,1},{4,6},{5,7},{6,4},{7,5},{8,10},{9,11},{10,... | collective-permute-start | bytes 884744 | tf_op jit(solution)/shard_map/ppermute | solution.py:44
  43.2 23.6 %collective-permute-start.13 = (bf16[256,768]{1,0:T(8,128)(2,1)}, bf16[256,768]{1,0:T(8,128)(2,1)}, u32[]{:S(2)}, u32[]{:S(2)}) collective-permute-start(bf16[256,768]{1,0:T(8,128)(2,1)} %get-tuple-element.115), channel_id=1, source_target_pairs={{0,16},{4,20},{8,24},{12,28},{16,0},{20,4},{24,8},{28,12},{1,17},{... | collective-permute-start | bytes 1179656 | tf_op jit(solution)/shard_map/ppermute | solution.py:44
  45.6 21.3 %collective-permute-start.10 = (bf16[192,768]{1,0:T(8,128)(2,1)}, bf16[192,768]{1,0:T(8,128)(2,1)}, u32[]{:S(2)}, u32[]{:S(2)}) collective-permute-start(bf16[192,768]{1,0:T(8,128)(2,1)} %get-tuple-element.114.refs_8_.refs_12_), channel_id=1, source_target_pairs={{0,1},{1,0},{2,3},{3,2},{4,5},{5,4},{6,7},{7,6},{8,9},{9,8},{10,11... | collective-permute-start | bytes 884744 | tf_op jit(solution)/shard_map/ppermute | solution.py:44
  57.6 9.3 %collective-permute-start.12 = (bf16[192,768]{1,0:T(8,128)(2,1)}, bf16[192,768]{1,0:T(8,128)(2,1)}, u32[]{:S(2)}, u32[]{:S(2)}) collective-permute-start(bf16[192,768]{1,0:T(8,128)(2,1)} %collective-permute-done.11.refs_10_.refs_14_), channel_id=1, source_target_pairs={{0,1},{1,0},{2,3},{3,2},{4,5},{5,4},{6,7},{7,6},{8,9},{9,8},{10,11... | collective-permute-start | bytes 884744 | tf_op jit(solution)/shard_map/ppermute | solution.py:44
  58.4 6.6 %collective-permute-start.8 = (bf16[256,192]{1,0:T(8,128)(2,1)}, bf16[256,192]{1,0:T(8,128)(2,1)}, u32[]{:S(2)}, u32[]{:S(2)}) collective-permute-start(bf16[256,192]{1,0:T(8,128)(2,1)} %get-tuple-element.112), channel_id=1, source_target_pairs={{0,2},{1,3},{2,0},{3,1},{4,6},{5,7},{6,4},{7,5},{8,10},{9,11},{10,... | collective-permute-start | bytes 294920 | tf_op jit(solution)/shard_map/ppermute | solution.py:44
  59.9 7.0 %collective-permute-start.9 = (bf16[256,192]{1,0:T(8,128)(2,1)}, bf16[256,192]{1,0:T(8,128)(2,1)}, u32[]{:S(2)}, u32[]{:S(2)}) collective-permute-start(bf16[256,192]{1,0:T(8,128)(2,1)} %get-tuple-element.113), channel_id=1, source_target_pairs={{0,3},{1,2},{2,1},{3,0},{4,7},{5,6},{6,5},{7,4},{8,11},{9,10},{10,... | collective-permute-start | bytes 294920 | tf_op jit(solution)/shard_map/ppermute | solution.py:44
  70.7 21.1 %collective-permute-start.14 = (bf16[256,768]{1,0:T(8,128)(2,1)}, bf16[256,768]{1,0:T(8,128)(2,1)}, u32[]{:S(2)}, u32[]{:S(2)}) collective-permute-start(bf16[256,768]{1,0:T(8,128)(2,1)} %get-tuple-element.117.refs_4_.refs_6_), channel_id=1, source_target_pairs={{0,16},{4,20},{8,24},{12,28},{16,0},{20,4},{24,8},{28,12},{1,17},{... | collective-permute-start | bytes 1179656 | tf_op jit(solution)/shard_map/ppermute | solution.py:44
  77.2 14.6 %collective-permute-start.16 = (bf16[256,768]{1,0:T(8,128)(2,1)}, bf16[256,768]{1,0:T(8,128)(2,1)}, u32[]{:S(2)}, u32[]{:S(2)}) collective-permute-start(bf16[256,768]{1,0:T(8,128)(2,1)} %get-tuple-element.118), channel_id=1, source_target_pairs={{0,4},{4,0},{8,12},{12,8},{16,20},{20,16},{24,28},{28,24},{1,5},{5... | collective-permute-start | bytes 1179656 | tf_op jit(solution)/shard_map/ppermute | solution.py:44
  78.7 19.4 %collective-permute-start.17 = (bf16[256,768]{1,0:T(8,128)(2,1)}, bf16[256,768]{1,0:T(8,128)(2,1)}, u32[]{:S(2)}, u32[]{:S(2)}) collective-permute-start(bf16[256,768]{1,0:T(8,128)(2,1)} %get-tuple-element.119), channel_id=1, source_target_pairs={{0,8},{4,12},{8,0},{12,4},{16,24},{20,28},{24,16},{28,20},{1,9},{5... | collective-permute-start | bytes 1179656 | tf_op jit(solution)/shard_map/ppermute | solution.py:44
  78.7 21.8 %collective-permute-start.22 = (bf16[128,768]{1,0:T(8,128)(2,1)}, bf16[128,768]{1,0:T(8,128)(2,1)}, u32[]{:S(2)}, u32[]{:S(2)}) collective-permute-start(bf16[128,768]{1,0:T(8,128)(2,1)} %get-tuple-element.127), channel_id=1, source_target_pairs={{0,4},{4,0},{8,12},{12,8},{16,20},{20,16},{24,28},{28,24},{1,5},{5... | collective-permute-start | bytes 589832 | tf_op jit(solution)/shard_map/ppermute | solution.py:44
  79.4 22.9 %collective-permute-start.23 = (bf16[128,768]{1,0:T(8,128)(2,1)}, bf16[128,768]{1,0:T(8,128)(2,1)}, u32[]{:S(2)}, u32[]{:S(2)}) collective-permute-start(bf16[128,768]{1,0:T(8,128)(2,1)} %get-tuple-element.128), channel_id=1, source_target_pairs={{0,8},{4,12},{8,0},{12,4},{16,24},{20,28},{24,16},{28,20},{1,9},{5... | collective-permute-start | bytes 589832 | tf_op jit(solution)/shard_map/ppermute | solution.py:44
  91.8 14.5 %collective-permute-start.24 = (bf16[128,768]{1,0:T(8,128)(2,1)}, bf16[128,768]{1,0:T(8,128)(2,1)}, u32[]{:S(2)}, u32[]{:S(2)}) collective-permute-start(bf16[128,768]{1,0:T(8,128)(2,1)} %get-tuple-element.129), channel_id=1, source_target_pairs={{0,12},{4,8},{8,4},{12,0},{16,28},{20,24},{24,20},{28,16},{1,13},{... | collective-permute-start | bytes 589832 | tf_op jit(solution)/shard_map/ppermute | solution.py:44
  91.8 27.3 %collective-permute-start.21 = (bf16[256,768]{1,0:T(8,128)(2,1)}, bf16[256,768]{1,0:T(8,128)(2,1)}, u32[]{:S(2)}, u32[]{:S(2)}) collective-permute-start(bf16[256,768]{1,0:T(8,128)(2,1)} %get-tuple-element.125), channel_id=1, source_target_pairs={{0,12},{4,8},{8,4},{12,0},{16,28},{20,24},{24,20},{28,16},{1,13},{... | collective-permute-start | bytes 1179656 | tf_op jit(solution)/shard_map/ppermute | solution.py:44
  100.2 18.9 %collective-permute-start.18 = (bf16[128,768]{1,0:T(8,128)(2,1)}, bf16[128,768]{1,0:T(8,128)(2,1)}, u32[]{:S(2)}, u32[]{:S(2)}) collective-permute-start(bf16[128,768]{1,0:T(8,128)(2,1)} %get-tuple-element.121), channel_id=1, source_target_pairs={{0,4},{4,0},{8,12},{12,8},{16,20},{20,16},{24,28},{28,24},{1,5},{5... | collective-permute-start | bytes 589832 | tf_op jit(solution)/shard_map/ppermute | solution.py:44
  100.5 18.7 %collective-permute-start.19 = (bf16[128,768]{1,0:T(8,128)(2,1)}, bf16[128,768]{1,0:T(8,128)(2,1)}, u32[]{:S(2)}, u32[]{:S(2)}) collective-permute-start(bf16[128,768]{1,0:T(8,128)(2,1)} %get-tuple-element.122), channel_id=1, source_target_pairs={{0,8},{4,12},{8,0},{12,4},{16,24},{20,28},{24,16},{28,20},{1,9},{5... | collective-permute-start | bytes 589832 | tf_op jit(solution)/shard_map/ppermute | solution.py:44
  102.3 19.5 %collective-permute-start.20 = (bf16[128,768]{1,0:T(8,128)(2,1)}, bf16[128,768]{1,0:T(8,128)(2,1)}, u32[]{:S(2)}, u32[]{:S(2)}) collective-permute-start(bf16[128,768]{1,0:T(8,128)(2,1)} %get-tuple-element.123), channel_id=1, source_target_pairs={{0,12},{4,8},{8,4},{12,0},{16,28},{20,24},{24,20},{28,16},{1,13},{... | collective-permute-start | bytes 589832 | tf_op jit(solution)/shard_map/ppermute | solution.py:44
  139.7 15.5 %collective-permute-start.28 = (bf16[128,896]{1,0:T(8,128)(2,1)}, bf16[128,896]{1,0:T(8,128)(2,1)}, u32[]{:S(2)}, u32[]{:S(2)}) collective-permute-start(bf16[128,896]{1,0:T(8,128)(2,1)} %get-tuple-element.141), channel_id=1, source_target_pairs={{0,4},{4,0},{8,12},{12,8},{16,20},{20,16},{24,28},{28,24},{1,5},{5... | collective-permute-start | bytes 688136 | tf_op jit(solution)/shard_map/ppermute | solution.py:44
  141.5 13.7 %collective-permute-start.29 = (bf16[128,896]{1,0:T(8,128)(2,1)}, bf16[128,896]{1,0:T(8,128)(2,1)}, u32[]{:S(2)}, u32[]{:S(2)}) collective-permute-start(bf16[128,896]{1,0:T(8,128)(2,1)} %get-tuple-element.142), channel_id=1, source_target_pairs={{0,8},{4,12},{8,0},{12,4},{16,24},{20,28},{24,16},{28,20},{1,9},{5... | collective-permute-start | bytes 688136 | tf_op jit(solution)/shard_map/ppermute | solution.py:44
  141.6 13.7 %collective-permute-start.30 = (bf16[128,896]{1,0:T(8,128)(2,1)}, bf16[128,896]{1,0:T(8,128)(2,1)}, u32[]{:S(2)}, u32[]{:S(2)}) collective-permute-start(bf16[128,896]{1,0:T(8,128)(2,1)} %get-tuple-element.143), channel_id=1, source_target_pairs={{0,12},{4,8},{8,4},{12,0},{16,28},{20,24},{24,20},{28,16},{1,13},{... | collective-permute-start | bytes 688136 | tf_op jit(solution)/shard_map/ppermute | solution.py:44
  158.0 23.1 %collective-permute-start.31 = (bf16[128,896]{1,0:T(8,128)(2,1)}, bf16[128,896]{1,0:T(8,128)(2,1)}, u32[]{:S(2)}, u32[]{:S(2)}) collective-permute-start(bf16[128,896]{1,0:T(8,128)(2,1)} %get-tuple-element.147), channel_id=1, source_target_pairs={{0,4},{4,0},{8,12},{12,8},{16,20},{20,16},{24,28},{28,24},{1,5},{5... | collective-permute-start | bytes 688136 | tf_op jit(solution)/shard_map/ppermute | solution.py:44
  159.8 21.4 %collective-permute-start.32 = (bf16[128,896]{1,0:T(8,128)(2,1)}, bf16[128,896]{1,0:T(8,128)(2,1)}, u32[]{:S(2)}, u32[]{:S(2)}) collective-permute-start(bf16[128,896]{1,0:T(8,128)(2,1)} %get-tuple-element.148), channel_id=1, source_target_pairs={{0,8},{4,12},{8,0},{12,4},{16,24},{20,28},{24,16},{28,20},{1,9},{5... | collective-permute-start | bytes 688136 | tf_op jit(solution)/shard_map/ppermute | solution.py:44
  159.8 21.4 %collective-permute-start.33 = (bf16[128,896]{1,0:T(8,128)(2,1)}, bf16[128,896]{1,0:T(8,128)(2,1)}, u32[]{:S(2)}, u32[]{:S(2)}) collective-permute-start(bf16[128,896]{1,0:T(8,128)(2,1)} %get-tuple-element.149), channel_id=1, source_target_pairs={{0,12},{4,8},{8,4},{12,0},{16,28},{20,24},{24,20},{28,16},{1,13},{... | collective-permute-start | bytes 688136 | tf_op jit(solution)/shard_map/ppermute | solution.py:44
  161.5 20.8 %collective-permute-start.34 = (bf16[256,896]{1,0:T(8,128)(2,1)}, bf16[256,896]{1,0:T(8,128)(2,1)}, u32[]{:S(2)}, u32[]{:S(2)}) collective-permute-start(bf16[256,896]{1,0:T(8,128)(2,1)} %get-tuple-element.150), channel_id=1, source_target_pairs={{0,16},{4,20},{8,24},{12,28},{16,0},{20,4},{24,8},{28,12},{1,17},{... | collective-permute-start | bytes 1376264 | tf_op jit(solution)/shard_map/ppermute | solution.py:44
  189.2 9.2 %collective-permute-start.38 = (bf16[3072,768]{1,0:T(8,128)(2,1)}, bf16[3072,768]{1,0:T(8,128)(2,1)}, u32[]{:S(2)}, u32[]{:S(2)}) collective-permute-start(bf16[3072,768]{1,0:T(8,128)(2,1)} %get-tuple-element.164), channel_id=1, source_target_pairs={{0,1},{1,0},{2,3},{3,2},{4,5},{5,4},{6,7},{7,6},{8,9},{9,8},{10,11... | collective-permute-start | bytes 14155784 | tf_op jit(solution)/shard_map/ppermute | solution.py:44
  189.2 9.1 %collective-permute-start.39 = (bf16[384,768]{1,0:T(8,128)(2,1)}, bf16[384,768]{1,0:T(8,128)(2,1)}, u32[]{:S(2)}, u32[]{:S(2)}) collective-permute-start(bf16[384,768]{1,0:T(8,128)(2,1)} %get-tuple-element.166), channel_id=1, source_target_pairs={{0,1},{1,0},{2,3},{3,2},{4,5},{5,4},{6,7},{7,6},{8,9},{9,8},{10,11... | collective-permute-start | bytes 1769480 | tf_op jit(solution)/shard_map/ppermute | solution.py:44
  189.7 6.7 %collective-permute-start.36 = (bf16[256,192]{1,0:T(8,128)(2,1)}, bf16[256,192]{1,0:T(8,128)(2,1)}, u32[]{:S(2)}, u32[]{:S(2)}) collective-permute-start(bf16[256,192]{1,0:T(8,128)(2,1)} %get-tuple-element.162), channel_id=1, source_target_pairs={{0,2},{1,3},{2,0},{3,1},{4,6},{5,7},{6,4},{7,5},{8,10},{9,11},{10,... | collective-permute-start | bytes 294920 | tf_op jit(solution)/shard_map/ppermute | solution.py:44
  191.2 6.2 %collective-permute-start.37 = (bf16[256,192]{1,0:T(8,128)(2,1)}, bf16[256,192]{1,0:T(8,128)(2,1)}, u32[]{:S(2)}, u32[]{:S(2)}) collective-permute-start(bf16[256,192]{1,0:T(8,128)(2,1)} %get-tuple-element.163), channel_id=1, source_target_pairs={{0,3},{1,2},{2,1},{3,0},{4,7},{5,6},{6,5},{7,4},{8,11},{9,10},{10,... | collective-permute-start | bytes 294920 | tf_op jit(solution)/shard_map/ppermute | solution.py:44
  203.2 23.3 %collective-permute-start.40 = (bf16[448,768]{1,0:T(8,128)(2,1)}, bf16[448,768]{1,0:T(8,128)(2,1)}, u32[]{:S(2)}, u32[]{:S(2)}) collective-permute-start(bf16[448,768]{1,0:T(8,128)(2,1)} %get-tuple-element.168.refs_11_), channel_id=1, source_target_pairs={{0,2},{1,3},{2,0},{3,1},{4,6},{5,7},{6,4},{7,5},{8,10},{9,11},{10,... | collective-permute-start | bytes 2064392 | tf_op jit(solution)/shard_map/ppermute | solution.py:44
  204.7 21.8 %collective-permute-start.25 = (bf16[256,768]{1,0:T(8,128)(2,1)}, bf16[256,768]{1,0:T(8,128)(2,1)}, u32[]{:S(2)}, u32[]{:S(2)}) collective-permute-start(bf16[256,768]{1,0:T(8,128)(2,1)} %get-tuple-element.132), channel_id=1, source_target_pairs={{0,4},{4,0},{8,12},{12,8},{16,20},{20,16},{24,28},{28,24},{1,5},{5... | collective-permute-start | bytes 1179656 | tf_op jit(solution)/shard_map/ppermute | solution.py:44
  206.4 20.1 %collective-permute-start.26 = (bf16[256,768]{1,0:T(8,128)(2,1)}, bf16[256,768]{1,0:T(8,128)(2,1)}, u32[]{:S(2)}, u32[]{:S(2)}) collective-permute-start(bf16[256,768]{1,0:T(8,128)(2,1)} %get-tuple-element.133), channel_id=1, source_target_pairs={{0,8},{4,12},{8,0},{12,4},{16,24},{20,28},{24,16},{28,20},{1,9},{5... | collective-permute-start | bytes 1179656 | tf_op jit(solution)/shard_map/ppermute | solution.py:44
  207.2 19.4 %collective-permute-start.27 = (bf16[256,768]{1,0:T(8,128)(2,1)}, bf16[256,768]{1,0:T(8,128)(2,1)}, u32[]{:S(2)}, u32[]{:S(2)}) collective-permute-start(bf16[256,768]{1,0:T(8,128)(2,1)} %get-tuple-element.134), channel_id=1, source_target_pairs={{0,12},{4,8},{8,4},{12,0},{16,28},{20,24},{24,20},{28,16},{1,13},{... | collective-permute-start | bytes 1179656 | tf_op jit(solution)/shard_map/ppermute | solution.py:44
  209.9 57.6 %collective-permute-start.49 = (bf16[768,768]{1,0:T(8,128)(2,1)}, bf16[768,768]{1,0:T(8,128)(2,1)}, u32[]{:S(2)}, u32[]{:S(2)}) collective-permute-start(bf16[768,768]{1,0:T(8,128)(2,1)} %get-tuple-element.194), channel_id=1, source_target_pairs={{0,2},{1,3},{2,0},{3,1},{4,6},{5,7},{6,4},{7,5},{8,10},{9,11},{10,... | collective-permute-start | bytes 3538952 | tf_op jit(solution)/shard_map/ppermute | solution.py:44
  233.7 21.7 %collective-permute-start.44 = (bf16[512,768]{1,0:T(8,128)(2,1)}, bf16[512,768]{1,0:T(8,128)(2,1)}, u32[]{:S(2)}, u32[]{:S(2)}) collective-permute-start(bf16[512,768]{1,0:T(8,128)(2,1)} %get-tuple-element.184), channel_id=1, source_target_pairs={{0,1},{1,0},{2,3},{3,2},{4,5},{5,4},{6,7},{7,6},{8,9},{9,8},{10,11... | collective-permute-start | bytes 2359304 | tf_op jit(solution)/shard_map/ppermute | solution.py:44
  233.8 10.8 %collective-permute-start.41 = (bf16[224,768]{1,0:T(8,128)(2,1)}, bf16[224,768]{1,0:T(8,128)(2,1)}, u32[]{:S(2)}, u32[]{:S(2)}) collective-permute-start(bf16[224,768]{1,0:T(8,128)(2,1)} %get-tuple-element.180), channel_id=1, source_target_pairs={{0,4},{4,0},{8,12},{12,8},{16,20},{20,16},{24,28},{28,24},{1,5},{5... | collective-permute-start | bytes 1032200 | tf_op jit(solution)/shard_map/ppermute | solution.py:44
  235.5 32.0 %collective-permute-start.48 = (bf16[512,768]{1,0:T(8,128)(2,1)}, bf16[512,768]{1,0:T(8,128)(2,1)}, u32[]{:S(2)}, u32[]{:S(2)}) collective-permute-start(bf16[512,768]{1,0:T(8,128)(2,1)} %get-tuple-element.193), channel_id=1, source_target_pairs={{0,2},{1,3},{2,0},{3,1},{4,6},{5,7},{6,4},{7,5},{8,10},{9,11},{10,... | collective-permute-start | bytes 2359304 | tf_op jit(solution)/shard_map/ppermute | solution.py:44
  237.0 10.2 %collective-permute-start.42 = (bf16[224,768]{1,0:T(8,128)(2,1)}, bf16[224,768]{1,0:T(8,128)(2,1)}, u32[]{:S(2)}, u32[]{:S(2)}) collective-permute-start(bf16[224,768]{1,0:T(8,128)(2,1)} %get-tuple-element.181), channel_id=1, source_target_pairs={{0,8},{4,12},{8,0},{12,4},{16,24},{20,28},{24,16},{28,20},{1,9},{5... | collective-permute-start | bytes 1032200 | tf_op jit(solution)/shard_map/ppermute | solution.py:44
  244.6 10.8 %collective-permute-start.43 = (bf16[224,768]{1,0:T(8,128)(2,1)}, bf16[224,768]{1,0:T(8,128)(2,1)}, u32[]{:S(2)}, u32[]{:S(2)}) collective-permute-start(bf16[224,768]{1,0:T(8,128)(2,1)} %get-tuple-element.182), channel_id=1, source_target_pairs={{0,12},{4,8},{8,4},{12,0},{16,28},{20,24},{24,20},{28,16},{1,13},{... | collective-permute-start | bytes 1032200 | tf_op jit(solution)/shard_map/ppermute | solution.py:44
  257.7 19.7 %collective-permute-start.47 = (bf16[128,768]{1,0:T(8,128)(2,1)}, bf16[128,768]{1,0:T(8,128)(2,1)}, u32[]{:S(2)}, u32[]{:S(2)}) collective-permute-start(bf16[128,768]{1,0:T(8,128)(2,1)} %get-tuple-element.192), channel_id=1, source_target_pairs={{0,16},{4,20},{8,24},{12,28},{16,0},{20,4},{24,8},{28,12},{1,17},{... | collective-permute-start | bytes 589832 | tf_op jit(solution)/shard_map/ppermute | solution.py:44
  262.3 23.5 %collective-permute-start.45 = (bf16[256,768]{1,0:T(8,128)(2,1)}, bf16[256,768]{1,0:T(8,128)(2,1)}, u32[]{:S(2)}, u32[]{:S(2)}) collective-permute-start(bf16[256,768]{1,0:T(8,128)(2,1)} %get-tuple-element.187), channel_id=1, source_target_pairs={{0,16},{4,20},{8,24},{12,28},{16,0},{20,4},{24,8},{28,12},{1,17},{... | collective-permute-start | bytes 1179656 | tf_op jit(solution)/shard_map/ppermute | solution.py:44
  266.0 11.4 %collective-permute-start.46 = (bf16[256,768]{1,0:T(8,128)(2,1)}, bf16[256,768]{1,0:T(8,128)(2,1)}, u32[]{:S(2)}, u32[]{:S(2)}) collective-permute-start(bf16[256,768]{1,0:T(8,128)(2,1)} %add_convert_fusion), channel_id=1, source_target_pairs={{0,2},{1,3},{2,0},{3,1},{4,6},{5,7},{6,4},{7,5},{8,10},{9,11},{10,... | collective-permute-start | bytes 1179656 | tf_op jit(solution)/shard_map/ppermute | solution.py:44
  (7 other events, 31.4 us)

commit v11 on v10

--- a/solution.py
+++ b/solution.py
@@ -957,7 +957,7 @@
     return upper, (values - upper.astype(f32)).astype(bf16)
 
 
-def fold_weights(base, arrived, small, after):
+def fold_weights(base, arrived, small, after, through):
     part, width, extra = base.shape[0] // 2, base.shape[1], small.shape[0]
 
     def kernel(base_ref, one_ref, two_ref, three_ref, small_ref, own_ref, far_ref, half_ref):
@@ -987,6 +987,7 @@
             shape((extra, width), f32),
         ],
         after=after,
+        through=through,
     )
 
 
@@ -1215,7 +1216,7 @@
     near_o, near_w = swap(near_o, "mp", 1), swap(near_w, "mp", 1)
     piece = w_in.shape[2] // members
     far_first, far_next, far_last = far_sums(
-        near_w, base_w, near_o, base_o, [rows, piece, 2 * piece], grad_in[2:]
+        near_w, base_w, near_o, base_o, [2 * rows, piece, 2 * piece], grad_in[2:]
     )
 
     *proj_grads, line_grad = attend_back(
@@ -1231,7 +1232,6 @@
         [far_first],
     )
     far_first = swap(far_first, "mp", 2)
-    far_next = swap(far_next, "mp", 2)
     far_last = swap(far_last, "mp", 2)
     near, base, base_far, small, *weight_sums = input_grads(
         place,
@@ -1250,19 +1250,21 @@
         buckets_all,
         result_in[1:],
     )
-    far_parts = [(far_first, span), (far_next, 0), (far_last, 0)]
     near = swap(near, "mp", 1)
     far_normed = swap((base_far + near[rows:].astype(f32)).astype(bf16), "mp", 2)
     if few:
         arrived_sums = [swap(weight_sums[r], "dp", r) for r in (1, 2, 3)]
-        own_sum, far_part, small = fold_weights(
-            weight_sums[0], arrived_sums, small, [near]
+        own_sum, far_part, small, far_next = fold_weights(
+            weight_sums[0], arrived_sums, small, [near], [far_next]
         )
+        far_next = swap(far_next, "mp", 2)
         own_result, far_result = from_slots(
             "result_from_slots", result_in, slots, size, [f32, bf16], after=[own_sum]
         )
         far_result = swap(far_result, "dp", 4)
-        w_in_grad, w_out_grad = add_up(base_w, near_w, far_parts, [own_result])
+        w_in_grad, w_out_grad = add_up(
+            base_w, near_w, [(far_first, span), (far_next, 0), (far_last, 0)], [own_result]
+        )
         *weight_grads, small = split_weights(
             own_sum, swap(far_part, "dp", 4), small, span, [w_in_grad, far_normed]
         )
@@ -1272,7 +1274,10 @@
             joined_grad, None, sum_over(small, "dp"), span, []
         )
         (own_result,) = from_slots("result_from_slots", result_in, slots, size, [f32])
-        w_in_grad, w_out_grad = add_up(base_w, near_w, far_parts, [])
+        far_next = swap(far_next, "mp", 2)
+        w_in_grad, w_out_grad = add_up(
+            base_w, near_w, [(far_first, span), (far_next, 0), (far_last, 0)], []
+        )
     small = sum_over(small, "mp")
     normed_grad = base + near[:rows].astype(f32) + far_normed.astype(f32)
     resid = tokens.astype(f32)

time: 292 us -> 296 us (1.014)
  waiting for transfers between devices: 64.2 us -> 69.8 us
    ppermute x52, waiting for transfers between devices: 64.2 us -> 69.8 us  [swap(): return lax.ppermute(values, axis, [(i, i ^ step) for i in range(count)])]
  transfers between devices with their start and end apart: 52 -> 52, of which waited for: 18 -> 20; matrix products, arithmetic and copies ran while one was open for 10% -> 10% of each run, Pallas kernels for 36% -> 33%
where the time goes in v11:
time: 296 us; the launch traced here: 295 us
  Pallas kernels  142 us (48%)
  waiting for transfers between devices  69.8 us (24%)
  starting transfers between devices  50.6 us (17%)
  local copies, waits for them, and re-layouts  15 us (5%)
  other arithmetic  14.7 us (5%)
    ppermute x52, waiting for transfers between devices, swap(): return lax.ppermute(values, axis, [(i, i ^ step) for i in range(count)])  69.8 us
    pallas_call x14, Pallas kernels, call(): pl.pallas_call(body, name=name, grid=(1,), in_specs=in_specs + [pl.BlockS...  69.3 us
    ppermute x52, starting transfers between devices, swap(): return lax.ppermute(values, axis, [(i, i ^ step) for i in range(count)])  50.6 us
    pallas_call x1, Pallas kernels, expert_weight_grads(): pl.pallas_call(kernel, name='expert_weight_grads', grid_spec=pltpu.Prefet...  19 us
    pallas_call x1, Pallas kernels, run_experts(): pl.pallas_call(kernel, name=name, grid=(units // piece,), in_specs=[pl.Bl...  17.9 us
    pallas_call x1, Pallas kernels, experts_forward(): pl.pallas_call(kernel, name='experts_forward', grid=(units // piece,), in...  12.8 us
    pallas_call x1, Pallas kernels, experts_backward(): pl.pallas_call(kernel, name='experts_backward', grid=(units // piece,), i...  12 us
    pallas_call x1, Pallas kernels, add_up(): pl.pallas_call(kernel, name='add_up', grid=(1,), in_specs=specs + [pl.Blo...  6.27 us
  transfers between devices with their start and end apart: 52, of which 20 were waited for; matrix products, arithmetic and copies ran while one was open for 10% of the time, Pallas kernels for 33%

profile of v11, /device:TPU:0, one launch (start us, length us, event | category | flops | bytes accessed | tf_op | source)
XLA Modules:
  0.0 295.1 jit_solution(8014437060060513121)
XLA Ops:
  0.6 3.0 %collective-permute-start.1 = (bf16[256,768]{1,0:T(8,128)(2,1)}, bf16[256,768]{1,0:T(8,128)(2,1)}, u32[]{:S(2)}, u32[]{:S(2)}) collective-permute-start(bf16[256,768]{1,0:T(8,128)(2,1)} %refs_0_.4), channel_id=1, source_target_pairs={{0,2},{1,3},{2,0},{3,1},{4,6},{5,7},{6,4},{7,5},{8,10},{9,11},{10,... | collective-permute-start | bytes 1179656 | tf_op jit(solution)/shard_map/ppermute | solution.py:44
  3.7 2.6 collective-permute-start.15
  10.4 7.9 %collective-permute-done.3.refs_1_ = bf16[96,768]{1,0:T(8,128)(2,1)} collective-permute-done((bf16[96,768]{1,0:T(8,128)(2,1)}, bf16[96,768]{1,0:T(8,128)(2,1)}, u32[]{:S(2)}, u32[]{:S(2)}) %collective-permute-start.3) | collective-permute-done | bytes 147488 | tf_op jit(solution)/shard_map/ppermute | solution.py:44
  20.0 3.0 collective-permute-start.5
  30.5 1.8 copy.38.refs_10_
  32.3 1.7 copy.35.refs_12_.refs_4_
  36.0 5.2 %project.1 = (bf16[1024,768]{1,0:T(8,128)(2,1)}, bf16[1024,192]{1,0:T(8,128)(2,1)}, bf16[1024,192]{1,0:T(8,128)(2,1)}, bf16[1024,192]{1,0:T(8,128)(2,1)}, bf16[7...) custom-call(s32[2]{0:T(128)} %pad_add_fusion.2.refs_0_.me_ref.place_, ...), custom_call_target="tpu_custom_call", output_to_operand_aliasing={{8}: (10, {})} | custom-call | flops 10000000 | bytes 10000 | tf_op jit(solution)/shard_map/project/pallas_call | solution.py:69
  45.6 11.5 %attend.1 = (bf16[256,192]{1,0:T(8,128)(2,1)}, bf16[256,192]{1,0:T(8,128)(2,1)}, bf16[256,192]{1,0:T(8,128)(2,1)}, bf16[256,192]{1,0:T(8,128)(2,1)}) custom-call(s32[2]{0:T(128)} %pad_add_fusion.2.refs_0_.me_ref.place_ref, bf16[1024,192]{1,0:T(8,128)(2,1)} %get-tuple-element.108.refs_1_, bf16[1024,192]{1,0:T(8,128)(2,1)} %get-tuple-element.109.refs_2_, ...), custom_call_target="tpu_custom_call" | custom-call | flops 10000000 | bytes 10000 | tf_op jit(solution)/shard_map/attend/pallas_call | solution.py:69
  61.7 3.3 %collective-permute-done.8.refs_6_.refs_18_ = bf16[256,192]{1,0:T(8,128)(2,1)} collective-permute-done((bf16[256,192]{1,0:T(8,128)(2,1)}, bf16[256,192]{1,0:T(8,128)(2,1)}, u32[]{:S(2)}, u32[]{:S(2)}) %collective-permute-start.8) | collective-permute-done | bytes 98336 | tf_op jit(solution)/shard_map/ppermute | solution.py:44
  65.0 1.9 collective-permute-done.9.refs_7_.refs_19_
  66.9 3.9 %middle.1 = (f32[256,768]{1,0:T(8,128)}, bf16[256,768]{1,0:T(8,128)(2,1)}, f32[256,128]{1,0:T(8,128)}, bf16[128,768]{1,0:T(8,128)(2,1)}, bf16[128,768]{1,0:T(8,1...) custom-call(bf16[256,768]{1,0:T(8,128)(2,1)} %refs_0_.4, f32[1,768]{1,0:T(1,128)} %reshape.191.refs_15_.refs_1_.refs_4_, ...), custom_call_target="tpu_custom_call" | custom-call | flops 10000000 | bytes 10000 | tf_op jit(solution)/shard_map/middle/pallas_call | solution.py:69
  70.7 2.3 collective-permute-start.14
  74.4 2.8 grads_to_slots.1
  79.4 1.8 collective-permute-start.23
  81.2 10.6 %collective-permute-done.14.refs_0_ = bf16[256,768]{1,0:T(8,128)(2,1)} collective-permute-done((bf16[256,768]{1,0:T(8,128)(2,1)}, bf16[256,768]{1,0:T(8,128)(2,1)}, u32[]{:S(2)}, u32[]{:S(2)}) %collective-permute-start.14) | collective-permute-done | bytes 393248 | tf_op jit(solution)/shard_map/ppermute | solution.py:44
  91.8 2.9 collective-permute-start.21
  94.7 3.4 %collective-permute-done.17.refs_3_.refs_6_.refs_2_ = bf16[256,768]{1,0:T(8,128)(2,1)} collective-permute-done((bf16[256,768]{1,0:T(8,128)(2,1)}, bf16[256,768]{1,0:T(8,128)(2,1)}, u32[]{:S(2)}, u32[]{:S(2)}) %collective-permute-start.17) | collective-permute-done | bytes 393248 | tf_op jit(solution)/shard_map/ppermute | solution.py:44
  98.1 2.1 far_to_slots.1
  100.5 1.8 collective-permute-done.23.refs_2_
  103.7 2.6 collective-permute-done.24.refs_3_
  106.3 12.8 %experts_forward.1 = (bf16[512,3072]{1,0:T(8,128)(2,1)}, bf16[512,3072]{1,0:T(8,128)(2,1)}, bf16[512,768]{1,0:T(8,128)(2,1)}, bf16[512,768]{1,0:T(8,128)(2,1)}, ...) custom-call(s32[2]{0:T(128)} %pad_add_fusion.2.refs_0_.me_ref.place_ref, bf16[768,3072]{1,0:T(8,128)(2,1)} %bitcast.45, ...), custom_call_target="tpu_custom_call" | custom-call | flops 20000000000 | bytes 10000000 | tf_op jit(solution)/shard_map/experts_forward/pallas_call | solution.py:460
  119.2 2.6 collective-permute-done.20.refs_3_
  121.8 17.9 %run_experts.1 = (bf16[128,896]{1,0:T(8,128)(2,1)}, bf16[128,896]{1,0:T(8,128)(2,1)}, bf16[128,896]{1,0:T(8,128)(2,1)}, bf16[128,896]{1,0:T(8,128)(2,1)}, bf16[2...) custom-call(s32[2]{0:T(128)} %pad_add_fusion.2.refs_0_.me_ref.place_, ...), custom_call_target="tpu_custom_call" | custom-call | flops 10000000 | bytes 10000 | tf_op jit(solution)/shard_map/run_experts/pallas_call | solution.py:614
  139.7 1.8 collective-permute-start.28
  141.6 1.7 collective-permute-start.30
  143.3 12.0 %experts_backward.1 = (bf16[128,896]{1,0:T(8,128)(2,1)}, bf16[128,896]{1,0:T(8,128)(2,1)}, bf16[128,896]{1,0:T(8,128)(2,1)}, bf16[128,896]{1,0:T(8,128)(2,1)}, b...) custom-call(s32[2]{0:T(128)} %pad_add_fusion.2.refs_0_.me_ref.place_ref, bf16[768,3072]{1,0:T(8,128)(2,1)} %bitcast.47, ...), custom_call_target="tpu_custom_call" | custom-call | flops 20000000000 | bytes 10000000 | tf_op jit(solution)/shard_map/experts_backward/pallas_call | solution.py:519
  155.3 2.7 back_from_slots.1
  158.0 1.8 collective-permute-start.31
  159.8 1.7 collective-permute-start.33
  162.1 19.0 %expert_weight_grads.1 = (bf16[3072,768]{1,0:T(8,128)(2,1)}, f32[3072,768]{1,0:T(8,128)}) custom-call(s32[2]{0:T(128)} %pad_add_fusion.2.refs_0_.me_ref.place_ref, bf16[512,768]{1,0:T(8,128)(2,1)} %get-tuple-element.152.refs_0_, bf16[512,768]{1,0:T(8,128)(2,1)} %get-tuple-element.153.refs_1_, bf16[512,3072]{1,0:T(8,128)(2,1)} %get-tuple-element.154.refs_2_, ...), custom_call_target="tpu_custom_call" | custom-call | flops 20000000000 | bytes 10000000 | tf_op jit(solution)/shard_map/expert_weight_grads/pallas_call | solution.py:765
  182.3 6.9 %home.1 = (bf16[256,192]{1,0:T(8,128)(2,1)}, bf16[256,192]{1,0:T(8,128)(2,1)}, bf16[256,192]{1,0:T(8,128)(2,1)}, bf16[256,192]{1,0:T(8,128)(2,1)}, f32[256,768]{...) custom-call(s32[8,256]{1,0:T(8,128)} %pad.24.refs_11_.refs_3_.refs_1, ...), custom_call_target="tpu_custom_call", output_to_operand_aliasing={{9}: (20, {})} | custom-call | flops 10000000 | bytes 10000 | tf_op jit(solution)/shard_map/home/pallas_call | solution.py:69
  191.2 5.2 %collective-permute-done.36.refs_0_.refs_9_ = bf16[256,192]{1,0:T(8,128)(2,1)} collective-permute-done((bf16[256,192]{1,0:T(8,128)(2,1)}, bf16[256,192]{1,0:T(8,128)(2,1)}, u32[]{:S(2)}, u32[]{:S(2)}) %collective-permute-start.36) | collective-permute-done | bytes 98336 | tf_op jit(solution)/shard_map/ppermute | solution.py:44
  198.3 4.8 %far_sums.1 = (bf16[704,768]{1,0:T(8,128)(2,1)}, bf16[256,768]{1,0:T(8,128)(2,1)}, bf16[768,768]{1,0:T(8,128)(2,1)}) custom-call(bf16[3072,768]{1,0:T(8,128)(2,1)} %collective-permute-done.38.near_in.near_out.in_near.out_near, bf16[3072,768]{1,0:T(8,128)(2,1)} %collective-permute-done.38.near_in.near_out.in_near.out_near, ...), custom_call_target="tpu_custom_call" | custom-call | flops 10000000 | bytes 10000 | tf_op jit(solution)/shard_map/far_sums/pallas_call | solution.py:810
  209.8 16.1 %attend_back.1 = (bf16[1024,192]{1,0:T(8,128)(2,1)}, bf16[1024,192]{1,0:T(8,128)(2,1)}, bf16[1024,192]{1,0:T(8,128)(2,1)}, f32[8,640]{1,0:T(8,128)}) custom-call(s32[2]{0:T(128)} %pad_add_fusion.2.refs_0_.me_ref.place_ref, bf16[1024,192]{1,0:T(8,128)(2,1)} %get-tuple-element.108.refs_1_, bf16[1024,192]{1,0:T(8,128)(2,1)} %get-tuple-element.109.refs_2_, ...), custom_call_target="tpu_custom_call" | custom-call | flops 10000000 | bytes 10000 | tf_op jit(solution)/shard_map/attend_back/pallas_call | solution.py:69
  225.9 3.4 %collective-permute-done.40.refs_15_.refs_0_ = bf16[704,768]{1,0:T(8,128)(2,1)} collective-permute-done((bf16[704,768]{1,0:T(8,128)(2,1)}, bf16[704,768]{1,0:T(8,128)(2,1)}, u32[]{:S(2)}, u32[]{:S(2)}) %collective-permute-start.40) | collective-permute-done | bytes 1081376 | tf_op jit(solution)/shard_map/ppermute | solution.py:44
  229.4 7.2 %input_grads.1 = (bf16[512,768]{1,0:T(8,128)(2,1)}, f32[256,768]{1,0:T(8,128)}, f32[256,768]{1,0:T(8,128)}, f32[16,768]{1,0:T(8,128)}, f32[192,768]{1,0:T(8,128)...) custom-call(s32[2]{0:T(128)} %pad_add_fusion.2.refs_0_.me_ref.place_ref, ...), custom_call_target="tpu_custom_call" | custom-call | flops 10000000 | bytes 10000 | tf_op jit(solution)/shard_map/input_grads/pallas_call | solution.py:69
  241.7 7.0 %collective-permute-done.41.refs_1_ = bf16[224,768]{1,0:T(8,128)(2,1)} collective-permute-done((bf16[224,768]{1,0:T(8,128)(2,1)}, bf16[224,768]{1,0:T(8,128)(2,1)}, u32[]{:S(2)}, u32[]{:S(2)}) %collective-permute-start.41) | collective-permute-done | bytes 344096 | tf_op jit(solution)/shard_map/ppermute | solution.py:44
  248.7 2.5 collective-permute-done.42.refs_2_
  251.1 6.1 %collective-permute-done.43.refs_3_ = bf16[224,768]{1,0:T(8,128)(2,1)} collective-permute-done((bf16[224,768]{1,0:T(8,128)(2,1)}, bf16[224,768]{1,0:T(8,128)(2,1)}, u32[]{:S(2)}, u32[]{:S(2)}) %collective-permute-start.43) | collective-permute-done | bytes 344096 | tf_op jit(solution)/shard_map/ppermute | solution.py:44
  257.2 2.2 fold_weights.1
  261.3 3.4 %result_from_slots.1 = (f32[256,768]{1,0:T(8,128)}, bf16[256,768]{1,0:T(8,128)(2,1)}) custom-call(bf16[256,768]{1,0:T(8,128)(2,1)} %get-tuple-element.132.refs_0_, bf16[256,768]{1,0:T(8,128)(2,1)} %collective-permute-done.25.refs_16_.refs_1_, bf16[256,768]{1,0:T(8,128)(2,1)} %collective-permute-done.26.refs_17_.refs_2_, ...), custom_call_target="tpu_custom_call" | custom-call | flops 10000000 | bytes 10000 | tf_op jit(solution)/shard_map/result_from_slots/pallas_call | solution.py:69
  266.3 2.0 add_convert_fusion
  269.8 4.4 %collective-permute-done.48.refs_1_ = bf16[256,768]{1,0:T(8,128)(2,1)} collective-permute-done((bf16[256,768]{1,0:T(8,128)(2,1)}, bf16[256,768]{1,0:T(8,128)(2,1)}, u32[]{:S(2)}, u32[]{:S(2)}) %collective-permute-start.48) | collective-permute-done | bytes 393248 | tf_op jit(solution)/shard_map/ppermute | solution.py:44
  274.2 6.3 %add_up.1 = (f32[768,768]{1,0:T(8,128)}, f32[768,768]{1,0:T(8,128)}) custom-call(f32[3072,768]{1,0:T(8,128)} %get-tuple-element.166.base_in.base_out.in_base.out_base, bf16[3072,768]{1,0:T(8,128)(2,1)} %collective-permute-done.38.near_in.near_out.in_near.out_near, f32[3072,768]{1,0:T(8,128)} %get-tuple-element.166.base_in.base_out.in_base.out_base, ...), custom_call_target="tpu_custom_call" | custom-call | flops 20000000000 | bytes 10000000 | tf_op jit(solution)/shard_map/add_up/pallas_call | solution.py:943
  282.2 1.9 split_weights.1
  284.2 1.9 fusion
  286.1 2.8 fusion.5
  290.5 1.9 add_convert_fusion.1
  (120 shorter events, 58.2 us)
Async XLA Ops:
  0.6 17.7 %collective-permute-start.1 = (bf16[256,768]{1,0:T(8,128)(2,1)}, bf16[256,768]{1,0:T(8,128)(2,1)}, u32[]{:S(2)}, u32[]{:S(2)}) collective-permute-start(bf16[256,768]{1,0:T(8,128)(2,1)} %refs_0_.4), channel_id=1, source_target_pairs={{0,2},{1,3},{2,0},{3,1},{4,6},{5,7},{6,4},{7,5},{8,10},{9,11},{10,... | collective-permute-start | bytes 1179656 | tf_op jit(solution)/shard_map/ppermute | solution.py:44
  3.7 14.6 %collective-permute-start = (bf16[256,768]{1,0:T(8,128)(2,1)}, bf16[256,768]{1,0:T(8,128)(2,1)}, u32[]{:S(2)}, u32[]{:S(2)}) collective-permute-start(bf16[256,768]{1,0:T(8,128)(2,1)} %refs_0_.4), channel_id=1, source_target_pairs={{0,1},{1,0},{2,3},{3,2},{4,5},{5,4},{6,7},{7,6},{8,9},{9,8},{10,11... | collective-permute-start | bytes 1179656 | tf_op jit(solution)/shard_map/ppermute | solution.py:44
  3.7 54.0 %collective-permute-start.15 = (s32[256,2]{0,1:T(2,128)}, s32[256,2]{0,1:T(2,128)}, u32[]{:S(2)}, u32[]{:S(2)}) collective-permute-start(s32[256,2]{0,1:T(2,128)} %param.28), channel_id=1, source_target_pairs={{0,16},{4,20},{8,24},{12,28},{16,0},{20,4},{24,8},{28,12},{1,17},{... | collective-permute-start | bytes 6152 | tf_op jit(solution)/shard_map/ppermute | solution.py:44
  8.0 10.4 %collective-permute-start.3 = (bf16[96,768]{1,0:T(8,128)(2,1)}, bf16[96,768]{1,0:T(8,128)(2,1)}, u32[]{:S(2)}, u32[]{:S(2)}) collective-permute-start(bf16[96,768]{1,0:T(8,128)(2,1)} %pack_weights.1.refs_0_), channel_id=1, source_target_pairs={{0,16},{4,20},{8,24},{12,28},{16,0},{20,4},{24,8},{28,12},{1,17},{... | collective-permute-start | bytes 442376 | tf_op jit(solution)/shard_map/ppermute | solution.py:44
  20.0 15.9 %collective-permute-start.6 = (bf16[192,768]{1,0:T(8,128)(2,1)}, bf16[192,768]{1,0:T(8,128)(2,1)}, u32[]{:S(2)}, u32[]{:S(2)}) collective-permute-start(bf16[192,768]{1,0:T(8,128)(2,1)} %pair_up.1.refs_6_), channel_id=1, source_target_pairs={{0,12},{4,8},{8,4},{12,0},{16,28},{20,24},{24,20},{28,16},{1,13},{... | collective-permute-start | bytes 884744 | tf_op jit(solution)/shard_map/ppermute | solution.py:44
  20.0 15.9 %collective-permute-start.5 = (bf16[192,768]{1,0:T(8,128)(2,1)}, bf16[192,768]{1,0:T(8,128)(2,1)}, u32[]{:S(2)}, u32[]{:S(2)}) collective-permute-start(bf16[192,768]{1,0:T(8,128)(2,1)} %pair_up.1.refs_6_), channel_id=1, source_target_pairs={{0,8},{4,12},{8,0},{12,4},{16,24},{20,28},{24,16},{28,20},{1,9},{5... | collective-permute-start | bytes 884744 | tf_op jit(solution)/shard_map/ppermute | solution.py:44
  23.0 13.0 %collective-permute-start.4 = (bf16[192,768]{1,0:T(8,128)(2,1)}, bf16[192,768]{1,0:T(8,128)(2,1)}, u32[]{:S(2)}, u32[]{:S(2)}) collective-permute-start(bf16[192,768]{1,0:T(8,128)(2,1)} %pair_up.1.refs_6_), channel_id=1, source_target_pairs={{0,4},{4,0},{8,12},{12,8},{16,20},{20,16},{24,28},{28,24},{1,5},{5... | collective-permute-start | bytes 884744 | tf_op jit(solution)/shard_map/ppermute | solution.py:44
  23.5 12.4 %collective-permute-start.2 = (bf16[256,768]{1,0:T(8,128)(2,1)}, bf16[256,768]{1,0:T(8,128)(2,1)}, u32[]{:S(2)}, u32[]{:S(2)}) collective-permute-start(bf16[256,768]{1,0:T(8,128)(2,1)} %collective-permute-done.1.refs_3_.refs_4_), channel_id=1, source_target_pairs={{0,1},{1,0},{2,3},{3,2},{4,5},{5,4},{6,7},{7,6},{8,9},{9,8},{10,11... | collective-permute-start | bytes 1179656 | tf_op jit(solution)/shard_map/ppermute | solution.py:44
  41.2 16.4 %collective-permute-start.11 = (bf16[192,768]{1,0:T(8,128)(2,1)}, bf16[192,768]{1,0:T(8,128)(2,1)}, u32[]{:S(2)}, u32[]{:S(2)}) collective-permute-start(bf16[192,768]{1,0:T(8,128)(2,1)} %get-tuple-element.115.refs_8_.refs_12_), channel_id=1, source_target_pairs={{0,2},{1,3},{2,0},{3,1},{4,6},{5,7},{6,4},{7,5},{8,10},{9,11},{10,... | collective-permute-start | bytes 884744 | tf_op jit(solution)/shard_map/ppermute | solution.py:44
  43.2 23.6 %collective-permute-start.13 = (bf16[256,768]{1,0:T(8,128)(2,1)}, bf16[256,768]{1,0:T(8,128)(2,1)}, u32[]{:S(2)}, u32[]{:S(2)}) collective-permute-start(bf16[256,768]{1,0:T(8,128)(2,1)} %get-tuple-element.116), channel_id=1, source_target_pairs={{0,16},{4,20},{8,24},{12,28},{16,0},{20,4},{24,8},{28,12},{1,17},{... | collective-permute-start | bytes 1179656 | tf_op jit(solution)/shard_map/ppermute | solution.py:44
  45.6 21.3 %collective-permute-start.10 = (bf16[192,768]{1,0:T(8,128)(2,1)}, bf16[192,768]{1,0:T(8,128)(2,1)}, u32[]{:S(2)}, u32[]{:S(2)}) collective-permute-start(bf16[192,768]{1,0:T(8,128)(2,1)} %get-tuple-element.115.refs_8_.refs_12_), channel_id=1, source_target_pairs={{0,1},{1,0},{2,3},{3,2},{4,5},{5,4},{6,7},{7,6},{8,9},{9,8},{10,11... | collective-permute-start | bytes 884744 | tf_op jit(solution)/shard_map/ppermute | solution.py:44
  57.6 9.3 %collective-permute-start.12 = (bf16[192,768]{1,0:T(8,128)(2,1)}, bf16[192,768]{1,0:T(8,128)(2,1)}, u32[]{:S(2)}, u32[]{:S(2)}) collective-permute-start(bf16[192,768]{1,0:T(8,128)(2,1)} %collective-permute-done.11.refs_10_.refs_14_), channel_id=1, source_target_pairs={{0,1},{1,0},{2,3},{3,2},{4,5},{5,4},{6,7},{7,6},{8,9},{9,8},{10,11... | collective-permute-start | bytes 884744 | tf_op jit(solution)/shard_map/ppermute | solution.py:44
  58.4 6.6 %collective-permute-start.8 = (bf16[256,192]{1,0:T(8,128)(2,1)}, bf16[256,192]{1,0:T(8,128)(2,1)}, u32[]{:S(2)}, u32[]{:S(2)}) collective-permute-start(bf16[256,192]{1,0:T(8,128)(2,1)} %get-tuple-element.113), channel_id=1, source_target_pairs={{0,2},{1,3},{2,0},{3,1},{4,6},{5,7},{6,4},{7,5},{8,10},{9,11},{10,... | collective-permute-start | bytes 294920 | tf_op jit(solution)/shard_map/ppermute | solution.py:44
  59.9 7.0 %collective-permute-start.9 = (bf16[256,192]{1,0:T(8,128)(2,1)}, bf16[256,192]{1,0:T(8,128)(2,1)}, u32[]{:S(2)}, u32[]{:S(2)}) collective-permute-start(bf16[256,192]{1,0:T(8,128)(2,1)} %get-tuple-element.114), channel_id=1, source_target_pairs={{0,3},{1,2},{2,1},{3,0},{4,7},{5,6},{6,5},{7,4},{8,11},{9,10},{10,... | collective-permute-start | bytes 294920 | tf_op jit(solution)/shard_map/ppermute | solution.py:44
  70.7 21.1 %collective-permute-start.14 = (bf16[256,768]{1,0:T(8,128)(2,1)}, bf16[256,768]{1,0:T(8,128)(2,1)}, u32[]{:S(2)}, u32[]{:S(2)}) collective-permute-start(bf16[256,768]{1,0:T(8,128)(2,1)} %get-tuple-element.118.refs_4_.refs_6_), channel_id=1, source_target_pairs={{0,16},{4,20},{8,24},{12,28},{16,0},{20,4},{24,8},{28,12},{1,17},{... | collective-permute-start | bytes 1179656 | tf_op jit(solution)/shard_map/ppermute | solution.py:44
  77.2 14.6 %collective-permute-start.16 = (bf16[256,768]{1,0:T(8,128)(2,1)}, bf16[256,768]{1,0:T(8,128)(2,1)}, u32[]{:S(2)}, u32[]{:S(2)}) collective-permute-start(bf16[256,768]{1,0:T(8,128)(2,1)} %get-tuple-element.119), channel_id=1, source_target_pairs={{0,4},{4,0},{8,12},{12,8},{16,20},{20,16},{24,28},{28,24},{1,5},{5... | collective-permute-start | bytes 1179656 | tf_op jit(solution)/shard_map/ppermute | solution.py:44
  78.7 19.4 %collective-permute-start.17 = (bf16[256,768]{1,0:T(8,128)(2,1)}, bf16[256,768]{1,0:T(8,128)(2,1)}, u32[]{:S(2)}, u32[]{:S(2)}) collective-permute-start(bf16[256,768]{1,0:T(8,128)(2,1)} %get-tuple-element.120), channel_id=1, source_target_pairs={{0,8},{4,12},{8,0},{12,4},{16,24},{20,28},{24,16},{28,20},{1,9},{5... | collective-permute-start | bytes 1179656 | tf_op jit(solution)/shard_map/ppermute | solution.py:44
  78.7 21.8 %collective-permute-start.22 = (bf16[128,768]{1,0:T(8,128)(2,1)}, bf16[128,768]{1,0:T(8,128)(2,1)}, u32[]{:S(2)}, u32[]{:S(2)}) collective-permute-start(bf16[128,768]{1,0:T(8,128)(2,1)} %get-tuple-element.128), channel_id=1, source_target_pairs={{0,4},{4,0},{8,12},{12,8},{16,20},{20,16},{24,28},{28,24},{1,5},{5... | collective-permute-start | bytes 589832 | tf_op jit(solution)/shard_map/ppermute | solution.py:44
  79.4 22.9 %collective-permute-start.23 = (bf16[128,768]{1,0:T(8,128)(2,1)}, bf16[128,768]{1,0:T(8,128)(2,1)}, u32[]{:S(2)}, u32[]{:S(2)}) collective-permute-start(bf16[128,768]{1,0:T(8,128)(2,1)} %get-tuple-element.129), channel_id=1, source_target_pairs={{0,8},{4,12},{8,0},{12,4},{16,24},{20,28},{24,16},{28,20},{1,9},{5... | collective-permute-start | bytes 589832 | tf_op jit(solution)/shard_map/ppermute | solution.py:44
  91.8 14.5 %collective-permute-start.24 = (bf16[128,768]{1,0:T(8,128)(2,1)}, bf16[128,768]{1,0:T(8,128)(2,1)}, u32[]{:S(2)}, u32[]{:S(2)}) collective-permute-start(bf16[128,768]{1,0:T(8,128)(2,1)} %get-tuple-element.130), channel_id=1, source_target_pairs={{0,12},{4,8},{8,4},{12,0},{16,28},{20,24},{24,20},{28,16},{1,13},{... | collective-permute-start | bytes 589832 | tf_op jit(solution)/shard_map/ppermute | solution.py:44
  91.8 27.3 %collective-permute-start.21 = (bf16[256,768]{1,0:T(8,128)(2,1)}, bf16[256,768]{1,0:T(8,128)(2,1)}, u32[]{:S(2)}, u32[]{:S(2)}) collective-permute-start(bf16[256,768]{1,0:T(8,128)(2,1)} %get-tuple-element.126), channel_id=1, source_target_pairs={{0,12},{4,8},{8,4},{12,0},{16,28},{20,24},{24,20},{28,16},{1,13},{... | collective-permute-start | bytes 1179656 | tf_op jit(solution)/shard_map/ppermute | solution.py:44
  100.2 18.9 %collective-permute-start.18 = (bf16[128,768]{1,0:T(8,128)(2,1)}, bf16[128,768]{1,0:T(8,128)(2,1)}, u32[]{:S(2)}, u32[]{:S(2)}) collective-permute-start(bf16[128,768]{1,0:T(8,128)(2,1)} %get-tuple-element.122), channel_id=1, source_target_pairs={{0,4},{4,0},{8,12},{12,8},{16,20},{20,16},{24,28},{28,24},{1,5},{5... | collective-permute-start | bytes 589832 | tf_op jit(solution)/shard_map/ppermute | solution.py:44
  100.5 18.7 %collective-permute-start.19 = (bf16[128,768]{1,0:T(8,128)(2,1)}, bf16[128,768]{1,0:T(8,128)(2,1)}, u32[]{:S(2)}, u32[]{:S(2)}) collective-permute-start(bf16[128,768]{1,0:T(8,128)(2,1)} %get-tuple-element.123), channel_id=1, source_target_pairs={{0,8},{4,12},{8,0},{12,4},{16,24},{20,28},{24,16},{28,20},{1,9},{5... | collective-permute-start | bytes 589832 | tf_op jit(solution)/shard_map/ppermute | solution.py:44
  102.3 19.5 %collective-permute-start.20 = (bf16[128,768]{1,0:T(8,128)(2,1)}, bf16[128,768]{1,0:T(8,128)(2,1)}, u32[]{:S(2)}, u32[]{:S(2)}) collective-permute-start(bf16[128,768]{1,0:T(8,128)(2,1)} %get-tuple-element.124), channel_id=1, source_target_pairs={{0,12},{4,8},{8,4},{12,0},{16,28},{20,24},{24,20},{28,16},{1,13},{... | collective-permute-start | bytes 589832 | tf_op jit(solution)/shard_map/ppermute | solution.py:44
  139.7 15.5 %collective-permute-start.28 = (bf16[128,896]{1,0:T(8,128)(2,1)}, bf16[128,896]{1,0:T(8,128)(2,1)}, u32[]{:S(2)}, u32[]{:S(2)}) collective-permute-start(bf16[128,896]{1,0:T(8,128)(2,1)} %get-tuple-element.142), channel_id=1, source_target_pairs={{0,4},{4,0},{8,12},{12,8},{16,20},{20,16},{24,28},{28,24},{1,5},{5... | collective-permute-start | bytes 688136 | tf_op jit(solution)/shard_map/ppermute | solution.py:44
  141.5 13.7 %collective-permute-start.29 = (bf16[128,896]{1,0:T(8,128)(2,1)}, bf16[128,896]{1,0:T(8,128)(2,1)}, u32[]{:S(2)}, u32[]{:S(2)}) collective-permute-start(bf16[128,896]{1,0:T(8,128)(2,1)} %get-tuple-element.143), channel_id=1, source_target_pairs={{0,8},{4,12},{8,0},{12,4},{16,24},{20,28},{24,16},{28,20},{1,9},{5... | collective-permute-start | bytes 688136 | tf_op jit(solution)/shard_map/ppermute | solution.py:44
  141.6 13.7 %collective-permute-start.30 = (bf16[128,896]{1,0:T(8,128)(2,1)}, bf16[128,896]{1,0:T(8,128)(2,1)}, u32[]{:S(2)}, u32[]{:S(2)}) collective-permute-start(bf16[128,896]{1,0:T(8,128)(2,1)} %get-tuple-element.144), channel_id=1, source_target_pairs={{0,12},{4,8},{8,4},{12,0},{16,28},{20,24},{24,20},{28,16},{1,13},{... | collective-permute-start | bytes 688136 | tf_op jit(solution)/shard_map/ppermute | solution.py:44
  158.0 23.1 %collective-permute-start.31 = (bf16[128,896]{1,0:T(8,128)(2,1)}, bf16[128,896]{1,0:T(8,128)(2,1)}, u32[]{:S(2)}, u32[]{:S(2)}) collective-permute-start(bf16[128,896]{1,0:T(8,128)(2,1)} %get-tuple-element.148), channel_id=1, source_target_pairs={{0,4},{4,0},{8,12},{12,8},{16,20},{20,16},{24,28},{28,24},{1,5},{5... | collective-permute-start | bytes 688136 | tf_op jit(solution)/shard_map/ppermute | solution.py:44
  159.8 21.4 %collective-permute-start.32 = (bf16[128,896]{1,0:T(8,128)(2,1)}, bf16[128,896]{1,0:T(8,128)(2,1)}, u32[]{:S(2)}, u32[]{:S(2)}) collective-permute-start(bf16[128,896]{1,0:T(8,128)(2,1)} %get-tuple-element.149), channel_id=1, source_target_pairs={{0,8},{4,12},{8,0},{12,4},{16,24},{20,28},{24,16},{28,20},{1,9},{5... | collective-permute-start | bytes 688136 | tf_op jit(solution)/shard_map/ppermute | solution.py:44
  159.8 21.4 %collective-permute-start.33 = (bf16[128,896]{1,0:T(8,128)(2,1)}, bf16[128,896]{1,0:T(8,128)(2,1)}, u32[]{:S(2)}, u32[]{:S(2)}) collective-permute-start(bf16[128,896]{1,0:T(8,128)(2,1)} %get-tuple-element.150), channel_id=1, source_target_pairs={{0,12},{4,8},{8,4},{12,0},{16,28},{20,24},{24,20},{28,16},{1,13},{... | collective-permute-start | bytes 688136 | tf_op jit(solution)/shard_map/ppermute | solution.py:44
  161.5 20.8 %collective-permute-start.34 = (bf16[256,896]{1,0:T(8,128)(2,1)}, bf16[256,896]{1,0:T(8,128)(2,1)}, u32[]{:S(2)}, u32[]{:S(2)}) collective-permute-start(bf16[256,896]{1,0:T(8,128)(2,1)} %get-tuple-element.151), channel_id=1, source_target_pairs={{0,16},{4,20},{8,24},{12,28},{16,0},{20,4},{24,8},{28,12},{1,17},{... | collective-permute-start | bytes 1376264 | tf_op jit(solution)/shard_map/ppermute | solution.py:44
  189.2 9.2 %collective-permute-start.38 = (bf16[3072,768]{1,0:T(8,128)(2,1)}, bf16[3072,768]{1,0:T(8,128)(2,1)}, u32[]{:S(2)}, u32[]{:S(2)}) collective-permute-start(bf16[3072,768]{1,0:T(8,128)(2,1)} %get-tuple-element.165), channel_id=1, source_target_pairs={{0,1},{1,0},{2,3},{3,2},{4,5},{5,4},{6,7},{7,6},{8,9},{9,8},{10,11... | collective-permute-start | bytes 14155784 | tf_op jit(solution)/shard_map/ppermute | solution.py:44
  189.2 9.1 %collective-permute-start.39 = (bf16[384,768]{1,0:T(8,128)(2,1)}, bf16[384,768]{1,0:T(8,128)(2,1)}, u32[]{:S(2)}, u32[]{:S(2)}) collective-permute-start(bf16[384,768]{1,0:T(8,128)(2,1)} %get-tuple-element.167), channel_id=1, source_target_pairs={{0,1},{1,0},{2,3},{3,2},{4,5},{5,4},{6,7},{7,6},{8,9},{9,8},{10,11... | collective-permute-start | bytes 1769480 | tf_op jit(solution)/shard_map/ppermute | solution.py:44
  189.7 6.7 %collective-permute-start.36 = (bf16[256,192]{1,0:T(8,128)(2,1)}, bf16[256,192]{1,0:T(8,128)(2,1)}, u32[]{:S(2)}, u32[]{:S(2)}) collective-permute-start(bf16[256,192]{1,0:T(8,128)(2,1)} %get-tuple-element.163), channel_id=1, source_target_pairs={{0,2},{1,3},{2,0},{3,1},{4,6},{5,7},{6,4},{7,5},{8,10},{9,11},{10,... | collective-permute-start | bytes 294920 | tf_op jit(solution)/shard_map/ppermute | solution.py:44
  191.2 6.2 %collective-permute-start.37 = (bf16[256,192]{1,0:T(8,128)(2,1)}, bf16[256,192]{1,0:T(8,128)(2,1)}, u32[]{:S(2)}, u32[]{:S(2)}) collective-permute-start(bf16[256,192]{1,0:T(8,128)(2,1)} %get-tuple-element.164), channel_id=1, source_target_pairs={{0,3},{1,2},{2,1},{3,0},{4,7},{5,6},{6,5},{7,4},{8,11},{9,10},{10,... | collective-permute-start | bytes 294920 | tf_op jit(solution)/shard_map/ppermute | solution.py:44
  203.2 26.2 %collective-permute-start.40 = (bf16[704,768]{1,0:T(8,128)(2,1)}, bf16[704,768]{1,0:T(8,128)(2,1)}, u32[]{:S(2)}, u32[]{:S(2)}) collective-permute-start(bf16[704,768]{1,0:T(8,128)(2,1)} %get-tuple-element.169.refs_11_), channel_id=1, source_target_pairs={{0,2},{1,3},{2,0},{3,1},{4,6},{5,7},{6,4},{7,5},{8,10},{9,11},{10,... | collective-permute-start | bytes 3244040 | tf_op jit(solution)/shard_map/ppermute | solution.py:44
  204.7 21.3 %collective-permute-start.25 = (bf16[256,768]{1,0:T(8,128)(2,1)}, bf16[256,768]{1,0:T(8,128)(2,1)}, u32[]{:S(2)}, u32[]{:S(2)}) collective-permute-start(bf16[256,768]{1,0:T(8,128)(2,1)} %get-tuple-element.133), channel_id=1, source_target_pairs={{0,4},{4,0},{8,12},{12,8},{16,20},{20,16},{24,28},{28,24},{1,5},{5... | collective-permute-start | bytes 1179656 | tf_op jit(solution)/shard_map/ppermute | solution.py:44
  206.3 19.6 %collective-permute-start.26 = (bf16[256,768]{1,0:T(8,128)(2,1)}, bf16[256,768]{1,0:T(8,128)(2,1)}, u32[]{:S(2)}, u32[]{:S(2)}) collective-permute-start(bf16[256,768]{1,0:T(8,128)(2,1)} %get-tuple-element.134), channel_id=1, source_target_pairs={{0,8},{4,12},{8,0},{12,4},{16,24},{20,28},{24,16},{28,20},{1,9},{5... | collective-permute-start | bytes 1179656 | tf_op jit(solution)/shard_map/ppermute | solution.py:44
  207.1 18.8 %collective-permute-start.27 = (bf16[256,768]{1,0:T(8,128)(2,1)}, bf16[256,768]{1,0:T(8,128)(2,1)}, u32[]{:S(2)}, u32[]{:S(2)}) collective-permute-start(bf16[256,768]{1,0:T(8,128)(2,1)} %get-tuple-element.135), channel_id=1, source_target_pairs={{0,12},{4,8},{8,4},{12,0},{16,28},{20,24},{24,20},{28,16},{1,13},{... | collective-permute-start | bytes 1179656 | tf_op jit(solution)/shard_map/ppermute | solution.py:44
  236.6 20.6 %collective-permute-start.44 = (bf16[512,768]{1,0:T(8,128)(2,1)}, bf16[512,768]{1,0:T(8,128)(2,1)}, u32[]{:S(2)}, u32[]{:S(2)}) collective-permute-start(bf16[512,768]{1,0:T(8,128)(2,1)} %get-tuple-element.186), channel_id=1, source_target_pairs={{0,1},{1,0},{2,3},{3,2},{4,5},{5,4},{6,7},{7,6},{8,9},{9,8},{10,11... | collective-permute-start | bytes 2359304 | tf_op jit(solution)/shard_map/ppermute | solution.py:44
  236.6 33.2 %collective-permute-start.49 = (bf16[768,768]{1,0:T(8,128)(2,1)}, bf16[768,768]{1,0:T(8,128)(2,1)}, u32[]{:S(2)}, u32[]{:S(2)}) collective-permute-start(bf16[768,768]{1,0:T(8,128)(2,1)} %get-tuple-element.196), channel_id=1, source_target_pairs={{0,2},{1,3},{2,0},{3,1},{4,6},{5,7},{6,4},{7,5},{8,10},{9,11},{10,... | collective-permute-start | bytes 3538952 | tf_op jit(solution)/shard_map/ppermute | solution.py:44
  238.2 10.4 %collective-permute-start.41 = (bf16[224,768]{1,0:T(8,128)(2,1)}, bf16[224,768]{1,0:T(8,128)(2,1)}, u32[]{:S(2)}, u32[]{:S(2)}) collective-permute-start(bf16[224,768]{1,0:T(8,128)(2,1)} %get-tuple-element.181), channel_id=1, source_target_pairs={{0,4},{4,0},{8,12},{12,8},{16,20},{20,16},{24,28},{28,24},{1,5},{5... | collective-permute-start | bytes 1032200 | tf_op jit(solution)/shard_map/ppermute | solution.py:44
  239.9 11.3 %collective-permute-start.42 = (bf16[224,768]{1,0:T(8,128)(2,1)}, bf16[224,768]{1,0:T(8,128)(2,1)}, u32[]{:S(2)}, u32[]{:S(2)}) collective-permute-start(bf16[224,768]{1,0:T(8,128)(2,1)} %get-tuple-element.182), channel_id=1, source_target_pairs={{0,8},{4,12},{8,0},{12,4},{16,24},{20,28},{24,16},{28,20},{1,9},{5... | collective-permute-start | bytes 1032200 | tf_op jit(solution)/shard_map/ppermute | solution.py:44
  240.6 16.6 %collective-permute-start.43 = (bf16[224,768]{1,0:T(8,128)(2,1)}, bf16[224,768]{1,0:T(8,128)(2,1)}, u32[]{:S(2)}, u32[]{:S(2)}) collective-permute-start(bf16[224,768]{1,0:T(8,128)(2,1)} %get-tuple-element.183), channel_id=1, source_target_pairs={{0,12},{4,8},{8,4},{12,0},{16,28},{20,24},{24,20},{28,16},{1,13},{... | collective-permute-start | bytes 1032200 | tf_op jit(solution)/shard_map/ppermute | solution.py:44
  259.5 14.8 %collective-permute-start.48 = (bf16[256,768]{1,0:T(8,128)(2,1)}, bf16[256,768]{1,0:T(8,128)(2,1)}, u32[]{:S(2)}, u32[]{:S(2)}) collective-permute-start(bf16[256,768]{1,0:T(8,128)(2,1)} %get-tuple-element.195), channel_id=1, source_target_pairs={{0,2},{1,3},{2,0},{3,1},{4,6},{5,7},{6,4},{7,5},{8,10},{9,11},{10,... | collective-permute-start | bytes 1179656 | tf_op jit(solution)/shard_map/ppermute | solution.py:44
  260.0 20.5 %collective-permute-start.47 = (bf16[128,768]{1,0:T(8,128)(2,1)}, bf16[128,768]{1,0:T(8,128)(2,1)}, u32[]{:S(2)}, u32[]{:S(2)}) collective-permute-start(bf16[128,768]{1,0:T(8,128)(2,1)} %get-tuple-element.194), channel_id=1, source_target_pairs={{0,16},{4,20},{8,24},{12,28},{16,0},{20,4},{24,8},{28,12},{1,17},{... | collective-permute-start | bytes 589832 | tf_op jit(solution)/shard_map/ppermute | solution.py:44
  264.6 25.9 %collective-permute-start.45 = (bf16[256,768]{1,0:T(8,128)(2,1)}, bf16[256,768]{1,0:T(8,128)(2,1)}, u32[]{:S(2)}, u32[]{:S(2)}) collective-permute-start(bf16[256,768]{1,0:T(8,128)(2,1)} %get-tuple-element.189), channel_id=1, source_target_pairs={{0,16},{4,20},{8,24},{12,28},{16,0},{20,4},{24,8},{28,12},{1,17},{... | collective-permute-start | bytes 1179656 | tf_op jit(solution)/shard_map/ppermute | solution.py:44
  268.3 13.9 %collective-permute-start.46 = (bf16[256,768]{1,0:T(8,128)(2,1)}, bf16[256,768]{1,0:T(8,128)(2,1)}, u32[]{:S(2)}, u32[]{:S(2)}) collective-permute-start(bf16[256,768]{1,0:T(8,128)(2,1)} %add_convert_fusion), channel_id=1, source_target_pairs={{0,2},{1,3},{2,0},{3,1},{4,6},{5,7},{6,4},{7,5},{8,10},{9,11},{10,... | collective-permute-start | bytes 1179656 | tf_op jit(solution)/shard_map/ppermute | solution.py:44
  (7 other events, 31.4 us)
